TPU v7x, 32 devices: a whole 2x2x4 slice. The times are simulated.
32 devices in a mesh: seq: 4 (over x, core), dp: 8 (over z, y).
Axes of the slice: x: 2, y: 2, z: 4, core: 2. Of those that a mesh axis runs over, the one named last changes fastest.
Arguments:
- tokens: bfloat16 [2048, 8, 1024], P('seq', 'dp'), may hold values from -6 to 6
- cotangent: bfloat16 [2048, 8, 1024], P('seq', 'dp'), may hold values from -6 to 6
- norm_attn: bfloat16 [1024], P('dp'), may hold values from 0.25 to 1.75
- w_qkv: bfloat16 [1024, 4096], P('dp'), may hold values from -0.1875 to 0.1875
- w_ba: bfloat16 [1024, 16], P('dp'), may hold values from -0.1875 to 0.1875
- conv_w: bfloat16 [4, 4096], P(None, 'dp'), may hold values from -3 to 3
- a_log: float32 [8], replicated, may hold values from 0 to 2.77
- dt_bias: float32 [8], replicated, may hold values from -6.9 to -2.3
- w_outgate: bfloat16 [1024, 2048], P('dp'), may hold values from -0.1875 to 0.1875
- head_gain: bfloat16 [256], replicated, may hold values from 0.25 to 1.75
- w_out: bfloat16 [2048, 1024], P('dp'), may hold values from -0.1875 to 0.1875
- norm_ffn: bfloat16 [1024], P('dp'), may hold values from 0.25 to 1.75
- w_gate: bfloat16 [1024, 2816], P('dp'), may hold values from -0.1875 to 0.1875
- w_up: bfloat16 [1024, 2816], P('dp'), may hold values from -0.1875 to 0.1875
- w_down: bfloat16 [2816, 1024], P('dp'), may hold values from -0.15625 to 0.15625
Outputs:
- block_out: bfloat16 [2048, 8, 1024], P('seq', 'dp')
- grad_tokens: bfloat16 [2048, 8, 1024], P('seq', 'dp')
- grad_norm_attn: float32 [1024], P('dp')
- grad_w_qkv: float32 [1024, 4096], P('dp')
- grad_w_ba: float32 [1024, 16], P('dp')
- grad_conv_w: float32 [4, 4096], P(None, 'dp')
- grad_a_log: float32 [8], replicated
- grad_dt_bias: float32 [8], replicated
- grad_w_outgate: float32 [1024, 2048], P('dp')
- grad_head_gain: float32 [256], replicated
- grad_w_out: float32 [2048, 1024], P('dp')
- grad_norm_ffn: float32 [1024], P('dp')
- grad_w_gate: float32 [1024, 2816], P('dp')
- grad_w_up: float32 [1024, 2816], P('dp')
- grad_w_down: float32 [2816, 1024], P('dp')
All inputs are finite; a program needn't handle non-finite values.
Results may differ from a plain program's by a relative error of at most 0.019.
Values may be sent and summed in bfloat16 or wider, within the bound.
No kernel may reach another device: no remote copies, remote signals or barrier semaphores. Data moves between devices by JAX's collectives and lax.ppermute only.
A program may use at most 320 MiB of HBM per device.

v0:
```python
import jax
import jax.numpy as jnp
from jax import lax
from jax.sharding import PartitionSpec as P

DK = 128
DV = 256
CONV = 4
GROUP = 64


epsilon = 1e-06
highest = lax.Precision.HIGHEST


def by_weight(left, right):
    return jnp.dot(left, right, preferred_element_type=jnp.float32)


def by_transpose(left, right):
    return lax.dot_general(
        left, right, (((1,), (1,)), ((), ())), preferred_element_type=jnp.float32
    )


def over_rows(left, right):
    return lax.dot_general(
        left, right, (((0,), (0,)), ((), ())), preferred_element_type=jnp.float32
    )


def row_norm(values, gain):
    inverse = lax.rsqrt(jnp.mean(values * values, axis=-1, keepdims=True) + epsilon)
    return (values * inverse * gain, inverse)


def norm_back(values, inverse, gain, grad_out):
    scaled = grad_out * gain
    grad_in = inverse * scaled - values * inverse * inverse * inverse * jnp.mean(
        scaled * values, axis=-1, keepdims=True
    )
    grad_gain = jnp.sum(grad_out * values * inverse, axis=tuple(range(values.ndim - 1)))
    return (grad_in, grad_gain)


def delta_mixer(projected, rates, conv_part, decay_log, decay_bias):
    length, head_count, row_width = projected.shape
    kernel = conv_part.reshape(CONV, head_count, row_width)
    padded = jnp.pad(projected, ((CONV - 1, 0), (0, 0), (0, 0)))
    summed = padded[0:length] * kernel[0]
    for offset in range(1, CONV):
        summed = summed + padded[offset : offset + length] * kernel[offset]
    active = jax.nn.silu(summed)
    queries = active[..., :DK]
    key_rows = active[..., DK : 2 * DK]
    values = active[..., 2 * DK :]
    queries = (
        queries
        * lax.rsqrt(jnp.sum(queries * queries, axis=-1, keepdims=True) + epsilon)
        * DK ** (-0.5)
    )
    key_rows = key_rows * lax.rsqrt(jnp.sum(key_rows * key_rows, axis=-1, keepdims=True) + epsilon)
    strength = jax.nn.sigmoid(rates[..., 0])
    decay = -jnp.exp(decay_log) * jax.nn.softplus(rates[..., 1] + decay_bias)
    blocks = length // GROUP

    def to_blocks(array):
        return jnp.swapaxes(array.reshape(blocks, GROUP, head_count, -1), 1, 2)

    query_blocks = to_blocks(queries)
    key_blocks = to_blocks(key_rows)
    value_blocks = to_blocks(values)
    strength_blocks = to_blocks(strength[..., None])[..., 0]
    cumulative = jnp.cumsum(to_blocks(decay[..., None])[..., 0], axis=-1)
    final_decay = cumulative[..., -1:]
    positions = jnp.arange(GROUP)
    strictly = positions[:, None] > positions[None, :]
    through = positions[:, None] >= positions[None, :]
    spread = cumulative[..., :, None] - cumulative[..., None, :]
    strict_fade = jnp.where(strictly, jnp.exp(jnp.where(strictly, spread, 0.0)), 0.0)
    full_fade = jnp.where(through, jnp.exp(jnp.where(through, spread, 0.0)), 0.0)
    key_dots = jnp.einsum("bhck,bhek->bhce", key_blocks, key_blocks, precision=highest)
    negated = -(strength_blocks[..., None] * strict_fade * key_dots)
    identity = jnp.eye(GROUP, dtype=jnp.float32)
    inverse = identity + negated
    power = negated
    for section in range(1, (GROUP - 1).bit_length()):
        power = jnp.einsum("bhce,bhef->bhcf", power, power, precision=highest)
        inverse = inverse + jnp.einsum("bhce,bhef->bhcf", inverse, power, precision=highest)
    right_side = jnp.concatenate(
        [
            strength_blocks[..., None] * value_blocks,
            (strength_blocks * jnp.exp(cumulative))[..., None] * key_blocks,
        ],
        axis=-1,
    )
    solved = jnp.einsum("bhce,bhef->bhcf", inverse, right_side, precision=highest)
    updates = solved[..., :DV]
    key_weights = solved[..., DV:]
    key_faded = key_blocks * jnp.exp(final_decay - cumulative)[..., None]

    def advance(state, block):
        block_updates, block_weights, block_faded, block_final = block
        corrected = block_updates - jnp.einsum(
            "hck,hvk->hcv", block_weights, state, precision=highest
        )
        following = state * jnp.exp(block_final)[:, :, None] + jnp.einsum(
            "hcv,hck->hvk", corrected, block_faded, precision=highest
        )
        return (following, (corrected, state))

    start_state = jnp.zeros((head_count, DV, DK), jnp.float32)
    unused, (corrected_all, states) = lax.scan(
        advance, start_state, (updates, key_weights, key_faded, final_decay)
    )
    query_dots = (
        jnp.einsum("bhck,bhek->bhce", query_blocks, key_blocks, precision=highest) * full_fade
    )
    result = jnp.einsum(
        "bhck,bhvk->bhcv", query_blocks * jnp.exp(cumulative)[..., None], states, precision=highest
    )
    result = result + jnp.einsum("bhce,bhev->bhcv", query_dots, corrected_all, precision=highest)
    return jnp.swapaxes(result, 1, 2).reshape(length, head_count, DV)


def per_device(
    tokens,
    cotangent,
    norm_attn,
    w_qkv,
    w_ba,
    conv_w,
    a_log,
    dt_bias,
    w_outgate,
    head_gain,
    w_out,
    norm_ffn,
    w_gate,
    w_up,
    w_down,
):
    gathered = (
        lax.all_gather(norm_attn, "dp", axis=0, tiled=True),
        lax.all_gather(w_qkv, "dp", axis=0, tiled=True),
        lax.all_gather(w_ba, "dp", axis=0, tiled=True),
        lax.all_gather(conv_w, "dp", axis=1, tiled=True),
        lax.all_gather(w_outgate, "dp", axis=0, tiled=True),
        lax.all_gather(w_out, "dp", axis=0, tiled=True),
        lax.all_gather(norm_ffn, "dp", axis=0, tiled=True),
        lax.all_gather(w_gate, "dp", axis=0, tiled=True),
        lax.all_gather(w_up, "dp", axis=0, tiled=True),
        lax.all_gather(w_down, "dp", axis=0, tiled=True),
    )
    rows = tokens[:, 0, :].astype(jnp.float32)
    count = rows.shape[0]
    head_count = a_log.shape[0]
    local_heads = head_count // lax.axis_size("seq")
    first_head = lax.axis_index("seq") * local_heads
    normed_one, inverse_one = row_norm(rows, gathered[0].astype(jnp.float32))
    normed_one = normed_one.astype(jnp.bfloat16)
    projected = (
        by_weight(normed_one, gathered[1]).astype(jnp.bfloat16).reshape(count, head_count, -1)
    )
    row_width = projected.shape[2]
    rates = by_weight(normed_one, gathered[2]).astype(jnp.bfloat16).reshape(count, head_count, 2)
    out_gate = by_weight(normed_one, gathered[4]).reshape(count, head_count, DV)
    head_proj, head_rates = (
        lax.all_to_all(projected, "seq", split_axis=1, concat_axis=0, tiled=True),
        lax.all_to_all(rates, "seq", split_axis=1, concat_axis=0, tiled=True),
    )
    conv_part = lax.dynamic_slice_in_dim(
        gathered[3].astype(jnp.float32).reshape(CONV, head_count, row_width),
        first_head,
        local_heads,
        1,
    ).reshape(CONV, local_heads * row_width)
    decay_part = lax.dynamic_slice_in_dim(a_log, first_head, local_heads, 0)
    bias_part = lax.dynamic_slice_in_dim(dt_bias, first_head, local_heads, 0)
    mixed, mixer_back = jax.vjp(
        delta_mixer,
        head_proj.astype(jnp.float32),
        head_rates.astype(jnp.float32),
        conv_part,
        decay_part,
        bias_part,
    )
    token_mixed = lax.all_to_all(
        mixed.astype(jnp.bfloat16), "seq", split_axis=0, concat_axis=1, tiled=True
    ).astype(jnp.float32)
    head_normed, head_inverse = row_norm(token_mixed, head_gain.astype(jnp.float32))
    sig_gate = jax.nn.sigmoid(out_gate)
    silu_gate = out_gate * sig_gate
    gated = (head_normed * silu_gate).reshape(count, -1).astype(jnp.bfloat16)
    after_mix = rows + by_weight(gated, gathered[5])
    normed_two, inverse_two = row_norm(after_mix, gathered[6].astype(jnp.float32))
    normed_two = normed_two.astype(jnp.bfloat16)
    gate_pre = by_weight(normed_two, gathered[7])
    up_pre = by_weight(normed_two, gathered[8])
    sig_ffn = jax.nn.sigmoid(gate_pre)
    hidden = (gate_pre * sig_ffn * up_pre).astype(jnp.bfloat16)
    result = after_mix + by_weight(hidden, gathered[9])
    incoming = cotangent[:, 0, :]
    cot_rows = incoming.astype(jnp.float32)
    grad_down = over_rows(hidden, incoming)
    grad_hidden = by_transpose(incoming, gathered[9])
    grad_gate_pre = (grad_hidden * up_pre * sig_ffn * (1.0 + gate_pre * (1.0 - sig_ffn))).astype(
        jnp.bfloat16
    )
    grad_up_pre = (grad_hidden * gate_pre * sig_ffn).astype(jnp.bfloat16)
    grad_gate = over_rows(normed_two, grad_gate_pre)
    grad_up = over_rows(normed_two, grad_up_pre)
    grad_normed_two = by_transpose(grad_gate_pre, gathered[7]) + by_transpose(
        grad_up_pre, gathered[8]
    )
    back_two, grad_norm_ffn = norm_back(
        after_mix, inverse_two, gathered[6].astype(jnp.float32), grad_normed_two
    )
    grad_after = cot_rows + back_two
    grad_branch = grad_after.astype(jnp.bfloat16)
    grad_out = over_rows(gated, grad_branch)
    grad_gated = by_transpose(grad_branch, gathered[5]).reshape(count, head_count, DV)
    grad_outgate_pre = (
        (grad_gated * head_normed * sig_gate * (1.0 + out_gate * (1.0 - sig_gate)))
        .reshape(count, -1)
        .astype(jnp.bfloat16)
    )
    back_head, grad_head_gain = norm_back(
        token_mixed, head_inverse, head_gain.astype(jnp.float32), grad_gated * silu_gate
    )
    grad_heads = lax.all_to_all(
        back_head.astype(jnp.bfloat16), "seq", split_axis=1, concat_axis=0, tiled=True
    )
    grad_proj_h, grad_rates_h, grad_conv_part, grad_decay, grad_bias = mixer_back(
        grad_heads.astype(jnp.float32)
    )
    grad_proj, grad_rates = (
        lax.all_to_all(
            grad_proj_h.astype(jnp.bfloat16), "seq", split_axis=0, concat_axis=1, tiled=True
        ),
        lax.all_to_all(
            grad_rates_h.astype(jnp.bfloat16), "seq", split_axis=0, concat_axis=1, tiled=True
        ),
    )
    grad_proj = grad_proj.reshape(count, -1)
    grad_rates = grad_rates.reshape(count, -1)
    grad_qkv = over_rows(normed_one, grad_proj)
    grad_ba = over_rows(normed_one, grad_rates)
    grad_outgate = over_rows(normed_one, grad_outgate_pre)
    grad_normed_one = (
        by_transpose(grad_proj, gathered[1])
        + by_transpose(grad_rates, gathered[2])
        + by_transpose(grad_outgate_pre, gathered[4])
    )
    back_one, grad_norm_attn = norm_back(
        rows, inverse_one, gathered[0].astype(jnp.float32), grad_normed_one
    )
    grad_rows = (grad_after + back_one).astype(jnp.bfloat16).reshape(count, 1, -1)
    grad_conv = lax.dynamic_update_slice_in_dim(
        jnp.zeros((CONV, head_count, row_width), jnp.float32),
        grad_conv_part.reshape(CONV, local_heads, row_width),
        first_head,
        1,
    ).reshape(CONV, -1)
    decay_full = lax.dynamic_update_slice_in_dim(
        jnp.zeros((head_count,), jnp.float32), grad_decay, first_head, 0
    )
    bias_full = lax.dynamic_update_slice_in_dim(
        jnp.zeros((head_count,), jnp.float32), grad_bias, first_head, 0
    )
    small_terms = jnp.concatenate([decay_full, bias_full, grad_head_gain])
    small_rows = jnp.broadcast_to(small_terms[None, :], (lax.axis_size("dp"), small_terms.shape[0]))
    shards = (
        lax.psum_scatter(grad_norm_attn, "dp", scatter_dimension=0, tiled=True),
        lax.psum_scatter(grad_qkv, "dp", scatter_dimension=0, tiled=True),
        lax.psum_scatter(grad_ba, "dp", scatter_dimension=0, tiled=True),
        lax.psum_scatter(grad_conv, "dp", scatter_dimension=1, tiled=True),
        lax.psum_scatter(grad_outgate, "dp", scatter_dimension=0, tiled=True),
        lax.psum_scatter(grad_out, "dp", scatter_dimension=0, tiled=True),
        lax.psum_scatter(grad_norm_ffn, "dp", scatter_dimension=0, tiled=True),
        lax.psum_scatter(grad_gate, "dp", scatter_dimension=0, tiled=True),
        lax.psum_scatter(grad_up, "dp", scatter_dimension=0, tiled=True),
        lax.psum_scatter(grad_down, "dp", scatter_dimension=0, tiled=True),
        lax.psum_scatter(small_rows, "dp", scatter_dimension=0, tiled=True),
    )
    totals = (
        lax.psum(shards[0].astype(jnp.bfloat16), "seq").astype(jnp.float32),
        lax.psum(shards[1].astype(jnp.bfloat16), "seq").astype(jnp.float32),
        lax.psum(shards[2].astype(jnp.bfloat16), "seq").astype(jnp.float32),
        lax.psum(shards[3].astype(jnp.bfloat16), "seq").astype(jnp.float32),
        lax.psum(shards[4].astype(jnp.bfloat16), "seq").astype(jnp.float32),
        lax.psum(shards[5].astype(jnp.bfloat16), "seq").astype(jnp.float32),
        lax.psum(shards[6].astype(jnp.bfloat16), "seq").astype(jnp.float32),
        lax.psum(shards[7].astype(jnp.bfloat16), "seq").astype(jnp.float32),
        lax.psum(shards[8].astype(jnp.bfloat16), "seq").astype(jnp.float32),
        lax.psum(shards[9].astype(jnp.bfloat16), "seq").astype(jnp.float32),
        lax.psum(shards[10].astype(jnp.bfloat16), "seq").astype(jnp.float32),
    )
    small_total = totals[10][0]
    return (
        result.astype(jnp.bfloat16).reshape(count, 1, -1),
        grad_rows,
        totals[0],
        totals[1],
        totals[2],
        totals[3],
        small_total[:head_count],
        small_total[head_count : 2 * head_count],
        totals[4],
        small_total[2 * head_count :],
        totals[5],
        totals[6],
        totals[7],
        totals[8],
        totals[9],
    )


def solution(mesh):
    return jax.shard_map(
        per_device,
        mesh=mesh,
        in_specs=(
            P("seq", "dp", None),
            P("seq", "dp", None),
            P("dp"),
            P("dp", None),
            P("dp", None),
            P(None, "dp"),
            P(),
            P(),
            P("dp", None),
            P(),
            P("dp", None),
            P("dp"),
            P("dp", None),
            P("dp", None),
            P("dp", None),
        ),
        out_specs=(
            P("seq", "dp", None),
            P("seq", "dp", None),
            P("dp"),
            P("dp", None),
            P("dp", None),
            P(None, "dp"),
            P(),
            P(),
            P("dp", None),
            P(),
            P("dp", None),
            P("dp"),
            P("dp", None),
            P("dp", None),
            P("dp", None),
        ),
        check_vma=False,
    )
```

profile of v0, /device:TPU:0, one launch (start us, length us, event | category | flops | bytes accessed | tf_op | source)
XLA Modules:
  0.0 2546.3 jit_solution(14586563623302411986)
XLA Ops:
  10.6 22.3 all-gather
  32.9 26.8 %all_gather.33 = bf16[1024,16]{0,1:T(8,128)(2,1)S(1)} all-gather(bf16[128,16]{0,1:T(8,128)(2,1)S(1)} %copy-done.115), channel_id=1, replica_groups=mesh['seq'=4,'dp'=8] {'dp'}, dimensions={0}, use_global_device_ids=true | all-gather | bytes 36864 | tf_op jit(solution)/shard_map/all_gather | solution.py:146
  64.7 73.8 %all-gather.9.cloned.1.call-done = bf16[1024,4096]{1,0:T(8,128)(2,1)} async-done(((bf16[128,4096]{1,0:T(8,128)(2,1)}), bf16[1024,4096]{1,0:T(8,128)(2,1)}) %all-gather.9.cloned.1.call-update) | async-done | bytes 8388624 | tf_op jit(solution)/shard_map/all_gather | solution.py:145
  154.8 31.3 %all_gather.32 = bf16[4,4096]{1,0:T(4,128)(2,1)S(1)} all-gather(bf16[4,512]{1,0:T(4,128)(2,1)S(1)} %copy-done.116), channel_id=1, replica_groups=mesh['seq'=4,'dp'=8] {'dp'}, dimensions={1}, use_global_device_ids=true | all-gather | bytes 36864 | tf_op jit(solution)/shard_map/all_gather | solution.py:147
  210.2 18.9 fusion.42
  295.8 193.4 %while.42 = (s32[]{:T(128)}, f32[2,256,128]{2,1,0:T(8,128)S(1)}, f32[32,2,64,256]{3,2,1,0:T(8,128)}, f32[32,2,256,128]{3,2,1,0:T(8,128)}, f32[32,2,1]{1,2,0:T(1,...) while((s32[]{:T(128)}, f32[2,256,128]{2,1,0:T(8,128)S(1)}, ...), condition=%wide.region_5.6_spmd.clone, body=%wide.region_4.5_spmd.clone.sunk | while | flops 101023744 | bytes 1969832 | solution.py:113
  494.5 12.7 fusion.119
  512.0 14.0 copy.511
  529.8 17.4 all-gather.1
  593.1 11.3 multiply_convert_fusion
  634.6 25.6 %all-to-all-done.3 = bf16[512,8,256]{0,2,1:T(8,128)(2,1)S(1)} async-done(((bf16[512,8,256]{0,2,1:T(8,128)(2,1)}), bf16[512,8,256]{0,2,1:T(8,128)(2,1)S(1)}, u32[]{:S(2)}, u32[]{:S(2)}) %all-to-all-start.3) | async-done | bytes 2097184 | tf_op jit(solution)/shard_map/all_to_all | solution.py:231
  683.2 289.3 %while.43 = (s32[]{:T(128)}, f32[2,256,128]{2,1,0:T(8,128)S(1)}, f32[32,2,64,256]{3,2,1,0:T(8,128)}, f32[32,2,64,128]{3,2,1,0:T(8,128)}, f32[32,2,64,128]{3,2,1,...) while((s32[]{:T(128)}, f32[2,256,128]{2,1,0:T(8,128)S(1)}, ...), condition=%wide.region_12.13_spmd.clone, body=%wide.region_10.12_spmd.clone.sunk | while | flops 202014720 | bytes 3153127 | solution.py:113
  1129.9 11.2 multiply_reduce_fusion.2
  1195.7 11.1 broadcast_multiply_fusion
  1206.9 12.4 fusion.41
  1227.7 51.4 %all_to_all.72 = bf16[2048,2,512]{2,1,0:T(2,128)(2,1)S(1)} all-to-all(bf16[2048,2,512]{2,1,0:T(2,128)(2,1)S(1)} %copy.544), channel_id=1, replica_groups=mesh['seq'=4,'dp'=8] {'seq'}, dimensions={0} | all-to-all | bytes 8388608 | tf_op jit(solution)/shard_map/all_to_all | solution.py:238
  1320.2 97.6 %reduce-scatter.15.cloned.1.call-done = f32[128,2048]{1,0:T(8,128)} async-done(((f32[1024,2048]{1,0:T(8,128)}), f32[128,2048]{1,0:T(8,128)}) %reduce-scatter.15.cloned.1.call-update) | async-done | bytes 1048592 | tf_op jit(solution)/shard_map/reduce_scatter | solution.py:278
  1419.8 149.9 %reduce-scatter.17.cloned.1.call-done = f32[256,1024]{1,0:T(8,128)} async-done(((f32[2048,1024]{1,0:T(8,128)}), f32[256,1024]{1,0:T(8,128)}) %reduce-scatter.17.cloned.1.call-update) | async-done | bytes 1048592 | tf_op jit(solution)/shard_map/reduce_scatter | solution.py:279
  1571.8 193.2 %reduce-scatter.19.cloned.1.call-done = f32[128,2816]{1,0:T(8,128)} async-done(((f32[1024,2816]{1,0:T(8,128)}), f32[128,2816]{1,0:T(8,128)}) %reduce-scatter.19.cloned.1.call-update) | async-done | bytes 1441808 | tf_op jit(solution)/shard_map/reduce_scatter | solution.py:281
  1767.3 192.9 %reduce-scatter.21.cloned.1.call-done = f32[128,2816]{1,0:T(8,128)} async-done(((f32[1024,2816]{1,0:T(8,128)}), f32[128,2816]{1,0:T(8,128)}) %reduce-scatter.21.cloned.1.call-update) | async-done | bytes 1441808 | tf_op jit(solution)/shard_map/reduce_scatter | solution.py:282
  1962.6 193.1 %reduce-scatter.23.cloned.1.call-done = f32[352,1024]{1,0:T(8,128)} async-done(((f32[2816,1024]{1,0:T(8,128)}), f32[352,1024]{1,0:T(8,128)}) %reduce-scatter.23.cloned.1.call-update) | async-done | bytes 1441808 | tf_op jit(solution)/shard_map/reduce_scatter | solution.py:283
  2158.0 282.8 %reduce-scatter.11.cloned.1.call-done = f32[128,4096]{1,0:T(8,128)} async-done(((f32[1024,4096]{1,0:T(8,128)}), f32[128,4096]{1,0:T(8,128)}) %reduce-scatter.11.cloned.1.call-update) | async-done | bytes 2097168 | tf_op jit(solution)/shard_map/reduce_scatter | solution.py:275
  2454.2 35.2 %all-reduce.20 = (bf16[1024]{0:T(1024)(128)(2,1)S(1)}, bf16[8,272]{1,0:T(8,128)(2,1)S(1)}, bf16[1024]{0:T(1024)(128)(2,1)S(1)}) all-reduce(f32[1024]{0:T(1024)S(1)} %get-tuple-element.517, f32[8,272]{1,0:T(8,128)S(1)} %broadcast_in_dim.143, f32[1024]{0:T(1024)S(1)} %copy-done.117), channel_id=2, replica_groups=mesh['seq'=4,'dp'=8] {'dp'}, use_global_device_ids=true, to_apply=%region_26.27.clone | all-reduce | flops 4224 | bytes 25344
  2507.5 23.4 all-reduce.25.cloned.1.call-done
  (916 shorter events, 1020.3 us)
Async XLA Ops:
  7.2 131.2 %all-gather.9.cloned.1.call-start = ((), (), s32[]{:S(2)}) async-start(), calls=%async_computation.14 | async-start | bytes 9437184 | tf_op jit(solution)/shard_map/all_gather | solution.py:145
  7.9 539.2 %all-gather.11.cloned.1.call-start = ((), (), s32[]{:S(2)}) async-start(), calls=%async_computation.15 | async-start | bytes 4718592 | tf_op jit(solution)/shard_map/all_gather | solution.py:148
  8.7 562.9 %all-gather.13.cloned.1.call-start = ((), (), s32[]{:S(2)}) async-start(), calls=%async_computation.16 | async-start | bytes 4718592 | tf_op jit(solution)/shard_map/all_gather | solution.py:149
  9.4 567.8 %all-gather.15.cloned.1.call-start = ((), (), s32[]{:S(2)}) async-start(), calls=%async_computation.17 | async-start | bytes 6488064 | tf_op jit(solution)/shard_map/all_gather | solution.py:151
  10.0 575.5 %all-gather.17.cloned.1.call-start = ((), (), s32[]{:S(2)}) async-start(), calls=%async_computation.18 | async-start | bytes 6488064 | tf_op jit(solution)/shard_map/all_gather | solution.py:152
  32.9 113.7 %copy-start.98 = (f32[8,1,128]{2,1,0:T(1,128)}, f32[8,1,128]{2,1,0:T(1,128)S(1)}, u32[]{:S(2)}) copy-start(f32[8,1,128]{2,1,0:T(1,128)S(1)} %convert_element_type.286) | copy-start | bytes 12292
  60.0 86.7 %copy-start.109 = (f32[512]{0:T(512)}, f32[512]{0:T(512)S(1)}, u32[]{:S(2)}) copy-start(f32[512]{0:T(512)S(1)} %add_rsqrt_fusion.4) | copy-start | bytes 6148
  61.4 87.7 %all-to-all-start.1 = ((bf16[512,8,2]{0,2,1:T(2,128)(2,1)}), bf16[512,8,2]{0,2,1:T(2,128)(2,1)S(1)}, u32[]{:S(2)}, u32[]{:S(2)}) async-start(bf16[512,8,2]{0,2,1:T(2,128)(2,1)} %reshape.518), calls=%async_computation.1 | async-start | bytes 32768 | tf_op jit(solution)/shard_map/all_to_all | solution.py:170
  149.1 53.3 %all-to-all-start = ((bf16[512,8,512]{2,0,1:T(8,128)(2,1)}), bf16[512,8,512]{2,0,1:T(8,128)(2,1)}, u32[]{:S(2)}, u32[]{:S(2)}) async-start(bf16[512,8,512]{2,0,1:T(8,128)(2,1)} %bitcast.525), calls=%async_computation | async-start | bytes 8388608 | tf_op jit(solution)/shard_map/all_to_all | solution.py:169
  154.2 438.9 %all-gather.19.cloned.1.call-start = ((), (), s32[]{:S(2)}) async-start(), calls=%async_computation.19 | async-start | bytes 6488064 | tf_op jit(solution)/shard_map/all_gather | solution.py:153
  241.9 247.4 %copy-start = (f32[2048,2,128]{2,0,1:T(8,128)}, f32[2048,2,128]{2,0,1:T(8,128)S(1)}, u32[]{:S(2)}) copy-start(f32[2048,2,128]{2,0,1:T(8,128)S(1)} %get-tuple-element.606) | copy-start | bytes 6291460
  526.0 29.4 %all-to-all-start.2 = ((bf16[2048,2,256]{2,1,0:T(2,128)(2,1)}), bf16[2048,2,256]{2,1,0:T(2,128)(2,1)S(1)}, u32[]{:S(2)}, u32[]{:S(2)}) async-start(bf16[2048,2,256]{2,1,0:T(2,128)(2,1)} %copy.511), calls=%async_computation.2 | async-start | bytes 4194304 | tf_op jit(solution)/shard_map/all_to_all | solution.py:188
  630.8 29.4 %all-to-all-start.3 = ((bf16[512,8,256]{0,2,1:T(8,128)(2,1)}), bf16[512,8,256]{0,2,1:T(8,128)(2,1)S(1)}, u32[]{:S(2)}, u32[]{:S(2)}) async-start(bf16[512,8,256]{0,2,1:T(8,128)(2,1)} %get-tuple-element.594), calls=%async_computation.3 | async-start | bytes 4194304 | tf_op jit(solution)/shard_map/all_to_all | solution.py:231
  683.2 289.3 %copy-start.41 = (f32[32,2,64,128]{3,2,1,0:T(8,128)S(1)}, f32[32,2,64,128]{3,2,1,0:T(8,128)}, u32[]{:S(2)}) copy-start(f32[32,2,64,128]{3,2,1,0:T(8,128)} %copy-done.40) | copy-start | bytes 6291460
  1115.3 28.0 %all-to-all-start.5 = ((bf16[4,2,1024]{2,1,0:T(2,128)(2,1)}), bf16[4,2,1024]{2,1,0:T(2,128)(2,1)S(1)}, u32[]{:S(2)}, u32[]{:S(2)}) async-start(bf16[4,2,1024]{2,1,0:T(2,128)(2,1)} %reshape.564), calls=%async_computation.5 | async-start | bytes 32768 | tf_op jit(solution)/shard_map/all_to_all | solution.py:241
  1118.5 199.8 %reduce-scatter.25.cloned.1.call-start = ((), (), s32[]{:S(2)}) async-start(), calls=%async_computation.27 | async-start | bytes 2359296
  1143.2 176.3 %reduce-scatter.13.cloned.1.call-start = ((), (), s32[]{:S(2)}) async-start(), calls=%async_computation.21 | async-start | bytes 73728 | tf_op jit(solution)/shard_map/reduce_scatter | solution.py:276
  1150.2 267.6 %reduce-scatter.15.cloned.1.call-start = ((), (), s32[]{:S(2)}) async-start(), calls=%async_computation.22 | async-start | bytes 9437184 | tf_op jit(solution)/shard_map/reduce_scatter | solution.py:278
  1157.8 412.0 %reduce-scatter.17.cloned.1.call-start = ((), (), s32[]{:S(2)}) async-start(), calls=%async_computation.23 | async-start | bytes 9437184 | tf_op jit(solution)/shard_map/reduce_scatter | solution.py:279
  1165.8 599.3 %reduce-scatter.19.cloned.1.call-start = ((), (), s32[]{:S(2)}) async-start(), calls=%async_computation.24 | async-start | bytes 12976128 | tf_op jit(solution)/shard_map/reduce_scatter | solution.py:281
  1175.4 784.8 %reduce-scatter.21.cloned.1.call-start = ((), (), s32[]{:S(2)}) async-start(), calls=%async_computation.25 | async-start | bytes 12976128 | tf_op jit(solution)/shard_map/reduce_scatter | solution.py:282
  1185.4 970.2 %reduce-scatter.23.cloned.1.call-start = ((), (), s32[]{:S(2)}) async-start(), calls=%async_computation.26 | async-start | bytes 12976128 | tf_op jit(solution)/shard_map/reduce_scatter | solution.py:283
  1195.1 1245.7 %reduce-scatter.11.cloned.1.call-start = ((), (), s32[]{:S(2)}) async-start(), calls=%async_computation.20 | async-start | bytes 18874368 | tf_op jit(solution)/shard_map/reduce_scatter | solution.py:275
  1299.9 1231.0 %all-reduce.25.cloned.1.call-start = ((), (), s32[]{:S(2)}) async-start(), calls=%async_computation.28 | async-start | bytes 8519680 | tf_op jit(solution)/shard_map/psum | solution.py:288
  (130 other events, 1043.0 us)
Sparse Core Ops, SparseCore 0:
  10.2 128.1 all-gather.8
  140.5 71.8 all-gather.10
  214.5 71.6 all-gather.12
  288.3 90.8 all-gather.14
  381.3 90.8 all-gather.16
  474.2 90.9 all-gather.18
  1143.3 66.1 reduce-scatter.24
  1213.2 52.7 reduce-scatter.12
  1269.6 148.0 reduce-scatter.14
  1421.7 148.0 reduce-scatter.16
  1573.3 191.6 reduce-scatter.18
  1768.5 191.7 reduce-scatter.20
  1963.9 191.7 reduce-scatter.22
  2159.3 281.4 reduce-scatter.10
  2444.2 86.6 all-reduce.24
where the time goes:
time: 2560 us; the launch traced here: 2550 us
  waiting for transfers between devices  1240 us (48%)
  matrix products  680 us (27%)
  local copies, waits for them, and re-layouts  198 us (8%)
  other arithmetic  196 us (8%)
  blocking collectives  195 us (8%)
    reduce_scatter x1, waiting for transfers between devices, per_device(): lax.psum_scatter(grad_qkv, 'dp', scatter_dimension=0, tiled=True)  283 us
    reduce_scatter x1, waiting for transfers between devices, per_device(): lax.psum_scatter(grad_gate, 'dp', scatter_dimension=0, tiled=True)  193 us
    reduce_scatter x1, waiting for transfers between devices, per_device(): lax.psum_scatter(grad_down, 'dp', scatter_dimension=0, tiled=True)  193 us
    reduce_scatter x1, waiting for transfers between devices, per_device(): lax.psum_scatter(grad_up, 'dp', scatter_dimension=0, tiled=True)  193 us
    dot_general x96, matrix products, advance(): jnp.einsum('hck,hvk->hcv', block_weights, state, precision=highest)  176 us
    dot_general x96, matrix products, advance(): jnp.einsum('hcv,hck->hvk', corrected, block_faded, precision=highest)  168 us
    reduce_scatter x1, waiting for transfers between devices, per_device(): lax.psum_scatter(grad_out, 'dp', scatter_dimension=0, tiled=True)  150 us
    reduce_scatter x1, waiting for transfers between devices, per_device(): lax.psum_scatter(grad_outgate, 'dp', scatter_dimension=0, tiled=True)  97.6 us
  transfers between devices with their start and end apart: 20, of which 11 were waited for; matrix products, arithmetic and copies ran while one was open for 22% of the time, Pallas kernels for 0%

commit v1 on v0

v1 whole, which is shorter than its diff:
```python
import jax
import jax.numpy as jnp
from jax import lax
from jax.experimental import pallas as pl
from jax.experimental.pallas import tpu as pltpu
from jax.sharding import PartitionSpec as P

DK = 128
DV = 256
CONV = 4
ROW = 2 * DK + DV
LANES = 128
CHUNK = 256
HALO = 8

epsilon = 1e-06
narrow = jnp.bfloat16
wide = jnp.float32


def by_weight(left, right):
    return jnp.dot(left, right, preferred_element_type=wide)


def by_transpose(left, right):
    return lax.dot_general(
        left, right, (((1,), (1,)), ((), ())), preferred_element_type=wide
    )


def over_rows(left, right):
    return lax.dot_general(
        left, right, (((0,), (0,)), ((), ())), preferred_element_type=wide
    )


def row_norm(values, gain):
    inverse = lax.rsqrt(jnp.mean(values * values, axis=-1, keepdims=True) + epsilon)
    return (values * inverse * gain, inverse)


def norm_back(values, inverse, gain, grad_out):
    scaled = grad_out * gain
    grad_in = inverse * scaled - values * inverse * inverse * inverse * jnp.mean(
        scaled * values, axis=-1, keepdims=True
    )
    grad_gain = jnp.sum(grad_out * values * inverse, axis=tuple(range(values.ndim - 1)))
    return (grad_in, grad_gain)


def lower(array):
    return array.astype(narrow)


def row_sum(array):
    return jnp.sum(array, axis=1, keepdims=True)


def grid_indices():
    rows = lax.broadcasted_iota(jnp.int32, (CHUNK, CHUNK), 0)
    columns = lax.broadcasted_iota(jnp.int32, (CHUNK, CHUNK), 1)
    return rows, columns


def exact_dot(left, right):
    return jnp.dot(
        left, right, precision=lax.Precision.HIGHEST, preferred_element_type=wide
    )


def convolved(rows, before, taps):
    extended = jnp.concatenate([before, rows], axis=0)
    start = HALO - CONV + 1
    summed = extended[start : start + CHUNK] * taps[0:1]
    for offset in range(1, CONV):
        summed = summed + extended[start + offset : start + offset + CHUNK] * taps[
            offset : offset + 1
        ]
    return extended, summed


def gates(rates, coefficients, rows, columns):
    strength = jax.nn.sigmoid(rates)
    shifted = rates + coefficients[0:1]
    decay = coefficients[1:2] * jax.nn.softplus(shifted)
    through = jnp.where(rows >= columns, 1.0, 0.0)
    cumulative = exact_dot(through, decay)
    return strength, shifted, decay, cumulative


def unit(values):
    return lax.rsqrt(row_sum(values * values) + epsilon)


def invert(lower_part, rows, columns):
    apart = jnp.bitwise_xor(rows, columns)
    inverse = jnp.where(rows == columns, 1.0, 0.0) - jnp.where(apart == 1, lower_part, 0.0)
    level = 1
    while (1 << level) < CHUNK:
        corner = lower(
            jnp.where(lax.shift_right_logical(apart, level) == 1, lower_part, 0.0)
        )
        held = lower(inverse)
        inverse = inverse - by_weight(held, lower(by_weight(corner, held)))
        level += 1
    return inverse


def forward_kernel(
    heads,
    proj_ref,
    rates_ref,
    gate_ref,
    taps_ref,
    coef_ref,
    gain_ref,
    gated_ref,
    mixed_ref,
    inverse_ref,
    state_ref,
    corrected_ref,
    update_ref,
    weight_ref,
    before,
    state,
):
    @pl.when(pl.program_id(0) == 0)
    def _():
        before[...] = jnp.zeros_like(before)
        state[...] = jnp.zeros_like(state)

    rows, columns = grid_indices()
    raw = proj_ref[...].astype(wide)
    unused, summed = convolved(raw, before[...], taps_ref[...])
    before[...] = raw[CHUNK - HALO :]
    active = summed * jax.nn.sigmoid(summed)
    strength_all, unused, unused, cumulative_all = gates(
        rates_ref[...].astype(wide), coef_ref[...], rows, columns
    )
    turned = cumulative_all.T
    gain = gain_ref[0:1]
    for head in range(heads):
        base = head * ROW
        query = active[:, base : base + DK]
        key = active[:, base + DK : base + 2 * DK]
        value = active[:, base + 2 * DK : base + ROW]
        query = query * (unit(query) * DK ** (-0.5))
        key = key * unit(key)
        strength = strength_all[:, 2 * head : 2 * head + 1]
        cumulative = cumulative_all[:, 2 * head + 1 : 2 * head + 2]
        across = turned[2 * head + 1 : 2 * head + 2]
        final = cumulative_all[CHUNK - 1 :, 2 * head + 1 : 2 * head + 2]
        fade = jnp.where(
            rows >= columns, jnp.exp(jnp.minimum(cumulative - across, 0.0)), 0.0
        )
        grown = jnp.exp(cumulative)
        key_low = lower(key)
        query_low = lower(query)
        dots = by_transpose(key_low, key_low)
        lower_part = jnp.where(rows > columns, strength * fade * dots, 0.0)
        inverse = lower(invert(lower_part, rows, columns))
        update = by_weight(inverse, lower(strength * value))
        weight = lower(by_weight(inverse, lower(strength * grown * key)))
        held = state[head]
        held_low = lower(held)
        corrected = lower(update - by_transpose(weight, held_low))
        faded = lower(key * jnp.exp(final - cumulative))
        state[head] = held * jnp.exp(final) + over_rows(corrected, faded)
        inner = lower(by_transpose(query_low, key_low) * fade)
        result = grown * by_transpose(query_low, held_low) + by_weight(inner, corrected)
        mixed = lower(result)
        span = slice(head * DV, head * DV + DV)
        mixed_ref[:, span] = mixed
        mixed = mixed.astype(wide)
        normed, unused = row_norm(mixed, gain)
        gate = gate_ref[:, span]
        gated_ref[:, span] = lower(normed * (gate * jax.nn.sigmoid(gate)))
        inverse_ref[0, head] = inverse
        state_ref[0, head] = held_low
        corrected_ref[:, span] = corrected
        update_ref[:, span] = lower(update)
        weight_ref[:, head * DK : head * DK + DK] = weight


def backward_kernel(
    heads,
    proj_ref,
    edge_ref,
    rates_ref,
    gate_ref,
    taps_ref,
    coef_ref,
    gain_ref,
    mixed_ref,
    inverse_ref,
    state_ref,
    corrected_ref,
    update_ref,
    weight_ref,
    grad_ref,
    out_ref,
    taps_grad_ref,
    gain_grad_ref,
    small_grad_ref,
    after,
    state_grad,
):
    step = pl.program_id(0)

    @pl.when(step == 0)
    def _():
        after[...] = jnp.zeros_like(after)
        state_grad[...] = jnp.zeros_like(state_grad)
        taps_grad_ref[...] = jnp.zeros_like(taps_grad_ref)
        gain_grad_ref[...] = jnp.zeros_like(gain_grad_ref)
        small_grad_ref[...] = jnp.zeros_like(small_grad_ref)

    rows, columns = grid_indices()
    lanes = lax.broadcasted_iota(jnp.int32, (CHUNK, LANES), 1)
    raw = proj_ref[...].astype(wide)
    edge = edge_ref[edge_ref.shape[0] - HALO :].astype(wide)
    edge = jnp.where(step == pl.num_programs(0) - 1, 0.0, edge)
    taps = taps_ref[...]
    extended, summed = convolved(raw, edge, taps)
    sig = jax.nn.sigmoid(summed)
    active = summed * sig
    coefficients = coef_ref[...]
    strength_all, shifted, decay, cumulative_all = gates(
        rates_ref[...].astype(wide), coefficients, rows, columns
    )
    turned = cumulative_all.T
    gain = gain_ref[0:1]
    proj_width = heads * ROW
    active_grads = []
    spread_grad = jnp.zeros((CHUNK, LANES), wide)
    extra_grad = jnp.zeros((CHUNK, LANES), wide)
    strength_grad = jnp.zeros((CHUNK, LANES), wide)
    gain_grad = jnp.zeros((1, DV), wide)
    for head in range(heads):
        span = slice(head * DV, head * DV + DV)
        grad_gated = grad_ref[:, span].astype(wide)
        mixed = mixed_ref[:, span].astype(wide)
        normed, head_inverse = row_norm(mixed, gain)
        gate = gate_ref[:, span]
        sig_gate = jax.nn.sigmoid(gate)
        gate_start = proj_width + LANES + head * DV
        out_ref[:, gate_start : gate_start + DV] = lower(
            grad_gated * normed * sig_gate * (1.0 + gate * (1.0 - sig_gate))
        )
        normed_grad = grad_gated * (gate * sig_gate)
        scaled = normed_grad * gain
        grad_mixed = lower(
            head_inverse * scaled
            - mixed
            * (head_inverse * head_inverse * head_inverse)
            * jnp.mean(scaled * mixed, axis=-1, keepdims=True)
        )
        gain_grad = gain_grad + jnp.sum(
            normed_grad * mixed * head_inverse, axis=0, keepdims=True
        )
        base = head * ROW
        query_raw = active[:, base : base + DK]
        key_raw = active[:, base + DK : base + 2 * DK]
        value = active[:, base + 2 * DK : base + ROW]
        query_unit = unit(query_raw)
        key_unit = unit(key_raw)
        query = query_raw * (query_unit * DK ** (-0.5))
        key = key_raw * key_unit
        strength = strength_all[:, 2 * head : 2 * head + 1]
        cumulative = cumulative_all[:, 2 * head + 1 : 2 * head + 2]
        across = turned[2 * head + 1 : 2 * head + 2]
        final = cumulative_all[CHUNK - 1 :, 2 * head + 1 : 2 * head + 2]
        fade = jnp.where(
            rows >= columns, jnp.exp(jnp.minimum(cumulative - across, 0.0)), 0.0
        )
        strict_fade = jnp.where(rows > columns, fade, 0.0)
        grown = jnp.exp(cumulative)
        remaining = jnp.exp(final - cumulative)
        kept = jnp.exp(final)
        key_low = lower(key)
        query_low = lower(query)
        dots = by_transpose(key_low, key_low)
        inner = by_transpose(query_low, key_low) * fade
        inverse = inverse_ref[0, head]
        held = state_ref[0, head]
        corrected = corrected_ref[:, span]
        update = update_ref[:, span]
        weight = weight_ref[:, head * DK : head * DK + DK]
        faded = key * remaining
        grown_query = query * grown
        later = state_grad[head]
        later_low = lower(later)
        corrected_grad = over_rows(lower(inner), grad_mixed) + by_transpose(
            lower(faded), later_low
        )
        corrected_grad_low = lower(corrected_grad)
        state_grad[head] = (
            later * kept
            + over_rows(grad_mixed, lower(grown_query))
            - over_rows(corrected_grad_low, weight)
        )
        dot_grad = by_transpose(grad_mixed, corrected) * fade
        dot_grad_low = lower(dot_grad)
        grown_grad = by_weight(grad_mixed, held)
        faded_grad = by_weight(corrected, later_low)
        weight_grad = -by_weight(corrected_grad_low, held)
        value_side = over_rows(inverse, corrected_grad_low)
        key_side = over_rows(inverse, lower(weight_grad))
        lower_grad = -(
            by_transpose(lower(value_side), update) + by_transpose(lower(key_side), weight)
        ) * strict_fade
        inner_query = by_weight(dot_grad_low, key_low)
        inner_key = over_rows(dot_grad_low, query_low)
        lower_grad_low = lower(lower_grad)
        first_key = by_weight(lower_grad_low, key_low)
        second_key = over_rows(lower_grad_low, lower(strength * key))
        pairs = lower_grad * dots
        both = pairs * strength + dot_grad * by_transpose(query_low, key_low)
        faded_sum = row_sum(faded_grad * faded)
        key_sum = row_sum(key_side * key)
        query_grad = grown * grown_grad + inner_query
        key_grad = (
            (strength * grown) * key_side
            + strength * first_key
            + second_key
            + inner_key
            + remaining * faded_grad
        )
        value_grad = strength * value_side
        head_strength_grad = row_sum(value_side * value) + grown * key_sum + row_sum(pairs)
        head_spread = (
            (strength * grown) * key_sum
            + row_sum(both)
            + row_sum(grown_grad * grown_query)
            - faded_sum
        )
        column_total = jnp.sum(both, axis=0, keepdims=True)
        late_total = row_sum(jnp.where(columns >= rows, column_total, 0.0))
        final_grad = kept * jnp.sum(held.astype(wide) * later, keepdims=True) + jnp.sum(
            faded_sum, axis=0, keepdims=True
        )
        spread_grad = jnp.where(lanes == 2 * head + 1, head_spread, spread_grad)
        extra_grad = jnp.where(lanes == 2 * head + 1, final_grad - late_total, extra_grad)
        strength_grad = jnp.where(lanes == 2 * head, head_strength_grad, strength_grad)
        active_grads.append(
            DK ** (-0.5)
            * query_unit
            * (
                query_grad
                - query_raw * (query_unit * query_unit) * row_sum(query_grad * query_raw)
            )
        )
        active_grads.append(
            key_unit
            * (key_grad - key_raw * (key_unit * key_unit) * row_sum(key_grad * key_raw))
        )
        active_grads.append(value_grad)
    onward = jnp.where(columns >= rows, 1.0, 0.0)
    decay_grad = exact_dot(onward, spread_grad) + extra_grad
    shift_grad = decay_grad * coefficients[1:2] * jax.nn.sigmoid(shifted)
    rates_grad = strength_grad * strength_all * (1.0 - strength_all) + shift_grad
    out_ref[:, proj_width : proj_width + LANES] = lower(rates_grad)
    small_grad_ref[0:1] += jnp.sum(shift_grad, axis=0, keepdims=True)
    small_grad_ref[1:2] += jnp.sum(decay_grad * decay, axis=0, keepdims=True)
    gain_grad_ref[0:1] += gain_grad
    summed_grad = jnp.concatenate(active_grads, axis=1) * (
        sig * (1.0 + summed * (1.0 - sig))
    )
    following = jnp.concatenate([summed_grad, after[...]], axis=0)
    after[...] = summed_grad[:HALO]
    proj_grad = following[CONV - 1 : CONV - 1 + CHUNK] * taps[0:1]
    start = HALO - CONV + 1
    for offset in range(CONV):
        if offset:
            shift = CONV - 1 - offset
            proj_grad = proj_grad + following[shift : shift + CHUNK] * taps[offset : offset + 1]
        taps_grad_ref[offset : offset + 1] += jnp.sum(
            summed_grad * extended[start + offset : start + offset + CHUNK],
            axis=0,
            keepdims=True,
        )
    out_ref[:, :proj_width] = lower(proj_grad)


def params():
    return pltpu.CompilerParams(
        dimension_semantics=("arbitrary",), vmem_limit_bytes=48 * 1024 * 1024
    )


def mixer_forward(heads, proj, gate, taps, coefficients, gain, interpret=False):
    length = proj.shape[0]
    steps = length // CHUNK
    width = heads * ROW
    values = heads * DV

    def tall(columns, place=0):
        return pl.BlockSpec((CHUNK, columns), lambda i: (i, place))

    def whole(array):
        return pl.BlockSpec(array.shape, lambda i: (0,) * array.ndim)

    def stacked(first, second):
        return pl.BlockSpec((1, heads, first, second), lambda i: (i, 0, 0, 0))

    return pl.pallas_call(
        lambda *refs: forward_kernel(heads, *refs),
        grid=(steps,),
        in_specs=[
            tall(width),
            tall(LANES, width // LANES),
            tall(values),
            whole(taps),
            whole(coefficients),
            whole(gain),
        ],
        out_specs=[
            tall(values),
            tall(values),
            stacked(CHUNK, CHUNK),
            stacked(DV, DK),
            tall(values),
            tall(values),
            tall(heads * DK),
        ],
        out_shape=[
            jax.ShapeDtypeStruct((length, values), narrow),
            jax.ShapeDtypeStruct((length, values), narrow),
            jax.ShapeDtypeStruct((steps, heads, CHUNK, CHUNK), narrow),
            jax.ShapeDtypeStruct((steps, heads, DV, DK), narrow),
            jax.ShapeDtypeStruct((length, values), narrow),
            jax.ShapeDtypeStruct((length, values), narrow),
            jax.ShapeDtypeStruct((length, heads * DK), narrow),
        ],
        scratch_shapes=[
            pltpu.VMEM((HALO, width), wide),
            pltpu.VMEM((heads, DV, DK), wide),
        ],
        compiler_params=params(),
        interpret=interpret,
    )(proj, proj, gate, taps, coefficients, gain)


def mixer_backward(
    heads, proj, gate, taps, coefficients, gain, kept, grad_gated, interpret=False
):
    length = proj.shape[0]
    steps = length // CHUNK
    width = heads * ROW
    values = heads * DV
    edge_rows = 2 * HALO
    ratio = CHUNK // edge_rows

    def tall(columns, place=0):
        return pl.BlockSpec((CHUNK, columns), lambda i: (steps - 1 - i, place))

    def whole(shape):
        return pl.BlockSpec(shape, lambda i: (0,) * len(shape))

    def stacked(first, second):
        return pl.BlockSpec((1, heads, first, second), lambda i: (steps - 1 - i, 0, 0, 0))

    total = width + LANES + values
    return pl.pallas_call(
        lambda *refs: backward_kernel(heads, *refs),
        grid=(steps,),
        in_specs=[
            tall(width),
            pl.BlockSpec(
                (edge_rows, width),
                lambda i: (jnp.maximum((steps - 1 - i) * ratio - 1, 0), 0),
            ),
            tall(LANES, width // LANES),
            tall(values),
            whole(taps.shape),
            whole(coefficients.shape),
            whole(gain.shape),
            tall(values),
            stacked(CHUNK, CHUNK),
            stacked(DV, DK),
            tall(values),
            tall(values),
            tall(heads * DK),
            tall(values),
        ],
        out_specs=[
            tall(total),
            whole((HALO, width)),
            whole((HALO, DV)),
            whole((HALO, LANES)),
        ],
        out_shape=[
            jax.ShapeDtypeStruct((length, total), narrow),
            jax.ShapeDtypeStruct((HALO, width), wide),
            jax.ShapeDtypeStruct((HALO, DV), wide),
            jax.ShapeDtypeStruct((HALO, LANES), wide),
        ],
        scratch_shapes=[
            pltpu.VMEM((HALO, width), wide),
            pltpu.VMEM((heads, DV, DK), wide),
        ],
        compiler_params=params(),
        interpret=interpret,
    )(proj, proj, proj, gate, taps, coefficients, gain, *kept, grad_gated)


def per_device(
    tokens,
    cotangent,
    norm_attn,
    w_qkv,
    w_ba,
    conv_w,
    a_log,
    dt_bias,
    w_outgate,
    head_gain,
    w_out,
    norm_ffn,
    w_gate,
    w_up,
    w_down,
    interpret=False,
):
    parts = lax.axis_size("seq")
    shards = lax.axis_size("dp")
    place = lax.axis_index("seq")
    shard = lax.axis_index("dp")
    head_count = a_log.shape[0]
    heads = head_count // parts
    width = heads * ROW
    values = heads * DV
    model = tokens.shape[2]
    count = tokens.shape[0]
    own = norm_attn.shape[0]

    def mine(array, size, axis):
        return lax.dynamic_slice_in_dim(array, place * size, size, axis)

    def over_dp(array):
        return lax.all_gather(array, "dp", axis=0, tiled=True)

    def over_seq(array):
        return lax.all_gather(array, "seq", axis=0, tiled=True)

    def sum_seq(array):
        return lax.psum_scatter(
            array.astype(narrow), "seq", scatter_dimension=0, tiled=True
        )

    def sum_dp(array):
        return lax.psum_scatter(array.astype(narrow), "dp", scatter_dimension=0, tiled=True)

    ffn = w_gate.shape[1]
    piece = ffn // (shards * parts)

    def ffn_columns(array):
        split = array.reshape(own, shards, parts, piece)
        return lax.dynamic_index_in_dim(split, place, 2, keepdims=False).reshape(own, -1)

    own_tokens = tokens[:, 0, :]
    own_cot = cotangent[:, 0, :]
    all_tokens = over_seq(own_tokens)
    small_flat = jnp.concatenate([norm_attn, norm_ffn, conv_w.reshape(-1)])
    small_all = over_dp(small_flat[None, :])
    first_gain = small_all[:, :own].reshape(-1).astype(wide)
    second_gain = small_all[:, own : 2 * own].reshape(-1).astype(wide)
    taps_all = jnp.swapaxes(small_all[:, 2 * own :].reshape(shards, CONV, -1), 0, 1)
    taps = mine(taps_all.reshape(CONV, -1), width, 1).astype(wide)
    taps = jnp.pad(taps, ((0, HALO - CONV), (0, 0)))
    w_in = over_dp(
        jnp.concatenate(
            [
                mine(w_qkv, width, 1),
                jnp.pad(mine(w_ba, 2 * heads, 1), ((0, 0), (0, LANES - 2 * heads))),
                mine(w_outgate, values, 1),
            ],
            axis=1,
        )
    )
    out_part = over_dp(mine(w_out, model // parts, 1))
    w_out_own = lax.all_to_all(out_part, "seq", split_axis=0, concat_axis=1, tiled=True)
    gate_own = over_dp(ffn_columns(w_gate))
    up_own = over_dp(ffn_columns(w_up))
    down_own = over_dp(mine(w_down, w_down.shape[0] // parts, 0))
    all_cot = over_seq(own_cot)

    decay_part = mine(a_log, heads, 0)
    bias_part = mine(dt_bias, heads, 0)

    def odd_lanes(vector):
        spaced = jnp.stack([jnp.zeros_like(vector), vector], axis=1).reshape(-1)
        return jnp.pad(spaced, (0, LANES - 2 * heads))[None, :]

    coefficients = jnp.pad(
        jnp.concatenate([odd_lanes(bias_part), odd_lanes(-jnp.exp(decay_part))], axis=0),
        ((0, HALO - 2), (0, 0)),
    )
    gain = jnp.broadcast_to(head_gain.astype(wide)[None, :], (HALO, DV))

    rows = own_tokens.astype(wide)
    inverse_one = row_norm(rows, first_gain)[1]
    normed_one = row_norm(all_tokens.astype(wide), first_gain)[0].astype(narrow)
    w_in_first = w_in[:, : width + LANES]
    w_in_gate = w_in[:, width + LANES :]
    proj = by_weight(normed_one, w_in_first).astype(narrow)
    out_gate = by_weight(normed_one, w_in_gate)
    gated, *kept = mixer_forward(
        heads, proj, out_gate, taps, coefficients, gain, interpret
    )
    after_mix = rows + sum_seq(by_weight(gated, w_out_own)).astype(wide)
    normed_two, inverse_two = row_norm(after_mix, second_gain)
    normed_two = over_seq(normed_two.astype(narrow))
    gate_pre = by_weight(normed_two, gate_own)
    up_pre = by_weight(normed_two, up_own)
    sig_ffn = jax.nn.sigmoid(gate_pre)
    hidden = (gate_pre * sig_ffn * up_pre).astype(narrow)
    grad_hidden = by_transpose(all_cot, down_own)
    grad_gate_pre = (grad_hidden * up_pre * sig_ffn * (1.0 + gate_pre * (1.0 - sig_ffn))).astype(
        narrow
    )
    grad_up_pre = (grad_hidden * gate_pre * sig_ffn).astype(narrow)
    grad_normed_two = sum_seq(
        by_transpose(grad_gate_pre, gate_own) + by_transpose(grad_up_pre, up_own)
    )
    back_two, grad_norm_ffn = norm_back(
        after_mix, inverse_two, second_gain, grad_normed_two.astype(wide)
    )
    grad_after = own_cot.astype(wide) + back_two
    grad_branch = over_seq(grad_after.astype(narrow))
    grad_gated = by_transpose(grad_branch, w_out_own)
    result = after_mix + sum_seq(by_weight(hidden, down_own)).astype(wide)
    grad_gate = sum_dp(over_rows(normed_two, grad_gate_pre))
    grad_up = sum_dp(over_rows(normed_two, grad_up_pre))
    grad_down = sum_dp(over_rows(hidden, all_cot))
    grad_out = sum_dp(
        lax.all_to_all(
            over_rows(gated, grad_branch).astype(narrow),
            "seq",
            split_axis=1,
            concat_axis=0,
            tiled=True,
        )
    )
    grad_in, grad_taps, grad_gain, grad_small = mixer_backward(
        heads, proj, out_gate, taps, coefficients, gain, kept, grad_gated, interpret
    )
    grad_normed_one = sum_seq(by_transpose(grad_in, w_in))
    grad_w_in = sum_dp(over_rows(normed_one, grad_in))
    back_one, grad_norm_attn = norm_back(
        rows, inverse_one, first_gain, grad_normed_one.astype(wide)
    )
    grad_rows = (grad_after + back_one).astype(narrow)[:, None, :]

    taps_full = lax.dynamic_update_slice_in_dim(
        jnp.zeros((CONV, head_count * ROW), wide), grad_taps[:CONV], place * width, 1
    )

    def to_heads(lane_row):
        return lax.dynamic_update_slice_in_dim(
            jnp.zeros((head_count,), wide), lane_row[1 : 2 * heads : 2], place * heads, 0
        )

    packed = lax.psum(
        jnp.concatenate(
            [
                grad_norm_attn,
                grad_norm_ffn,
                taps_full.reshape(-1),
                grad_gain[0],
                to_heads(grad_small[1]),
                to_heads(grad_small[0]),
            ]
        ),
        ("dp", "seq"),
    )
    taps_at = 2 * model
    gain_at = taps_at + CONV * head_count * ROW
    heads_at = gain_at + DV
    norm_attn_total = lax.dynamic_slice_in_dim(packed[:model], shard * own, own, 0)
    norm_ffn_total = lax.dynamic_slice_in_dim(packed[model:taps_at], shard * own, own, 0)
    own_taps = conv_w.shape[1]
    taps_total = lax.dynamic_slice_in_dim(
        packed[taps_at:gain_at].reshape(CONV, -1), shard * own_taps, own_taps, 1
    )

    def stack_seq(array):
        return lax.all_gather(array, "seq", axis=0)

    in_all = stack_seq(grad_w_in)

    def columns_of(array):
        return jnp.swapaxes(array, 0, 1).reshape(own, -1).astype(wide)

    def ffn_full(array):
        stacked = stack_seq(array).reshape(parts, own, shards, piece)
        return jnp.transpose(stacked, (1, 2, 0, 3)).reshape(own, -1).astype(wide)

    return (
        result.astype(narrow)[:, None, :],
        grad_rows,
        norm_attn_total,
        columns_of(in_all[:, :, :width]),
        columns_of(in_all[:, :, width : width + 2 * heads]),
        taps_total,
        packed[heads_at : heads_at + head_count],
        packed[heads_at + head_count : heads_at + 2 * head_count],
        columns_of(in_all[:, :, width + LANES :]),
        packed[gain_at:heads_at],
        lax.all_gather(grad_out, "seq", axis=1, tiled=True).astype(wide),
        norm_ffn_total,
        ffn_full(grad_gate),
        ffn_full(grad_up),
        lax.all_gather(grad_down, "seq", axis=0, tiled=True).astype(wide),
    )


def solution(mesh):
    return jax.shard_map(
        per_device,
        mesh=mesh,
        in_specs=(
            P("seq", "dp", None),
            P("seq", "dp", None),
            P("dp"),
            P("dp", None),
            P("dp", None),
            P(None, "dp"),
            P(),
            P(),
            P("dp", None),
            P(),
            P("dp", None),
            P("dp"),
            P("dp", None),
            P("dp", None),
            P("dp", None),
        ),
        out_specs=(
            P("seq", "dp", None),
            P("seq", "dp", None),
            P("dp"),
            P("dp", None),
            P("dp", None),
            P(None, "dp"),
            P(),
            P(),
            P("dp", None),
            P(),
            P("dp", None),
            P("dp"),
            P("dp", None),
            P("dp", None),
            P("dp", None),
        ),
        check_vma=False,
    )
```

time: 2560 us -> 1290 us (0.50)
  matrix products: 680 us -> 121 us
  waiting for transfers between devices: 1240 us -> 873 us
  other arithmetic: 196 us -> 25.3 us
  local copies, waits for them, and re-layouts: 198 us -> 38.4 us
  Pallas kernels: 0 us -> 117 us
  blocking collectives: 195 us -> 82.4 us
    reduce_scatter x7, waiting for transfers between devices: 1110 us -> 284 us  [the longest x3 165 us: sum_dp(): lax.psum_scatter(array.astype(narrow), 'dp', scatter_dimension=0, tiled=T...]
    dot_general x244 -> x6, matrix products: 581 us -> 48.1 us  [by_weight(): return jnp.dot(left, right, preferred_element_type=wide)]
    all_gather x6 -> x10, waiting for transfers between devices: 73.8 us -> 324 us  [the longest x5 186 us: over_dp(): return lax.all_gather(array, 'dp', axis=0, tiled=True)]
    unnamed x16 -> x22, waiting for transfers between devices: 3.79 us -> 123 us
    pallas_call x0 -> x2, Pallas kernels: none -> 117 us  [the longest x1 62.7 us: mixer_forward(): pl.pallas_call(lambda *refs: forward_kernel(heads, *refs), grid=(steps,),...]
    psum x1, waiting for transfers between devices: 23.4 us -> 121 us  [per_device(): lax.psum(jnp.concatenate([grad_norm_attn, grad_norm_ffn, taps_full.reshap...]
    reduce_sum x40 -> x0, other arithmetic: 63.1 us -> none  [the longest x32 34.8 us: advance(): state * jnp.exp(block_final)[:, :, None]]
    dynamic_update_slice x65 -> x3, local copies, waits for them, and re-layouts: 60.2 us -> 0.43 us  [the longest x2 0.42 us: to_heads(): lax.dynamic_update_slice_in_dim(jnp.zeros((head_count,), wide), lane_row[...]
  transfers between devices with their start and end apart: 20 -> 21, of which waited for: 11 -> 20; matrix products, arithmetic and copies ran while one was open for 22% -> 9% of each run, Pallas kernels for 0% -> 0%
where the time goes in v1:
time: 1290 us; the launch traced here: 1280 us
  waiting for transfers between devices  873 us (68%)
  matrix products  121 us (9%)
  Pallas kernels  117 us (9%)
  blocking collectives  82.4 us (6%)
  local copies, waits for them, and re-layouts  38.4 us (3%)
  other arithmetic  25.3 us (2%)
  between operations  15.3 us (1%)
    all_gather x5, waiting for transfers between devices, over_dp(): return lax.all_gather(array, 'dp', axis=0, tiled=True)  186 us
    reduce_scatter x3, waiting for transfers between devices, sum_dp(): lax.psum_scatter(array.astype(narrow), 'dp', scatter_dimension=0, tiled=T...  165 us
    unnamed x22, waiting for transfers between devices  123 us
    psum x1, waiting for transfers between devices, per_device(): lax.psum(jnp.concatenate([grad_norm_attn, grad_norm_ffn, taps_full.reshap...  121 us
    all_gather x4, waiting for transfers between devices, over_seq(): return lax.all_gather(array, 'seq', axis=0, tiled=True)  120 us
    reduce_scatter x4, waiting for transfers between devices, sum_seq(): lax.psum_scatter(array.astype(narrow), 'seq', scatter_dimension=0, tiled=...  119 us
    pallas_call x1, Pallas kernels, mixer_forward(): pl.pallas_call(lambda *refs: forward_kernel(heads, *refs), grid=(steps,),...  62.7 us
    pallas_call x1, Pallas kernels, mixer_backward(): pl.pallas_call(lambda *refs: backward_kernel(heads, *refs), grid=(steps,)...  54.4 us
  transfers between devices with their start and end apart: 21, of which 20 were waited for; matrix products, arithmetic and copies ran while one was open for 9% of the time, Pallas kernels for 0%

profile of v1, /device:TPU:0, one launch (start us, length us, event | category | flops | bytes accessed | tf_op | source)
XLA Modules:
  0.0 1277.1 jit_solution(9156442527365961849)
XLA Ops:
  12.5 32.5 %all-gather.6 = bf16[8,1,2304]{2,1,0:T(2,128)(2,1)S(1)} all-gather(bf16[1,1,2304]{2,1,0:T(2,128)(2,1)S(1)} %reshape.174), channel_id=3, replica_groups=mesh['seq'=4,'dp'=8] {'dp'}, dimensions={0}, use_global_device_ids=true | all-gather | bytes 41472 | tf_op jit(solution)/shard_map/all_gather | solution.py:541
  57.9 21.2 %all-to-all-done = bf16[4,512,256]{2,1,0:T(8,128)(2,1)S(1)} async-done(((bf16[4,512,256]{2,1,0:T(8,128)(2,1)}), bf16[4,512,256]{2,1,0:T(8,128)(2,1)S(1)}, u32[]{:S(2)}, u32[]{:S(2)}) %all-to-all-start) | async-done | bytes 1048608 | tf_op jit(solution)/shard_map/all_to_all | solution.py:582
  79.7 16.0 %all-gather.32.cloned.1.call-done = bf16[2048,1,1024]{2,0,1:T(8,128)(2,1)} async-done(((bf16[512,1,1024]{2,0,1:T(8,128)(2,1)}), bf16[2048,1,1024]{2,0,1:T(8,128)(2,1)}) %all-gather.32.cloned.1.call-update) | async-done | bytes 4194320 | tf_op jit(solution)/shard_map/all_gather | solution.py:544
  98.9 61.1 %all-gather.18.cloned.1.call-done = bf16[1024,1664]{1,0:T(8,128)(2,1)} async-done(((bf16[128,1664]{1,0:T(8,128)(2,1)}), bf16[1024,1664]{1,0:T(8,128)(2,1)}) %all-gather.18.cloned.1.call-update) | async-done | bytes 3407888 | tf_op jit(solution)/shard_map/all_gather | solution.py:541
  175.5 62.7 %shard_map.262 = (bf16[2048,512]{1,0:T(8,128)(2,1)S(1)}, bf16[2048,512]{1,0:T(8,128)(2,1)}, bf16[8,2,256,256]{3,2,1,0:T(8,128)(2,1)}, bf16[8,2,256,128]{3,2,1,0:...) custom-call(bf16[2048,1152]{1,0:T(8,128)(2,1)} %convolution_convert_fusion.re, ...), custom_call_target="tpu_custom_call" | custom-call | tf_op jit(solution)/shard_map/pallas_call | solution.py:406
  249.5 38.6 %reduce-scatter.14.cloned.1.call-done = bf16[512,1024]{1,0:T(8,128)(2,1)} async-done(((bf16[2048,1024]{1,0:T(8,128)(2,1)}), bf16[512,1024]{1,0:T(8,128)(2,1)}) %reduce-scatter.14.cloned.1.call-update) | async-done | bytes 1048592 | tf_op jit(solution)/shard_map/reduce_scatter | solution.py:547
  294.6 39.4 %all-gather.28.cloned.1.call-done = bf16[704,1024]{1,0:T(8,128)(2,1)} async-done(((bf16[88,1024]{1,0:T(8,128)(2,1)}), bf16[704,1024]{1,0:T(8,128)(2,1)}) %all-gather.28.cloned.1.call-update) | async-done | bytes 1441808 | tf_op jit(solution)/shard_map/all_gather | solution.py:541
  334.0 34.3 %all-gather.34.cloned.1.call-done = bf16[2048,1,1024]{2,0,1:T(8,128)(2,1)} async-done(((bf16[512,1,1024]{2,0,1:T(8,128)(2,1)}), bf16[2048,1,1024]{2,0,1:T(8,128)(2,1)}) %all-gather.34.cloned.1.call-update) | async-done | bytes 4194320 | tf_op jit(solution)/shard_map/all_gather | solution.py:544
  376.7 38.3 %all-gather.26.cloned.1.call-done = bf16[1024,704]{0,1:T(8,128)(2,1)} async-done(((bf16[128,704]{0,1:T(8,128)(2,1)}), bf16[1024,704]{0,1:T(8,128)(2,1)}) %all-gather.26.cloned.1.call-update) | async-done | bytes 1441808 | tf_op jit(solution)/shard_map/all_gather | solution.py:541
  415.0 35.1 %all-gather.22.cloned.1.call-done = bf16[2048,1024]{1,0:T(8,128)(2,1)} async-done(((bf16[512,1024]{1,0:T(8,128)(2,1)}), bf16[2048,1024]{1,0:T(8,128)(2,1)}) %all-gather.22.cloned.1.call-update) | async-done | bytes 4194320 | tf_op jit(solution)/shard_map/all_gather | solution.py:544
  458.4 38.3 %all-gather.24.cloned.1.call-done = bf16[1024,704]{0,1:T(8,128)(2,1)} async-done(((bf16[128,704]{0,1:T(8,128)(2,1)}), bf16[1024,704]{0,1:T(8,128)(2,1)}) %all-gather.24.cloned.1.call-update) | async-done | bytes 1441808 | tf_op jit(solution)/shard_map/all_gather | solution.py:541
  518.7 43.0 %reduce-scatter.18.cloned.1.call-done = bf16[512,1024]{1,0:T(8,128)(2,1)} async-done(((bf16[2048,1024]{1,0:T(8,128)(2,1)}), bf16[512,1024]{1,0:T(8,128)(2,1)}) %reduce-scatter.18.cloned.1.call-update) | async-done | bytes 1048592 | tf_op jit(solution)/shard_map/reduce_scatter | solution.py:547
  566.2 34.6 %all-gather.30.cloned.1.call-done = bf16[2048,1024]{1,0:T(8,128)(2,1)} async-done(((bf16[512,1024]{1,0:T(8,128)(2,1)}), bf16[2048,1024]{1,0:T(8,128)(2,1)}) %all-gather.30.cloned.1.call-update) | async-done | bytes 4194320 | tf_op jit(solution)/shard_map/all_gather | solution.py:544
  607.7 54.4 %shard_map.263 = (bf16[2048,1664]{1,0:T(8,128)(2,1)}, f32[8,1024]{1,0:T(8,128)S(1)}, f32[8,256]{1,0:T(8,128)S(1)}, f32[8,128]{1,0:T(8,128)S(1)}) custom-call(bf16[2048,1152]{1,0:T(8,128)(2,1)} %convolution_convert_fusion.refs_0_.refs_1_.refs_2_, bf16[2048,1152]{1,0:T(8,128)(2,1)} %convolution_convert_fusion.refs_0_.refs_1_.refs_2_, ...), custom_call_target="tpu_custom_call" | custom-call | tf_op jit(solution)/shard_map/pallas_call | solution.py:464
  673.4 13.5 %convolution_convert_fusion.1 = bf16[1024,1664]{1,0:T(8,128)(2,1)} fusion(bf16[2048,1664]{1,0:T(8,128)(2,1)} %get-tuple-element.33, bf16[2048,1,1024]{2,0,1:T(8,128)(2,1)} %all-gather.32.cloned.1.call-done, f32[1024]{0:T(1024)S(1)} %get-tuple-element.112, f32[2048]{0:T(1024)S(1)} %add_rsqrt_fusion), kind=kOutput, calls=%fused_computation.25 | convolution fusion | flops 6989414400 | bytes 14430208 | tf_op jit(solution)/shard_map/dot_general | solution.py:32
  715.2 17.7 %all_to_all.38 = bf16[512,4,256]{2,0,1:T(8,128)(2,1)} all-to-all(bf16[512,4,256]{2,0,1:T(8,128)(2,1)S(1)} %bitcast.156), channel_id=1, replica_groups=mesh['seq'=4,'dp'=8] {'seq'}, dimensions={1} | all-to-all | bytes 2097152 | tf_op jit(solution)/shard_map/all_to_all | solution.py:637
  744.2 55.4 %reduce-scatter.22.cloned.1.call-done = bf16[128,1664]{1,0:T(8,128)(2,1)} async-done(((bf16[1024,1664]{1,0:T(8,128)(2,1)}), bf16[128,1664]{1,0:T(8,128)(2,1)}) %reduce-scatter.22.cloned.1.call-update) | async-done | bytes 426000 | tf_op jit(solution)/shard_map/reduce_scatter | solution.py:552
  799.6 68.1 %reduce-scatter.28.cloned.1.call-done = bf16[128,704]{1,0:T(8,128)(2,1)} async-done(((bf16[1024,704]{1,0:T(8,128)(2,1)}), bf16[128,704]{1,0:T(8,128)(2,1)}) %reduce-scatter.28.cloned.1.call-update) | async-done | bytes 180240
  881.6 53.5 %reduce-scatter.30.cloned.1.call-done = bf16[128,704]{1,0:T(8,128)(2,1)} async-done(((bf16[1024,704]{1,0:T(8,128)(2,1)}), bf16[128,704]{1,0:T(8,128)(2,1)}) %reduce-scatter.30.cloned.1.call-update) | async-done | bytes 180240
  949.0 53.2 %reduce-scatter.26.cloned.1.call-done = bf16[88,1024]{1,0:T(8,128)(2,1)} async-done(((bf16[704,1024]{1,0:T(8,128)(2,1)}), bf16[88,1024]{1,0:T(8,128)(2,1)}) %reduce-scatter.26.cloned.1.call-update) | async-done | bytes 180240 | tf_op jit(solution)/shard_map/reduce_scatter | solution.py:552
  1011.8 56.1 %reduce-scatter.24.cloned.1.call-done = bf16[256,256]{1,0:T(8,128)(2,1)} async-done(((bf16[2048,256]{1,0:T(8,128)(2,1)}), bf16[256,256]{1,0:T(8,128)(2,1)}) %reduce-scatter.24.cloned.1.call-update) | async-done | bytes 131088 | tf_op jit(solution)/shard_map/reduce_scatter | solution.py:552
  1076.4 37.6 %reduce-scatter.16.cloned.1.call-done = bf16[512,1024]{1,0:T(8,128)(2,1)} async-done(((bf16[2048,1024]{1,0:T(8,128)(2,1)}), bf16[512,1024]{1,0:T(8,128)(2,1)}) %reduce-scatter.16.cloned.1.call-update) | async-done | bytes 1048592 | tf_op jit(solution)/shard_map/reduce_scatter | solution.py:547
  1118.6 120.6 %all-reduce.9.cloned.1.call-done = f32[18704]{0:T(1024)} async-done(((f32[18704]{0:T(1024)}), f32[18704]{0:T(1024)}) %all-reduce.9.cloned.1.call-update) | async-done | bytes 74832 | tf_op jit(solution)/shard_map/psum | solution.py:664
  1245.0 17.9 %all-gather.36.cloned.1.call-done = bf16[512,1664]{1,0:T(8,128)(2,1)} async-done(((bf16[128,1664]{1,0:T(8,128)(2,1)}), bf16[512,1664]{1,0:T(8,128)(2,1)}) %all-gather.36.cloned.1.call-update) | async-done | bytes 1703952 | tf_op jit(solution)/shard_map/all_gather | solution.py:688
  (201 shorter events, 218.6 us)
Async XLA Ops:
  7.2 46.5 %all-gather.20.cloned.1.call-start = ((), (), s32[]{:S(2)}) async-start(), calls=%async_computation.12 | async-start | bytes 1179648 | tf_op jit(solution)/shard_map/all_gather | solution.py:541
  9.0 86.8 %all-gather.32.cloned.1.call-start = ((), (), s32[]{:S(2)}) async-start(), calls=%async_computation.26 | async-start | bytes 5242880 | tf_op jit(solution)/shard_map/all_gather | solution.py:544
  9.7 150.3 %all-gather.18.cloned.1.call-start = ((), (), s32[]{:S(2)}) async-start(), calls=%async_computation.11 | async-start | bytes 3833856 | tf_op jit(solution)/shard_map/all_gather | solution.py:541
  53.7 25.5 %all-to-all-start = ((bf16[4,512,256]{2,1,0:T(8,128)(2,1)}), bf16[4,512,256]{2,1,0:T(8,128)(2,1)S(1)}, u32[]{:S(2)}, u32[]{:S(2)}) async-start(bf16[4,512,256]{2,1,0:T(8,128)(2,1)} %bitcast.165), calls=%async_computation | async-start | bytes 2097152 | tf_op jit(solution)/shard_map/all_to_all | solution.py:582
  57.3 230.8 %reduce-scatter.14.cloned.1.call-start = ((), (), s32[]{:S(2)}) async-start(), calls=%async_computation.13 | async-start | bytes 5242880 | tf_op jit(solution)/shard_map/reduce_scatter | solution.py:547
  79.7 159.4 %copy-start.15 = (bf16[512,4,256]{0,2,1:T(8,128)(2,1)}, bf16[512,4,256]{0,2,1:T(8,128)(2,1)S(1)}, u32[]{:S(2)}) copy-start(bf16[512,4,256]{0,2,1:T(8,128)(2,1)S(1)} %copy.81) | copy-start | bytes 3145732
  244.9 89.1 %all-gather.28.cloned.1.call-start = ((), (), s32[]{:S(2)}) async-start(), calls=%async_computation.17 | async-start | bytes 1622016 | tf_op jit(solution)/shard_map/all_gather | solution.py:541
  246.6 121.7 %all-gather.34.cloned.1.call-start = ((), (), s32[]{:S(2)}) async-start(), calls=%async_computation.27 | async-start | bytes 5242880 | tf_op jit(solution)/shard_map/all_gather | solution.py:544
  247.2 167.8 %all-gather.26.cloned.1.call-start = ((), (), s32[]{:S(2)}) async-start(), calls=%async_computation.16 | async-start | bytes 1622016 | tf_op jit(solution)/shard_map/all_gather | solution.py:541
  249.4 200.7 %all-gather.22.cloned.1.call-start = ((), (), s32[]{:S(2)}) async-start(), calls=%async_computation.14 | async-start | bytes 5242880 | tf_op jit(solution)/shard_map/all_gather | solution.py:544
  292.4 204.4 %all-gather.24.cloned.1.call-start = ((), (), s32[]{:S(2)}) async-start(), calls=%async_computation.15 | async-start | bytes 1622016 | tf_op jit(solution)/shard_map/all_gather | solution.py:541
  294.6 267.1 %reduce-scatter.18.cloned.1.call-start = ((), (), s32[]{:S(2)}) async-start(), calls=%async_computation.19 | async-start | bytes 5242880 | tf_op jit(solution)/shard_map/reduce_scatter | solution.py:547
  518.6 82.1 %all-gather.30.cloned.1.call-start = ((), (), s32[]{:S(2)}) async-start(), calls=%async_computation.20 | async-start | bytes 5242880 | tf_op jit(solution)/shard_map/all_gather | solution.py:544
  566.1 174.7 %reduce-scatter.20.cloned.1.call-start = ((), (), s32[]{:S(2)}) async-start(), calls=%async_computation.21 | async-start | bytes 5242880 | tf_op jit(solution)/shard_map/reduce_scatter | solution.py:547
  673.4 126.2 %reduce-scatter.22.cloned.1.call-start = ((), (), s32[]{:S(2)}) async-start(), calls=%async_computation.23 | async-start | bytes 3833856 | tf_op jit(solution)/shard_map/reduce_scatter | solution.py:552
  686.9 180.8 %reduce-scatter.28.cloned.1.call-start = ((), (), s32[]{:S(2)}) async-start(), calls=%async_computation.29 | async-start | bytes 1769472
  694.8 240.4 %reduce-scatter.30.cloned.1.call-start = ((), (), s32[]{:S(2)}) async-start(), calls=%async_computation.30 | async-start | bytes 1769472
  702.7 299.6 %reduce-scatter.26.cloned.1.call-start = ((), (), s32[]{:S(2)}) async-start(), calls=%async_computation.25 | async-start | bytes 1622016 | tf_op jit(solution)/shard_map/reduce_scatter | solution.py:552
  710.3 357.6 %reduce-scatter.24.cloned.1.call-start = ((), (), s32[]{:S(2)}) async-start(), calls=%async_computation.24 | async-start | bytes 1179648 | tf_op jit(solution)/shard_map/reduce_scatter | solution.py:552
  733.0 381.0 %reduce-scatter.16.cloned.1.call-start = ((), (), s32[]{:S(2)}) async-start(), calls=%async_computation.18 | async-start | bytes 5242880 | tf_op jit(solution)/shard_map/reduce_scatter | solution.py:547
  740.1 499.1 %all-reduce.9.cloned.1.call-start = ((), (), s32[]{:S(2)}) async-start(), calls=%async_computation.22 | async-start | bytes 155648 | tf_op jit(solution)/shard_map/psum | solution.py:664
  744.1 518.8 %all-gather.36.cloned.1.call-start = ((), (), s32[]{:S(2)}) async-start(), calls=%async_computation.28 | async-start | bytes 2129920 | tf_op jit(solution)/shard_map/all_gather | solution.py:688
  949.0 165.0 %copy-start.10 = (bf16[512,1024]{1,0:T(8,128)(2,1)S(1)}, bf16[512,1024]{1,0:T(8,128)(2,1)}, u32[]{:S(2)}) copy-start(bf16[512,1024]{1,0:T(8,128)(2,1)} %reduce-scatter.14.cloned.1.call-done) | copy-start | bytes 3145732
  949.0 165.0 %copy-start.12 = (bf16[512,1,1024]{2,0,1:T(8,128)(2,1)S(1)}, bf16[512,1,1024]{2,0,1:T(8,128)(2,1)}, u32[]{:S(2)}) copy-start(bf16[512,1,1024]{2,0,1:T(8,128)(2,1)} %param.16) | copy-start | bytes 3145732
  (25 other events, 362.2 us)
Sparse Core Ops, SparseCore 0:
  10.8 42.9 all-gather.19
  55.3 40.4 all-gather.31
  98.5 61.4 all-gather.17
  245.0 43.0 reduce-scatter.13
  290.9 43.0 all-gather.27
  335.5 32.7 all-gather.33
  371.1 43.8 all-gather.25
  417.2 32.8 all-gather.21
  452.9 43.8 all-gather.23
  518.8 42.8 reduce-scatter.17
  566.2 34.4 all-gather.29
  673.5 44.5 reduce-scatter.19
  722.1 77.4 reduce-scatter.21
  803.5 64.2 reduce-scatter.27
  871.4 63.7 reduce-scatter.29
  938.4 63.7 reduce-scatter.25
  1005.5 62.3 reduce-scatter.23
  1070.4 43.5 reduce-scatter.15
  1120.2 118.9 all-reduce.8
  1240.5 22.3 all-gather.35

commit v2 on v1

v2 whole, which is shorter than its diff:
```python
import jax
import jax.numpy as jnp
from jax import lax
from jax.experimental import pallas as pl
from jax.experimental.pallas import tpu as pltpu
from jax.sharding import PartitionSpec as P

DK = 128
DV = 256
CONV = 4
ROW = 2 * DK + DV
LANES = 128
CHUNK = 256
HALO = 8

epsilon = 1e-06
narrow = jnp.bfloat16
wide = jnp.float32


def by_weight(left, right):
    return jnp.dot(left, right, preferred_element_type=wide)


def by_transpose(left, right):
    return lax.dot_general(
        left, right, (((1,), (1,)), ((), ())), preferred_element_type=wide
    )


def over_rows(left, right):
    return lax.dot_general(
        left, right, (((0,), (0,)), ((), ())), preferred_element_type=wide
    )


def row_norm(values, gain):
    inverse = lax.rsqrt(jnp.mean(values * values, axis=-1, keepdims=True) + epsilon)
    return (values * inverse * gain, inverse)


def norm_back(values, inverse, gain, grad_out):
    scaled = grad_out * gain
    grad_in = inverse * scaled - values * inverse * inverse * inverse * jnp.mean(
        scaled * values, axis=-1, keepdims=True
    )
    grad_gain = jnp.sum(grad_out * values * inverse, axis=tuple(range(values.ndim - 1)))
    return (grad_in, grad_gain)


def lower(array):
    return array.astype(narrow)


def row_sum(array):
    return jnp.sum(array, axis=1, keepdims=True)


def grid_indices():
    rows = lax.broadcasted_iota(jnp.int32, (CHUNK, CHUNK), 0)
    columns = lax.broadcasted_iota(jnp.int32, (CHUNK, CHUNK), 1)
    return rows, columns


def exact_dot(left, right):
    return jnp.dot(
        left, right, precision=lax.Precision.HIGHEST, preferred_element_type=wide
    )


def shifted_rows(rows, before):
    return jnp.concatenate([before, rows], axis=0)


def convolved(extended, taps, count):
    start = HALO - CONV + 1
    summed = extended[start : start + count] * taps[0:1]
    for offset in range(1, CONV):
        summed = summed + extended[start + offset : start + offset + count] * taps[
            offset : offset + 1
        ]
    return summed


def gates(rates, coefficients):
    strength = jax.nn.sigmoid(rates)
    shifted = rates + coefficients[0:1]
    decay = coefficients[1:2] * jax.nn.softplus(shifted)
    return strength, shifted, decay


def unit(values):
    return lax.rsqrt(row_sum(values * values) + epsilon)


def in_turn(parts):
    waiting = list(parts)
    while waiting:
        still = []
        for part in waiting:
            try:
                next(part)
                still.append(part)
            except StopIteration:
                pass
        waiting = still


def invert(lower_part, rows, columns, store):
    apart = jnp.bitwise_xor(rows, columns)
    inverse = jnp.where(rows == columns, 1.0, 0.0) - jnp.where(apart == 1, lower_part, 0.0)
    level = 1
    while (1 << level) < CHUNK:
        corner = lower(
            jnp.where(lax.shift_right_logical(apart, level) == 1, lower_part, 0.0)
        )
        held = lower(inverse)
        yield
        side = lower(by_weight(corner, held))
        yield
        inverse = inverse - by_weight(held, side)
        level += 1
    store.append(lower(inverse))


def forward_kernel(
    heads,
    place_ref,
    proj_ref,
    rates_ref,
    gate_ref,
    taps_ref,
    coef_ref,
    gain_ref,
    gated_ref,
    mixed_ref,
    inverse_ref,
    state_ref,
    corrected_ref,
    update_ref,
    weight_ref,
    before,
    state,
):
    @pl.when(pl.program_id(0) == 0)
    def _():
        before[...] = jnp.zeros_like(before)
        state[...] = jnp.zeros_like(state)

    count = proj_ref.shape[0]
    rows, columns = grid_indices()
    raw = proj_ref[...].astype(wide)
    summed = convolved(shifted_rows(raw, before[...]), taps_ref[...], count)
    before[...] = raw[count - HALO :]
    active = summed * jax.nn.sigmoid(summed)
    strength_rows, unused, decay_rows = gates(rates_ref[...].astype(wide), coef_ref[...])
    through = jnp.where(rows >= columns, 1.0, 0.0)
    gain = gain_ref[0:1]
    states = {(0, head): state[head] for head in range(heads)}
    blocks = count // CHUNK
    cumulative_rows = [
        exact_dot(through, decay_rows[block * CHUNK : (block + 1) * CHUNK])
        for block in range(blocks)
    ]
    turned_rows = [item.T for item in cumulative_rows]

    def one(block, head):
        base = head * ROW
        here = slice(block * CHUNK, (block + 1) * CHUNK)
        query = active[here, base : base + DK]
        key = active[here, base + DK : base + 2 * DK]
        value = active[here, base + 2 * DK : base + ROW]
        query = query * (unit(query) * DK ** (-0.5))
        key = key * unit(key)
        strength = strength_rows[here, 2 * head : 2 * head + 1]
        cumulative = cumulative_rows[block][:, 2 * head + 1 : 2 * head + 2]
        across = turned_rows[block][2 * head + 1 : 2 * head + 2]
        final = cumulative[CHUNK - 1 :]
        fade = jnp.where(
            rows >= columns, jnp.exp(jnp.minimum(cumulative - across, 0.0)), 0.0
        )
        grown = jnp.exp(cumulative)
        key_low = lower(key)
        query_low = lower(query)
        dots = by_transpose(key_low, key_low)
        yield
        lower_part = jnp.where(rows > columns, strength * fade * dots, 0.0)
        store = []
        yield from invert(lower_part, rows, columns, store)
        inverse = store[0]
        yield
        update = by_weight(inverse, lower(strength * value))
        weight = lower(by_weight(inverse, lower(strength * grown * key)))
        inner = lower(by_transpose(query_low, key_low) * fade)
        faded = lower(key * jnp.exp(final - cumulative))
        inverse_ref[block, head] = inverse
        span = slice(head * DV, head * DV + DV)
        update_ref[here, span] = lower(update)
        weight_ref[here, head * DK : head * DK + DK] = weight
        yield
        while (block, head) not in states:
            yield
        held = states[block, head]
        held_low = lower(held)
        state_ref[block, head] = held_low
        corrected = lower(update - by_transpose(weight, held_low))
        yield
        states[block + 1, head] = held * jnp.exp(final) + over_rows(corrected, faded)
        corrected_ref[here, span] = corrected
        result = grown * by_transpose(query_low, held_low) + by_weight(inner, corrected)
        yield
        mixed = lower(result)
        mixed_ref[here, span] = mixed
        normed, unused = row_norm(mixed.astype(wide), gain)
        gate = gate_ref[here, span]
        gated_ref[here, span] = lower(normed * (gate * jax.nn.sigmoid(gate)))

    in_turn(one(block, head) for block in range(blocks) for head in range(heads))
    for head in range(heads):
        state[head] = states[blocks, head]


def backward_kernel(
    heads,
    place_ref,
    proj_ref,
    edge_ref,
    rates_ref,
    gate_ref,
    taps_ref,
    coef_ref,
    gain_ref,
    mixed_ref,
    inverse_ref,
    state_ref,
    corrected_ref,
    update_ref,
    weight_ref,
    grad_ref,
    out_ref,
    taps_grad_ref,
    gain_grad_ref,
    small_grad_ref,
    after,
    state_grad,
):
    step = pl.program_id(0)

    @pl.when(step == 0)
    def _():
        after[...] = jnp.zeros_like(after)
        state_grad[...] = jnp.zeros_like(state_grad)
        taps_grad_ref[...] = jnp.zeros_like(taps_grad_ref)
        gain_grad_ref[...] = jnp.zeros_like(gain_grad_ref)
        small_grad_ref[...] = jnp.zeros_like(small_grad_ref)

    count = proj_ref.shape[0]
    blocks = count // CHUNK
    rows, columns = grid_indices()
    lanes = lax.broadcasted_iota(jnp.int32, (CHUNK, LANES), 1)
    raw = proj_ref[...].astype(wide)
    edge = edge_ref[edge_ref.shape[0] - HALO :].astype(wide)
    edge = jnp.where(step == pl.num_programs(0) - 1, 0.0, edge)
    taps = taps_ref[...]
    extended = shifted_rows(raw, edge)
    summed = convolved(extended, taps, count)
    sig = jax.nn.sigmoid(summed)
    active = summed * sig
    coefficients = coef_ref[...]
    strength_rows, shifted_rates, decay_rows = gates(
        rates_ref[...].astype(wide), coefficients
    )
    through = jnp.where(rows >= columns, 1.0, 0.0)
    onward = jnp.where(columns >= rows, 1.0, 0.0)
    gain = gain_ref[0:1]
    proj_width = heads * ROW
    cumulative_rows = [
        exact_dot(through, decay_rows[block * CHUNK : (block + 1) * CHUNK])
        for block in range(blocks)
    ]
    turned_rows = [item.T for item in cumulative_rows]
    laters = {(blocks - 1, head): state_grad[head] for head in range(heads)}
    active_grads = {}
    column_grads = {}
    gain_grads = []

    def one(block, head):
        here = slice(block * CHUNK, (block + 1) * CHUNK)
        span = slice(head * DV, head * DV + DV)
        grad_gated = grad_ref[here, span].astype(wide)
        mixed = mixed_ref[here, span].astype(wide)
        normed, head_inverse = row_norm(mixed, gain)
        gate = gate_ref[here, span]
        sig_gate = jax.nn.sigmoid(gate)
        gate_start = proj_width + LANES + head * DV
        out_ref[here, gate_start : gate_start + DV] = lower(
            grad_gated * normed * sig_gate * (1.0 + gate * (1.0 - sig_gate))
        )
        normed_grad = grad_gated * (gate * sig_gate)
        scaled = normed_grad * gain
        grad_mixed = lower(
            head_inverse * scaled
            - mixed
            * (head_inverse * head_inverse * head_inverse)
            * jnp.mean(scaled * mixed, axis=-1, keepdims=True)
        )
        gain_grads.append(
            jnp.sum(normed_grad * mixed * head_inverse, axis=0, keepdims=True)
        )
        base = head * ROW
        query_raw = active[here, base : base + DK]
        key_raw = active[here, base + DK : base + 2 * DK]
        value = active[here, base + 2 * DK : base + ROW]
        query_unit = unit(query_raw)
        key_unit = unit(key_raw)
        query = query_raw * (query_unit * DK ** (-0.5))
        key = key_raw * key_unit
        strength = strength_rows[here, 2 * head : 2 * head + 1]
        cumulative = cumulative_rows[block][:, 2 * head + 1 : 2 * head + 2]
        across = turned_rows[block][2 * head + 1 : 2 * head + 2]
        final = cumulative[CHUNK - 1 :]
        fade = jnp.where(
            rows >= columns, jnp.exp(jnp.minimum(cumulative - across, 0.0)), 0.0
        )
        strict_fade = jnp.where(rows > columns, fade, 0.0)
        grown = jnp.exp(cumulative)
        remaining = jnp.exp(final - cumulative)
        kept = jnp.exp(final)
        key_low = lower(key)
        query_low = lower(query)
        yield
        dots = by_transpose(key_low, key_low)
        cross = by_transpose(query_low, key_low)
        held = state_ref[block, head]
        corrected = corrected_ref[here, span]
        weight = weight_ref[here, head * DK : head * DK + DK]
        faded = key * remaining
        faded_low = lower(faded)
        grown_query = query * grown
        yield
        inner_side = over_rows(lower(cross * fade), grad_mixed)
        state_side = over_rows(grad_mixed, lower(grown_query))
        dot_grad = by_transpose(grad_mixed, corrected) * fade
        dot_grad_low = lower(dot_grad)
        grown_grad = by_weight(grad_mixed, held)
        yield
        while (block, head) not in laters:
            yield
        later = laters[block, head]
        later_low = lower(later)
        corrected_grad_low = lower(inner_side + by_transpose(faded_low, later_low))
        yield
        laters[block - 1, head] = (
            later * kept + state_side - over_rows(corrected_grad_low, weight)
        )
        faded_grad = by_weight(corrected, later_low)
        weight_grad = lower(-by_weight(corrected_grad_low, held))
        inverse = inverse_ref[block, head]
        yield
        value_side = over_rows(inverse, corrected_grad_low)
        key_side = over_rows(inverse, weight_grad)
        yield
        lower_grad = -(
            by_transpose(lower(value_side), update_ref[here, span])
            + by_transpose(lower(key_side), weight)
        ) * strict_fade
        inner_query = by_weight(dot_grad_low, key_low)
        inner_key = over_rows(dot_grad_low, query_low)
        yield
        lower_grad_low = lower(lower_grad)
        first_key = by_weight(lower_grad_low, key_low)
        second_key = over_rows(lower_grad_low, lower(strength * key))
        pairs = lower_grad * dots
        both = pairs * strength + dot_grad * cross
        faded_sum = row_sum(faded_grad * faded)
        key_sum = row_sum(key_side * key)
        yield
        query_grad = grown * grown_grad + inner_query
        key_grad = (
            (strength * grown) * key_side
            + strength * first_key
            + second_key
            + inner_key
            + remaining * faded_grad
        )
        head_strength_grad = row_sum(value_side * value) + grown * key_sum + row_sum(pairs)
        head_spread = (
            (strength * grown) * key_sum
            + row_sum(both)
            + row_sum(grown_grad * grown_query)
            - faded_sum
        )
        column_total = jnp.sum(both, axis=0, keepdims=True)
        late_total = row_sum(jnp.where(columns >= rows, column_total, 0.0))
        final_grad = kept * jnp.sum(held.astype(wide) * later, keepdims=True) + jnp.sum(
            faded_sum, axis=0, keepdims=True
        )
        column_grads[block, head] = (
            head_strength_grad,
            head_spread,
            final_grad - late_total,
        )
        active_grads[block, head] = (
            DK ** (-0.5)
            * query_unit
            * (
                query_grad
                - query_raw * (query_unit * query_unit) * row_sum(query_grad * query_raw)
            ),
            key_unit
            * (key_grad - key_raw * (key_unit * key_unit) * row_sum(key_grad * key_raw)),
            strength * value_side,
        )

    in_turn(
        one(block, head) for block in reversed(range(blocks)) for head in range(heads)
    )
    for head in range(heads):
        state_grad[head] = laters[-1, head]
    for block in range(blocks):
        here = slice(block * CHUNK, (block + 1) * CHUNK)
        strength_grad = jnp.zeros((CHUNK, LANES), wide)
        spread_grad = jnp.zeros((CHUNK, LANES), wide)
        extra_grad = jnp.zeros((CHUNK, LANES), wide)
        for head in range(heads):
            first, second, third = column_grads[block, head]
            strength_grad = jnp.where(lanes == 2 * head, first, strength_grad)
            spread_grad = jnp.where(lanes == 2 * head + 1, second, spread_grad)
            extra_grad = jnp.where(lanes == 2 * head + 1, third, extra_grad)
        decay_grad = exact_dot(onward, spread_grad) + extra_grad
        shift_grad = decay_grad * coefficients[1:2] * jax.nn.sigmoid(shifted_rates[here])
        strength_here = strength_rows[here]
        rates_grad = strength_grad * strength_here * (1.0 - strength_here) + shift_grad
        out_ref[here, proj_width : proj_width + LANES] = lower(rates_grad)
        small_grad_ref[0:1] += jnp.sum(shift_grad, axis=0, keepdims=True)
        small_grad_ref[1:2] += jnp.sum(decay_grad * decay_rows[here], axis=0, keepdims=True)
    gain_grad_ref[0:1] += sum(gain_grads)
    joined = jnp.concatenate(
        [
            jnp.concatenate(
                [part for head in range(heads) for part in active_grads[block, head]], axis=1
            )
            for block in range(blocks)
        ],
        axis=0,
    )
    summed_grad = joined * (sig * (1.0 + summed * (1.0 - sig)))
    following = jnp.concatenate([summed_grad, after[...]], axis=0)
    after[...] = summed_grad[:HALO]
    proj_grad = following[CONV - 1 : CONV - 1 + count] * taps[0:1]
    start = HALO - CONV + 1
    for offset in range(CONV):
        if offset:
            shift = CONV - 1 - offset
            proj_grad = proj_grad + following[shift : shift + count] * taps[offset : offset + 1]
        taps_grad_ref[offset : offset + 1] += jnp.sum(
            summed_grad * extended[start + offset : start + offset + count],
            axis=0,
            keepdims=True,
        )
    out_ref[:, :proj_width] = lower(proj_grad)


def params():
    return pltpu.CompilerParams(
        dimension_semantics=("arbitrary",), vmem_limit_bytes=52 * 1024 * 1024
    )


def effort(length, heads):
    return pl.CostEstimate(
        flops=length * heads * 10000000,
        bytes_accessed=length * heads * 8192,
        transcendentals=length * heads * 2048,
    )


def mixer_forward(heads, parts, place, proj, gate, taps, coefficients, gain, interpret=False):
    length = proj.shape[0]
    count = length // parts
    blocks = count // CHUNK
    width = heads * ROW
    values = heads * DV

    def tall(columns, at=0):
        return pl.BlockSpec((count, columns), lambda i, me: (jnp.bitwise_xor(i, me[0]), at))

    def whole(array):
        return pl.BlockSpec(array.shape, lambda i, me: (0,) * array.ndim)

    def stacked(first, second):
        return pl.BlockSpec((blocks, heads, first, second), lambda i, me: (i, 0, 0, 0))

    chunks = parts * blocks
    return pl.pallas_call(
        lambda *refs: forward_kernel(heads, *refs),
        grid_spec=pltpu.PrefetchScalarGridSpec(
            num_scalar_prefetch=1,
            grid=(parts,),
            in_specs=[
                tall(width),
                tall(LANES, width // LANES),
                tall(values),
                whole(taps),
                whole(coefficients),
                whole(gain),
            ],
            out_specs=[
                tall(values),
                tall(values),
                stacked(CHUNK, CHUNK),
                stacked(DV, DK),
                tall(values),
                tall(values),
                tall(heads * DK),
            ],
            scratch_shapes=[
                pltpu.VMEM((HALO, width), wide),
                pltpu.VMEM((heads, DV, DK), wide),
            ],
        ),
        out_shape=[
            jax.ShapeDtypeStruct((length, values), narrow),
            jax.ShapeDtypeStruct((length, values), narrow),
            jax.ShapeDtypeStruct((chunks, heads, CHUNK, CHUNK), narrow),
            jax.ShapeDtypeStruct((chunks, heads, DV, DK), narrow),
            jax.ShapeDtypeStruct((length, values), narrow),
            jax.ShapeDtypeStruct((length, values), narrow),
            jax.ShapeDtypeStruct((length, heads * DK), narrow),
        ],
        compiler_params=params(),
        cost_estimate=effort(length, heads),
        interpret=interpret,
    )(place, proj, proj, gate, taps, coefficients, gain)


def mixer_backward(
    heads, parts, place, proj, gate, taps, coefficients, gain, kept, grad_gated, interpret=False
):
    length = proj.shape[0]
    count = length // parts
    blocks = count // CHUNK
    width = heads * ROW
    values = heads * DV
    edge_rows = 2 * HALO
    ratio = count // edge_rows

    def tall(columns, at=0):
        return pl.BlockSpec(
            (count, columns), lambda i, me: (jnp.bitwise_xor(parts - 1 - i, me[0]), at)
        )

    def edge_at(i, me):
        previous = jnp.bitwise_xor(jnp.maximum(parts - 2 - i, 0), me[0])
        return (previous * ratio + ratio - 1, 0)

    def whole(shape):
        return pl.BlockSpec(shape, lambda i, me: (0,) * len(shape))

    def stacked(first, second):
        return pl.BlockSpec(
            (blocks, heads, first, second), lambda i, me: (parts - 1 - i, 0, 0, 0)
        )

    total = width + LANES + values
    return pl.pallas_call(
        lambda *refs: backward_kernel(heads, *refs),
        grid_spec=pltpu.PrefetchScalarGridSpec(
            num_scalar_prefetch=1,
            grid=(parts,),
            in_specs=[
                tall(width),
                pl.BlockSpec((edge_rows, width), edge_at),
                tall(LANES, width // LANES),
                tall(values),
                whole(taps.shape),
                whole(coefficients.shape),
                whole(gain.shape),
                tall(values),
                stacked(CHUNK, CHUNK),
                stacked(DV, DK),
                tall(values),
                tall(values),
                tall(heads * DK),
                tall(values),
            ],
            out_specs=[
                tall(total),
                whole((HALO, width)),
                whole((HALO, DV)),
                whole((HALO, LANES)),
            ],
            scratch_shapes=[
                pltpu.VMEM((HALO, width), wide),
                pltpu.VMEM((heads, DV, DK), wide),
            ],
        ),
        out_shape=[
            jax.ShapeDtypeStruct((length, total), narrow),
            jax.ShapeDtypeStruct((HALO, width), wide),
            jax.ShapeDtypeStruct((HALO, DV), wide),
            jax.ShapeDtypeStruct((HALO, LANES), wide),
        ],
        compiler_params=params(),
        cost_estimate=effort(length, heads),
        interpret=interpret,
    )(place, proj, proj, proj, gate, taps, coefficients, gain, *kept, grad_gated)


def to_lanes(array):
    groups, rows, columns = array.shape
    split = array.reshape(groups, rows, columns // LANES, LANES)
    return jnp.swapaxes(split, 1, 2).reshape(groups, -1, LANES)


def from_lanes(array, rows):
    groups = array.shape[0]
    split = array.reshape(groups, -1, rows, LANES)
    return jnp.swapaxes(split, 1, 2).reshape(groups, rows, -1)


def per_device(
    tokens,
    cotangent,
    norm_attn,
    w_qkv,
    w_ba,
    conv_w,
    a_log,
    dt_bias,
    w_outgate,
    head_gain,
    w_out,
    norm_ffn,
    w_gate,
    w_up,
    w_down,
    interpret=False,
):
    parts = lax.axis_size("seq")
    shards = lax.axis_size("dp")
    place = lax.axis_index("seq")
    head_count = a_log.shape[0]
    heads = head_count // parts
    width = heads * ROW
    values = heads * DV
    model = tokens.shape[2]
    own = norm_attn.shape[0]
    out_rows = w_out.shape[0]
    quarter = model // parts

    def mine(array, size, axis):
        return lax.dynamic_slice_in_dim(array, place * size, size, axis)

    def flip(array, bit):
        return lax.ppermute(array, "seq", [(i, i ^ bit) for i in range(parts)])

    def over_dp(array):
        return lax.all_gather(array, "dp", axis=0, tiled=True)

    def sum_dp(array):
        return lax.psum_scatter(array, "dp", scatter_dimension=0, tiled=True)

    def gather_seq(array):
        across = flip(array, 2)
        near = jnp.concatenate([array, flip(array, 1)], axis=0)
        far = jnp.concatenate([across, flip(across, 1)], axis=0)
        return near, far

    def scatter_seq(near, far):
        half = near.shape[0] // 2
        across = far[:half] + flip(lower(far[half:]), 1).astype(wide)
        across = flip(lower(across), 2)
        beside = flip(lower(near[half:]), 1)
        return near[:half] + beside.astype(wide) + across.astype(wide)

    def absolute(stack):
        return jnp.concatenate(
            [
                lax.dynamic_index_in_dim(stack, jnp.bitwise_xor(place, at), 0)
                for at in range(parts)
            ],
            axis=0,
        )

    def stack_seq(array):
        near, far = gather_seq(array[None])
        return jnp.concatenate([near, far], axis=0)

    def exchange(stack):
        pieces = [
            lax.dynamic_index_in_dim(stack, jnp.bitwise_xor(place, at), 0)
            for at in range(parts)
        ]
        return absolute(
            jnp.concatenate(
                [pieces[0]] + [flip(pieces[at], at) for at in range(1, parts)], axis=0
            )
        )

    ffn = w_gate.shape[1]
    piece = ffn // (shards * parts)
    ffn_own = -(-(piece * shards) // LANES) * LANES
    padded = ffn_own // shards

    def ffn_columns(array):
        split = array.reshape(own, shards, parts, piece)
        split = lax.dynamic_index_in_dim(split, place, 2, keepdims=False)
        split = jnp.pad(split, ((0, 0), (0, 0), (0, padded - piece)))
        return to_lanes(split.reshape(1, own, ffn_own))[0]

    own_tokens = tokens[:, 0, :]
    own_cot = cotangent[:, 0, :]
    all_tokens = jnp.concatenate(gather_seq(own_tokens), axis=0)
    small_flat = jnp.concatenate([norm_attn, norm_ffn, conv_w.reshape(-1)])
    small_all = over_dp(small_flat[None, :])
    first_gain = small_all[:, :own].reshape(-1).astype(wide)
    second_gain = small_all[:, own : 2 * own].reshape(-1).astype(wide)
    taps_all = jnp.swapaxes(small_all[:, 2 * own :].reshape(shards, CONV, -1), 0, 1)
    taps = mine(taps_all.reshape(CONV, -1), width, 1).astype(wide)
    taps = jnp.pad(taps, ((0, HALO - CONV), (0, 0)))
    w_in = over_dp(
        jnp.concatenate(
            [
                mine(w_qkv, width, 1),
                jnp.pad(mine(w_ba, 2 * heads, 1), ((0, 0), (0, LANES - 2 * heads))),
                mine(w_outgate, values, 1),
            ],
            axis=1,
        )
    )
    ffn_part = jnp.concatenate(
        [
            ffn_columns(w_gate),
            ffn_columns(w_up),
            to_lanes(
                jnp.pad(
                    mine(w_down, piece, 0), ((0, padded - piece), (0, 0))
                )[None]
            )[0],
            to_lanes(mine(w_out, quarter, 1)[None])[0],
        ],
        axis=0,
    )
    ffn_part, w_in = lax.optimization_barrier((ffn_part, w_in))
    ffn_all = over_dp(ffn_part).reshape(shards, -1, LANES)
    decay_part = mine(a_log, heads, 0)
    bias_part = mine(dt_bias, heads, 0)

    def odd_lanes(vector):
        spaced = jnp.stack([jnp.zeros_like(vector), vector], axis=1).reshape(-1)
        return jnp.pad(spaced, (0, LANES - 2 * heads))[None, :]

    coefficients = jnp.pad(
        jnp.concatenate([odd_lanes(bias_part), odd_lanes(-jnp.exp(decay_part))], axis=0),
        ((0, HALO - 2), (0, 0)),
    )
    gain = jnp.broadcast_to(head_gain.astype(wide)[None, :], (HALO, DV))
    place_row = place.astype(jnp.int32)[None]

    rows = own_tokens.astype(wide)
    inverse_one = row_norm(rows, first_gain)[1]
    all_rows = all_tokens.astype(wide)
    normed_one, all_inverse = row_norm(all_rows, first_gain)
    normed_one = lower(normed_one)
    proj = lower(by_weight(normed_one, w_in[:, : width + LANES]))
    out_gate = by_weight(normed_one, w_in[:, width + LANES :])
    proj, cot_halves = lax.optimization_barrier((proj, gather_seq(own_cot)))
    gated, *kept = mixer_forward(
        heads, parts, place_row, proj, out_gate, taps, coefficients, gain, interpret
    )
    ffn_all, gated = lax.optimization_barrier((ffn_all, gated))
    out_part = from_lanes(ffn_all[:, -out_rows * (quarter // LANES) :], out_rows)
    w_out_own = jnp.swapaxes(
        exchange(out_part.reshape(parts, values, quarter)), 0, 1
    ).reshape(values, model)
    wide_rows = own * (ffn_own // LANES)
    gate_own = from_lanes(ffn_all[:, :wide_rows], own).reshape(model, ffn_own)
    up_own = from_lanes(ffn_all[:, wide_rows : 2 * wide_rows], own).reshape(model, ffn_own)
    down_own = from_lanes(ffn_all[:, 2 * wide_rows : 2 * wide_rows + padded * (model // LANES)], padded).reshape(ffn_own, model)
    half = gated.shape[0] // 2
    mixed_far = by_weight(gated[half:], w_out_own)
    mixed_near = by_weight(gated[:half], w_out_own)
    after_mix = rows + scatter_seq(mixed_near, mixed_far)
    normed_two, inverse_two = row_norm(after_mix, second_gain)
    sides = []
    for normed_half, cot_half in zip(gather_seq(lower(normed_two)), cot_halves):
        gate_pre = by_weight(normed_half, gate_own)
        up_pre = by_weight(normed_half, up_own)
        sig_ffn = jax.nn.sigmoid(gate_pre)
        hidden = lower(gate_pre * sig_ffn * up_pre)
        grad_hidden = by_transpose(cot_half, down_own)
        grad_gate_pre = lower(
            grad_hidden * up_pre * sig_ffn * (1.0 + gate_pre * (1.0 - sig_ffn))
        )
        grad_up_pre = lower(grad_hidden * gate_pre * sig_ffn)
        back = by_transpose(grad_gate_pre, gate_own) + by_transpose(grad_up_pre, up_own)
        sides.append(
            (
                back,
                by_weight(hidden, down_own),
                over_rows(normed_half, grad_gate_pre),
                over_rows(normed_half, grad_up_pre),
                over_rows(hidden, cot_half),
            )
        )
    near_side, far_side = sides
    back_two, grad_norm_ffn = norm_back(
        after_mix, inverse_two, second_gain, scatter_seq(near_side[0], far_side[0])
    )
    grad_after = own_cot.astype(wide) + back_two
    result = after_mix + scatter_seq(near_side[1], far_side[1])
    grad_ffn = sum_dp(
        jnp.concatenate(
            [
                to_lanes(lower(near_side[2] + far_side[2]).reshape(shards, own, ffn_own)),
                to_lanes(lower(near_side[3] + far_side[3]).reshape(shards, own, ffn_own)),
                to_lanes(lower(near_side[4] + far_side[4]).reshape(shards, padded, model)),
            ],
            axis=1,
        ).reshape(-1, LANES)
    )
    grad_branch = jnp.concatenate(gather_seq(lower(grad_after)), axis=0)
    grad_gated = by_transpose(grad_branch, w_out_own)
    grad_out = jnp.swapaxes(
        lower(over_rows(gated, grad_branch)).reshape(values, parts, quarter), 0, 1
    )
    grad_out = exchange(grad_out).reshape(shards, out_rows, quarter)
    grad_in, grad_taps, grad_gain, grad_small = mixer_backward(
        heads, parts, place_row, proj, out_gate, taps, coefficients, gain, kept, grad_gated, interpret
    )
    one_far = by_transpose(grad_in[half:], w_in)
    one_near = by_transpose(grad_in[:half], w_in)
    hat = all_rows * all_inverse
    grad_norm_attn = jnp.sum(one_far * hat[half:], axis=0) + jnp.sum(
        one_near * hat[:half], axis=0
    )
    grad_w_in = lower(over_rows(normed_one, grad_in)).reshape(shards, own, -1)

    taps_full = lax.dynamic_update_slice_in_dim(
        jnp.zeros((CONV, head_count * ROW), wide), grad_taps[:CONV], place * width, 1
    )

    def to_heads(lane_row):
        return lax.dynamic_update_slice_in_dim(
            jnp.zeros((head_count,), wide), lane_row[1 : 2 * heads : 2], place * heads, 0
        )

    common = jnp.concatenate([grad_gain[0], to_heads(grad_small[1]), to_heads(grad_small[0])])
    own_taps = conv_w.shape[1]
    packed = jnp.concatenate(
        [
            grad_norm_attn.reshape(shards, own),
            grad_norm_ffn.reshape(shards, own),
            jnp.swapaxes(taps_full.reshape(CONV, shards, own_taps), 0, 1).reshape(shards, -1),
            jnp.broadcast_to(common[None], (shards, common.shape[0])),
        ],
        axis=1,
    )
    tile = 2 * HALO * LANES
    packed = jnp.pad(packed, ((0, 0), (0, -packed.shape[1] % tile)))
    in_rows = own * (grad_w_in.shape[2] // LANES)
    lane_rows = out_rows * (quarter // LANES)
    last = sum_dp(
        jnp.concatenate(
            [
                to_lanes(grad_w_in),
                to_lanes(grad_out),
                lower(packed).reshape(shards, -1, LANES),
            ],
            axis=1,
        ).reshape(-1, LANES)
    )
    back_one = norm_back(rows, inverse_one, first_gain, scatter_seq(one_near, one_far))[0]
    grad_rows = lower(grad_after + back_one)[:, None, :]

    last_all = stack_seq(last)
    small_total = jnp.sum(
        last_all[:, in_rows + lane_rows :].astype(wide), axis=0
    ).reshape(-1)
    last_all = absolute(last_all)
    ffn_grads = absolute(stack_seq(grad_ffn))

    def side_by_side(array):
        return jnp.swapaxes(array, 0, 1).reshape(array.shape[1], -1).astype(wide)

    in_all = from_lanes(last_all[:, :in_rows], own)
    out_all = from_lanes(last_all[:, in_rows : in_rows + lane_rows], out_rows)

    def ffn_full(array):
        split = from_lanes(array, own).reshape(parts, own, shards, padded)[..., :piece]
        return jnp.transpose(split, (1, 2, 0, 3)).reshape(own, -1).astype(wide)

    down_all = from_lanes(ffn_grads[:, 2 * wide_rows :], padded)[:, :piece]
    taps_at = 2 * own
    gain_at = taps_at + CONV * own_taps
    heads_at = gain_at + DV

    return (
        lower(result)[:, None, :],
        grad_rows,
        small_total[:own],
        side_by_side(in_all[:, :, :width]),
        side_by_side(in_all[:, :, width : width + 2 * heads]),
        small_total[taps_at:gain_at].reshape(CONV, own_taps),
        small_total[heads_at : heads_at + head_count],
        small_total[heads_at + head_count : heads_at + 2 * head_count],
        side_by_side(in_all[:, :, width + LANES :]),
        small_total[gain_at:heads_at],
        side_by_side(out_all),
        small_total[own:taps_at],
        ffn_full(ffn_grads[:, :wide_rows]),
        ffn_full(ffn_grads[:, wide_rows : 2 * wide_rows]),
        down_all.reshape(parts * piece, model).astype(wide),
    )


def solution(mesh):
    return jax.shard_map(
        per_device,
        mesh=mesh,
        in_specs=(
            P("seq", "dp", None),
            P("seq", "dp", None),
            P("dp"),
            P("dp", None),
            P("dp", None),
            P(None, "dp"),
            P(),
            P(),
            P("dp", None),
            P(),
            P("dp", None),
            P("dp"),
            P("dp", None),
            P("dp", None),
            P("dp", None),
        ),
        out_specs=(
            P("seq", "dp", None),
            P("seq", "dp", None),
            P("dp"),
            P("dp", None),
            P("dp", None),
            P(None, "dp"),
            P(),
            P(),
            P("dp", None),
            P(),
            P("dp", None),
            P("dp"),
            P("dp", None),
            P("dp", None),
            P("dp", None),
        ),
        check_vma=False,
    )
```

time: 1290 us -> 687 us (0.53)
  waiting for transfers between devices: 873 us -> 274 us
  local copies, waits for them, and re-layouts: 38.4 us -> 89.7 us
  blocking collectives: 82.4 us -> 31.1 us
  Pallas kernels: 117 us -> 83 us
  other arithmetic: 25.3 us -> 55.2 us
  starting transfers between devices: 4.59 us -> 19.7 us
    reduce_scatter x7 -> x2, waiting for transfers between devices: 284 us -> 44.3 us  [sum_dp(): return lax.psum_scatter(array, 'dp', scatter_dimension=0, tiled=True)]
    ppermute x0 -> x36, waiting for transfers between devices: none -> 167 us  [flip(): return lax.ppermute(array, 'seq', [(i, i ^ bit) for i in range(parts)])]
    all_gather x5 -> x0, waiting for transfers between devices: 138 us -> none  [the longest x4 120 us: over_seq(): return lax.all_gather(array, 'seq', axis=0, tiled=True)]
    all_gather x5 -> x2, waiting for transfers between devices: 186 us -> 62.4 us  [over_dp(): return lax.all_gather(array, 'dp', axis=0, tiled=True)]
    unnamed x22 -> x4, waiting for transfers between devices: 123 us -> 0.07 us
    psum x1 -> x0, waiting for transfers between devices: 121 us -> none  [per_device(): lax.psum(jnp.concatenate([grad_norm_attn, grad_norm_ffn, taps_full.reshap...]
    pallas_call x2, Pallas kernels: 117 us -> 83 us  [the longest x1 53.7 us: mixer_backward(): pl.pallas_call(lambda *refs: backward_kernel(heads, *refs), grid_spec=plt...]
    all_gather x4 -> x0, blocking collectives: 32.2 us -> none  [the longest x2 16.5 us: stack_seq(): return lax.all_gather(array, 'seq', axis=0)]
  transfers between devices with their start and end apart: 21 -> 40, of which waited for: 20 -> 15; matrix products, arithmetic and copies ran while one was open for 9% -> 31% of each run, Pallas kernels for 0% -> 12%
where the time goes in v2:
time: 687 us; the launch traced here: 679 us
  waiting for transfers between devices  274 us (40%)
  matrix products  110 us (16%)
  local copies, waits for them, and re-layouts  89.7 us (13%)
  Pallas kernels  83 us (12%)
  other arithmetic  55.2 us (8%)
  blocking collectives  31.1 us (5%)
  starting transfers between devices  19.7 us (3%)
  between operations  15.7 us (2%)
    ppermute x36, waiting for transfers between devices, flip(): return lax.ppermute(array, 'seq', [(i, i ^ bit) for i in range(parts)])  167 us
    all_gather x2, waiting for transfers between devices, over_dp(): return lax.all_gather(array, 'dp', axis=0, tiled=True)  62.4 us
    pallas_call x1, Pallas kernels, mixer_backward(): pl.pallas_call(lambda *refs: backward_kernel(heads, *refs), grid_spec=plt...  53.7 us
    reduce_scatter x2, waiting for transfers between devices, sum_dp(): return lax.psum_scatter(array, 'dp', scatter_dimension=0, tiled=True)  44.3 us
    dot_general x9, matrix products, by_transpose(): lax.dot_general(left, right, (((1,), (1,)), ((), ())), preferred_element_...  38.9 us
    dot_general x8, matrix products, over_rows(): lax.dot_general(left, right, (((0,), (0,)), ((), ())), preferred_element_...  36.4 us
    dot_general x10, matrix products, by_weight(): return jnp.dot(left, right, preferred_element_type=wide)  35.2 us
    all_gather x1, blocking collectives, over_dp(): return lax.all_gather(array, 'dp', axis=0, tiled=True)  31.1 us
  transfers between devices with their start and end apart: 40, of which 15 were waited for; matrix products, arithmetic and copies ran while one was open for 31% of the time, Pallas kernels for 12%

profile of v2, /device:TPU:0, one launch (start us, length us, event | category | flops | bytes accessed | tf_op | source)
XLA Modules:
  0.0 678.7 jit_solution(8304695203706821771)
XLA Ops:
  14.7 62.3 %all-gather.5.cloned.1.call-done = bf16[1024,1664]{1,0:T(8,128)(2,1)} async-done(((bf16[128,1664]{1,0:T(8,128)(2,1)}), bf16[1024,1664]{1,0:T(8,128)(2,1)}) %all-gather.5.cloned.1.call-update) | async-done | bytes 3407888 | tf_op jit(solution)/shard_map/all_gather | solution.py:659
  80.1 23.3 %collective-permute-done.4 = bf16[512,1024]{1,0:T(8,128)(2,1)} collective-permute-done((bf16[512,1024]{1,0:T(8,128)(2,1)S(1)}, bf16[512,1024]{1,0:T(8,128)(2,1)}, u32[]{:S(2)}, u32[]{:S(2)}) %collective-permute-start.4) | collective-permute-done | bytes 1048608 | tf_op jit(solution)/shard_map/ppermute | solution.py:656
  103.5 20.2 %collective-permute-done.1 = bf16[512,1024]{1,0:T(8,128)(2,1)S(1)} collective-permute-done((bf16[512,1024]{1,0:T(8,128)(2,1)S(1)}, bf16[512,1024]{1,0:T(8,128)(2,1)S(1)}, u32[]{:S(2)}, u32[]{:S(2)}) %collective-permute-start.1) | collective-permute-done | bytes 1048608 | tf_op jit(solution)/shard_map/ppermute | solution.py:656
  123.7 31.1 %all-gather.1 = bf16[8,1,2304]{2,1,0:T(2,128)(2,1)S(1)} all-gather(bf16[1,1,2304]{2,1,0:T(2,128)(2,1)S(1)} %reshape.269), channel_id=2, replica_groups=mesh['seq'=4,'dp'=8] {'dp'}, dimensions={0}, use_global_device_ids=true | all-gather | bytes 41472 | tf_op jit(solution)/shard_map/all_gather | solution.py:659
  163.6 10.8 %convolution_convert_fusion.refs_1_.refs_2_.refs_3_ = bf16[2048,1152]{1,0:T(8,128)(2,1)} fusion(bf16[1024,1664]{1,0:T(8,128)(2,1)S(1)} %copy-done.43, f32[1024]{0:T(1024)S(1)} %get-tuple-element.144, f32[2048]{0:T(1024)S(1)} %add_rsqrt_fusion, bf16[512,1024]{1,0:T(8,128)(2,1)} %collective-permute-done.2, bf16[512,1024]{1,0:T(8,128)(2,1)S(1)} %collective-permute-done.1, ...), kind=kOutput, calls=%fused_computation.4 | convolution fusion | flops 4857266176 | bytes 11284480 | tf_op jit(solution)/shard_map/dot_general | solution.py:22
  174.4 6.0 fusion.56.refs_3_.refs_4_
  180.4 29.3 %shard_map.262 = (bf16[2048,512]{1,0:T(8,128)(2,1)}, bf16[2048,512]{1,0:T(8,128)(2,1)}, bf16[8,2,256,256]{3,2,1,0:T(8,128)(2,1)}, bf16[8,2,256,128]{3,2,1,0:T(8,...) custom-call(s32[1]{0:T(128)} %bitcast.17.refs_0_, ...), custom_call_target="tpu_custom_call" | custom-call | flops 40960000000 | bytes 33554432 | tf_op jit(solution)/shard_map/pallas_call | solution.py:495
  214.9 7.3 %collective-permute-done.7 = bf16[1,512,256]{2,1,0:T(8,128)(2,1)S(1)} collective-permute-done((bf16[1,512,256]{2,1,0:T(8,128)(2,1)S(1)}, bf16[1,512,256]{2,1,0:T(8,128)(2,1)S(1)}, u32[]{:S(2)}, u32[]{:S(2)}) %collective-permute-start.7) | collective-permute-done | bytes 262176 | tf_op jit(solution)/shard_map/ppermute | solution.py:656
  235.8 23.9 %collective-permute-done.11 = bf16[512,1024]{1,0:T(8,128)(2,1)S(1)} collective-permute-done((bf16[512,1024]{1,0:T(8,128)(2,1)S(1)}, bf16[512,1024]{1,0:T(8,128)(2,1)S(1)}, u32[]{:S(2)}, u32[]{:S(2)}) %collective-permute-start.11) | collective-permute-done | bytes 1048608 | tf_op jit(solution)/shard_map/ppermute | solution.py:656
  285.6 6.8 collective-permute-done.14
  346.5 5.8 collective-permute-done.20
  355.5 18.4 %collective-permute-done.17 = bf16[512,1024]{1,0:T(8,128)(2,1)} collective-permute-done((bf16[512,1024]{1,0:T(8,128)(2,1)}, bf16[512,1024]{1,0:T(8,128)(2,1)}, u32[]{:S(2)}, u32[]{:S(2)}) %collective-permute-start.17) | collective-permute-done | bytes 1048608 | tf_op jit(solution)/shard_map/ppermute | solution.py:656
  393.2 10.3 %collective-permute-done.22 = bf16[512,1024]{1,0:T(8,128)(2,1)} collective-permute-done((bf16[512,1024]{1,0:T(8,128)(2,1)}, bf16[512,1024]{1,0:T(8,128)(2,1)}, u32[]{:S(2)}, u32[]{:S(2)}) %collective-permute-start.22) | collective-permute-done | bytes 1048608 | tf_op jit(solution)/shard_map/ppermute | solution.py:656
  421.3 6.2 fusion.72.refs_14_
  427.5 53.7 %shard_map.263 = (bf16[2048,1664]{1,0:T(8,128)(2,1)}, f32[8,1024]{1,0:T(8,128)S(1)}, f32[8,256]{1,0:T(8,128)S(1)}, f32[8,128]{1,0:T(8,128)S(1)}) custom-call(s32[1]{0:T(128)} %bitcast.17.refs_0_, bf16[2048,1152]{1,0:T(8,128)(2,1)} %convolution_convert_fusion.refs_1_.refs_2_.refs_3_, bf16[2048,1152]{1,0:T(8,128)(2,1)} %convolution_convert_fusion.refs_1_.refs_2_.refs_3_, ...), custom_call_target="tpu_custom_call" | custom-call | flops 40960000000 | bytes 33554432 | tf_op jit(solution)/shard_map/pallas_call | solution.py:566
  482.1 7.5 %fusion.3 = f32[1024,1024]{1,0:T(8,128)S(1)} fusion(bf16[1024,1664]{1,0:T(8,128)(2,1)} %all-gather.5.cloned.1.call-done, bf16[2048,1664]{1,0:T(8,128)(2,1)} %get-tuple-element.47), kind=kOutput, calls=%fused_computation.18 | convolution fusion | flops 3489660928 | bytes 11010048 | tf_op jit(solution)/shard_map/dot_general | solution.py:26
  489.7 9.8 %fusion.1 = (f32[1024]{0:T(1024)S(1)}, f32[1024]{0:T(1024)S(1)}, f32[1024,1024]{1,0:T(8,128)}) fusion(f32[2048,1024]{1,0:T(8,128)} %convert_multiply_fusion, f32[1024,1024]{1,0:T(8,128)S(1)} %fusion.3, bf16[1024,1664]{1,0:T(8,128)(2,1)S(1)} %copy-done.44, bf16[2048,1664]{1,0:T(8,128)(2,1)S(1)} %copy-done.53), kind=kOutput, calls=%fused_computation.8 | convolution fusion | flops 3493853184 | bytes 23601152 | tf_op jit(solution)/shard_map/dot_general | solution.py:26
  499.5 11.4 %convolution_convert_fusion.1 = bf16[1024,1664]{1,0:T(8,128)(2,1)} fusion(bf16[2048,1664]{1,0:T(8,128)(2,1)S(1)} %copy-done.53, f32[1024]{0:T(1024)S(1)} %copy-done.34, f32[2048]{0:T(1024)S(1)} %copy-done.36, bf16[512,1024]{1,0:T(8,128)(2,1)} %collective-permute-done.2, bf16[512,1024]{1,0:T(8,128)(2,1)S(1)} %copy-done.17, ...), kind=kOutput, calls=%fused_computation.13 | convolution fusion | flops 7004094464 | bytes 14430208 | tf_op jit(solution)/shard_map/dot_general | solution.py:32
  511.0 5.6 copy.115
  521.2 5.9 copy.116
  541.6 24.1 %collective-permute-done.26 = bf16[512,1024]{1,0:T(8,128)(2,1)S(1)} collective-permute-done((bf16[512,1024]{1,0:T(8,128)(2,1)}, bf16[512,1024]{1,0:T(8,128)(2,1)S(1)}, u32[]{:S(2)}, u32[]{:S(2)}) %collective-permute-start.26) | collective-permute-done | bytes 1048608 | tf_op jit(solution)/shard_map/ppermute | solution.py:656
  568.2 9.8 %collective-permute-done.34 = bf16[1,2304,128]{2,1,0:T(8,128)(2,1)S(1)} collective-permute-done((bf16[1,2304,128]{2,1,0:T(8,128)(2,1)}, bf16[1,2304,128]{2,1,0:T(8,128)(2,1)S(1)}, u32[]{:S(2)}, u32[]{:S(2)}) %collective-permute-start.34) | collective-permute-done | bytes 589856 | tf_op jit(solution)/shard_map/ppermute | solution.py:656
  582.0 44.3 %reduce-scatter.3.cloned.1.call-done = bf16[2208,128]{1,0:T(8,128)(2,1)} async-done(((bf16[17664,128]{1,0:T(8,128)(2,1)}), bf16[2208,128]{1,0:T(8,128)(2,1)}) %reduce-scatter.3.cloned.1.call-update) | async-done | bytes 565264 | tf_op jit(solution)/shard_map/reduce_scatter | solution.py:662
  629.4 11.7 %collective-permute-done.31 = bf16[1,2208,128]{2,1,0:T(8,128)(2,1)} collective-permute-done((bf16[1,2208,128]{2,1,0:T(8,128)(2,1)}, bf16[1,2208,128]{2,1,0:T(8,128)(2,1)}, u32[]{:S(2)}, u32[]{:S(2)}) %collective-permute-start.31) | collective-permute-done | bytes 565280 | tf_op jit(solution)/shard_map/ppermute | solution.py:656
  (361 shorter events, 217.6 us)
Async XLA Ops:
  7.2 69.9 %all-gather.5.cloned.1.call-start = ((), (), s32[]{:S(2)}) async-start(), calls=%async_computation.2 | async-start | bytes 3833856 | tf_op jit(solution)/shard_map/all_gather | solution.py:659
  10.2 199.5 %all-gather.7.cloned.1.call-start = ((), (), s32[]{:S(2)}) async-start(), calls=%async_computation.3 | async-start | bytes 6488064 | tf_op jit(solution)/shard_map/all_gather | solution.py:659
  77.1 464.1 %reduce-scatter.5.cloned.1.call-start = ((), (), s32[]{:S(2)}) async-start(), calls=%async_computation.5 | async-start | bytes 5308416 | tf_op jit(solution)/shard_map/reduce_scatter | solution.py:662
  77.2 26.3 %collective-permute-start.4 = (bf16[512,1024]{1,0:T(8,128)(2,1)S(1)}, bf16[512,1024]{1,0:T(8,128)(2,1)}, u32[]{:S(2)}, u32[]{:S(2)}) collective-permute-start(bf16[512,1024]{1,0:T(8,128)(2,1)S(1)} %bitcast.313), channel_id=1, source_target_pairs={{0,16},{8,24},{16,0},{24,8},{1,17},{9,25},{17,1},{25,9},{2,18},{10... | collective-permute-start | bytes 3145736 | tf_op jit(solution)/shard_map/ppermute | solution.py:656
  78.7 45.0 %collective-permute-start.1 = (bf16[512,1024]{1,0:T(8,128)(2,1)S(1)}, bf16[512,1024]{1,0:T(8,128)(2,1)S(1)}, u32[]{:S(2)}, u32[]{:S(2)}) collective-permute-start(bf16[512,1024]{1,0:T(8,128)(2,1)S(1)} %bitcast.278), channel_id=1, source_target_pairs={{0,16},{8,24},{16,0},{24,8},{1,17},{9,25},{17,1},{25,9},{2,18},{10... | collective-permute-start | bytes 3145736 | tf_op jit(solution)/shard_map/ppermute | solution.py:656
  79.3 76.0 %collective-permute-start.3 = (bf16[512,1024]{1,0:T(8,128)(2,1)S(1)}, bf16[512,1024]{1,0:T(8,128)(2,1)}, u32[]{:S(2)}, u32[]{:S(2)}) collective-permute-start(bf16[512,1024]{1,0:T(8,128)(2,1)S(1)} %bitcast.314), channel_id=1, source_target_pairs={{0,8},{8,0},{16,24},{24,16},{1,9},{9,1},{17,25},{25,17},{2,10},{10... | collective-permute-start | bytes 3145736 | tf_op jit(solution)/shard_map/ppermute | solution.py:656
  79.3 81.8 %collective-permute-start = (bf16[512,1024]{1,0:T(8,128)(2,1)S(1)}, bf16[512,1024]{1,0:T(8,128)(2,1)}, u32[]{:S(2)}, u32[]{:S(2)}) collective-permute-start(bf16[512,1024]{1,0:T(8,128)(2,1)S(1)} %bitcast.279), channel_id=1, source_target_pairs={{0,8},{8,0},{16,24},{24,16},{1,9},{9,1},{17,25},{25,17},{2,10},{10... | collective-permute-start | bytes 3145736 | tf_op jit(solution)/shard_map/ppermute | solution.py:656
  103.4 54.6 %collective-permute-start.5 = (bf16[512,1024]{1,0:T(8,128)(2,1)}, bf16[512,1024]{1,0:T(8,128)(2,1)}, u32[]{:S(2)}, u32[]{:S(2)}) collective-permute-start(bf16[512,1024]{1,0:T(8,128)(2,1)} %collective-permute-done.4), channel_id=1, source_target_pairs={{0,8},{8,0},{16,24},{24,16},{1,9},{9,1},{17,25},{25,17},{2,10},{10... | collective-permute-start | bytes 3145736 | tf_op jit(solution)/shard_map/ppermute | solution.py:656
  123.7 37.4 %collective-permute-start.2 = (bf16[512,1024]{1,0:T(8,128)(2,1)S(1)}, bf16[512,1024]{1,0:T(8,128)(2,1)}, u32[]{:S(2)}, u32[]{:S(2)}) collective-permute-start(bf16[512,1024]{1,0:T(8,128)(2,1)S(1)} %collective-permute-done.1), channel_id=1, source_target_pairs={{0,8},{8,0},{16,24},{24,16},{1,9},{9,1},{17,25},{25,17},{2,10},{10... | collective-permute-start | bytes 3145736 | tf_op jit(solution)/shard_map/ppermute | solution.py:656
  234.3 25.4 %collective-permute-start.11 = (bf16[512,1024]{1,0:T(8,128)(2,1)S(1)}, bf16[512,1024]{1,0:T(8,128)(2,1)S(1)}, u32[]{:S(2)}, u32[]{:S(2)}) collective-permute-start(bf16[512,1024]{1,0:T(8,128)(2,1)S(1)} %fusion.25), channel_id=1, source_target_pairs={{0,16},{8,24},{16,0},{24,8},{1,17},{9,25},{17,1},{25,9},{2,18},{10... | collective-permute-start | bytes 3145736 | tf_op jit(solution)/shard_map/ppermute | solution.py:656
  267.2 25.2 %collective-permute-start.14 = (bf16[512,1024]{1,0:T(8,128)(2,1)}, bf16[512,1024]{1,0:T(8,128)(2,1)}, u32[]{:S(2)}, u32[]{:S(2)}) collective-permute-start(bf16[512,1024]{1,0:T(8,128)(2,1)} %multiply_convert_fusion.7), channel_id=1, source_target_pairs={{0,16},{8,24},{16,0},{24,8},{1,17},{9,25},{17,1},{25,9},{2,18},{10... | collective-permute-start | bytes 3145736 | tf_op jit(solution)/shard_map/ppermute | solution.py:656
  299.9 55.6 %collective-permute-start.13 = (bf16[512,1024]{1,0:T(8,128)(2,1)}, bf16[512,1024]{1,0:T(8,128)(2,1)}, u32[]{:S(2)}, u32[]{:S(2)}) collective-permute-start(bf16[512,1024]{1,0:T(8,128)(2,1)} %slice.372), channel_id=1, source_target_pairs={{0,8},{8,0},{16,24},{24,16},{1,9},{9,1},{17,25},{25,17},{2,10},{10... | collective-permute-start | bytes 3145736 | tf_op jit(solution)/shard_map/ppermute | solution.py:656
  318.6 27.9 %collective-permute-start.18 = (bf16[512,1024]{1,0:T(8,128)(2,1)}, bf16[512,1024]{1,0:T(8,128)(2,1)}, u32[]{:S(2)}, u32[]{:S(2)}) collective-permute-start(bf16[512,1024]{1,0:T(8,128)(2,1)} %slice.370), channel_id=1, source_target_pairs={{0,8},{8,0},{16,24},{24,16},{1,9},{9,1},{17,25},{25,17},{2,10},{10... | collective-permute-start | bytes 3145736 | tf_op jit(solution)/shard_map/ppermute | solution.py:656
  325.9 26.3 %collective-permute-start.20 = (bf16[512,1024]{1,0:T(8,128)(2,1)}, bf16[512,1024]{1,0:T(8,128)(2,1)}, u32[]{:S(2)}, u32[]{:S(2)}) collective-permute-start(bf16[512,1024]{1,0:T(8,128)(2,1)} %fusion.19), channel_id=1, source_target_pairs={{0,16},{8,24},{16,0},{24,8},{1,17},{9,25},{17,1},{25,9},{2,18},{10... | collective-permute-start | bytes 3145736 | tf_op jit(solution)/shard_map/ppermute | solution.py:656
  333.9 40.0 %collective-permute-start.17 = (bf16[512,1024]{1,0:T(8,128)(2,1)}, bf16[512,1024]{1,0:T(8,128)(2,1)}, u32[]{:S(2)}, u32[]{:S(2)}) collective-permute-start(bf16[512,1024]{1,0:T(8,128)(2,1)} %fusion.21), channel_id=1, source_target_pairs={{0,16},{8,24},{16,0},{24,8},{1,17},{9,25},{17,1},{25,9},{2,18},{10... | collective-permute-start | bytes 3145736 | tf_op jit(solution)/shard_map/ppermute | solution.py:656
  378.9 24.7 %collective-permute-start.22 = (bf16[512,1024]{1,0:T(8,128)(2,1)}, bf16[512,1024]{1,0:T(8,128)(2,1)}, u32[]{:S(2)}, u32[]{:S(2)}) collective-permute-start(bf16[512,1024]{1,0:T(8,128)(2,1)} %get-tuple-element.102), channel_id=1, source_target_pairs={{0,16},{8,24},{16,0},{24,8},{1,17},{9,25},{17,1},{25,9},{2,18},{10... | collective-permute-start | bytes 3145736 | tf_op jit(solution)/shard_map/ppermute | solution.py:656
  393.1 17.1 %collective-permute-start.21 = (bf16[512,1024]{1,0:T(8,128)(2,1)}, bf16[512,1024]{1,0:T(8,128)(2,1)S(1)}, u32[]{:S(2)}, u32[]{:S(2)}) collective-permute-start(bf16[512,1024]{1,0:T(8,128)(2,1)} %get-tuple-element.102), channel_id=1, source_target_pairs={{0,8},{8,0},{16,24},{24,16},{1,9},{9,1},{17,25},{25,17},{2,10},{10... | collective-permute-start | bytes 3145736 | tf_op jit(solution)/shard_map/ppermute | solution.py:656
  410.1 216.2 %reduce-scatter.3.cloned.1.call-start = ((), (), s32[]{:S(2)}) async-start(), calls=%async_computation.4 | async-start | bytes 5087232 | tf_op jit(solution)/shard_map/reduce_scatter | solution.py:662
  419.1 108.1 %collective-permute-start.27 = (bf16[1,512,256]{2,1,0:T(8,128)(2,1)S(1)}, bf16[1,512,256]{2,1,0:T(8,128)(2,1)S(1)}, u32[]{:S(2)}, u32[]{:S(2)}) collective-permute-start(bf16[1,512,256]{2,1,0:T(8,128)(2,1)S(1)} %bitcast.356), channel_id=1, source_target_pairs={{0,8},{8,0},{16,24},{24,16},{1,9},{9,1},{17,25},{25,17},{2,10},{10... | collective-permute-start | bytes 786440 | tf_op jit(solution)/shard_map/ppermute | solution.py:656
  419.7 107.5 %collective-permute-start.28 = (bf16[1,512,256]{2,1,0:T(8,128)(2,1)S(1)}, bf16[1,512,256]{2,1,0:T(8,128)(2,1)S(1)}, u32[]{:S(2)}, u32[]{:S(2)}) collective-permute-start(bf16[1,512,256]{2,1,0:T(8,128)(2,1)S(1)} %bitcast.357), channel_id=1, source_target_pairs={{0,16},{8,24},{16,0},{24,8},{1,17},{9,25},{17,1},{25,9},{2,18},{10... | collective-permute-start | bytes 786440 | tf_op jit(solution)/shard_map/ppermute | solution.py:656
  421.2 105.9 %collective-permute-start.29 = (bf16[1,512,256]{2,1,0:T(8,128)(2,1)S(1)}, bf16[1,512,256]{2,1,0:T(8,128)(2,1)}, u32[]{:S(2)}, u32[]{:S(2)}) collective-permute-start(bf16[1,512,256]{2,1,0:T(8,128)(2,1)S(1)} %bitcast.358), channel_id=1, source_target_pairs={{0,24},{8,16},{16,8},{24,0},{1,25},{9,17},{17,9},{25,1},{2,26},{10... | collective-permute-start | bytes 786440 | tf_op jit(solution)/shard_map/ppermute | solution.py:656
  539.6 26.2 %collective-permute-start.26 = (bf16[512,1024]{1,0:T(8,128)(2,1)}, bf16[512,1024]{1,0:T(8,128)(2,1)S(1)}, u32[]{:S(2)}, u32[]{:S(2)}) collective-permute-start(bf16[512,1024]{1,0:T(8,128)(2,1)} %fusion.16), channel_id=1, source_target_pairs={{0,16},{8,24},{16,0},{24,8},{1,17},{9,25},{17,1},{25,9},{2,18},{10... | collective-permute-start | bytes 3145736 | tf_op jit(solution)/shard_map/ppermute | solution.py:656
  541.2 36.8 %collective-permute-start.34 = (bf16[1,2304,128]{2,1,0:T(8,128)(2,1)}, bf16[1,2304,128]{2,1,0:T(8,128)(2,1)S(1)}, u32[]{:S(2)}, u32[]{:S(2)}) collective-permute-start(bf16[1,2304,128]{2,1,0:T(8,128)(2,1)} %bitcast.350), channel_id=1, source_target_pairs={{0,16},{8,24},{16,0},{24,8},{1,17},{9,25},{17,1},{25,9},{2,18},{10... | collective-permute-start | bytes 1769480 | tf_op jit(solution)/shard_map/ppermute | solution.py:656
  629.4 18.4 %collective-permute-start.30 = (bf16[1,2208,128]{2,1,0:T(8,128)(2,1)}, bf16[1,2208,128]{2,1,0:T(8,128)(2,1)}, u32[]{:S(2)}, u32[]{:S(2)}) collective-permute-start(bf16[1,2208,128]{2,1,0:T(8,128)(2,1)} %bitcast.56), channel_id=1, source_target_pairs={{0,8},{8,0},{16,24},{24,16},{1,9},{9,1},{17,25},{25,17},{2,10},{10... | collective-permute-start | bytes 1695752 | tf_op jit(solution)/shard_map/ppermute | solution.py:656
  (72 other events, 1264.3 us)
Sparse Core Ops, SparseCore 0:
  10.8 66.2 all-gather.4
  79.8 92.5 all-gather.6
  410.2 95.1 reduce-scatter.4
  533.1 93.1 reduce-scatter.2

commit v3 on v2

--- a/solution.py
+++ b/solution.py
@@ -128,11 +128,8 @@
     place_ref,
     proj_ref,
     rates_ref,
-    gate_ref,
     taps_ref,
     coef_ref,
-    gain_ref,
-    gated_ref,
     mixed_ref,
     inverse_ref,
     state_ref,
@@ -155,7 +152,6 @@
     active = summed * jax.nn.sigmoid(summed)
     strength_rows, unused, decay_rows = gates(rates_ref[...].astype(wide), coef_ref[...])
     through = jnp.where(rows >= columns, 1.0, 0.0)
-    gain = gain_ref[0:1]
     states = {(0, head): state[head] for head in range(heads)}
     blocks = count // CHUNK
     cumulative_rows = [
@@ -209,15 +205,22 @@
         corrected_ref[here, span] = corrected
         result = grown * by_transpose(query_low, held_low) + by_weight(inner, corrected)
         yield
-        mixed = lower(result)
-        mixed_ref[here, span] = mixed
-        normed, unused = row_norm(mixed.astype(wide), gain)
-        gate = gate_ref[here, span]
-        gated_ref[here, span] = lower(normed * (gate * jax.nn.sigmoid(gate)))
+        mixed_ref[here, span] = lower(result)
 
     in_turn(one(block, head) for block in range(blocks) for head in range(heads))
     for head in range(heads):
         state[head] = states[blocks, head]
+
+
+def gate_kernel(heads, mixed_ref, normed_ref, weight_ref, gain_ref, gated_ref, gate_ref):
+    gate = by_weight(normed_ref[...], weight_ref[...])
+    gate_ref[...] = gate
+    gain = gain_ref[0:1]
+    for head in range(heads):
+        span = slice(head * DV, head * DV + DV)
+        normed, unused = row_norm(mixed_ref[:, span].astype(wide), gain)
+        here = gate[:, span]
+        gated_ref[:, span] = lower(normed * (here * jax.nn.sigmoid(here)))
 
 
 def backward_kernel(
@@ -467,15 +470,15 @@
     )
 
 
-def effort(length, heads):
+def effort(length, heads, each=10000000):
     return pl.CostEstimate(
-        flops=length * heads * 10000000,
-        bytes_accessed=length * heads * 8192,
-        transcendentals=length * heads * 2048,
-    )
-
-
-def mixer_forward(heads, parts, place, proj, gate, taps, coefficients, gain, interpret=False):
+        flops=length * heads * each,
+        bytes_accessed=length * heads * 1024,
+        transcendentals=length * heads,
+    )
+
+
+def mixer_forward(heads, parts, place, proj, taps, coefficients, interpret=False):
     length = proj.shape[0]
     count = length // parts
     blocks = count // CHUNK
@@ -500,13 +503,10 @@
             in_specs=[
                 tall(width),
                 tall(LANES, width // LANES),
-                tall(values),
                 whole(taps),
                 whole(coefficients),
-                whole(gain),
             ],
             out_specs=[
-                tall(values),
                 tall(values),
                 stacked(CHUNK, CHUNK),
                 stacked(DV, DK),
@@ -521,7 +521,6 @@
         ),
         out_shape=[
             jax.ShapeDtypeStruct((length, values), narrow),
-            jax.ShapeDtypeStruct((length, values), narrow),
             jax.ShapeDtypeStruct((chunks, heads, CHUNK, CHUNK), narrow),
             jax.ShapeDtypeStruct((chunks, heads, DV, DK), narrow),
             jax.ShapeDtypeStruct((length, values), narrow),
@@ -531,7 +530,36 @@
         compiler_params=params(),
         cost_estimate=effort(length, heads),
         interpret=interpret,
-    )(place, proj, proj, gate, taps, coefficients, gain)
+    )(place, proj, proj, taps, coefficients)
+
+
+def gate_rows(heads, mixed, normed, weight, gain, interpret=False):
+    length, values = mixed.shape
+    model = normed.shape[1]
+    block = 2 * CHUNK
+
+    def tall(columns):
+        return pl.BlockSpec((block, columns), lambda i: (i, 0))
+
+    def whole(shape):
+        return pl.BlockSpec(shape, lambda i: (0, 0))
+
+    return pl.pallas_call(
+        lambda *refs: gate_kernel(heads, *refs),
+        grid=(length // block,),
+        in_specs=[tall(values), tall(model), whole(weight.shape), whole(gain.shape)],
+        out_specs=[tall(values), tall(values)],
+        out_shape=[
+            jax.ShapeDtypeStruct((length, values), narrow),
+            jax.ShapeDtypeStruct((length, values), wide),
+        ],
+        compiler_params=params(),
+        cost_estimate=pl.CostEstimate(
+            flops=4 * length * model * values, bytes_accessed=length * values * 8,
+            transcendentals=length * values,
+        ),
+        interpret=interpret,
+    )(mixed, normed, weight, gain)
 
 
 def mixer_backward(
@@ -602,7 +630,7 @@
             jax.ShapeDtypeStruct((HALO, LANES), wide),
         ],
         compiler_params=params(),
-        cost_estimate=effort(length, heads),
+        cost_estimate=effort(length, heads, 100000),
         interpret=interpret,
     )(place, proj, proj, proj, gate, taps, coefficients, gain, *kept, grad_gated)
 
@@ -667,12 +695,25 @@
         far = jnp.concatenate([across, flip(across, 1)], axis=0)
         return near, far
 
-    def scatter_seq(near, far):
+    def scatter_seq(near, far, beside=None):
         half = near.shape[0] // 2
         across = far[:half] + flip(lower(far[half:]), 1).astype(wide)
         across = flip(lower(across), 2)
-        beside = flip(lower(near[half:]), 1)
-        return near[:half] + beside.astype(wide) + across.astype(wide)
+        sibling = flip(lower(near[half:]), 1)
+        if beside is not None:
+            across, beside = lax.optimization_barrier((across, beside))
+        total = near[:half] + sibling.astype(wide) + across.astype(wide)
+        return (total, beside)
+
+    def sum_all(array):
+        for bit in range(1, parts):
+            if bit & (bit - 1) == 0:
+                array = array + flip(array, bit)
+        bit = 1
+        while bit < shards:
+            array = array + lax.ppermute(array, "dp", [(i, i ^ bit) for i in range(shards)])
+            bit *= 2
+        return array
 
     def absolute(stack):
         return jnp.concatenate(
@@ -707,43 +748,66 @@
         split = array.reshape(own, shards, parts, piece)
         split = lax.dynamic_index_in_dim(split, place, 2, keepdims=False)
         split = jnp.pad(split, ((0, 0), (0, 0), (0, padded - piece)))
-        return to_lanes(split.reshape(1, own, ffn_own))[0]
-
+        return split.reshape(own, ffn_own)
+
+    tie = lax.optimization_barrier
     own_tokens = tokens[:, 0, :]
     own_cot = cotangent[:, 0, :]
+    half_lanes = LANES // 2
+    small_flat = jnp.concatenate([norm_attn, norm_ffn, conv_w.reshape(-1)])
+    small_count = small_flat.shape[0]
+    small_flat = jnp.pad(small_flat, (0, own * half_lanes - small_count))
+    w_in = over_dp(
+        jnp.concatenate(
+            [
+                mine(w_qkv, width, 1),
+                jnp.pad(
+                    mine(w_ba, 2 * heads, 1), ((0, 0), (0, half_lanes - 2 * heads))
+                ),
+                small_flat.reshape(own, half_lanes),
+            ],
+            axis=1,
+        )
+    )
     all_tokens = jnp.concatenate(gather_seq(own_tokens), axis=0)
-    small_flat = jnp.concatenate([norm_attn, norm_ffn, conv_w.reshape(-1)])
-    small_all = over_dp(small_flat[None, :])
+    small_all = w_in[:, width + half_lanes :].reshape(shards, -1)[:, :small_count]
     first_gain = small_all[:, :own].reshape(-1).astype(wide)
     second_gain = small_all[:, own : 2 * own].reshape(-1).astype(wide)
     taps_all = jnp.swapaxes(small_all[:, 2 * own :].reshape(shards, CONV, -1), 0, 1)
     taps = mine(taps_all.reshape(CONV, -1), width, 1).astype(wide)
     taps = jnp.pad(taps, ((0, HALO - CONV), (0, 0)))
-    w_in = over_dp(
-        jnp.concatenate(
-            [
-                mine(w_qkv, width, 1),
-                jnp.pad(mine(w_ba, 2 * heads, 1), ((0, 0), (0, LANES - 2 * heads))),
-                mine(w_outgate, values, 1),
-            ],
-            axis=1,
-        )
-    )
+
+    out_ratio = out_rows // own
+    second = jnp.concatenate(
+        [
+            mine(w_outgate, values, 1),
+            jnp.swapaxes(
+                mine(w_out, quarter, 1).reshape(out_ratio, own, quarter), 0, 1
+            ).reshape(own, -1),
+        ],
+        axis=1,
+    )
+    cot_near, cot_far = gather_seq(own_cot)
+    second, w_in, all_tokens, cot_near, cot_far = tie(
+        (second, w_in, all_tokens, cot_near, cot_far)
+    )
+    second_all = over_dp(second)
+    down_part = jnp.pad(mine(w_down, piece, 0), ((0, padded - piece), (0, 0)))
     ffn_part = jnp.concatenate(
         [
             ffn_columns(w_gate),
             ffn_columns(w_up),
-            to_lanes(
-                jnp.pad(
-                    mine(w_down, piece, 0), ((0, padded - piece), (0, 0))
-                )[None]
-            )[0],
-            to_lanes(mine(w_out, quarter, 1)[None])[0],
+            from_lanes(to_lanes(down_part[None]), own)[0],
         ],
-        axis=0,
-    )
-    ffn_part, w_in = lax.optimization_barrier((ffn_part, w_in))
-    ffn_all = over_dp(ffn_part).reshape(shards, -1, LANES)
+        axis=1,
+    )
+    ffn_part, w_in = tie((ffn_part, w_in))
+    ffn_all = over_dp(ffn_part)
+    both_own = ffn_all[:, : 2 * ffn_own]
+    down_own = from_lanes(
+        to_lanes(ffn_all[:, 2 * ffn_own :].reshape(shards, own, -1)), padded
+    ).reshape(ffn_own, model)
+
     decay_part = mine(a_log, heads, 0)
     bias_part = mine(dt_bias, heads, 0)
 
@@ -760,33 +824,35 @@
 
     rows = own_tokens.astype(wide)
     inverse_one = row_norm(rows, first_gain)[1]
-    all_rows = all_tokens.astype(wide)
-    normed_one, all_inverse = row_norm(all_rows, first_gain)
-    normed_one = lower(normed_one)
-    proj = lower(by_weight(normed_one, w_in[:, : width + LANES]))
-    out_gate = by_weight(normed_one, w_in[:, width + LANES :])
-    proj, cot_halves = lax.optimization_barrier((proj, gather_seq(own_cot)))
-    gated, *kept = mixer_forward(
-        heads, parts, place_row, proj, out_gate, taps, coefficients, gain, interpret
-    )
-    ffn_all, gated = lax.optimization_barrier((ffn_all, gated))
-    out_part = from_lanes(ffn_all[:, -out_rows * (quarter // LANES) :], out_rows)
+    normed_one = lower(row_norm(all_tokens.astype(wide), first_gain)[0])
+    proj = lower(by_weight(normed_one, w_in))
+    mixed, *kept = mixer_forward(
+        heads, parts, place_row, proj, taps, coefficients, interpret
+    )
+    second_all, mixed = tie((second_all, mixed))
+    w_gate_in = second_all[:, :values]
+    out_part = jnp.swapaxes(
+        second_all[:, values:].reshape(shards, own, out_ratio, quarter), 1, 2
+    )
     w_out_own = jnp.swapaxes(
         exchange(out_part.reshape(parts, values, quarter)), 0, 1
     ).reshape(values, model)
-    wide_rows = own * (ffn_own // LANES)
-    gate_own = from_lanes(ffn_all[:, :wide_rows], own).reshape(model, ffn_own)
-    up_own = from_lanes(ffn_all[:, wide_rows : 2 * wide_rows], own).reshape(model, ffn_own)
-    down_own = from_lanes(ffn_all[:, 2 * wide_rows : 2 * wide_rows + padded * (model // LANES)], padded).reshape(ffn_own, model)
+    gated, out_gate = gate_rows(heads, mixed, normed_one, w_gate_in, gain, interpret)
     half = gated.shape[0] // 2
     mixed_far = by_weight(gated[half:], w_out_own)
     mixed_near = by_weight(gated[:half], w_out_own)
-    after_mix = rows + scatter_seq(mixed_near, mixed_far)
+    after_mix = rows + scatter_seq(mixed_near, mixed_far)[0]
     normed_two, inverse_two = row_norm(after_mix, second_gain)
-    sides = []
-    for normed_half, cot_half in zip(gather_seq(lower(normed_two)), cot_halves):
-        gate_pre = by_weight(normed_half, gate_own)
-        up_pre = by_weight(normed_half, up_own)
+    normed_two = lower(normed_two)
+    across = flip(normed_two, 2)
+    normed_near = jnp.concatenate([normed_two, flip(normed_two, 1)], axis=0)
+    pre_near = by_weight(normed_near, both_own)
+    across, pre_near = tie((across, pre_near))
+    normed_far = jnp.concatenate([across, flip(across, 1)], axis=0)
+
+    def ffn_side(pre, cot_half):
+        gate_pre = pre[:, :ffn_own]
+        up_pre = pre[:, ffn_own:]
         sig_ffn = jax.nn.sigmoid(gate_pre)
         hidden = lower(gate_pre * sig_ffn * up_pre)
         grad_hidden = by_transpose(cot_half, down_own)
@@ -794,48 +860,50 @@
             grad_hidden * up_pre * sig_ffn * (1.0 + gate_pre * (1.0 - sig_ffn))
         )
         grad_up_pre = lower(grad_hidden * gate_pre * sig_ffn)
-        back = by_transpose(grad_gate_pre, gate_own) + by_transpose(grad_up_pre, up_own)
-        sides.append(
-            (
-                back,
-                by_weight(hidden, down_own),
-                over_rows(normed_half, grad_gate_pre),
-                over_rows(normed_half, grad_up_pre),
-                over_rows(hidden, cot_half),
-            )
-        )
-    near_side, far_side = sides
-    back_two, grad_norm_ffn = norm_back(
-        after_mix, inverse_two, second_gain, scatter_seq(near_side[0], far_side[0])
-    )
+        grad_both = jnp.concatenate([grad_gate_pre, grad_up_pre], axis=1)
+        return hidden, grad_both, by_transpose(grad_both, both_own)
+
+    hidden_near, grad_near, back_near = ffn_side(pre_near, cot_near)
+    hidden_far, grad_far, back_far = ffn_side(by_weight(normed_far, both_own), cot_far)
+    grad_both = over_rows(normed_near, grad_near) + over_rows(normed_far, grad_far)
+    grad_down = over_rows(hidden_near, cot_near) + over_rows(hidden_far, cot_far)
+    grad_down = from_lanes(
+        to_lanes(lower(grad_down).reshape(shards, padded, model)), own
+    ).reshape(model, -1)
+    grad_ffn = jnp.concatenate([lower(grad_both), grad_down], axis=1)
+    grad_normed_two, grad_ffn = scatter_seq(back_near, back_far, grad_ffn)
+    grad_ffn = sum_dp(grad_ffn)
+    back_two, grad_norm_ffn = norm_back(after_mix, inverse_two, second_gain, grad_normed_two)
     grad_after = own_cot.astype(wide) + back_two
-    result = after_mix + scatter_seq(near_side[1], far_side[1])
-    grad_ffn = sum_dp(
-        jnp.concatenate(
-            [
-                to_lanes(lower(near_side[2] + far_side[2]).reshape(shards, own, ffn_own)),
-                to_lanes(lower(near_side[3] + far_side[3]).reshape(shards, own, ffn_own)),
-                to_lanes(lower(near_side[4] + far_side[4]).reshape(shards, padded, model)),
-            ],
-            axis=1,
-        ).reshape(-1, LANES)
-    )
     grad_branch = jnp.concatenate(gather_seq(lower(grad_after)), axis=0)
+    grad_branch, hidden_near, hidden_far = tie((grad_branch, hidden_near, hidden_far))
     grad_gated = by_transpose(grad_branch, w_out_own)
     grad_out = jnp.swapaxes(
         lower(over_rows(gated, grad_branch)).reshape(values, parts, quarter), 0, 1
     )
-    grad_out = exchange(grad_out).reshape(shards, out_rows, quarter)
+    grad_out = jnp.swapaxes(
+        exchange(grad_out).reshape(shards, out_ratio, own, quarter), 1, 2
+    ).reshape(model, -1)
+    result = after_mix + scatter_seq(
+        by_weight(hidden_near, down_own), by_weight(hidden_far, down_own)
+    )[0]
     grad_in, grad_taps, grad_gain, grad_small = mixer_backward(
-        heads, parts, place_row, proj, out_gate, taps, coefficients, gain, kept, grad_gated, interpret
-    )
-    one_far = by_transpose(grad_in[half:], w_in)
-    one_near = by_transpose(grad_in[:half], w_in)
-    hat = all_rows * all_inverse
-    grad_norm_attn = jnp.sum(one_far * hat[half:], axis=0) + jnp.sum(
-        one_near * hat[:half], axis=0
-    )
-    grad_w_in = lower(over_rows(normed_one, grad_in)).reshape(shards, own, -1)
+        heads, parts, place_row, proj, out_gate, taps, coefficients, gain, [mixed, *kept],
+        grad_gated, interpret
+    )
+    grad_w_in = lower(over_rows(normed_one, grad_in))
+    grad_in, grad_w_in = tie((grad_in, grad_w_in))
+    grad_w_in = sum_dp(jnp.concatenate([grad_w_in, grad_out], axis=1))
+    grad_first = grad_in[:, : width + LANES]
+    grad_gate = grad_in[:, width + LANES :]
+    one_far = by_transpose(grad_first[half:], w_in) + by_transpose(grad_gate[half:], w_gate_in)
+    one_near = by_transpose(grad_first[:half], w_in) + by_transpose(
+        grad_gate[:half], w_gate_in
+    )
+    back_one, grad_norm_attn = norm_back(
+        rows, inverse_one, first_gain, scatter_seq(one_near, one_far)[0]
+    )
+    grad_rows = lower(grad_after + back_one)[:, None, :]
 
     taps_full = lax.dynamic_update_slice_in_dim(
         jnp.zeros((CONV, head_count * ROW), wide), grad_taps[:CONV], place * width, 1
@@ -847,71 +915,84 @@
         )
 
     common = jnp.concatenate([grad_gain[0], to_heads(grad_small[1]), to_heads(grad_small[0])])
-    own_taps = conv_w.shape[1]
     packed = jnp.concatenate(
+        [grad_norm_attn, grad_norm_ffn, taps_full.reshape(-1), common]
+    )
+    packed_count = packed.shape[0]
+    packed = jnp.pad(packed, (0, -packed_count % (HALO * LANES)))
+    packed = sum_all(packed.reshape(-1, LANES)).reshape(-1)
+    def pieces_of(array):
+        stack = stack_seq(array)
+        return [
+            lax.dynamic_index_in_dim(stack, jnp.bitwise_xor(place, at), 0, keepdims=False)
+            for at in range(parts)
+        ]
+
+    def side_by_side(pieces):
+        return jnp.concatenate(pieces, axis=1).astype(wide)
+
+    def ffn_full(pieces):
+        split = jnp.stack(
+            [item.reshape(own, shards, padded)[..., :piece] for item in pieces], axis=2
+        )
+        return split.reshape(own, -1).astype(wide)
+
+    ffn_pieces = pieces_of(grad_ffn)
+    grad_w_gate = ffn_full([item[:, :ffn_own] for item in ffn_pieces])
+    grad_w_up = ffn_full([item[:, ffn_own : 2 * ffn_own] for item in ffn_pieces])
+    grad_w_down = jnp.concatenate(
         [
-            grad_norm_attn.reshape(shards, own),
-            grad_norm_ffn.reshape(shards, own),
-            jnp.swapaxes(taps_full.reshape(CONV, shards, own_taps), 0, 1).reshape(shards, -1),
-            jnp.broadcast_to(common[None], (shards, common.shape[0])),
+            from_lanes(to_lanes(item[None, :, 2 * ffn_own :]), padded)[0][:piece]
+            for item in ffn_pieces
         ],
-        axis=1,
-    )
-    tile = 2 * HALO * LANES
-    packed = jnp.pad(packed, ((0, 0), (0, -packed.shape[1] % tile)))
-    in_rows = own * (grad_w_in.shape[2] // LANES)
-    lane_rows = out_rows * (quarter // LANES)
-    last = sum_dp(
-        jnp.concatenate(
-            [
-                to_lanes(grad_w_in),
-                to_lanes(grad_out),
-                lower(packed).reshape(shards, -1, LANES),
-            ],
-            axis=1,
-        ).reshape(-1, LANES)
-    )
-    back_one = norm_back(rows, inverse_one, first_gain, scatter_seq(one_near, one_far))[0]
-    grad_rows = lower(grad_after + back_one)[:, None, :]
-
-    last_all = stack_seq(last)
-    small_total = jnp.sum(
-        last_all[:, in_rows + lane_rows :].astype(wide), axis=0
-    ).reshape(-1)
-    last_all = absolute(last_all)
-    ffn_grads = absolute(stack_seq(grad_ffn))
-
-    def side_by_side(array):
-        return jnp.swapaxes(array, 0, 1).reshape(array.shape[1], -1).astype(wide)
-
-    in_all = from_lanes(last_all[:, :in_rows], own)
-    out_all = from_lanes(last_all[:, in_rows : in_rows + lane_rows], out_rows)
-
-    def ffn_full(array):
-        split = from_lanes(array, own).reshape(parts, own, shards, padded)[..., :piece]
-        return jnp.transpose(split, (1, 2, 0, 3)).reshape(own, -1).astype(wide)
-
-    down_all = from_lanes(ffn_grads[:, 2 * wide_rows :], padded)[:, :piece]
-    taps_at = 2 * own
-    gain_at = taps_at + CONV * own_taps
-    heads_at = gain_at + DV
-
-    return (
+        axis=0,
+    ).astype(wide)
+    early = (
         lower(result)[:, None, :],
         grad_rows,
-        small_total[:own],
-        side_by_side(in_all[:, :, :width]),
-        side_by_side(in_all[:, :, width : width + 2 * heads]),
-        small_total[taps_at:gain_at].reshape(CONV, own_taps),
-        small_total[heads_at : heads_at + head_count],
-        small_total[heads_at + head_count : heads_at + 2 * head_count],
-        side_by_side(in_all[:, :, width + LANES :]),
-        small_total[gain_at:heads_at],
-        side_by_side(out_all),
-        small_total[own:taps_at],
-        ffn_full(ffn_grads[:, :wide_rows]),
-        ffn_full(ffn_grads[:, wide_rows : 2 * wide_rows]),
-        down_all.reshape(parts * piece, model).astype(wide),
+        grad_w_gate,
+        grad_w_up,
+        grad_w_down,
+        packed,
+    )
+    grad_w_in, early = tie((grad_w_in, early))
+    block_out, grad_rows, grad_w_gate, grad_w_up, grad_w_down, packed = early
+    taps_at = 2 * model
+    gain_at = taps_at + CONV * head_count * ROW
+    heads_at = gain_at + DV
+    shard = lax.axis_index("dp")
+    norm_attn_total = lax.dynamic_slice_in_dim(packed[:model], shard * own, own, 0)
+    norm_ffn_total = lax.dynamic_slice_in_dim(packed[model:taps_at], shard * own, own, 0)
+    own_taps = conv_w.shape[1]
+    taps_total = lax.dynamic_slice_in_dim(
+        packed[taps_at:gain_at].reshape(CONV, -1), shard * own_taps, own_taps, 1
+    )
+
+    in_pieces = pieces_of(grad_w_in)
+    total = width + LANES + values
+    return (
+        block_out,
+        grad_rows,
+        norm_attn_total,
+        side_by_side([item[:, :width] for item in in_pieces]),
+        side_by_side([item[:, width : width + 2 * heads] for item in in_pieces]),
+        taps_total,
+        packed[heads_at : heads_at + head_count],
+        packed[heads_at + head_count : heads_at + 2 * head_count],
+        side_by_side([item[:, width + LANES : total] for item in in_pieces]),
+        packed[gain_at:heads_at],
+        side_by_side(
+            [
+                jnp.swapaxes(item[:, total:].reshape(own, out_ratio, quarter), 0, 1).reshape(
+                    out_rows, quarter
+                )
+                for item in in_pieces
+            ]
+        ),
+        norm_ffn_total,
+        grad_w_gate,
+        grad_w_up,
+        grad_w_down,
     )
 
 

time: 687 us -> 579 us (0.84)
  waiting for transfers between devices: 274 us -> 220 us
  blocking collectives: 31.1 us -> 0 us
  matrix products: 110 us -> 89.6 us
  local copies, waits for them, and re-layouts: 89.7 us -> 73.2 us
    reduce_scatter x2, waiting for transfers between devices: 44.3 us -> 6.46 us  [sum_dp(): return lax.psum_scatter(array, 'dp', scatter_dimension=0, tiled=True)]
    all_gather x2 -> x3, waiting for transfers between devices: 62.4 us -> 29.4 us  [over_dp(): return lax.all_gather(array, 'dp', axis=0, tiled=True)]
    all_gather x1 -> x0, blocking collectives: 31.1 us -> none  [over_dp(): return lax.all_gather(array, 'dp', axis=0, tiled=True)]
    ppermute x36 -> x38, waiting for transfers between devices: 167 us -> 180 us  [flip(): return lax.ppermute(array, 'seq', [(i, i ^ bit) for i in range(parts)])]
    convert_element_type x6 -> x0, local copies, waits for them, and re-layouts: 11.4 us -> none  [the longest x3 9.87 us: lower(): return array.astype(narrow)]
    transpose x7 -> x2, local copies, waits for them, and re-layouts: 14 us -> 3.99 us  [from_lanes(): return jnp.swapaxes(split, 1, 2).reshape(groups, rows, -1)]
    transpose x8 -> x7, local copies, waits for them, and re-layouts: 12.7 us -> 3.6 us  [to_lanes(): return jnp.swapaxes(split, 1, 2).reshape(groups, -1, LANES)]
    dot_general x8 -> x6, matrix products: 36.4 us -> 28 us  [over_rows(): lax.dot_general(left, right, (((0,), (0,)), ((), ())), preferred_element_...]
  transfers between devices with their start and end apart: 40 -> 46, of which waited for: 15 -> 19; matrix products, arithmetic and copies ran while one was open for 31% -> 34% of each run, Pallas kernels for 12% -> 16%
where the time goes in v3:
time: 579 us; the launch traced here: 573 us
  waiting for transfers between devices  220 us (38%)
  matrix products  89.6 us (15%)
  Pallas kernels  88.8 us (15%)
  local copies, waits for them, and re-layouts  73.2 us (13%)
  other arithmetic  59.5 us (10%)
  starting transfers between devices  26.2 us (5%)
  between operations  15.6 us (3%)
    ppermute x38, waiting for transfers between devices, flip(): return lax.ppermute(array, 'seq', [(i, i ^ bit) for i in range(parts)])  180 us
    pallas_call x1, Pallas kernels, mixer_backward(): pl.pallas_call(lambda *refs: backward_kernel(heads, *refs), grid_spec=plt...  54.2 us
    dot_general x9, matrix products, by_transpose(): lax.dot_general(left, right, (((1,), (1,)), ((), ())), preferred_element_...  32.6 us
    all_gather x3, waiting for transfers between devices, over_dp(): return lax.all_gather(array, 'dp', axis=0, tiled=True)  29.4 us
    dot_general x7, matrix products, by_weight(): return jnp.dot(left, right, preferred_element_type=wide)  29 us
    dot_general x6, matrix products, over_rows(): lax.dot_general(left, right, (((0,), (0,)), ((), ())), preferred_element_...  28 us
    pallas_call x1, Pallas kernels, mixer_forward(): pl.pallas_call(lambda *refs: forward_kernel(heads, *refs), grid_spec=pltp...  27.1 us
    unnamed x126, local copies, waits for them, and re-layouts  23.4 us
  transfers between devices with their start and end apart: 46, of which 19 were waited for; matrix products, arithmetic and copies ran while one was open for 34% of the time, Pallas kernels for 16%

profile of v3, /device:TPU:0, one launch (start us, length us, event | category | flops | bytes accessed | tf_op | source)
XLA Modules:
  0.0 572.6 jit_solution(10709947572921304123)
XLA Ops:
  13.7 24.1 %collective-permute-done.4 = bf16[512,1024]{1,0:T(8,128)(2,1)S(1)} collective-permute-done((bf16[512,1024]{1,0:T(8,128)(2,1)}, bf16[512,1024]{1,0:T(8,128)(2,1)S(1)}, u32[]{:S(2)}, u32[]{:S(2)}) %collective-permute-start.4) | collective-permute-done | bytes 1048608 | tf_op jit(solution)/shard_map/ppermute | solution.py:684
  38.3 21.2 %collective-permute-done.1 = bf16[512,1024]{1,0:T(8,128)(2,1)} collective-permute-done((bf16[512,1024]{1,0:T(8,128)(2,1)}, bf16[512,1024]{1,0:T(8,128)(2,1)}, u32[]{:S(2)}, u32[]{:S(2)}) %collective-permute-start.1) | collective-permute-done | bytes 1048608 | tf_op jit(solution)/shard_map/ppermute | solution.py:684
  86.3 7.2 %convolution_convert_fusion.refs_1_.refs_2_.refs_3_ = bf16[2048,1152]{1,0:T(8,128)(2,1)} fusion(bf16[2048,1024]{1,0:T(8,128)(2,1)S(1)} %fusion.2.refs_1_, bf16[1024,1152]{1,0:T(8,128)(2,1)S(1)} %copy-done.35), kind=kOutput, calls=%fused_computation.5 | convolution fusion | flops 4834197504 | bytes 11272192 | tf_op jit(solution)/shard_map/dot_general | solution.py:22
  93.9 27.1 %shard_map.262 = (bf16[2048,512]{1,0:T(8,128)(2,1)}, bf16[8,2,256,256]{3,2,1,0:T(8,128)(2,1)}, bf16[8,2,256,128]{3,2,1,0:T(8,128)(2,1)S(1)}, bf16[2048,512]{1,0:...) custom-call(s32[1]{0:T(128)} %bitcast.refs_0_, ...), custom_call_target="tpu_custom_call" | custom-call | flops 40960000000 | bytes 4194304 | tf_op jit(solution)/shard_map/pallas_call | solution.py:498
  121.0 6.8 %all-gather.6.cloned.1.call-done = bf16[1024,1024]{1,0:T(8,128)(2,1)} async-done(((bf16[128,1024]{1,0:T(8,128)(2,1)}), bf16[1024,1024]{1,0:T(8,128)(2,1)}) %all-gather.6.cloned.1.call-update) | async-done | bytes 2097168 | tf_op jit(solution)/shard_map/all_gather | solution.py:687
  136.0 7.5 %shard_map.263 = (bf16[2048,512]{1,0:T(8,128)(2,1)}, f32[2048,512]{1,0:T(8,128)}) custom-call(bf16[2048,512]{1,0:T(8,128)(2,1)} %get-tuple-element.57.refs_0_.refs_8_, bf16[2048,1024]{1,0:T(8,128)(2,1)} %copy-done.13, bf16[1024,512]{1,0:T(8,128)(2,1)S(1)} %get-tuple-element.187.refs_2_, f32[8,256]{1,0:T(8,128)S(1)} %broadcast_in_dim.42.refs_3_.refs_7_), custom_call_target="tpu_custom_call" | custom-call | flops 4294967296 | bytes 8388608 | tf_op jit(solution)/shard_map/pallas_call | solution.py:547
  143.5 4.8 collective-permute-done.7
  158.1 24.0 %collective-permute-done.11 = bf16[512,1024]{1,0:T(8,128)(2,1)S(1)} collective-permute-done((bf16[512,1024]{1,0:T(8,128)(2,1)S(1)}, bf16[512,1024]{1,0:T(8,128)(2,1)S(1)}, u32[]{:S(2)}, u32[]{:S(2)}) %collective-permute-start.11) | collective-permute-done | bytes 1048608 | tf_op jit(solution)/shard_map/ppermute | solution.py:684
  187.2 22.7 %all-gather.8.cloned.1.call-done = bf16[1024,2304]{0,1:T(8,128)(2,1)} async-done(((bf16[128,2304]{0,1:T(8,128)(2,1)}), bf16[1024,2304]{0,1:T(8,128)(2,1)}) %all-gather.8.cloned.1.call-update) | async-done | bytes 4718608 | tf_op jit(solution)/shard_map/all_gather | solution.py:687
  209.9 8.2 %fusion.34 = f32[1024,1536]{1,0:T(8,128)} fusion(bf16[1024,2304]{0,1:T(8,128)(2,1)} %all-gather.8.cloned.1.call-done, bf16[512,1024]{1,0:T(8,128)(2,1)} %collective-permute-done.13, bf16[512,1024]{1,0:T(8,128)(2,1)S(1)} %multiply_convert_fusion.6), kind=kOutput, calls=%fused_computation.87 | convolution fusion | flops 3225419776 | bytes 11534336 | tf_op jit(solution)/shard_map/dot_general | solution.py:22
  227.3 6.8 %copy.191 = f32[1024,1536]{0,1:T(8,128)} copy(f32[1024,1536]{1,0:T(8,128)} %fusion.34) | data formatting | bytes 12582912 | tf_op jit(solution)/shard_map/optimization_barrier | solution.py:850
  234.1 6.8 %multiply_convert_fusion.5 = (bf16[1024,768]{0,1:T(8,128)(2,1)S(1)}, bf16[1024,768]{0,1:T(8,128)(2,1)S(1)}, bf16[1024,768]{0,1:T(8,128)(2,1)S(1)}) fusion(f32[1024,1536]{0,1:T(8,128)} %copy.191, bf16[1024,1024]{1,0:T(8,128)(2,1)} %pad_maximum_fusion.8, bf16[96,8,8,128]{3,2,1,0:T(8,128)(2,1)} %bitcast.282), kind=kOutput, calls=%fused_computation.26 | convolution fusion | flops 1623195648 | bytes 14680064 | tf_op jit(solution)/shard_map/dot_general | solution.py:26
  240.9 6.0 %fusion.29 = f32[1024,1024]{1,0:T(8,128)S(1)} fusion(bf16[1024,768]{0,1:T(8,128)(2,1)S(1)} %get-tuple-element.173, bf16[1024,768]{0,1:T(8,128)(2,1)S(1)} %get-tuple-element.172, bf16[1024,2304]{0,1:T(8,128)(2,1)} %all-gather.8.cloned.1.call-done), kind=kOutput, calls=%fused_computation.82 | convolution fusion | flops 3227516928 | bytes 10485760 | tf_op jit(solution)/shard_map/dot_general | solution.py:26
  251.4 5.6 fusion.31
  276.9 6.3 %add_convert_fusion = bf16[1024,1536]{1,0:T(8,128)(2,1)S(1)} fusion(f32[1024,1536]{1,0:T(8,128)S(1)} %fusion.27, bf16[1024,768]{0,1:T(8,128)(2,1)S(1)} %get-tuple-element.173, bf16[1024,768]{0,1:T(8,128)(2,1)S(1)} %get-tuple-element.172, bf16[512,1024]{1,0:T(8,128)(2,1)} %collective-permute-done.13, bf16[512,1024]{1,0:T(8,128)(2,1)S(1)} %multiply_convert_fusion.6), kind=kOutput, calls=%fused_computation.6 | convolution fusion | flops 3234856960 | bytes 14680064 | tf_op jit(solution)/shard_map/dot_general | solution.py:32
  285.8 15.1 %collective-permute-done.17 = bf16[512,1024]{1,0:T(8,128)(2,1)} collective-permute-done((bf16[512,1024]{1,0:T(8,128)(2,1)}, bf16[512,1024]{1,0:T(8,128)(2,1)}, u32[]{:S(2)}, u32[]{:S(2)}) %collective-permute-start.17) | collective-permute-done | bytes 1048608 | tf_op jit(solution)/shard_map/ppermute | solution.py:684
  310.5 22.8 %collective-permute-done.19 = bf16[512,1024]{1,0:T(8,128)(2,1)S(1)} collective-permute-done((bf16[512,1024]{1,0:T(8,128)(2,1)}, bf16[512,1024]{1,0:T(8,128)(2,1)S(1)}, u32[]{:S(2)}, u32[]{:S(2)}) %collective-permute-start.19) | collective-permute-done | bytes 1048608 | tf_op jit(solution)/shard_map/ppermute | solution.py:684
  353.7 54.2 %shard_map.264 = (bf16[2048,1664]{1,0:T(8,128)(2,1)}, f32[8,1024]{1,0:T(8,128)S(1)}, f32[8,256]{1,0:T(8,128)S(1)}, f32[8,128]{1,0:T(8,128)S(1)}) custom-call(s32[1]{0:T(128)} %bitcast.refs_0_, bf16[2048,1152]{1,0:T(8,128)(2,1)} %convolution_convert_fusion.refs_1_.refs_2_.refs_3_, bf16[2048,1152]{1,0:T(8,128)(2,1)} %convolution_convert_fusion.refs_1_.refs_2_.refs_3_, ...), custom_call_target="tpu_custom_call" | custom-call | flops 409600000 | bytes 4194304 | tf_op jit(solution)/shard_map/pallas_call | solution.py:594
  407.9 11.3 %convolution_convert_fusion.1 = bf16[1024,1664]{1,0:T(8,128)(2,1)S(1)} fusion(bf16[2048,1024]{1,0:T(8,128)(2,1)S(1)} %copy-done.14, bf16[2048,1664]{1,0:T(8,128)(2,1)} %get-tuple-element.77), kind=kOutput, calls=%fused_computation.16 | convolution fusion | flops 6981025792 | bytes 14417920 | tf_op jit(solution)/shard_map/dot_general | solution.py:32
  447.5 19.3 %collective-permute-done.29 = bf16[512,1024]{1,0:T(8,128)(2,1)} collective-permute-done((bf16[512,1024]{1,0:T(8,128)(2,1)}, bf16[512,1024]{1,0:T(8,128)(2,1)}, u32[]{:S(2)}, u32[]{:S(2)}) %collective-permute-start.29) | collective-permute-done | bytes 1048608 | tf_op jit(solution)/shard_map/ppermute | solution.py:684
  475.2 25.3 %collective-permute-done.34 = f32[152,128]{1,0:T(8,128)S(1)} collective-permute-done((f32[152,128]{1,0:T(8,128)S(1)}, f32[152,128]{1,0:T(8,128)S(1)}, u32[]{:S(2)}, u32[]{:S(2)}) %collective-permute-start.34) | collective-permute-done | bytes 77856 | tf_op jit(solution)/shard_map/ppermute | solution.py:684
  508.0 4.7 fusion.46
  531.1 6.5 %reduce-scatter.3.cloned.1.call-done = bf16[128,2176]{1,0:T(8,128)(2,1)} async-done(((bf16[1024,2176]{1,0:T(8,128)(2,1)}), bf16[128,2176]{1,0:T(8,128)(2,1)}) %reduce-scatter.3.cloned.1.call-update) | async-done | bytes 557072 | tf_op jit(solution)/shard_map/reduce_scatter | solution.py:690
  539.6 12.5 %collective-permute-done.39 = bf16[1,128,2176]{2,1,0:T(8,128)(2,1)S(1)} collective-permute-done((bf16[1,128,2176]{2,1,0:T(8,128)(2,1)}, bf16[1,128,2176]{2,1,0:T(8,128)(2,1)S(1)}, u32[]{:S(2)}, u32[]{:S(2)}) %collective-permute-start.39) | collective-permute-done | bytes 557088 | tf_op jit(solution)/shard_map/ppermute | solution.py:684
  (409 shorter events, 200.1 us)
Async XLA Ops:
  7.2 69.4 %all-gather.4.cloned.1.call-start = ((), (), s32[]{:S(2)}) async-start(), calls=%async_computation.2 | async-start | bytes 2654208 | tf_op jit(solution)/shard_map/all_gather | solution.py:687
  10.5 117.2 %all-gather.6.cloned.1.call-start = ((), (), s32[]{:S(2)}) async-start(), calls=%async_computation.3 | async-start | bytes 2359296 | tf_op jit(solution)/shard_map/all_gather | solution.py:687
  10.6 27.2 %collective-permute-start.4 = (bf16[512,1024]{1,0:T(8,128)(2,1)}, bf16[512,1024]{1,0:T(8,128)(2,1)S(1)}, u32[]{:S(2)}, u32[]{:S(2)}) collective-permute-start(bf16[512,1024]{1,0:T(8,128)(2,1)} %bitcast.277), channel_id=1, source_target_pairs={{0,16},{8,24},{16,0},{24,8},{1,17},{9,25},{17,1},{25,9},{2,18},{10... | collective-permute-start | bytes 3145736 | tf_op jit(solution)/shard_map/ppermute | solution.py:684
  13.6 45.9 %collective-permute-start.1 = (bf16[512,1024]{1,0:T(8,128)(2,1)}, bf16[512,1024]{1,0:T(8,128)(2,1)}, u32[]{:S(2)}, u32[]{:S(2)}) collective-permute-start(bf16[512,1024]{1,0:T(8,128)(2,1)} %bitcast.266), channel_id=1, source_target_pairs={{0,16},{8,24},{16,0},{24,8},{1,17},{9,25},{17,1},{25,9},{2,18},{10... | collective-permute-start | bytes 3145736 | tf_op jit(solution)/shard_map/ppermute | solution.py:684
  13.6 53.7 %collective-permute-start.3 = (bf16[512,1024]{1,0:T(8,128)(2,1)}, bf16[512,1024]{1,0:T(8,128)(2,1)}, u32[]{:S(2)}, u32[]{:S(2)}) collective-permute-start(bf16[512,1024]{1,0:T(8,128)(2,1)} %bitcast.278), channel_id=1, source_target_pairs={{0,8},{8,0},{16,24},{24,16},{1,9},{9,1},{17,25},{25,17},{2,10},{10... | collective-permute-start | bytes 3145736 | tf_op jit(solution)/shard_map/ppermute | solution.py:684
  37.8 32.4 %collective-permute-start.5 = (bf16[512,1024]{1,0:T(8,128)(2,1)S(1)}, bf16[512,1024]{1,0:T(8,128)(2,1)}, u32[]{:S(2)}, u32[]{:S(2)}) collective-permute-start(bf16[512,1024]{1,0:T(8,128)(2,1)S(1)} %collective-permute-done.4), channel_id=1, source_target_pairs={{0,8},{8,0},{16,24},{24,16},{1,9},{9,1},{17,25},{25,17},{2,10},{10... | collective-permute-start | bytes 3145736 | tf_op jit(solution)/shard_map/ppermute | solution.py:684
  37.8 35.2 %collective-permute-start = (bf16[512,1024]{1,0:T(8,128)(2,1)}, bf16[512,1024]{1,0:T(8,128)(2,1)}, u32[]{:S(2)}, u32[]{:S(2)}) collective-permute-start(bf16[512,1024]{1,0:T(8,128)(2,1)} %bitcast.267), channel_id=1, source_target_pairs={{0,8},{8,0},{16,24},{24,16},{1,9},{9,1},{17,25},{25,17},{2,10},{10... | collective-permute-start | bytes 3145736 | tf_op jit(solution)/shard_map/ppermute | solution.py:684
  76.6 133.2 %all-gather.8.cloned.1.call-start = ((), (), s32[]{:S(2)}) async-start(), calls=%async_computation.4 | async-start | bytes 5308416 | tf_op jit(solution)/shard_map/all_gather | solution.py:687
  93.5 413.0 %reduce-scatter.5.cloned.1.call-start = ((), (), s32[]{:S(2)}) async-start(), calls=%async_computation.6 | async-start | bytes 5308416 | tf_op jit(solution)/shard_map/reduce_scatter | solution.py:690
  156.8 25.3 %collective-permute-start.11 = (bf16[512,1024]{1,0:T(8,128)(2,1)S(1)}, bf16[512,1024]{1,0:T(8,128)(2,1)S(1)}, u32[]{:S(2)}, u32[]{:S(2)}) collective-permute-start(bf16[512,1024]{1,0:T(8,128)(2,1)S(1)} %fusion.25), channel_id=1, source_target_pairs={{0,16},{8,24},{16,0},{24,8},{1,17},{9,25},{17,1},{25,9},{2,18},{10... | collective-permute-start | bytes 3145736 | tf_op jit(solution)/shard_map/ppermute | solution.py:684
  184.4 33.7 %collective-permute-start.12 = (bf16[512,1024]{1,0:T(8,128)(2,1)S(1)}, bf16[512,1024]{1,0:T(8,128)(2,1)}, u32[]{:S(2)}, u32[]{:S(2)}) collective-permute-start(bf16[512,1024]{1,0:T(8,128)(2,1)S(1)} %multiply_convert_fusion.6), channel_id=1, source_target_pairs={{0,16},{8,24},{16,0},{24,8},{1,17},{9,25},{17,1},{25,9},{2,18},{10... | collective-permute-start | bytes 3145736 | tf_op jit(solution)/shard_map/ppermute | solution.py:684
  218.1 31.9 %collective-permute-start.15 = (bf16[512,1024]{1,0:T(8,128)(2,1)}, bf16[512,1024]{1,0:T(8,128)(2,1)}, u32[]{:S(2)}, u32[]{:S(2)}) collective-permute-start(bf16[512,1024]{1,0:T(8,128)(2,1)} %collective-permute-done.12), channel_id=1, source_target_pairs={{0,8},{8,0},{16,24},{24,16},{1,9},{9,1},{17,25},{25,17},{2,10},{10... | collective-permute-start | bytes 3145736 | tf_op jit(solution)/shard_map/ppermute | solution.py:684
  248.2 52.7 %collective-permute-start.14 = (bf16[512,1024]{1,0:T(8,128)(2,1)}, bf16[512,1024]{1,0:T(8,128)(2,1)}, u32[]{:S(2)}, u32[]{:S(2)}) collective-permute-start(bf16[512,1024]{1,0:T(8,128)(2,1)} %slice.553), channel_id=1, source_target_pairs={{0,8},{8,0},{16,24},{24,16},{1,9},{9,1},{17,25},{25,17},{2,10},{10... | collective-permute-start | bytes 3145736 | tf_op jit(solution)/shard_map/ppermute | solution.py:684
  275.5 25.4 %collective-permute-start.17 = (bf16[512,1024]{1,0:T(8,128)(2,1)}, bf16[512,1024]{1,0:T(8,128)(2,1)}, u32[]{:S(2)}, u32[]{:S(2)}) collective-permute-start(bf16[512,1024]{1,0:T(8,128)(2,1)} %fusion.23), channel_id=1, source_target_pairs={{0,16},{8,24},{16,0},{24,8},{1,17},{9,25},{17,1},{25,9},{2,18},{10... | collective-permute-start | bytes 3145736 | tf_op jit(solution)/shard_map/ppermute | solution.py:684
  308.8 24.5 %collective-permute-start.19 = (bf16[512,1024]{1,0:T(8,128)(2,1)}, bf16[512,1024]{1,0:T(8,128)(2,1)S(1)}, u32[]{:S(2)}, u32[]{:S(2)}) collective-permute-start(bf16[512,1024]{1,0:T(8,128)(2,1)} %get-tuple-element.168), channel_id=1, source_target_pairs={{0,16},{8,24},{16,0},{24,8},{1,17},{9,25},{17,1},{25,9},{2,18},{10... | collective-permute-start | bytes 3145736 | tf_op jit(solution)/shard_map/ppermute | solution.py:684
  310.3 227.2 %reduce-scatter.3.cloned.1.call-start = ((), (), s32[]{:S(2)}) async-start(), calls=%async_computation.5 | async-start | bytes 5013504 | tf_op jit(solution)/shard_map/reduce_scatter | solution.py:690
  347.1 93.8 %collective-permute-start.23 = (bf16[1,512,256]{2,1,0:T(8,128)(2,1)S(1)}, bf16[1,512,256]{2,1,0:T(8,128)(2,1)S(1)}, u32[]{:S(2)}, u32[]{:S(2)}) collective-permute-start(bf16[1,512,256]{2,1,0:T(8,128)(2,1)S(1)} %bitcast.343), channel_id=1, source_target_pairs={{0,24},{8,16},{16,8},{24,0},{1,25},{9,17},{17,9},{25,1},{2,26},{10... | collective-permute-start | bytes 786440 | tf_op jit(solution)/shard_map/ppermute | solution.py:684
  348.3 92.7 %collective-permute-start.22 = (bf16[1,512,256]{2,1,0:T(8,128)(2,1)S(1)}, bf16[1,512,256]{2,1,0:T(8,128)(2,1)S(1)}, u32[]{:S(2)}, u32[]{:S(2)}) collective-permute-start(bf16[1,512,256]{2,1,0:T(8,128)(2,1)S(1)} %bitcast.342), channel_id=1, source_target_pairs={{0,16},{8,24},{16,0},{24,8},{1,17},{9,25},{17,1},{25,9},{2,18},{10... | collective-permute-start | bytes 786440 | tf_op jit(solution)/shard_map/ppermute | solution.py:684
  349.0 93.5 %collective-permute-start.21 = (bf16[1,512,256]{2,1,0:T(8,128)(2,1)S(1)}, bf16[1,512,256]{2,1,0:T(8,128)(2,1)S(1)}, u32[]{:S(2)}, u32[]{:S(2)}) collective-permute-start(bf16[1,512,256]{2,1,0:T(8,128)(2,1)S(1)} %bitcast.341), channel_id=1, source_target_pairs={{0,8},{8,0},{16,24},{24,16},{1,9},{9,1},{17,25},{25,17},{2,10},{10... | collective-permute-start | bytes 786440 | tf_op jit(solution)/shard_map/ppermute | solution.py:684
  423.7 46.1 %collective-permute-start.25 = (bf16[512,1024]{1,0:T(8,128)(2,1)}, bf16[512,1024]{1,0:T(8,128)(2,1)}, u32[]{:S(2)}, u32[]{:S(2)}) collective-permute-start(bf16[512,1024]{1,0:T(8,128)(2,1)} %slice.550), channel_id=1, source_target_pairs={{0,8},{8,0},{16,24},{24,16},{1,9},{9,1},{17,25},{25,17},{2,10},{10... | collective-permute-start | bytes 3145736 | tf_op jit(solution)/shard_map/ppermute | solution.py:684
  439.1 75.9 %collective-permute-start.24 = (bf16[512,1024]{1,0:T(8,128)(2,1)}, bf16[512,1024]{1,0:T(8,128)(2,1)}, u32[]{:S(2)}, u32[]{:S(2)}) collective-permute-start(bf16[512,1024]{1,0:T(8,128)(2,1)} %slice.551), channel_id=1, source_target_pairs={{0,8},{8,0},{16,24},{24,16},{1,9},{9,1},{17,25},{25,17},{2,10},{10... | collective-permute-start | bytes 3145736 | tf_op jit(solution)/shard_map/ppermute | solution.py:684
  441.0 25.7 %collective-permute-start.29 = (bf16[512,1024]{1,0:T(8,128)(2,1)}, bf16[512,1024]{1,0:T(8,128)(2,1)}, u32[]{:S(2)}, u32[]{:S(2)}) collective-permute-start(bf16[512,1024]{1,0:T(8,128)(2,1)} %fusion.17), channel_id=1, source_target_pairs={{0,16},{8,24},{16,0},{24,8},{1,17},{9,25},{17,1},{25,9},{2,18},{10... | collective-permute-start | bytes 3145736 | tf_op jit(solution)/shard_map/ppermute | solution.py:684
  473.1 41.9 %collective-permute-start.26 = (bf16[512,1024]{1,0:T(8,128)(2,1)}, bf16[512,1024]{1,0:T(8,128)(2,1)}, u32[]{:S(2)}, u32[]{:S(2)}) collective-permute-start(bf16[512,1024]{1,0:T(8,128)(2,1)} %fusion.19), channel_id=1, source_target_pairs={{0,16},{8,24},{16,0},{24,8},{1,17},{9,25},{17,1},{25,9},{2,18},{10... | collective-permute-start | bytes 3145736 | tf_op jit(solution)/shard_map/ppermute | solution.py:684
  474.6 25.9 %collective-permute-start.34 = (f32[152,128]{1,0:T(8,128)S(1)}, f32[152,128]{1,0:T(8,128)S(1)}, u32[]{:S(2)}, u32[]{:S(2)}) collective-permute-start(f32[152,128]{1,0:T(8,128)S(1)} %fusion.69), channel_id=1, source_target_pairs={{0,16},{8,24},{16,0},{24,8},{1,17},{9,25},{17,1},{25,9},{2,18},{10... | collective-permute-start | bytes 233480 | tf_op jit(solution)/shard_map/ppermute | solution.py:684
  (72 other events, 634.6 us)
Sparse Core Ops, SparseCore 0:
  10.8 54.7 all-gather.3
  76.8 50.9 all-gather.5
  130.4 79.4 all-gather.7
  310.5 92.6 reduce-scatter.4
  447.0 90.4 reduce-scatter.2

commit v4 on v3

--- a/solution.py
+++ b/solution.py
@@ -212,15 +212,80 @@
         state[head] = states[blocks, head]
 
 
-def gate_kernel(heads, mixed_ref, normed_ref, weight_ref, gain_ref, gated_ref, gate_ref):
+def on_piece(pieces, body):
+    for at, piece in enumerate(pieces):
+
+        @pl.when(pl.program_id(0) == at)
+        def _(at=at, piece=piece):
+            body(at, piece)
+
+
+def entry_kernel(count, *refs):
+    weight_ref, gain_ref, normed_ref, proj_ref = refs[count:]
+
+    def body(at, piece):
+        normed = lower(row_norm(piece[...].astype(wide), gain_ref[0:1])[0])
+        normed_ref[...] = normed
+        proj_ref[...] = lower(by_weight(normed, weight_ref[...]))
+
+    on_piece(refs[:count], body)
+
+
+def gate_kernel(
+    heads, mixed_ref, normed_ref, weight_ref, gain_ref, out_ref, gated_ref, gate_ref, *partials
+):
     gate = by_weight(normed_ref[...], weight_ref[...])
     gate_ref[...] = gate
     gain = gain_ref[0:1]
     for head in range(heads):
         span = slice(head * DV, head * DV + DV)
-        normed, unused = row_norm(mixed_ref[:, span].astype(wide), gain)
+        normed = row_norm(mixed_ref[:, span].astype(wide), gain)[0]
         here = gate[:, span]
         gated_ref[:, span] = lower(normed * (here * jax.nn.sigmoid(here)))
+    partial = lower(by_weight(gated_ref[...], out_ref[...]))
+
+    def body(at, piece):
+        piece[...] = partial
+
+    on_piece(partials, body)
+
+
+def ffn_kernel(count, *refs):
+    normed_pieces, cot_pieces = refs[:count], refs[count : 2 * count]
+    both_ref, down_ref, normed_ref, cot_ref, hidden_ref, grad_ref = refs[
+        2 * count : 2 * count + 6
+    ]
+    backs = refs[2 * count + 6 :]
+    units = down_ref.shape[0]
+
+    def body(at, piece):
+        normed = piece[...]
+        cot = cot_pieces[at][...]
+        normed_ref[...] = normed
+        cot_ref[...] = cot
+        gate_pre = by_weight(normed, both_ref[:, :units])
+        up_pre = by_weight(normed, both_ref[:, units:])
+        sig = jax.nn.sigmoid(gate_pre)
+        silu = gate_pre * sig
+        hidden_ref[...] = lower(silu * up_pre)
+        grad_hidden = by_transpose(cot, down_ref[...])
+        grad_ref[:, :units] = lower(
+            grad_hidden * up_pre * sig * (1.0 + gate_pre * (1.0 - sig))
+        )
+        grad_ref[:, units:] = lower(grad_hidden * silu)
+        backs[at][...] = lower(by_transpose(grad_ref[...], both_ref[...]))
+
+    on_piece(normed_pieces, body)
+
+
+def branch_kernel(count, *refs):
+    weight_ref, branch_ref, grad_ref = refs[count:]
+
+    def body(at, piece):
+        branch_ref[...] = piece[...]
+        grad_ref[...] = by_transpose(piece[...], weight_ref[...])
+
+    on_piece(refs[:count], body)
 
 
 def backward_kernel(
@@ -533,33 +598,111 @@
     )(place, proj, proj, taps, coefficients)
 
 
-def gate_rows(heads, mixed, normed, weight, gain, interpret=False):
+def fixed(shape):
+    return pl.BlockSpec(shape, lambda i: (0,) * len(shape))
+
+
+def rows_of(rows, columns):
+    return pl.BlockSpec((rows, columns), lambda i: (i, 0))
+
+
+def shape_of(rows, columns, kind=narrow):
+    return jax.ShapeDtypeStruct((rows, columns), kind)
+
+
+def row_call(kernel, steps, in_specs, out_specs, out_shape, flops, interpret):
+    return pl.pallas_call(
+        kernel,
+        grid=(steps,),
+        in_specs=in_specs,
+        out_specs=out_specs,
+        out_shape=out_shape,
+        compiler_params=params(),
+        cost_estimate=pl.CostEstimate(
+            flops=flops, bytes_accessed=flops // 1024, transcendentals=0
+        ),
+        interpret=interpret,
+    )
+
+
+def enter(pieces, weight, gain, interpret):
+    steps = len(pieces)
+    rows, model = pieces[0].shape
+    width = weight.shape[1]
+    return row_call(
+        lambda *refs: entry_kernel(steps, *refs),
+        steps,
+        [fixed(item.shape) for item in (*pieces, weight, gain)],
+        [rows_of(rows, model), rows_of(rows, width)],
+        [shape_of(steps * rows, model), shape_of(steps * rows, width)],
+        2 * steps * rows * model * width,
+        interpret,
+    )(*pieces, weight, gain)
+
+
+def gate_rows(heads, steps, mixed, normed, weight, gain, w_out, interpret):
     length, values = mixed.shape
     model = normed.shape[1]
-    block = 2 * CHUNK
-
-    def tall(columns):
-        return pl.BlockSpec((block, columns), lambda i: (i, 0))
-
-    def whole(shape):
-        return pl.BlockSpec(shape, lambda i: (0, 0))
-
-    return pl.pallas_call(
+    rows = length // steps
+    return row_call(
         lambda *refs: gate_kernel(heads, *refs),
-        grid=(length // block,),
-        in_specs=[tall(values), tall(model), whole(weight.shape), whole(gain.shape)],
-        out_specs=[tall(values), tall(values)],
-        out_shape=[
-            jax.ShapeDtypeStruct((length, values), narrow),
-            jax.ShapeDtypeStruct((length, values), wide),
+        steps,
+        [
+            rows_of(rows, values),
+            rows_of(rows, model),
+            fixed(weight.shape),
+            fixed(gain.shape),
+            fixed(w_out.shape),
         ],
-        compiler_params=params(),
-        cost_estimate=pl.CostEstimate(
-            flops=4 * length * model * values, bytes_accessed=length * values * 8,
-            transcendentals=length * values,
-        ),
-        interpret=interpret,
-    )(mixed, normed, weight, gain)
+        [rows_of(rows, values), rows_of(rows, values)] + [fixed((rows, model))] * steps,
+        [shape_of(length, values), shape_of(length, values, wide)]
+        + [shape_of(rows, model)] * steps,
+        4 * length * model * values,
+        interpret,
+    )(mixed, normed, weight, gain, w_out)
+
+
+def ffn_rows(normed_pieces, cot_pieces, both, down, interpret):
+    steps = len(normed_pieces)
+    rows, model = normed_pieces[0].shape
+    units = down.shape[0]
+    length = steps * rows
+    return row_call(
+        lambda *refs: ffn_kernel(steps, *refs),
+        steps,
+        [fixed(item.shape) for item in (*normed_pieces, *cot_pieces, both, down)],
+        [
+            rows_of(rows, model),
+            rows_of(rows, model),
+            rows_of(rows, units),
+            rows_of(rows, 2 * units),
+        ]
+        + [fixed((rows, model))] * steps,
+        [
+            shape_of(length, model),
+            shape_of(length, model),
+            shape_of(length, units),
+            shape_of(length, 2 * units),
+        ]
+        + [shape_of(rows, model)] * steps,
+        10 * length * model * units,
+        interpret,
+    )(*normed_pieces, *cot_pieces, both, down)
+
+
+def branch_rows(pieces, weight, interpret):
+    steps = len(pieces)
+    rows, model = pieces[0].shape
+    values = weight.shape[0]
+    return row_call(
+        lambda *refs: branch_kernel(steps, *refs),
+        steps,
+        [fixed(item.shape) for item in (*pieces, weight)],
+        [rows_of(rows, model), rows_of(rows, values)],
+        [shape_of(steps * rows, model), shape_of(steps * rows, values, wide)],
+        2 * steps * rows * model * values,
+        interpret,
+    )(*pieces, weight)
 
 
 def mixer_backward(
@@ -680,6 +823,8 @@
     def mine(array, size, axis):
         return lax.dynamic_slice_in_dim(array, place * size, size, axis)
 
+    tie = lax.optimization_barrier
+
     def flip(array, bit):
         return lax.ppermute(array, "seq", [(i, i ^ bit) for i in range(parts)])
 
@@ -691,19 +836,43 @@
 
     def gather_seq(array):
         across = flip(array, 2)
-        near = jnp.concatenate([array, flip(array, 1)], axis=0)
-        far = jnp.concatenate([across, flip(across, 1)], axis=0)
-        return near, far
-
-    def scatter_seq(near, far, beside=None):
-        half = near.shape[0] // 2
-        across = far[:half] + flip(lower(far[half:]), 1).astype(wide)
+        return [array, flip(array, 1), across, flip(across, 1)]
+
+    def scatter_seq(pieces, beside=None):
+        own_piece, sibling, across, corner = pieces
+        across = across.astype(wide) + flip(lower(corner), 1).astype(wide)
         across = flip(lower(across), 2)
-        sibling = flip(lower(near[half:]), 1)
+        sibling = flip(lower(sibling), 1)
         if beside is not None:
-            across, beside = lax.optimization_barrier((across, beside))
-        total = near[:half] + sibling.astype(wide) + across.astype(wide)
+            across, beside = tie((across, beside))
+        total = own_piece.astype(wide) + sibling.astype(wide) + across.astype(wide)
         return (total, beside)
+
+    def gather_dp(array):
+        shard = lax.axis_index("dp")
+        stack = array[None]
+        bits = shards.bit_length() - 1
+        done = bits // 2
+        for low, high in ((done, bits), (0, done)):
+            size = 1 << (high - low)
+            pieces = [stack] + [
+                lax.ppermute(stack, "dp", [(i, i ^ (at << low)) for i in range(shards)])
+                for at in range(1, size)
+            ]
+            for bit in range(high - low):
+                upper = jnp.bitwise_and(shard, 1 << (low + bit)) != 0
+                pieces = [
+                    jnp.where(upper, pieces[at ^ (1 << bit)], pieces[at])
+                    for at in range(size)
+                ]
+            stack = jnp.stack(pieces, axis=1).reshape((-1,) + array.shape)
+        return stack
+
+    def scatter_direct(pieces):
+        total = pieces[0].astype(wide)
+        for bit in range(1, parts):
+            total = total + flip(lower(pieces[bit]), bit).astype(wide)
+        return total
 
     def sum_all(array):
         for bit in range(1, parts):
@@ -724,10 +893,6 @@
             axis=0,
         )
 
-    def stack_seq(array):
-        near, far = gather_seq(array[None])
-        return jnp.concatenate([near, far], axis=0)
-
     def exchange(stack):
         pieces = [
             lax.dynamic_index_in_dim(stack, jnp.bitwise_xor(place, at), 0)
@@ -750,26 +915,39 @@
         split = jnp.pad(split, ((0, 0), (0, 0), (0, padded - piece)))
         return split.reshape(own, ffn_own)
 
-    tie = lax.optimization_barrier
     own_tokens = tokens[:, 0, :]
     own_cot = cotangent[:, 0, :]
-    half_lanes = LANES // 2
     small_flat = jnp.concatenate([norm_attn, norm_ffn, conv_w.reshape(-1)])
     small_count = small_flat.shape[0]
+    half_lanes = LANES // 2
     small_flat = jnp.pad(small_flat, (0, own * half_lanes - small_count))
     w_in = over_dp(
         jnp.concatenate(
             [
                 mine(w_qkv, width, 1),
-                jnp.pad(
-                    mine(w_ba, 2 * heads, 1), ((0, 0), (0, half_lanes - 2 * heads))
-                ),
+                jnp.pad(mine(w_ba, 2 * heads, 1), ((0, 0), (0, half_lanes - 2 * heads))),
                 small_flat.reshape(own, half_lanes),
             ],
             axis=1,
         )
     )
-    all_tokens = jnp.concatenate(gather_seq(own_tokens), axis=0)
+    token_pieces = gather_seq(own_tokens)
+    out_ratio = out_rows // own
+    second_all = gather_dp(
+        jnp.concatenate(
+            [
+                mine(w_outgate, values, 1),
+                jnp.swapaxes(
+                    mine(w_out, quarter, 1).reshape(out_ratio, own, quarter), 0, 1
+                ).reshape(own, -1),
+            ],
+            axis=1,
+        )
+    )
+    w_gate_in = second_all[:, :, :values].reshape(model, values)
+    out_part = jnp.swapaxes(
+        second_all[:, :, values:].reshape(shards, own, out_ratio, quarter), 1, 2
+    )
     small_all = w_in[:, width + half_lanes :].reshape(shards, -1)[:, :small_count]
     first_gain = small_all[:, :own].reshape(-1).astype(wide)
     second_gain = small_all[:, own : 2 * own].reshape(-1).astype(wide)
@@ -777,21 +955,6 @@
     taps = mine(taps_all.reshape(CONV, -1), width, 1).astype(wide)
     taps = jnp.pad(taps, ((0, HALO - CONV), (0, 0)))
 
-    out_ratio = out_rows // own
-    second = jnp.concatenate(
-        [
-            mine(w_outgate, values, 1),
-            jnp.swapaxes(
-                mine(w_out, quarter, 1).reshape(out_ratio, own, quarter), 0, 1
-            ).reshape(own, -1),
-        ],
-        axis=1,
-    )
-    cot_near, cot_far = gather_seq(own_cot)
-    second, w_in, all_tokens, cot_near, cot_far = tie(
-        (second, w_in, all_tokens, cot_near, cot_far)
-    )
-    second_all = over_dp(second)
     down_part = jnp.pad(mine(w_down, piece, 0), ((0, padded - piece), (0, 0)))
     ffn_part = jnp.concatenate(
         [
@@ -822,86 +985,76 @@
     gain = jnp.broadcast_to(head_gain.astype(wide)[None, :], (HALO, DV))
     place_row = place.astype(jnp.int32)[None]
 
-    rows = own_tokens.astype(wide)
-    inverse_one = row_norm(rows, first_gain)[1]
-    normed_one = lower(row_norm(all_tokens.astype(wide), first_gain)[0])
-    proj = lower(by_weight(normed_one, w_in))
+    first_rows = jnp.broadcast_to(first_gain[None, :], (HALO, model))
+    w_in, first_rows, *token_pieces = tie((w_in, first_rows, *token_pieces))
+    normed_one, proj = enter(token_pieces, w_in, first_rows, interpret)
     mixed, *kept = mixer_forward(
         heads, parts, place_row, proj, taps, coefficients, interpret
     )
-    second_all, mixed = tie((second_all, mixed))
-    w_gate_in = second_all[:, :values]
-    out_part = jnp.swapaxes(
-        second_all[:, values:].reshape(shards, own, out_ratio, quarter), 1, 2
-    )
+    mixed, *cot_pieces = tie((mixed, *gather_seq(own_cot)))
     w_out_own = jnp.swapaxes(
         exchange(out_part.reshape(parts, values, quarter)), 0, 1
     ).reshape(values, model)
-    gated, out_gate = gate_rows(heads, mixed, normed_one, w_gate_in, gain, interpret)
-    half = gated.shape[0] // 2
-    mixed_far = by_weight(gated[half:], w_out_own)
-    mixed_near = by_weight(gated[:half], w_out_own)
-    after_mix = rows + scatter_seq(mixed_near, mixed_far)[0]
+    gated, out_gate, *mixed_pieces = gate_rows(
+        heads, parts, mixed, normed_one, w_gate_in, gain, w_out_own, interpret
+    )
+    rows = own_tokens.astype(wide)
+    inverse_one = row_norm(rows, first_gain)[1]
+    after_mix = rows + scatter_seq(mixed_pieces)[0]
     normed_two, inverse_two = row_norm(after_mix, second_gain)
-    normed_two = lower(normed_two)
+    normed_two, both_own, down_own = tie((lower(normed_two), both_own, down_own))
     across = flip(normed_two, 2)
-    normed_near = jnp.concatenate([normed_two, flip(normed_two, 1)], axis=0)
-    pre_near = by_weight(normed_near, both_own)
-    across, pre_near = tie((across, pre_near))
-    normed_far = jnp.concatenate([across, flip(across, 1)], axis=0)
-
-    def ffn_side(pre, cot_half):
-        gate_pre = pre[:, :ffn_own]
-        up_pre = pre[:, ffn_own:]
-        sig_ffn = jax.nn.sigmoid(gate_pre)
-        hidden = lower(gate_pre * sig_ffn * up_pre)
-        grad_hidden = by_transpose(cot_half, down_own)
-        grad_gate_pre = lower(
-            grad_hidden * up_pre * sig_ffn * (1.0 + gate_pre * (1.0 - sig_ffn))
-        )
-        grad_up_pre = lower(grad_hidden * gate_pre * sig_ffn)
-        grad_both = jnp.concatenate([grad_gate_pre, grad_up_pre], axis=1)
-        return hidden, grad_both, by_transpose(grad_both, both_own)
-
-    hidden_near, grad_near, back_near = ffn_side(pre_near, cot_near)
-    hidden_far, grad_far, back_far = ffn_side(by_weight(normed_far, both_own), cot_far)
+    beside = flip(normed_two, 1)
+    half = parts // 2
+    normed_near, cot_near, hidden_near, grad_near, *back_near = ffn_rows(
+        [normed_two, beside], cot_pieces[:half], both_own, down_own, interpret
+    )
+    normed_far, cot_far, hidden_far, grad_far, *back_far = ffn_rows(
+        [across, flip(across, 1)], cot_pieces[half:], both_own, down_own, interpret
+    )
     grad_both = over_rows(normed_near, grad_near) + over_rows(normed_far, grad_far)
     grad_down = over_rows(hidden_near, cot_near) + over_rows(hidden_far, cot_far)
     grad_down = from_lanes(
         to_lanes(lower(grad_down).reshape(shards, padded, model)), own
     ).reshape(model, -1)
     grad_ffn = jnp.concatenate([lower(grad_both), grad_down], axis=1)
-    grad_normed_two, grad_ffn = scatter_seq(back_near, back_far, grad_ffn)
+    grad_normed_two, grad_ffn = scatter_seq(back_near + back_far, grad_ffn)
     grad_ffn = sum_dp(grad_ffn)
     back_two, grad_norm_ffn = norm_back(after_mix, inverse_two, second_gain, grad_normed_two)
     grad_after = own_cot.astype(wide) + back_two
-    grad_branch = jnp.concatenate(gather_seq(lower(grad_after)), axis=0)
-    grad_branch, hidden_near, hidden_far = tie((grad_branch, hidden_near, hidden_far))
-    grad_gated = by_transpose(grad_branch, w_out_own)
+    branch_pieces = gather_seq(lower(grad_after))
+    down_near = lower(by_weight(hidden_near, down_own))
+    down_far = lower(by_weight(hidden_far, down_own))
+    down_near, down_far, *branch_pieces = tie((down_near, down_far, *branch_pieces))
+    grad_branch, grad_gated = branch_rows(branch_pieces, w_out_own, interpret)
     grad_out = jnp.swapaxes(
         lower(over_rows(gated, grad_branch)).reshape(values, parts, quarter), 0, 1
     )
     grad_out = jnp.swapaxes(
         exchange(grad_out).reshape(shards, out_ratio, own, quarter), 1, 2
     ).reshape(model, -1)
+    count = own_tokens.shape[0]
     result = after_mix + scatter_seq(
-        by_weight(hidden_near, down_own), by_weight(hidden_far, down_own)
+        [down_near[:count], down_near[count:], down_far[:count], down_far[count:]]
     )[0]
     grad_in, grad_taps, grad_gain, grad_small = mixer_backward(
         heads, parts, place_row, proj, out_gate, taps, coefficients, gain, [mixed, *kept],
         grad_gated, interpret
     )
-    grad_w_in = lower(over_rows(normed_one, grad_in))
+    grad_w_in = jnp.concatenate([lower(over_rows(normed_one, grad_in)), grad_out], axis=1)
     grad_in, grad_w_in = tie((grad_in, grad_w_in))
-    grad_w_in = sum_dp(jnp.concatenate([grad_w_in, grad_out], axis=1))
+    grad_w_in = sum_dp(grad_w_in)
     grad_first = grad_in[:, : width + LANES]
     grad_gate = grad_in[:, width + LANES :]
-    one_far = by_transpose(grad_first[half:], w_in) + by_transpose(grad_gate[half:], w_gate_in)
-    one_near = by_transpose(grad_first[:half], w_in) + by_transpose(
-        grad_gate[:half], w_gate_in
+    one_far, one_near = (
+        by_transpose(grad_first[span], w_in) + by_transpose(grad_gate[span], w_gate_in)
+        for span in (slice(2 * count, None), slice(0, 2 * count))
     )
     back_one, grad_norm_attn = norm_back(
-        rows, inverse_one, first_gain, scatter_seq(one_near, one_far)[0]
+        rows,
+        inverse_one,
+        first_gain,
+        scatter_direct([one_near[:count], one_near[count:], one_far[:count], one_far[count:]]),
     )
     grad_rows = lower(grad_after + back_one)[:, None, :]
 
@@ -920,11 +1073,16 @@
     )
     packed_count = packed.shape[0]
     packed = jnp.pad(packed, (0, -packed_count % (HALO * LANES)))
-    packed = sum_all(packed.reshape(-1, LANES)).reshape(-1)
     def pieces_of(array):
-        stack = stack_seq(array)
+        near = gather_seq(array)
+        low_bit = jnp.bitwise_and(place, 1) != 0
+        high_bit = jnp.bitwise_and(place, 2) != 0
         return [
-            lax.dynamic_index_in_dim(stack, jnp.bitwise_xor(place, at), 0, keepdims=False)
+            jnp.where(
+                high_bit,
+                jnp.where(low_bit, near[at ^ 3], near[at ^ 2]),
+                jnp.where(low_bit, near[at ^ 1], near[at]),
+            )
             for at in range(parts)
         ]
 
@@ -957,6 +1115,7 @@
     )
     grad_w_in, early = tie((grad_w_in, early))
     block_out, grad_rows, grad_w_gate, grad_w_up, grad_w_down, packed = early
+    packed = sum_all(packed.reshape(-1, LANES)).reshape(-1)
     taps_at = 2 * model
     gain_at = taps_at + CONV * head_count * ROW
     heads_at = gain_at + DV

time: 579 us -> 607 us (1.048)
  Pallas kernels: 88.8 us -> 142 us
  matrix products: 89.6 us -> 49.8 us
  starting transfers between devices: 26.2 us -> 42.1 us
  other arithmetic: 59.5 us -> 50.5 us
    pallas_call x1 -> x5, Pallas kernels: 7.51 us -> 61.7 us  [the longest x2 31.2 us: ffn_rows(): row_call(lambda *refs: ffn_kernel(steps, *refs), steps, [fixed(item.shape...]
    ppermute x0 -> x4, waiting for transfers between devices: none -> 45.1 us  [gather_dp(): lax.ppermute(stack, 'dp', [(i, i ^ at << low) for i in range(shards)])]
    all_gather x3 -> x2, waiting for transfers between devices: 29.4 us -> 5.05 us  [over_dp(): return lax.all_gather(array, 'dp', axis=0, tiled=True)]
    dot_general x7 -> x2, matrix products: 29 us -> 4.97 us  [by_weight(): return jnp.dot(left, right, preferred_element_type=wide)]
    dot_general x9 -> x4, matrix products: 32.6 us -> 11.8 us  [by_transpose(): lax.dot_general(left, right, (((1,), (1,)), ((), ())), preferred_element_...]
    concatenate x8 -> x1, other arithmetic: 16.9 us -> 2.41 us  [per_device(): jnp.concatenate([lower(over_rows(normed_one, grad_in)), grad_out], axis=1)]
    ppermute x38, waiting for transfers between devices: 180 us -> 169 us  [flip(): return lax.ppermute(array, 'seq', [(i, i ^ bit) for i in range(parts)])]
    slice x9 -> x8, local copies, waits for them, and re-layouts: 8.04 us -> 17.7 us  [the longest x2 5.23 us: per_device(): ffn_all[:, 2 * ffn_own:].reshape(shards, own, -1)]
  transfers between devices with their start and end apart: 46 -> 49, of which waited for: 19 -> 19; matrix products, arithmetic and copies ran while one was open for 34% -> 23% of each run, Pallas kernels for 16% -> 21%
where the time goes in v4:
time: 607 us; the launch traced here: 602 us
  waiting for transfers between devices  226 us (37%)
  Pallas kernels  142 us (23%)
  local copies, waits for them, and re-layouts  75.2 us (12%)
  other arithmetic  50.5 us (8%)
  matrix products  49.8 us (8%)
  starting transfers between devices  42.1 us (7%)
  between operations  15.6 us (3%)
    ppermute x38, waiting for transfers between devices, flip(): return lax.ppermute(array, 'seq', [(i, i ^ bit) for i in range(parts)])  169 us
    pallas_call x1, Pallas kernels, mixer_backward(): pl.pallas_call(lambda *refs: backward_kernel(heads, *refs), grid_spec=plt...  53.7 us
    ppermute x4, waiting for transfers between devices, gather_dp(): lax.ppermute(stack, 'dp', [(i, i ^ at << low) for i in range(shards)])  45.1 us
    dot_general x6, matrix products, over_rows(): lax.dot_general(left, right, (((0,), (0,)), ((), ())), preferred_element_...  33 us
    pallas_call x2, Pallas kernels, ffn_rows(): row_call(lambda *refs: ffn_kernel(steps, *refs), steps, [fixed(item.shape...  31.2 us
    pallas_call x1, Pallas kernels, mixer_forward(): pl.pallas_call(lambda *refs: forward_kernel(heads, *refs), grid_spec=pltp...  27 us
    ppermute x38, starting transfers between devices, flip(): return lax.ppermute(array, 'seq', [(i, i ^ bit) for i in range(parts)])  23.1 us
    unnamed x118, local copies, waits for them, and re-layouts  21 us
  transfers between devices with their start and end apart: 49, of which 19 were waited for; matrix products, arithmetic and copies ran while one was open for 23% of the time, Pallas kernels for 21%

profile of v4, /device:TPU:0, one launch (start us, length us, event | category | flops | bytes accessed | tf_op | source)
XLA Modules:
  0.0 601.5 jit_solution(3401236158519123031)
XLA Ops:
  20.1 8.7 %collective-permute-done.8 = bf16[1,128,1024]{1,2,0:T(8,128)(2,1)S(1)} collective-permute-done((bf16[1,128,1024]{1,2,0:T(8,128)(2,1)S(1)}, bf16[1,128,1024]{1,2,0:T(8,128)(2,1)S(1)}, u32[]{:S(2)}, u32[]{:S(2)}) %collective-permute-start.8) | collective-permute-done | bytes 262176 | tf_op jit(solution)/shard_map/ppermute | solution.py:859
  28.8 12.7 %collective-permute-done.7 = bf16[1,128,1024]{1,2,0:T(8,128)(2,1)S(1)} collective-permute-done((bf16[1,128,1024]{1,2,0:T(8,128)(2,1)S(1)}, bf16[1,128,1024]{1,2,0:T(8,128)(2,1)S(1)}, u32[]{:S(2)}, u32[]{:S(2)}) %collective-permute-start.7) | collective-permute-done | bytes 262176 | tf_op jit(solution)/shard_map/ppermute | solution.py:859
  55.2 23.8 %collective-permute-done.9 = bf16[4,128,1024]{1,2,0:T(8,128)(2,1)} collective-permute-done((bf16[4,128,1024]{1,2,0:T(8,128)(2,1)}, bf16[4,128,1024]{1,2,0:T(8,128)(2,1)}, u32[]{:S(2)}, u32[]{:S(2)}) %collective-permute-start.9) | collective-permute-done | bytes 1048608 | tf_op jit(solution)/shard_map/ppermute | solution.py:859
  92.2 6.0 collective-permute-done.12
  98.4 5.6 collective-permute-done.11
  109.7 11.0 %shard_map.262 = (bf16[2048,1024]{1,0:T(8,128)(2,1)}, bf16[2048,1152]{1,0:T(8,128)(2,1)}) custom-call(bf16[512,1024]{1,0:T(8,128)(2,1)S(1)} %bitcast.270, bf16[512,1024]{1,0:T(8,128)(2,1)} %collective-permute-done.refs_1_, bf16[512,1024]{1,0:T(8,128)(2,1)} %collective-permute-done.1.refs_2_, bf16[512,1024]{1,0:T(8,128)(2,1)} %collective-permute-done.2.refs_3_, ...), custom_call_target="tpu_custom_call" | custom-call | flops 4831838208 | bytes 4718592 | tf_op jit(solution)/shard_map/pallas_call | solution.py:632
  120.8 27.0 %shard_map.263 = (bf16[2048,512]{1,0:T(8,128)(2,1)}, bf16[8,2,256,256]{3,2,1,0:T(8,128)(2,1)}, bf16[8,2,256,128]{3,2,1,0:T(8,128)(2,1)S(1)}, bf16[2048,512]{1,0:...) custom-call(s32[1]{0:T(128)} %bitcast.refs_0_, ...), custom_call_target="tpu_custom_call" | custom-call | flops 40960000000 | bytes 4194304 | tf_op jit(solution)/shard_map/pallas_call | solution.py:563
  147.8 11.2 %shard_map.264 = (bf16[2048,512]{1,0:T(8,128)(2,1)}, f32[2048,512]{1,0:T(8,128)}, bf16[512,1024]{1,0:T(8,128)(2,1)S(1)}, bf16[512,1024]{1,0:T(8,128)(2,1)}, bf16...) custom-call(bf16[2048,512]{1,0:T(8,128)(2,1)} %get-tuple-element.89.refs_0_.refs_8_, ...), custom_call_target="tpu_custom_call" | custom-call | flops 4294967296 | bytes 4194304 | tf_op jit(solution)/shard_map/pallas_call | solution.py:647
  163.7 25.2 %collective-permute-done.15 = bf16[512,1024]{1,0:T(8,128)(2,1)S(1)} collective-permute-done((bf16[512,1024]{1,0:T(8,128)(2,1)S(1)}, bf16[512,1024]{1,0:T(8,128)(2,1)S(1)}, u32[]{:S(2)}, u32[]{:S(2)}) %collective-permute-start.15) | collective-permute-done | bytes 1048608 | tf_op jit(solution)/shard_map/ppermute | solution.py:829
  192.7 5.0 all-gather.5.cloned.1.call-done
  217.7 22.4 %collective-permute-done.17.refs_0_ = bf16[512,1024]{1,0:T(8,128)(2,1)S(1)} collective-permute-done((bf16[512,1024]{1,0:T(8,128)(2,1)S(1)}, bf16[512,1024]{1,0:T(8,128)(2,1)S(1)}, u32[]{:S(2)}, u32[]{:S(2)}) %collective-permute-start.17) | collective-permute-done | bytes 1048608 | tf_op jit(solution)/shard_map/ppermute | solution.py:829
  241.1 15.3 %shard_map.265 = (bf16[1024,1024]{1,0:T(8,128)(2,1)}, bf16[1024,1024]{1,0:T(8,128)(2,1)}, bf16[1024,768]{1,0:T(8,128)(2,1)}, bf16[1024,1536]{1,0:T(8,128)(2,1)},...) custom-call(bf16[512,1024]{1,0:T(8,128)(2,1)} %copy-done.10, bf16[512,1024]{1,0:T(8,128)(2,1)} %copy-done.34, ...), custom_call_target="tpu_custom_call" | custom-call | flops 8053063680 | bytes 7864320 | tf_op jit(solution)/shard_map/pallas_call | solution.py:670
  256.4 8.6 %fusion.48 = f32[1024,1536]{1,0:T(8,128)} fusion(bf16[1024,1024]{1,0:T(8,128)(2,1)} %get-tuple-element.115, bf16[1024,1536]{1,0:T(8,128)(2,1)} %get-tuple-element.116), kind=kOutput, calls=%fused_computation.177 | convolution fusion | flops 3221225472 | bytes 11534336 | tf_op jit(solution)/shard_map/dot_general | solution.py:32
  266.0 15.9 %shard_map.266 = (bf16[1024,1024]{1,0:T(8,128)(2,1)}, bf16[1024,1024]{1,0:T(8,128)(2,1)}, bf16[1024,768]{1,0:T(8,128)(2,1)}, bf16[1024,1536]{1,0:T(8,128)(2,1)},...) custom-call(bf16[512,1024]{1,0:T(8,128)(2,1)} %copy-done.29, bf16[512,1024]{1,0:T(8,128)(2,1)} %copy-done.31, ...), custom_call_target="tpu_custom_call" | custom-call | flops 8053063680 | bytes 7864320 | tf_op jit(solution)/shard_map/pallas_call | solution.py:670
  297.8 17.5 %collective-permute-done.21 = bf16[512,1024]{1,0:T(8,128)(2,1)} collective-permute-done((bf16[512,1024]{1,0:T(8,128)(2,1)}, bf16[512,1024]{1,0:T(8,128)(2,1)}, u32[]{:S(2)}, u32[]{:S(2)}) %collective-permute-start.21) | collective-permute-done | bytes 1048608 | tf_op jit(solution)/shard_map/ppermute | solution.py:829
  327.6 23.7 %collective-permute-done.23.refs_2_ = bf16[512,1024]{1,0:T(8,128)(2,1)S(1)} collective-permute-done((bf16[512,1024]{1,0:T(8,128)(2,1)S(1)}, bf16[512,1024]{1,0:T(8,128)(2,1)S(1)}, u32[]{:S(2)}, u32[]{:S(2)}) %collective-permute-start.23) | collective-permute-done | bytes 1048608 | tf_op jit(solution)/shard_map/ppermute | solution.py:829
  358.0 8.2 %shard_map.267 = (bf16[2048,1024]{1,0:T(8,128)(2,1)}, f32[2048,512]{1,0:T(8,128)}) custom-call(bf16[512,1024]{1,0:T(8,128)(2,1)S(1)} %get-tuple-element.122.refs_0_, bf16[512,1024]{1,0:T(8,128)(2,1)} %copy-done.32, bf16[512,1024]{1,0:T(8,128)(2,1)} %copy-done.30, bf16[512,1024]{1,0:T(8,128)(2,1)} %copy-done.33, bf16[512,1024]{1,0:T(8,128)(2,1)} %bitcast.296), custom_call_target="tpu_custom_call" | custom-call | flops 2147483648 | bytes 2097152 | tf_op jit(solution)/shard_map/pallas_call | solution.py:697
  366.2 5.6 convolution_convert_fusion.3
  378.2 53.7 %shard_map.268 = (bf16[2048,1664]{1,0:T(8,128)(2,1)}, f32[8,1024]{1,0:T(8,128)S(1)}, f32[8,256]{1,0:T(8,128)S(1)}, f32[8,128]{1,0:T(8,128)S(1)}) custom-call(s32[1]{0:T(128)} %bitcast.refs_0_, bf16[2048,1152]{1,0:T(8,128)(2,1)} %get-tuple-element.87.refs_1_.refs_2_.refs_3_, bf16[2048,1152]{1,0:T(8,128)(2,1)} %get-tuple-element.87.refs_1_.refs_2_.refs_3_, ...), custom_call_target="tpu_custom_call" | custom-call | flops 409600000 | bytes 4194304 | tf_op jit(solution)/shard_map/pallas_call | solution.py:737
  432.0 11.2 %convolution_convert_fusion = bf16[1024,1664]{1,0:T(8,128)(2,1)S(1)} fusion(bf16[2048,1024]{1,0:T(8,128)(2,1)S(1)} %copy-done.39, bf16[2048,1664]{1,0:T(8,128)(2,1)} %get-tuple-element.133), kind=kOutput, calls=%fused_computation.9 | convolution fusion | flops 6981025792 | bytes 14417920 | tf_op jit(solution)/shard_map/dot_general | solution.py:32
  474.0 10.0 %collective-permute-done.32 = bf16[512,1024]{1,0:T(8,128)(2,1)S(1)} collective-permute-done((bf16[512,1024]{1,0:T(8,128)(2,1)}, bf16[512,1024]{1,0:T(8,128)(2,1)S(1)}, u32[]{:S(2)}, u32[]{:S(2)}) %collective-permute-start.32) | collective-permute-done | bytes 1048608 | tf_op jit(solution)/shard_map/ppermute | solution.py:829
  485.5 20.1 %collective-permute-done.33 = bf16[512,1024]{1,0:T(8,128)(2,1)} collective-permute-done((bf16[512,1024]{1,0:T(8,128)(2,1)}, bf16[512,1024]{1,0:T(8,128)(2,1)}, u32[]{:S(2)}, u32[]{:S(2)}) %collective-permute-start.33) | collective-permute-done | bytes 1048608 | tf_op jit(solution)/shard_map/ppermute | solution.py:829
  511.2 29.8 %collective-permute-done.34 = bf16[128,2304]{1,0:T(8,128)(2,1)} collective-permute-done((bf16[128,2304]{1,0:T(8,128)(2,1)}, bf16[128,2304]{1,0:T(8,128)(2,1)}, u32[]{:S(2)}, u32[]{:S(2)}) %collective-permute-start.34) | collective-permute-done | bytes 589856 | tf_op jit(solution)/shard_map/ppermute | solution.py:829
  567.7 6.7 %collective-permute-start.40 = (f32[152,128]{1,0:T(8,128)S(1)}, f32[152,128]{1,0:T(8,128)S(1)}, u32[]{:S(2)}, u32[]{:S(2)}) collective-permute-start(f32[152,128]{1,0:T(8,128)S(1)} %add.211), channel_id=1, source_target_pairs={{0,2},{1,3},{2,0},{3,1},{4,6},{5,7},{6,4},{7,5},{8,10},{9,11},{10,... | collective-permute-start | bytes 233480 | tf_op jit(solution)/shard_map/ppermute | solution.py:883
  (395 shorter events, 200.9 us)
Async XLA Ops:
  7.2 100.7 %all-gather.3.cloned.1.call-start = ((), (), s32[]{:S(2)}) async-start(), calls=%async_computation.2 | async-start | bytes 2654208 | tf_op jit(solution)/shard_map/all_gather | solution.py:832
  10.6 187.2 %all-gather.5.cloned.1.call-start = ((), (), s32[]{:S(2)}) async-start(), calls=%async_computation.3 | async-start | bytes 5308416 | tf_op jit(solution)/shard_map/all_gather | solution.py:832
  18.4 36.4 %collective-permute-start.1 = (bf16[512,1024]{1,0:T(8,128)(2,1)S(1)}, bf16[512,1024]{1,0:T(8,128)(2,1)}, u32[]{:S(2)}, u32[]{:S(2)}) collective-permute-start(bf16[512,1024]{1,0:T(8,128)(2,1)S(1)} %bitcast.268), channel_id=1, source_target_pairs={{0,16},{8,24},{16,0},{24,8},{1,17},{9,25},{17,1},{25,9},{2,18},{10... | collective-permute-start | bytes 3145736 | tf_op jit(solution)/shard_map/ppermute | solution.py:829
  42.9 36.0 %collective-permute-start.9 = (bf16[4,128,1024]{1,2,0:T(8,128)(2,1)}, bf16[4,128,1024]{1,2,0:T(8,128)(2,1)}, u32[]{:S(2)}, u32[]{:S(2)}) collective-permute-start(bf16[4,128,1024]{1,2,0:T(8,128)(2,1)} %maximum_bitcast_fusion), channel_id=1, source_target_pairs={{0,1},{1,0},{2,3},{3,2},{4,5},{5,4},{6,7},{7,6},{8,9},{9,8},{10,11... | collective-permute-start | bytes 3145736 | tf_op jit(solution)/shard_map/ppermute | solution.py:859
  44.5 65.2 %collective-permute-start = (bf16[512,1024]{1,0:T(8,128)(2,1)S(1)}, bf16[512,1024]{1,0:T(8,128)(2,1)}, u32[]{:S(2)}, u32[]{:S(2)}) collective-permute-start(bf16[512,1024]{1,0:T(8,128)(2,1)S(1)} %bitcast.269), channel_id=1, source_target_pairs={{0,8},{8,0},{16,24},{24,16},{1,9},{9,1},{17,25},{25,17},{2,10},{10... | collective-permute-start | bytes 3145736 | tf_op jit(solution)/shard_map/ppermute | solution.py:829
  44.5 46.6 %collective-permute-start.4 = (bf16[512,1024]{1,0:T(8,128)(2,1)}, bf16[512,1024]{1,0:T(8,128)(2,1)}, u32[]{:S(2)}, u32[]{:S(2)}) collective-permute-start(bf16[512,1024]{1,0:T(8,128)(2,1)} %bitcast.19.refs_2_), channel_id=1, source_target_pairs={{0,16},{8,24},{16,0},{24,8},{1,17},{9,25},{17,1},{25,9},{2,18},{10... | collective-permute-start | bytes 3145736 | tf_op jit(solution)/shard_map/ppermute | solution.py:829
  54.9 54.8 %collective-permute-start.2 = (bf16[512,1024]{1,0:T(8,128)(2,1)}, bf16[512,1024]{1,0:T(8,128)(2,1)}, u32[]{:S(2)}, u32[]{:S(2)}) collective-permute-start(bf16[512,1024]{1,0:T(8,128)(2,1)} %collective-permute-done.1.refs_2_), channel_id=1, source_target_pairs={{0,8},{8,0},{16,24},{24,16},{1,9},{9,1},{17,25},{25,17},{2,10},{10... | collective-permute-start | bytes 3145736 | tf_op jit(solution)/shard_map/ppermute | solution.py:829
  98.2 49.6 %collective-permute-start.3 = (bf16[512,1024]{1,0:T(8,128)(2,1)}, bf16[512,1024]{1,0:T(8,128)(2,1)}, u32[]{:S(2)}, u32[]{:S(2)}) collective-permute-start(bf16[512,1024]{1,0:T(8,128)(2,1)} %bitcast.19.refs_2_), channel_id=1, source_target_pairs={{0,8},{8,0},{16,24},{24,16},{1,9},{9,1},{17,25},{25,17},{2,10},{10... | collective-permute-start | bytes 3145736 | tf_op jit(solution)/shard_map/ppermute | solution.py:829
  103.9 43.9 %collective-permute-start.5 = (bf16[512,1024]{1,0:T(8,128)(2,1)}, bf16[512,1024]{1,0:T(8,128)(2,1)}, u32[]{:S(2)}, u32[]{:S(2)}) collective-permute-start(bf16[512,1024]{1,0:T(8,128)(2,1)} %collective-permute-done.4.refs_2_), channel_id=1, source_target_pairs={{0,8},{8,0},{16,24},{24,16},{1,9},{9,1},{17,25},{25,17},{2,10},{10... | collective-permute-start | bytes 3145736 | tf_op jit(solution)/shard_map/ppermute | solution.py:829
  109.3 374.7 %reduce-scatter.5.cloned.1.call-start = ((), (), s32[]{:S(2)}) async-start(), calls=%async_computation.5 | async-start | bytes 5308416 | tf_op jit(solution)/shard_map/reduce_scatter | solution.py:835
  315.4 241.5 %reduce-scatter.3.cloned.1.call-start = ((), (), s32[]{:S(2)}) async-start(), calls=%async_computation.4 | async-start | bytes 5013504 | tf_op jit(solution)/shard_map/reduce_scatter | solution.py:835
  327.6 28.8 %collective-permute-start.22 = (bf16[512,1024]{1,0:T(8,128)(2,1)S(1)}, bf16[512,1024]{1,0:T(8,128)(2,1)S(1)}, u32[]{:S(2)}, u32[]{:S(2)}) collective-permute-start(bf16[512,1024]{1,0:T(8,128)(2,1)S(1)} %get-tuple-element.122.refs_0_), channel_id=1, source_target_pairs={{0,8},{8,0},{16,24},{24,16},{1,9},{9,1},{17,25},{25,17},{2,10},{10... | collective-permute-start | bytes 3145736 | tf_op jit(solution)/shard_map/ppermute | solution.py:829
  357.5 112.9 %collective-permute-start.29 = (bf16[512,1024]{1,0:T(8,128)(2,1)}, bf16[512,1024]{1,0:T(8,128)(2,1)}, u32[]{:S(2)}, u32[]{:S(2)}) collective-permute-start(bf16[512,1024]{1,0:T(8,128)(2,1)} %slice.262), channel_id=1, source_target_pairs={{0,8},{8,0},{16,24},{24,16},{1,9},{9,1},{17,25},{25,17},{2,10},{10... | collective-permute-start | bytes 3145736 | tf_op jit(solution)/shard_map/ppermute | solution.py:829
  376.0 67.2 %collective-permute-start.27 = (bf16[1,512,256]{2,1,0:T(8,128)(2,1)S(1)}, bf16[1,512,256]{2,1,0:T(8,128)(2,1)S(1)}, u32[]{:S(2)}, u32[]{:S(2)}) collective-permute-start(bf16[1,512,256]{2,1,0:T(8,128)(2,1)S(1)} %bitcast.343), channel_id=1, source_target_pairs={{0,24},{8,16},{16,8},{24,0},{1,25},{9,17},{17,9},{25,1},{2,26},{10... | collective-permute-start | bytes 786440 | tf_op jit(solution)/shard_map/ppermute | solution.py:829
  377.6 65.6 %collective-permute-start.25 = (bf16[1,512,256]{2,1,0:T(8,128)(2,1)S(1)}, bf16[1,512,256]{2,1,0:T(8,128)(2,1)S(1)}, u32[]{:S(2)}, u32[]{:S(2)}) collective-permute-start(bf16[1,512,256]{2,1,0:T(8,128)(2,1)S(1)} %bitcast.342), channel_id=1, source_target_pairs={{0,8},{8,0},{16,24},{24,16},{1,9},{9,1},{17,25},{25,17},{2,10},{10... | collective-permute-start | bytes 786440 | tf_op jit(solution)/shard_map/ppermute | solution.py:829
  377.7 65.6 %collective-permute-start.26 = (bf16[1,512,256]{2,1,0:T(8,128)(2,1)S(1)}, bf16[1,512,256]{2,1,0:T(8,128)(2,1)S(1)}, u32[]{:S(2)}, u32[]{:S(2)}) collective-permute-start(bf16[1,512,256]{2,1,0:T(8,128)(2,1)S(1)} %bitcast.341), channel_id=1, source_target_pairs={{0,16},{8,24},{16,0},{24,8},{1,17},{9,25},{17,1},{25,9},{2,18},{10... | collective-permute-start | bytes 786440 | tf_op jit(solution)/shard_map/ppermute | solution.py:829
  457.8 26.2 %collective-permute-start.32 = (bf16[512,1024]{1,0:T(8,128)(2,1)}, bf16[512,1024]{1,0:T(8,128)(2,1)S(1)}, u32[]{:S(2)}, u32[]{:S(2)}) collective-permute-start(bf16[512,1024]{1,0:T(8,128)(2,1)} %get-tuple-element.222), channel_id=1, source_target_pairs={{0,16},{8,24},{16,0},{24,8},{1,17},{9,25},{17,1},{25,9},{2,18},{10... | collective-permute-start | bytes 3145736 | tf_op jit(solution)/shard_map/ppermute | solution.py:829
  459.3 46.3 %collective-permute-start.33 = (bf16[512,1024]{1,0:T(8,128)(2,1)}, bf16[512,1024]{1,0:T(8,128)(2,1)}, u32[]{:S(2)}, u32[]{:S(2)}) collective-permute-start(bf16[512,1024]{1,0:T(8,128)(2,1)} %get-tuple-element.223), channel_id=1, source_target_pairs={{0,24},{8,16},{16,8},{24,0},{1,25},{9,17},{17,9},{25,1},{2,26},{10... | collective-permute-start | bytes 3145736 | tf_op jit(solution)/shard_map/ppermute | solution.py:829
  466.7 38.9 %collective-permute-start.31 = (bf16[512,1024]{1,0:T(8,128)(2,1)}, bf16[512,1024]{1,0:T(8,128)(2,1)}, u32[]{:S(2)}, u32[]{:S(2)}) collective-permute-start(bf16[512,1024]{1,0:T(8,128)(2,1)} %slice.428), channel_id=1, source_target_pairs={{0,8},{8,0},{16,24},{24,16},{1,9},{9,1},{17,25},{25,17},{2,10},{10... | collective-permute-start | bytes 3145736 | tf_op jit(solution)/shard_map/ppermute | solution.py:829
  469.6 75.5 %collective-permute-start.28 = (bf16[512,1024]{1,0:T(8,128)(2,1)}, bf16[512,1024]{1,0:T(8,128)(2,1)}, u32[]{:S(2)}, u32[]{:S(2)}) collective-permute-start(bf16[512,1024]{1,0:T(8,128)(2,1)} %slice.260), channel_id=1, source_target_pairs={{0,8},{8,0},{16,24},{24,16},{1,9},{9,1},{17,25},{25,17},{2,10},{10... | collective-permute-start | bytes 3145736 | tf_op jit(solution)/shard_map/ppermute | solution.py:829
  472.4 72.6 %collective-permute-start.30 = (bf16[512,1024]{1,0:T(8,128)(2,1)S(1)}, bf16[512,1024]{1,0:T(8,128)(2,1)}, u32[]{:S(2)}, u32[]{:S(2)}) collective-permute-start(bf16[512,1024]{1,0:T(8,128)(2,1)S(1)} %add_convert_fusion.4), channel_id=1, source_target_pairs={{0,16},{8,24},{16,0},{24,8},{1,17},{9,25},{17,1},{25,9},{2,18},{10... | collective-permute-start | bytes 3145736 | tf_op jit(solution)/shard_map/ppermute | solution.py:829
  484.0 56.9 %collective-permute-start.34 = (bf16[128,2304]{1,0:T(8,128)(2,1)}, bf16[128,2304]{1,0:T(8,128)(2,1)}, u32[]{:S(2)}, u32[]{:S(2)}) collective-permute-start(bf16[128,2304]{1,0:T(8,128)(2,1)} %reduce-scatter.5.cloned.1.call-done), channel_id=1, source_target_pairs={{0,16},{8,24},{16,0},{24,8},{1,17},{9,25},{17,1},{25,9},{2,18},{10... | collective-permute-start | bytes 1769480 | tf_op jit(solution)/shard_map/ppermute | solution.py:829
  510.4 38.6 %collective-permute-start.36 = (bf16[128,2304]{1,0:T(8,128)(2,1)}, bf16[128,2304]{1,0:T(8,128)(2,1)S(1)}, u32[]{:S(2)}, u32[]{:S(2)}) collective-permute-start(bf16[128,2304]{1,0:T(8,128)(2,1)} %reduce-scatter.5.cloned.1.call-done), channel_id=1, source_target_pairs={{0,8},{8,0},{16,24},{24,16},{1,9},{9,1},{17,25},{25,17},{2,10},{10... | collective-permute-start | bytes 1769480 | tf_op jit(solution)/shard_map/ppermute | solution.py:829
  559.9 25.8 %collective-permute-start.42 = (bf16[128,2176]{1,0:T(8,128)(2,1)}, bf16[128,2176]{1,0:T(8,128)(2,1)}, u32[]{:S(2)}, u32[]{:S(2)}) collective-permute-start(bf16[128,2176]{1,0:T(8,128)(2,1)} %reduce-scatter.3.cloned.1.call-done), channel_id=1, source_target_pairs={{0,16},{8,24},{16,0},{24,8},{1,17},{9,25},{17,1},{25,9},{2,18},{10... | collective-permute-start | bytes 1671176 | tf_op jit(solution)/shard_map/ppermute | solution.py:829
  (71 other events, 786.6 us)
Sparse Core Ops, SparseCore 0:
  10.8 80.9 all-gather.2
  109.4 88.2 all-gather.4
  315.5 99.3 reduce-scatter.4
  447.5 96.1 reduce-scatter.2

commit v5 on v4

--- a/solution.py
+++ b/solution.py
@@ -136,6 +136,10 @@
     corrected_ref,
     update_ref,
     weight_ref,
+    active_ref,
+    slope_ref,
+    inner_ref,
+    pair_ref,
     before,
     state,
 ):
@@ -149,7 +153,10 @@
     raw = proj_ref[...].astype(wide)
     summed = convolved(shifted_rows(raw, before[...]), taps_ref[...], count)
     before[...] = raw[count - HALO :]
-    active = summed * jax.nn.sigmoid(summed)
+    sig = jax.nn.sigmoid(summed)
+    active = summed * sig
+    active_ref[...] = lower(active)
+    slope_ref[...] = lower(sig * (1.0 + summed * (1.0 - sig)))
     strength_rows, unused, decay_rows = gates(rates_ref[...].astype(wide), coef_ref[...])
     through = jnp.where(rows >= columns, 1.0, 0.0)
     states = {(0, head): state[head] for head in range(heads)}
@@ -180,7 +187,9 @@
         query_low = lower(query)
         dots = by_transpose(key_low, key_low)
         yield
-        lower_part = jnp.where(rows > columns, strength * fade * dots, 0.0)
+        pair = jnp.where(rows > columns, fade * dots, 0.0)
+        pair_ref[block, head] = lower(pair)
+        lower_part = strength * pair
         store = []
         yield from invert(lower_part, rows, columns, store)
         inverse = store[0]
@@ -188,6 +197,7 @@
         update = by_weight(inverse, lower(strength * value))
         weight = lower(by_weight(inverse, lower(strength * grown * key)))
         inner = lower(by_transpose(query_low, key_low) * fade)
+        inner_ref[block, head] = inner
         faded = lower(key * jnp.exp(final - cumulative))
         inverse_ref[block, head] = inverse
         span = slice(head * DV, head * DV + DV)
@@ -221,12 +231,14 @@
 
 
 def entry_kernel(count, *refs):
-    weight_ref, gain_ref, normed_ref, proj_ref = refs[count:]
+    weight_ref, rates_ref, gain_ref, normed_ref, proj_ref = refs[count:]
+    width = weight_ref.shape[1]
 
     def body(at, piece):
         normed = lower(row_norm(piece[...].astype(wide), gain_ref[0:1])[0])
         normed_ref[...] = normed
-        proj_ref[...] = lower(by_weight(normed, weight_ref[...]))
+        proj_ref[:, :width] = lower(by_weight(normed, weight_ref[...]))
+        proj_ref[:, width:] = lower(by_weight(normed, rates_ref[...]))
 
     on_piece(refs[:count], body)
 
@@ -279,13 +291,21 @@
 
 
 def branch_kernel(count, *refs):
-    weight_ref, branch_ref, grad_ref = refs[count:]
+    gated_ref, weight_ref, grad_ref, out_ref, total = refs[count:]
+    quarter = out_ref.shape[2]
 
     def body(at, piece):
-        branch_ref[...] = piece[...]
-        grad_ref[...] = by_transpose(piece[...], weight_ref[...])
+        branch = piece[...]
+        grad_ref[...] = by_transpose(branch, weight_ref[...])
+        product = over_rows(gated_ref[...], branch)
+        total[...] = product if at == 0 else total[...] + product
 
     on_piece(refs[:count], body)
+
+    @pl.when(pl.program_id(0) == count - 1)
+    def _():
+        for at in range(out_ref.shape[0]):
+            out_ref[at] = lower(total[:, at * quarter : (at + 1) * quarter])
 
 
 def backward_kernel(
@@ -304,6 +324,10 @@
     corrected_ref,
     update_ref,
     weight_ref,
+    active_ref,
+    slope_ref,
+    inner_ref,
+    pair_ref,
     grad_ref,
     out_ref,
     taps_grad_ref,
@@ -331,9 +355,7 @@
     edge = jnp.where(step == pl.num_programs(0) - 1, 0.0, edge)
     taps = taps_ref[...]
     extended = shifted_rows(raw, edge)
-    summed = convolved(extended, taps, count)
-    sig = jax.nn.sigmoid(summed)
-    active = summed * sig
+    active = active_ref[...].astype(wide)
     coefficients = coef_ref[...]
     strength_rows, shifted_rates, decay_rows = gates(
         rates_ref[...].astype(wide), coefficients
@@ -342,6 +364,7 @@
     onward = jnp.where(columns >= rows, 1.0, 0.0)
     gain = gain_ref[0:1]
     proj_width = heads * ROW
+    total = out_ref.shape[1]
     cumulative_rows = [
         exact_dot(through, decay_rows[block * CHUNK : (block + 1) * CHUNK])
         for block in range(blocks)
@@ -360,7 +383,7 @@
         normed, head_inverse = row_norm(mixed, gain)
         gate = gate_ref[here, span]
         sig_gate = jax.nn.sigmoid(gate)
-        gate_start = proj_width + LANES + head * DV
+        gate_start = proj_width + head * DV
         out_ref[here, gate_start : gate_start + DV] = lower(
             grad_gated * normed * sig_gate * (1.0 + gate * (1.0 - sig_gate))
         )
@@ -397,8 +420,6 @@
         key_low = lower(key)
         query_low = lower(query)
         yield
-        dots = by_transpose(key_low, key_low)
-        cross = by_transpose(query_low, key_low)
         held = state_ref[block, head]
         corrected = corrected_ref[here, span]
         weight = weight_ref[here, head * DK : head * DK + DK]
@@ -406,10 +427,11 @@
         faded_low = lower(faded)
         grown_query = query * grown
         yield
-        inner_side = over_rows(lower(cross * fade), grad_mixed)
+        inner = inner_ref[block, head]
+        inner_side = over_rows(inner, grad_mixed)
         state_side = over_rows(grad_mixed, lower(grown_query))
-        dot_grad = by_transpose(grad_mixed, corrected) * fade
-        dot_grad_low = lower(dot_grad)
+        dot_raw = by_transpose(grad_mixed, corrected)
+        dot_grad_low = lower(dot_raw * fade)
         grown_grad = by_weight(grad_mixed, held)
         yield
         while (block, head) not in laters:
@@ -428,18 +450,18 @@
         value_side = over_rows(inverse, corrected_grad_low)
         key_side = over_rows(inverse, weight_grad)
         yield
-        lower_grad = -(
+        lower_raw = -(
             by_transpose(lower(value_side), update_ref[here, span])
             + by_transpose(lower(key_side), weight)
-        ) * strict_fade
+        )
         inner_query = by_weight(dot_grad_low, key_low)
         inner_key = over_rows(dot_grad_low, query_low)
         yield
-        lower_grad_low = lower(lower_grad)
+        lower_grad_low = lower(lower_raw * strict_fade)
         first_key = by_weight(lower_grad_low, key_low)
         second_key = over_rows(lower_grad_low, lower(strength * key))
-        pairs = lower_grad * dots
-        both = pairs * strength + dot_grad * cross
+        pairs = lower_raw * pair_ref[block, head].astype(wide)
+        both = pairs * strength + dot_raw * inner.astype(wide)
         faded_sum = row_sum(faded_grad * faded)
         key_sum = row_sum(key_side * key)
         yield
@@ -499,7 +521,7 @@
         shift_grad = decay_grad * coefficients[1:2] * jax.nn.sigmoid(shifted_rates[here])
         strength_here = strength_rows[here]
         rates_grad = strength_grad * strength_here * (1.0 - strength_here) + shift_grad
-        out_ref[here, proj_width : proj_width + LANES] = lower(rates_grad)
+        out_ref[here, total - LANES :] = lower(rates_grad)
         small_grad_ref[0:1] += jnp.sum(shift_grad, axis=0, keepdims=True)
         small_grad_ref[1:2] += jnp.sum(decay_grad * decay_rows[here], axis=0, keepdims=True)
     gain_grad_ref[0:1] += sum(gain_grads)
@@ -512,7 +534,7 @@
         ],
         axis=0,
     )
-    summed_grad = joined * (sig * (1.0 + summed * (1.0 - sig)))
+    summed_grad = joined * slope_ref[...].astype(wide)
     following = jnp.concatenate([summed_grad, after[...]], axis=0)
     after[...] = summed_grad[:HALO]
     proj_grad = following[CONV - 1 : CONV - 1 + count] * taps[0:1]
@@ -578,6 +600,10 @@
                 tall(values),
                 tall(values),
                 tall(heads * DK),
+                tall(width),
+                tall(width),
+                stacked(CHUNK, CHUNK),
+                stacked(CHUNK, CHUNK),
             ],
             scratch_shapes=[
                 pltpu.VMEM((HALO, width), wide),
@@ -591,9 +617,13 @@
             jax.ShapeDtypeStruct((length, values), narrow),
             jax.ShapeDtypeStruct((length, values), narrow),
             jax.ShapeDtypeStruct((length, heads * DK), narrow),
+            jax.ShapeDtypeStruct((length, width), narrow),
+            jax.ShapeDtypeStruct((length, width), narrow),
+            jax.ShapeDtypeStruct((chunks, heads, CHUNK, CHUNK), narrow),
+            jax.ShapeDtypeStruct((chunks, heads, CHUNK, CHUNK), narrow),
         ],
         compiler_params=params(),
-        cost_estimate=effort(length, heads),
+        cost_estimate=effort(length, heads, 100000),
         interpret=interpret,
     )(place, proj, proj, taps, coefficients)
 
@@ -625,22 +655,31 @@
     )
 
 
-def enter(pieces, weight, gain, interpret):
+def columns_at(rows, columns, start):
+    return pl.BlockSpec((rows, columns), lambda i: (0, start // columns))
+
+
+def enter(pieces, weights, width, rates_at, gain, interpret):
     steps = len(pieces)
     rows, model = pieces[0].shape
-    width = weight.shape[1]
+    total = width + LANES
     return row_call(
         lambda *refs: entry_kernel(steps, *refs),
         steps,
-        [fixed(item.shape) for item in (*pieces, weight, gain)],
-        [rows_of(rows, model), rows_of(rows, width)],
-        [shape_of(steps * rows, model), shape_of(steps * rows, width)],
-        2 * steps * rows * model * width,
+        [fixed(item.shape) for item in pieces]
+        + [
+            columns_at(model, width, 0),
+            columns_at(model, LANES, rates_at),
+            fixed(gain.shape),
+        ],
+        [rows_of(rows, model), rows_of(rows, total)],
+        [shape_of(steps * rows, model), shape_of(steps * rows, total)],
+        steps * rows * total,
         interpret,
-    )(*pieces, weight, gain)
-
-
-def gate_rows(heads, steps, mixed, normed, weight, gain, w_out, interpret):
+    )(*pieces, weights, weights, gain)
+
+
+def gate_rows(heads, steps, mixed, normed, weights, start, gain, w_out, interpret):
     length, values = mixed.shape
     model = normed.shape[1]
     rows = length // steps
@@ -650,16 +689,16 @@
         [
             rows_of(rows, values),
             rows_of(rows, model),
-            fixed(weight.shape),
+            columns_at(model, values, start),
             fixed(gain.shape),
             fixed(w_out.shape),
         ],
         [rows_of(rows, values), rows_of(rows, values)] + [fixed((rows, model))] * steps,
         [shape_of(length, values), shape_of(length, values, wide)]
         + [shape_of(rows, model)] * steps,
-        4 * length * model * values,
+        length * values,
         interpret,
-    )(mixed, normed, weight, gain, w_out)
+    )(mixed, normed, weights, gain, w_out)
 
 
 def ffn_rows(normed_pieces, cot_pieces, both, down, interpret):
@@ -670,7 +709,8 @@
     return row_call(
         lambda *refs: ffn_kernel(steps, *refs),
         steps,
-        [fixed(item.shape) for item in (*normed_pieces, *cot_pieces, both, down)],
+        [fixed(item.shape) for item in (*normed_pieces, *cot_pieces)]
+        + [columns_at(model, 2 * units, 0), fixed(down.shape)],
         [
             rows_of(rows, model),
             rows_of(rows, model),
@@ -690,19 +730,29 @@
     )(*normed_pieces, *cot_pieces, both, down)
 
 
-def branch_rows(pieces, weight, interpret):
+def branch_rows(pieces, gated, weight, interpret):
     steps = len(pieces)
     rows, model = pieces[0].shape
     values = weight.shape[0]
-    return row_call(
+    split = (steps, values, model // steps)
+    return pl.pallas_call(
         lambda *refs: branch_kernel(steps, *refs),
-        steps,
-        [fixed(item.shape) for item in (*pieces, weight)],
-        [rows_of(rows, model), rows_of(rows, values)],
-        [shape_of(steps * rows, model), shape_of(steps * rows, values, wide)],
-        2 * steps * rows * model * values,
-        interpret,
-    )(*pieces, weight)
+        grid=(steps,),
+        in_specs=[fixed(item.shape) for item in pieces]
+        + [rows_of(rows, values), fixed(weight.shape)],
+        out_specs=[rows_of(rows, values), fixed(split)],
+        out_shape=[
+            shape_of(steps * rows, values, wide),
+            jax.ShapeDtypeStruct(split, narrow),
+        ],
+        scratch_shapes=[pltpu.VMEM((values, model), wide)],
+        compiler_params=params(),
+        cost_estimate=pl.CostEstimate(
+            flops=4 * steps * rows * model * values, bytes_accessed=rows * model,
+            transcendentals=0,
+        ),
+        interpret=interpret,
+    )(*pieces, gated, weight)
 
 
 def mixer_backward(
@@ -753,6 +803,10 @@
                 tall(values),
                 tall(values),
                 tall(heads * DK),
+                tall(width),
+                tall(width),
+                stacked(CHUNK, CHUNK),
+                stacked(CHUNK, CHUNK),
                 tall(values),
             ],
             out_specs=[
@@ -848,41 +902,14 @@
         total = own_piece.astype(wide) + sibling.astype(wide) + across.astype(wide)
         return (total, beside)
 
-    def gather_dp(array):
-        shard = lax.axis_index("dp")
-        stack = array[None]
-        bits = shards.bit_length() - 1
-        done = bits // 2
-        for low, high in ((done, bits), (0, done)):
-            size = 1 << (high - low)
-            pieces = [stack] + [
-                lax.ppermute(stack, "dp", [(i, i ^ (at << low)) for i in range(shards)])
-                for at in range(1, size)
-            ]
-            for bit in range(high - low):
-                upper = jnp.bitwise_and(shard, 1 << (low + bit)) != 0
-                pieces = [
-                    jnp.where(upper, pieces[at ^ (1 << bit)], pieces[at])
-                    for at in range(size)
-                ]
-            stack = jnp.stack(pieces, axis=1).reshape((-1,) + array.shape)
-        return stack
-
-    def scatter_direct(pieces):
-        total = pieces[0].astype(wide)
-        for bit in range(1, parts):
-            total = total + flip(lower(pieces[bit]), bit).astype(wide)
-        return total
-
-    def sum_all(array):
-        for bit in range(1, parts):
-            if bit & (bit - 1) == 0:
-                array = array + flip(array, bit)
-        bit = 1
-        while bit < shards:
-            array = array + lax.ppermute(array, "dp", [(i, i ^ bit) for i in range(shards)])
-            bit *= 2
-        return array
+    def sum_bits(array, low, high):
+        return sum(
+            [
+                lax.ppermute(array, "dp", [(i, i ^ (at << low)) for i in range(shards)])
+                for at in range(1, 1 << (high - low))
+            ],
+            array,
+        )
 
     def absolute(stack):
         return jnp.concatenate(
@@ -921,10 +948,15 @@
     small_count = small_flat.shape[0]
     half_lanes = LANES // 2
     small_flat = jnp.pad(small_flat, (0, own * half_lanes - small_count))
-    w_in = over_dp(
+    out_ratio = out_rows // own
+    w_all = over_dp(
         jnp.concatenate(
             [
                 mine(w_qkv, width, 1),
+                mine(w_outgate, values, 1),
+                jnp.swapaxes(
+                    mine(w_out, quarter, 1).reshape(out_ratio, own, quarter), 0, 1
+                ).reshape(own, -1),
                 jnp.pad(mine(w_ba, 2 * heads, 1), ((0, 0), (0, half_lanes - 2 * heads))),
                 small_flat.reshape(own, half_lanes),
             ],
@@ -932,44 +964,20 @@
         )
     )
     token_pieces = gather_seq(own_tokens)
-    out_ratio = out_rows // own
-    second_all = gather_dp(
-        jnp.concatenate(
-            [
-                mine(w_outgate, values, 1),
-                jnp.swapaxes(
-                    mine(w_out, quarter, 1).reshape(out_ratio, own, quarter), 0, 1
-                ).reshape(own, -1),
-            ],
-            axis=1,
-        )
-    )
-    w_gate_in = second_all[:, :, :values].reshape(model, values)
-    out_part = jnp.swapaxes(
-        second_all[:, :, values:].reshape(shards, own, out_ratio, quarter), 1, 2
-    )
-    small_all = w_in[:, width + half_lanes :].reshape(shards, -1)[:, :small_count]
+    rates_at = w_all.shape[1] - LANES
+    small_all = w_all[:, -half_lanes:].reshape(shards, -1)[:, :small_count]
     first_gain = small_all[:, :own].reshape(-1).astype(wide)
     second_gain = small_all[:, own : 2 * own].reshape(-1).astype(wide)
     taps_all = jnp.swapaxes(small_all[:, 2 * own :].reshape(shards, CONV, -1), 0, 1)
     taps = mine(taps_all.reshape(CONV, -1), width, 1).astype(wide)
     taps = jnp.pad(taps, ((0, HALO - CONV), (0, 0)))
-
+    both_part = jnp.concatenate([ffn_columns(w_gate), ffn_columns(w_up)], axis=1)
     down_part = jnp.pad(mine(w_down, piece, 0), ((0, padded - piece), (0, 0)))
     ffn_part = jnp.concatenate(
-        [
-            ffn_columns(w_gate),
-            ffn_columns(w_up),
-            from_lanes(to_lanes(down_part[None]), own)[0],
-        ],
-        axis=1,
-    )
-    ffn_part, w_in = tie((ffn_part, w_in))
+        [both_part, from_lanes(to_lanes(down_part[None]), own)[0]], axis=1
+    )
+    ffn_part, w_all = tie((ffn_part, w_all))
     ffn_all = over_dp(ffn_part)
-    both_own = ffn_all[:, : 2 * ffn_own]
-    down_own = from_lanes(
-        to_lanes(ffn_all[:, 2 * ffn_own :].reshape(shards, own, -1)), padded
-    ).reshape(ffn_own, model)
 
     decay_part = mine(a_log, heads, 0)
     bias_part = mine(dt_bias, heads, 0)
@@ -986,31 +994,36 @@
     place_row = place.astype(jnp.int32)[None]
 
     first_rows = jnp.broadcast_to(first_gain[None, :], (HALO, model))
-    w_in, first_rows, *token_pieces = tie((w_in, first_rows, *token_pieces))
-    normed_one, proj = enter(token_pieces, w_in, first_rows, interpret)
+    normed_one, proj = enter(token_pieces, w_all, width, rates_at, first_rows, interpret)
+    proj, out_part = tie((proj, w_all[:, width + values : rates_at]))
     mixed, *kept = mixer_forward(
         heads, parts, place_row, proj, taps, coefficients, interpret
     )
     mixed, *cot_pieces = tie((mixed, *gather_seq(own_cot)))
+    out_part = jnp.swapaxes(out_part.reshape(shards, own, out_ratio, quarter), 1, 2)
     w_out_own = jnp.swapaxes(
         exchange(out_part.reshape(parts, values, quarter)), 0, 1
     ).reshape(values, model)
     gated, out_gate, *mixed_pieces = gate_rows(
-        heads, parts, mixed, normed_one, w_gate_in, gain, w_out_own, interpret
+        heads, parts, mixed, normed_one, w_all, width, gain, w_out_own, interpret
     )
     rows = own_tokens.astype(wide)
     inverse_one = row_norm(rows, first_gain)[1]
     after_mix = rows + scatter_seq(mixed_pieces)[0]
     normed_two, inverse_two = row_norm(after_mix, second_gain)
-    normed_two, both_own, down_own = tie((lower(normed_two), both_own, down_own))
+    normed_two, ffn_all = tie((lower(normed_two), ffn_all))
+    down_own = from_lanes(
+        to_lanes(ffn_all[:, 2 * ffn_own :].reshape(shards, own, -1)), padded
+    ).reshape(ffn_own, model)
     across = flip(normed_two, 2)
     beside = flip(normed_two, 1)
     half = parts // 2
     normed_near, cot_near, hidden_near, grad_near, *back_near = ffn_rows(
-        [normed_two, beside], cot_pieces[:half], both_own, down_own, interpret
-    )
+        [normed_two, beside], cot_pieces[:half], ffn_all, down_own, interpret
+    )
+    across, *back_near = tie((across, *back_near))
     normed_far, cot_far, hidden_far, grad_far, *back_far = ffn_rows(
-        [across, flip(across, 1)], cot_pieces[half:], both_own, down_own, interpret
+        [across, flip(across, 1)], cot_pieces[half:], ffn_all, down_own, interpret
     )
     grad_both = over_rows(normed_near, grad_near) + over_rows(normed_far, grad_far)
     grad_down = over_rows(hidden_near, cot_near) + over_rows(hidden_far, cot_far)
@@ -1020,19 +1033,21 @@
     grad_ffn = jnp.concatenate([lower(grad_both), grad_down], axis=1)
     grad_normed_two, grad_ffn = scatter_seq(back_near + back_far, grad_ffn)
     grad_ffn = sum_dp(grad_ffn)
-    back_two, grad_norm_ffn = norm_back(after_mix, inverse_two, second_gain, grad_normed_two)
+    back_two, unused = norm_back(after_mix, inverse_two, second_gain, grad_normed_two)
     grad_after = own_cot.astype(wide) + back_two
-    branch_pieces = gather_seq(lower(grad_after))
+    grad_low = lower(grad_after)
+    across = flip(grad_low, 2)
+    beside = flip(grad_low, 1)
     down_near = lower(by_weight(hidden_near, down_own))
     down_far = lower(by_weight(hidden_far, down_own))
-    down_near, down_far, *branch_pieces = tie((down_near, down_far, *branch_pieces))
-    grad_branch, grad_gated = branch_rows(branch_pieces, w_out_own, interpret)
-    grad_out = jnp.swapaxes(
-        lower(over_rows(gated, grad_branch)).reshape(values, parts, quarter), 0, 1
-    )
-    grad_out = jnp.swapaxes(
-        exchange(grad_out).reshape(shards, out_ratio, own, quarter), 1, 2
-    ).reshape(model, -1)
+    across, down_near, down_far = tie((across, down_near, down_far))
+    grad_gated, grad_out = branch_rows(
+        [grad_low, beside, across, flip(across, 1)], gated, w_out_own, interpret
+    )
+    grad_out = exchange(grad_out)
+    grad_out = jnp.swapaxes(grad_out.reshape(shards, out_ratio, own, quarter), 1, 2).reshape(
+        model, -1
+    )
     count = own_tokens.shape[0]
     result = after_mix + scatter_seq(
         [down_near[:count], down_near[count:], down_far[:count], down_far[count:]]
@@ -1044,19 +1059,18 @@
     grad_w_in = jnp.concatenate([lower(over_rows(normed_one, grad_in)), grad_out], axis=1)
     grad_in, grad_w_in = tie((grad_in, grad_w_in))
     grad_w_in = sum_dp(grad_w_in)
-    grad_first = grad_in[:, : width + LANES]
-    grad_gate = grad_in[:, width + LANES :]
+    split = width + values
     one_far, one_near = (
-        by_transpose(grad_first[span], w_in) + by_transpose(grad_gate[span], w_gate_in)
+        by_transpose(grad_in[span, :split], w_all[:, :split])
+        + by_transpose(grad_in[span, split:], w_all[:, rates_at:])
         for span in (slice(2 * count, None), slice(0, 2 * count))
     )
-    back_one, grad_norm_attn = norm_back(
-        rows,
-        inverse_one,
-        first_gain,
-        scatter_direct([one_near[:count], one_near[count:], one_far[:count], one_far[count:]]),
-    )
-    grad_rows = lower(grad_after + back_one)[:, None, :]
+    first_pieces = [
+        one_near[:count],
+        flip(lower(one_near[count:]), 1),
+        flip(lower(one_far[:count]), 2),
+        flip(lower(one_far[count:]), 3),
+    ]
 
     taps_full = lax.dynamic_update_slice_in_dim(
         jnp.zeros((CONV, head_count * ROW), wide), grad_taps[:CONV], place * width, 1
@@ -1067,14 +1081,23 @@
             jnp.zeros((head_count,), wide), lane_row[1 : 2 * heads : 2], place * heads, 0
         )
 
-    common = jnp.concatenate([grad_gain[0], to_heads(grad_small[1]), to_heads(grad_small[0])])
     packed = jnp.concatenate(
-        [grad_norm_attn, grad_norm_ffn, taps_full.reshape(-1), common]
-    )
-    packed_count = packed.shape[0]
-    packed = jnp.pad(packed, (0, -packed_count % (HALO * LANES)))
-    def pieces_of(array):
-        near = gather_seq(array)
+        [
+            taps_full.reshape(-1, LANES),
+            grad_gain[0].reshape(-1, LANES),
+            jnp.pad(
+                jnp.stack([to_heads(grad_small[1]), to_heads(grad_small[0])]),
+                ((0, 0), (0, LANES - head_count)),
+            ),
+        ],
+        axis=0,
+    )
+    packed = jnp.pad(packed, ((0, -packed.shape[0] % HALO), (0, 0)))
+    packed = sum([flip(packed, at) for at in range(1, parts)], packed)
+    bits = shards.bit_length() - 1
+    packed = sum_bits(packed, bits // 2, bits)
+
+    def in_order(near):
         low_bit = jnp.bitwise_and(place, 1) != 0
         high_bit = jnp.bitwise_and(place, 2) != 0
         return [
@@ -1095,7 +1118,19 @@
         )
         return split.reshape(own, -1).astype(wide)
 
-    ffn_pieces = pieces_of(grad_ffn)
+    grad_w_in, packed, ffn_pieces, first_pieces = tie(
+        (grad_w_in, packed, gather_seq(grad_ffn), first_pieces)
+    )
+    in_pieces = in_order(gather_seq(grad_w_in))
+    packed = sum_bits(packed, 0, bits // 2)
+    back_one, unused = norm_back(
+        rows,
+        inverse_one,
+        first_gain,
+        sum([item.astype(wide) for item in first_pieces[1:]], first_pieces[0]),
+    )
+    grad_rows = lower(grad_after + back_one)[:, None, :]
+    ffn_pieces = in_order(ffn_pieces)
     grad_w_gate = ffn_full([item[:, :ffn_own] for item in ffn_pieces])
     grad_w_up = ffn_full([item[:, ffn_own : 2 * ffn_own] for item in ffn_pieces])
     grad_w_down = jnp.concatenate(
@@ -1105,50 +1140,47 @@
         ],
         axis=0,
     ).astype(wide)
-    early = (
+    def along(weights, grads):
+        return sum(
+            jnp.sum(weight.astype(wide) * grad, axis=1)
+            for weight, grad in zip(weights, grads)
+        )
+
+    grad_norm_ffn = along((w_gate, w_up), (grad_w_gate, grad_w_up)) / norm_ffn.astype(wide)
+    taps_rows = CONV * head_count * ROW // LANES
+    gain_rows = taps_rows + DV // LANES
+    own_taps = conv_w.shape[1]
+    taps_total = lax.dynamic_slice_in_dim(
+        packed[:taps_rows].reshape(CONV, -1), lax.axis_index("dp") * own_taps, own_taps, 1
+    )
+    total = split + LANES
+    grad_w_qkv = side_by_side([item[:, :width] for item in in_pieces])
+    grad_w_ba = side_by_side([item[:, split : split + 2 * heads] for item in in_pieces])
+    grad_w_outgate = side_by_side([item[:, width:split] for item in in_pieces])
+    grad_w_out = side_by_side(
+        [
+            jnp.swapaxes(item[:, total:].reshape(own, out_ratio, quarter), 0, 1).reshape(
+                out_rows, quarter
+            )
+            for item in in_pieces
+        ]
+    )
+    grad_norm_attn = along(
+        (w_qkv, w_ba, w_outgate), (grad_w_qkv, grad_w_ba, grad_w_outgate)
+    ) / norm_attn.astype(wide)
+    return (
         lower(result)[:, None, :],
         grad_rows,
-        grad_w_gate,
-        grad_w_up,
-        grad_w_down,
-        packed,
-    )
-    grad_w_in, early = tie((grad_w_in, early))
-    block_out, grad_rows, grad_w_gate, grad_w_up, grad_w_down, packed = early
-    packed = sum_all(packed.reshape(-1, LANES)).reshape(-1)
-    taps_at = 2 * model
-    gain_at = taps_at + CONV * head_count * ROW
-    heads_at = gain_at + DV
-    shard = lax.axis_index("dp")
-    norm_attn_total = lax.dynamic_slice_in_dim(packed[:model], shard * own, own, 0)
-    norm_ffn_total = lax.dynamic_slice_in_dim(packed[model:taps_at], shard * own, own, 0)
-    own_taps = conv_w.shape[1]
-    taps_total = lax.dynamic_slice_in_dim(
-        packed[taps_at:gain_at].reshape(CONV, -1), shard * own_taps, own_taps, 1
-    )
-
-    in_pieces = pieces_of(grad_w_in)
-    total = width + LANES + values
-    return (
-        block_out,
-        grad_rows,
-        norm_attn_total,
-        side_by_side([item[:, :width] for item in in_pieces]),
-        side_by_side([item[:, width : width + 2 * heads] for item in in_pieces]),
+        grad_norm_attn,
+        grad_w_qkv,
+        grad_w_ba,
         taps_total,
-        packed[heads_at : heads_at + head_count],
-        packed[heads_at + head_count : heads_at + 2 * head_count],
-        side_by_side([item[:, width + LANES : total] for item in in_pieces]),
-        packed[gain_at:heads_at],
-        side_by_side(
-            [
-                jnp.swapaxes(item[:, total:].reshape(own, out_ratio, quarter), 0, 1).reshape(
-                    out_rows, quarter
-                )
-                for item in in_pieces
-            ]
-        ),
-        norm_ffn_total,
+        packed[gain_rows, :head_count],
+        packed[gain_rows + 1, :head_count],
+        grad_w_outgate,
+        packed[taps_rows:gain_rows].reshape(-1),
+        grad_w_out,
+        grad_norm_ffn,
         grad_w_gate,
         grad_w_up,
         grad_w_down,

time: 607 us -> 629 us (1.036)
  local copies, waits for them, and re-layouts: 75.2 us -> 104 us
  waiting for transfers between devices: 226 us -> 246 us
  starting transfers between devices: 42.1 us -> 27.5 us
    all_gather x2, waiting for transfers between devices: 5.05 us -> 76.7 us  [over_dp(): return lax.all_gather(array, 'dp', axis=0, tiled=True)]
    ppermute x7 -> x4, waiting for transfers between devices: 51.4 us -> 0.01 us  [sum_bits(): lax.ppermute(array, 'dp', [(i, i ^ at << low) for i in range(shards)])]
    ppermute x7 -> x4, starting transfers between devices: 18.2 us -> 6.02 us  [sum_bits(): lax.ppermute(array, 'dp', [(i, i ^ at << low) for i in range(shards)])]
    slice x8, local copies, waits for them, and re-layouts: 0.81 us -> 12.5 us  [per_device(): item[None, :, 2 * ffn_own:]]
    pallas_call x1, Pallas kernels: 53.7 us -> 44.6 us  [mixer_backward(): pl.pallas_call(lambda *refs: backward_kernel(heads, *refs), grid_spec=plt...]
    dot_general x6 -> x5, matrix products: 33 us -> 25 us  [over_rows(): lax.dot_general(left, right, (((0,), (0,)), ((), ())), preferred_element_...]
    another operation x8, local copies, waits for them, and re-layouts: 0.12 us -> 8.08 us  [ffn_full(): jnp.stack([item.reshape(own, shards, padded)[..., :piece] for item in pie...]
    slice x4, local copies, waits for them, and re-layouts: 0.64 us -> 6.96 us  [per_device(): grad_w_up = ffn_full([item[:, ffn_own:2 * ffn_own] for item in ffn_pieces])]
  transfers between devices with their start and end apart: 49 -> 47, of which waited for: 19 -> 17; matrix products, arithmetic and copies ran while one was open for 23% -> 27% of each run, Pallas kernels for 21% -> 20%
where the time goes in v5:
time: 629 us; the launch traced here: 621 us
  waiting for transfers between devices  246 us (39%)
  Pallas kernels  137 us (22%)
  local copies, waits for them, and re-layouts  104 us (17%)
  other arithmetic  47 us (7%)
  matrix products  44.4 us (7%)
  starting transfers between devices  27.5 us (4%)
  between operations  15.5 us (2%)
    ppermute x39, waiting for transfers between devices, flip(): return lax.ppermute(array, 'seq', [(i, i ^ bit) for i in range(parts)])  165 us
    all_gather x2, waiting for transfers between devices, over_dp(): return lax.all_gather(array, 'dp', axis=0, tiled=True)  76.7 us
    pallas_call x1, Pallas kernels, mixer_backward(): pl.pallas_call(lambda *refs: backward_kernel(heads, *refs), grid_spec=plt...  44.6 us
    pallas_call x2, Pallas kernels, ffn_rows(): row_call(lambda *refs: ffn_kernel(steps, *refs), steps, [fixed(item.shape...  30.7 us
    pallas_call x1, Pallas kernels, mixer_forward(): pl.pallas_call(lambda *refs: forward_kernel(heads, *refs), grid_spec=pltp...  30.4 us
    unnamed x140, local copies, waits for them, and re-layouts  26.2 us
    dot_general x5, matrix products, over_rows(): lax.dot_general(left, right, (((0,), (0,)), ((), ())), preferred_element_...  25 us
    ppermute x39, starting transfers between devices, flip(): return lax.ppermute(array, 'seq', [(i, i ^ bit) for i in range(parts)])  21.1 us
  transfers between devices with their start and end apart: 47, of which 17 were waited for; matrix products, arithmetic and copies ran while one was open for 27% of the time, Pallas kernels for 20%

profile of v5, /device:TPU:0, one launch (start us, length us, event | category | flops | bytes accessed | tf_op | source)
XLA Modules:
  0.0 621.1 jit_solution(3376804166960342287)
XLA Ops:
  16.4 76.7 %all-gather.3.cloned.1.call-done.refs_4_.refs_5_.refs_2_ = bf16[1024,2176]{1,0:T(8,128)(2,1)} async-done(((bf16[128,2176]{1,0:T(8,128)(2,1)}), bf16[1024,2176]{1,0:T(8,128)(2,1)}) %all-gather.3.cloned.1.call-update) | async-done | bytes 4456464 | tf_op jit(solution)/shard_map/all_gather | solution.py:886
  95.3 24.1 %collective-permute-done.1.refs_2_ = bf16[512,1024]{1,0:T(8,128)(2,1)S(1)} collective-permute-done((bf16[512,1024]{1,0:T(8,128)(2,1)S(1)}, bf16[512,1024]{1,0:T(8,128)(2,1)S(1)}, u32[]{:S(2)}, u32[]{:S(2)}) %collective-permute-start.1) | collective-permute-done | bytes 1048608 | tf_op jit(solution)/shard_map/ppermute | solution.py:883
  119.8 19.6 %collective-permute-done.4.refs_2_ = bf16[512,1024]{1,0:T(8,128)(2,1)} collective-permute-done((bf16[512,1024]{1,0:T(8,128)(2,1)}, bf16[512,1024]{1,0:T(8,128)(2,1)}, u32[]{:S(2)}, u32[]{:S(2)}) %collective-permute-start.4) | collective-permute-done | bytes 1048608 | tf_op jit(solution)/shard_map/ppermute | solution.py:883
  142.5 11.1 %shard_map.262 = (bf16[2048,1024]{1,0:T(8,128)(2,1)}, bf16[2048,1152]{1,0:T(8,128)(2,1)}) custom-call(bf16[512,1024]{1,0:T(8,128)(2,1)S(1)} %bitcast.215, bf16[512,1024]{1,0:T(8,128)(2,1)} %copy-done.22, bf16[512,1024]{1,0:T(8,128)(2,1)} %copy-done.21, bf16[512,1024]{1,0:T(8,128)(2,1)} %collective-permute-done.2.refs_3_, ...), custom_call_target="tpu_custom_call" | custom-call | flops 2359296 | bytes 2304 | tf_op jit(solution)/shard_map/pallas_call | solution.py:666
  156.2 30.4 %shard_map.263 = (bf16[2048,512]{1,0:T(8,128)(2,1)}, bf16[8,2,256,256]{3,2,1,0:T(8,128)(2,1)}, bf16[8,2,256,128]{3,2,1,0:T(8,128)(2,1)S(1)}, bf16[2048,512]{1,0:...) custom-call(s32[1]{0:T(128)} %bitcast.1.refs_0_, ...), custom_call_target="tpu_custom_call" | custom-call | flops 409600000 | bytes 4194304 | tf_op jit(solution)/shard_map/pallas_call | solution.py:585
  188.2 10.7 %shard_map.264 = (bf16[2048,512]{1,0:T(8,128)(2,1)}, f32[2048,512]{1,0:T(8,128)}, bf16[512,1024]{1,0:T(8,128)(2,1)S(1)}, bf16[512,1024]{1,0:T(8,128)(2,1)}, bf16...) custom-call(bf16[2048,512]{1,0:T(8,128)(2,1)} %get-tuple-element.86.refs_0_.refs_8_, ...), custom_call_target="tpu_custom_call" | custom-call | flops 1048576 | bytes 1024 | tf_op jit(solution)/shard_map/pallas_call | solution.py:686
  205.4 23.9 %collective-permute-done.11 = bf16[512,1024]{1,0:T(8,128)(2,1)S(1)} collective-permute-done((bf16[512,1024]{1,0:T(8,128)(2,1)S(1)}, bf16[512,1024]{1,0:T(8,128)(2,1)S(1)}, u32[]{:S(2)}, u32[]{:S(2)}) %collective-permute-start.11) | collective-permute-done | bytes 1048608 | tf_op jit(solution)/shard_map/ppermute | solution.py:883
  250.2 15.3 %shard_map.265 = (bf16[1024,1024]{1,0:T(8,128)(2,1)}, bf16[1024,1024]{1,0:T(8,128)(2,1)}, bf16[1024,768]{1,0:T(8,128)(2,1)}, bf16[1024,1536]{1,0:T(8,128)(2,1)},...) custom-call(bf16[512,1024]{1,0:T(8,128)(2,1)} %multiply_convert_fusion.refs_0_, bf16[512,1024]{1,0:T(8,128)(2,1)} %copy-done.45, ...), custom_call_target="tpu_custom_call" | custom-call | flops 8053063680 | bytes 7864320 | tf_op jit(solution)/shard_map/pallas_call | solution.py:709
  269.4 15.4 %shard_map.266 = (bf16[1024,1024]{1,0:T(8,128)(2,1)}, bf16[1024,1024]{1,0:T(8,128)(2,1)}, bf16[1024,768]{1,0:T(8,128)(2,1)}, bf16[1024,1536]{1,0:T(8,128)(2,1)},...) custom-call(bf16[512,1024]{1,0:T(8,128)(2,1)} %collective-permute-done.12.refs_0_, ...), custom_call_target="tpu_custom_call" | custom-call | flops 8053063680 | bytes 7864320 | tf_op jit(solution)/shard_map/pallas_call | solution.py:709
  285.1 4.1 fusion.39
  295.1 3.6 fusion.38
  300.9 4.0 add_convert_fusion
  307.4 18.3 %collective-permute-done.17 = bf16[512,1024]{1,0:T(8,128)(2,1)} collective-permute-done((bf16[512,1024]{1,0:T(8,128)(2,1)}, bf16[512,1024]{1,0:T(8,128)(2,1)}, u32[]{:S(2)}, u32[]{:S(2)}) %collective-permute-start.17) | collective-permute-done | bytes 1048608 | tf_op jit(solution)/shard_map/ppermute | solution.py:883
  331.5 4.1 fusion.28
  342.4 18.5 %collective-permute-done.18.refs_2_ = bf16[512,1024]{1,0:T(8,128)(2,1)S(1)} collective-permute-done((bf16[512,1024]{1,0:T(8,128)(2,1)S(1)}, bf16[512,1024]{1,0:T(8,128)(2,1)S(1)}, u32[]{:S(2)}, u32[]{:S(2)}) %collective-permute-start.18) | collective-permute-done | bytes 1048608 | tf_op jit(solution)/shard_map/ppermute | solution.py:883
  364.5 9.1 %shard_map.267 = (f32[2048,512]{1,0:T(8,128)}, bf16[4,512,256]{2,1,0:T(8,128)(2,1)S(1)}) custom-call(bf16[512,1024]{1,0:T(8,128)(2,1)} %copy-done.23, bf16[512,1024]{1,0:T(8,128)(2,1)} %copy-done.46, bf16[512,1024]{1,0:T(8,128)(2,1)} %copy-done.44, bf16[512,1024]{1,0:T(8,128)(2,1)} %copy-done.48, bf16[2048,512]{1,0:T(8,128)(2,1)} %get-tuple-element.129.refs_4_, ...), custom_call_target="tpu_custom_call" | custom-call | flops 4294967296 | bytes 524288 | tf_op jit(solution)/shard_map/pallas_call | solution.py:738
  375.6 44.6 %shard_map.268 = (bf16[2048,1664]{1,0:T(8,128)(2,1)}, f32[8,1024]{1,0:T(8,128)S(1)}, f32[8,256]{1,0:T(8,128)S(1)}, f32[8,128]{1,0:T(8,128)S(1)}) custom-call(s32[1]{0:T(128)} %bitcast.1.refs_0_, bf16[2048,1152]{1,0:T(8,128)(2,1)} %get-tuple-element.84.refs_1_.refs_2_.refs_3_, bf16[2048,1152]{1,0:T(8,128)(2,1)} %get-tuple-element.84.refs_1_.refs_2_.refs_3_, ...), custom_call_target="tpu_custom_call" | custom-call | flops 409600000 | bytes 4194304 | tf_op jit(solution)/shard_map/pallas_call | solution.py:787
  420.2 11.3 %convolution_convert_fusion = bf16[1024,1664]{1,0:T(8,128)(2,1)S(1)} fusion(bf16[2048,1024]{1,0:T(8,128)(2,1)S(1)} %copy-done.12, bf16[2048,1664]{1,0:T(8,128)(2,1)} %get-tuple-element.138), kind=kOutput, calls=%fused_computation.4 | convolution fusion | flops 6981025792 | bytes 14417920 | tf_op jit(solution)/shard_map/dot_general | solution.py:32
  450.0 6.3 %fusion.2 = f32[1024,1024]{1,0:T(8,128)S(1)} fusion(bf16[2048,1664]{1,0:T(8,128)(2,1)} %get-tuple-element.138, bf16[1024,2176]{1,0:T(8,128)(2,1)} %all-gather.3.cloned.1.call-done.refs_4_.refs_5_.refs_2_), kind=kOutput, calls=%fused_computation.11 | convolution fusion | flops 3221225472 | bytes 10485760 | tf_op jit(solution)/shard_map/dot_general | solution.py:26
  471.1 12.3 %collective-permute-done.34 = bf16[128,2304]{1,0:T(8,128)(2,1)} collective-permute-done((bf16[128,2304]{1,0:T(8,128)(2,1)}, bf16[128,2304]{1,0:T(8,128)(2,1)}, u32[]{:S(2)}, u32[]{:S(2)}) %collective-permute-start.34) | collective-permute-done | bytes 589856 | tf_op jit(solution)/shard_map/ppermute | solution.py:883
  490.3 15.6 %collective-permute-done.37 = bf16[512,1024]{1,0:T(8,128)(2,1)} collective-permute-done((bf16[512,1024]{1,0:T(8,128)(2,1)}, bf16[512,1024]{1,0:T(8,128)(2,1)}, u32[]{:S(2)}, u32[]{:S(2)}) %collective-permute-start.37) | collective-permute-done | bytes 1048608 | tf_op jit(solution)/shard_map/ppermute | solution.py:883
  505.9 21.8 %collective-permute-done.38 = bf16[512,1024]{1,0:T(8,128)(2,1)} collective-permute-done((bf16[512,1024]{1,0:T(8,128)(2,1)}, bf16[512,1024]{1,0:T(8,128)(2,1)}, u32[]{:S(2)}, u32[]{:S(2)}) %collective-permute-start.38) | collective-permute-done | bytes 1048608 | tf_op jit(solution)/shard_map/ppermute | solution.py:883
  527.7 4.4 reduce-scatter.3.cloned.1.call-done
  590.6 4.0 fusion.16
  (408 shorter events, 196.4 us)
Async XLA Ops:
  7.2 85.9 %all-gather.3.cloned.1.call-start = ((), (), s32[]{:S(2)}) async-start(), calls=%async_computation.2 | async-start | bytes 5013504 | tf_op jit(solution)/shard_map/all_gather | solution.py:886
  13.6 218.9 %all-gather.5.cloned.1.call-start = ((), (), s32[]{:S(2)}) async-start(), calls=%async_computation.3 | async-start | bytes 5308416 | tf_op jit(solution)/shard_map/all_gather | solution.py:886
  93.1 370.1 %reduce-scatter.5.cloned.1.call-start = ((), (), s32[]{:S(2)}) async-start(), calls=%async_computation.5 | async-start | bytes 5308416 | tf_op jit(solution)/shard_map/reduce_scatter | solution.py:889
  93.2 26.2 %collective-permute-start.1 = (bf16[512,1024]{1,0:T(8,128)(2,1)S(1)}, bf16[512,1024]{1,0:T(8,128)(2,1)S(1)}, u32[]{:S(2)}, u32[]{:S(2)}) collective-permute-start(bf16[512,1024]{1,0:T(8,128)(2,1)S(1)} %bitcast.213), channel_id=1, source_target_pairs={{0,16},{8,24},{16,0},{24,8},{1,17},{9,25},{17,1},{25,9},{2,18},{10... | collective-permute-start | bytes 3145736 | tf_op jit(solution)/shard_map/ppermute | solution.py:883
  94.7 44.7 %collective-permute-start.4 = (bf16[512,1024]{1,0:T(8,128)(2,1)}, bf16[512,1024]{1,0:T(8,128)(2,1)}, u32[]{:S(2)}, u32[]{:S(2)}) collective-permute-start(bf16[512,1024]{1,0:T(8,128)(2,1)} %bitcast.21.refs_2_), channel_id=1, source_target_pairs={{0,16},{8,24},{16,0},{24,8},{1,17},{9,25},{17,1},{25,9},{2,18},{10... | collective-permute-start | bytes 3145736 | tf_op jit(solution)/shard_map/ppermute | solution.py:883
  95.2 46.2 %collective-permute-start = (bf16[512,1024]{1,0:T(8,128)(2,1)S(1)}, bf16[512,1024]{1,0:T(8,128)(2,1)S(1)}, u32[]{:S(2)}, u32[]{:S(2)}) collective-permute-start(bf16[512,1024]{1,0:T(8,128)(2,1)S(1)} %bitcast.214), channel_id=1, source_target_pairs={{0,8},{8,0},{16,24},{24,16},{1,9},{9,1},{17,25},{25,17},{2,10},{10... | collective-permute-start | bytes 3145736 | tf_op jit(solution)/shard_map/ppermute | solution.py:883
  119.3 67.3 %collective-permute-start.3 = (bf16[512,1024]{1,0:T(8,128)(2,1)}, bf16[512,1024]{1,0:T(8,128)(2,1)}, u32[]{:S(2)}, u32[]{:S(2)}) collective-permute-start(bf16[512,1024]{1,0:T(8,128)(2,1)} %bitcast.21.refs_2_), channel_id=1, source_target_pairs={{0,8},{8,0},{16,24},{24,16},{1,9},{9,1},{17,25},{25,17},{2,10},{10... | collective-permute-start | bytes 3145736 | tf_op jit(solution)/shard_map/ppermute | solution.py:883
  139.4 47.2 %collective-permute-start.5 = (bf16[512,1024]{1,0:T(8,128)(2,1)}, bf16[512,1024]{1,0:T(8,128)(2,1)}, u32[]{:S(2)}, u32[]{:S(2)}) collective-permute-start(bf16[512,1024]{1,0:T(8,128)(2,1)} %collective-permute-done.4.refs_2_), channel_id=1, source_target_pairs={{0,8},{8,0},{16,24},{24,16},{1,9},{9,1},{17,25},{25,17},{2,10},{10... | collective-permute-start | bytes 3145736 | tf_op jit(solution)/shard_map/ppermute | solution.py:883
  154.2 32.5 %collective-permute-start.6 = (bf16[1,512,256]{2,1,0:T(8,128)(2,1)S(1)}, bf16[1,512,256]{2,1,0:T(8,128)(2,1)S(1)}, u32[]{:S(2)}, u32[]{:S(2)}) collective-permute-start(bf16[1,512,256]{2,1,0:T(8,128)(2,1)S(1)} %get-tuple-element.246), channel_id=1, source_target_pairs={{0,8},{8,0},{16,24},{24,16},{1,9},{9,1},{17,25},{25,17},{2,10},{10... | collective-permute-start | bytes 786440 | tf_op jit(solution)/shard_map/ppermute | solution.py:883
  154.7 32.0 %collective-permute-start.7 = (bf16[1,512,256]{2,1,0:T(8,128)(2,1)S(1)}, bf16[1,512,256]{2,1,0:T(8,128)(2,1)S(1)}, u32[]{:S(2)}, u32[]{:S(2)}) collective-permute-start(bf16[1,512,256]{2,1,0:T(8,128)(2,1)S(1)} %get-tuple-element.245), channel_id=1, source_target_pairs={{0,16},{8,24},{16,0},{24,8},{1,17},{9,25},{17,1},{25,9},{2,18},{10... | collective-permute-start | bytes 786440 | tf_op jit(solution)/shard_map/ppermute | solution.py:883
  156.2 30.5 %collective-permute-start.8 = (bf16[1,512,256]{2,1,0:T(8,128)(2,1)S(1)}, bf16[1,512,256]{2,1,0:T(8,128)(2,1)S(1)}, u32[]{:S(2)}, u32[]{:S(2)}) collective-permute-start(bf16[1,512,256]{2,1,0:T(8,128)(2,1)S(1)} %get-tuple-element.244), channel_id=1, source_target_pairs={{0,24},{8,16},{16,8},{24,0},{1,25},{9,17},{17,9},{25,1},{2,26},{10... | collective-permute-start | bytes 786440 | tf_op jit(solution)/shard_map/ppermute | solution.py:883
  232.5 33.0 %collective-permute-start.12 = (bf16[512,1024]{1,0:T(8,128)(2,1)}, bf16[512,1024]{1,0:T(8,128)(2,1)}, u32[]{:S(2)}, u32[]{:S(2)}) collective-permute-start(bf16[512,1024]{1,0:T(8,128)(2,1)} %multiply_convert_fusion.refs_0_), channel_id=1, source_target_pairs={{0,16},{8,24},{16,0},{24,8},{1,17},{9,25},{17,1},{25,9},{2,18},{10... | collective-permute-start | bytes 3145736 | tf_op jit(solution)/shard_map/ppermute | solution.py:883
  325.8 206.3 %reduce-scatter.3.cloned.1.call-start = ((), (), s32[]{:S(2)}) async-start(), calls=%async_computation.4 | async-start | bytes 5013504 | tf_op jit(solution)/shard_map/reduce_scatter | solution.py:889
  373.7 57.9 %collective-permute-start.24 = (bf16[1,512,256]{2,1,0:T(8,128)(2,1)S(1)}, bf16[1,512,256]{2,1,0:T(8,128)(2,1)S(1)}, u32[]{:S(2)}, u32[]{:S(2)}) collective-permute-start(bf16[1,512,256]{2,1,0:T(8,128)(2,1)S(1)} %get-tuple-element.238), channel_id=1, source_target_pairs={{0,8},{8,0},{16,24},{24,16},{1,9},{9,1},{17,25},{25,17},{2,10},{10... | collective-permute-start | bytes 786440 | tf_op jit(solution)/shard_map/ppermute | solution.py:883
  373.8 57.7 %collective-permute-start.25 = (bf16[1,512,256]{2,1,0:T(8,128)(2,1)S(1)}, bf16[1,512,256]{2,1,0:T(8,128)(2,1)S(1)}, u32[]{:S(2)}, u32[]{:S(2)}) collective-permute-start(bf16[1,512,256]{2,1,0:T(8,128)(2,1)S(1)} %get-tuple-element.237), channel_id=1, source_target_pairs={{0,16},{8,24},{16,0},{24,8},{1,17},{9,25},{17,1},{25,9},{2,18},{10... | collective-permute-start | bytes 786440 | tf_op jit(solution)/shard_map/ppermute | solution.py:883
  374.4 57.2 %collective-permute-start.26 = (bf16[1,512,256]{2,1,0:T(8,128)(2,1)S(1)}, bf16[1,512,256]{2,1,0:T(8,128)(2,1)S(1)}, u32[]{:S(2)}, u32[]{:S(2)}) collective-permute-start(bf16[1,512,256]{2,1,0:T(8,128)(2,1)S(1)} %get-tuple-element.236), channel_id=1, source_target_pairs={{0,24},{8,16},{16,8},{24,0},{1,25},{9,17},{17,9},{25,1},{2,26},{10... | collective-permute-start | bytes 786440 | tf_op jit(solution)/shard_map/ppermute | solution.py:883
  444.5 26.5 %collective-permute-start.21 = (bf16[512,1024]{1,0:T(8,128)(2,1)}, bf16[512,1024]{1,0:T(8,128)(2,1)}, u32[]{:S(2)}, u32[]{:S(2)}) collective-permute-start(bf16[512,1024]{1,0:T(8,128)(2,1)} %add_convert_fusion.4), channel_id=1, source_target_pairs={{0,16},{8,24},{16,0},{24,8},{1,17},{9,25},{17,1},{25,9},{2,18},{10... | collective-permute-start | bytes 3145736 | tf_op jit(solution)/shard_map/ppermute | solution.py:883
  468.9 37.0 %collective-permute-start.37 = (bf16[512,1024]{1,0:T(8,128)(2,1)}, bf16[512,1024]{1,0:T(8,128)(2,1)}, u32[]{:S(2)}, u32[]{:S(2)}) collective-permute-start(bf16[512,1024]{1,0:T(8,128)(2,1)} %get-tuple-element.230), channel_id=1, source_target_pairs={{0,16},{8,24},{16,0},{24,8},{1,17},{9,25},{17,1},{25,9},{2,18},{10... | collective-permute-start | bytes 3145736 | tf_op jit(solution)/shard_map/ppermute | solution.py:883
  469.6 58.2 %collective-permute-start.38 = (bf16[512,1024]{1,0:T(8,128)(2,1)}, bf16[512,1024]{1,0:T(8,128)(2,1)}, u32[]{:S(2)}, u32[]{:S(2)}) collective-permute-start(bf16[512,1024]{1,0:T(8,128)(2,1)} %get-tuple-element.229), channel_id=1, source_target_pairs={{0,24},{8,16},{16,8},{24,0},{1,25},{9,17},{17,9},{25,1},{2,26},{10... | collective-permute-start | bytes 3145736 | tf_op jit(solution)/shard_map/ppermute | solution.py:883
  469.6 58.2 %collective-permute-start.36 = (bf16[512,1024]{1,0:T(8,128)(2,1)}, bf16[512,1024]{1,0:T(8,128)(2,1)}, u32[]{:S(2)}, u32[]{:S(2)}) collective-permute-start(bf16[512,1024]{1,0:T(8,128)(2,1)} %slice.396), channel_id=1, source_target_pairs={{0,8},{8,0},{16,24},{24,16},{1,9},{9,1},{17,25},{25,17},{2,10},{10... | collective-permute-start | bytes 3145736 | tf_op jit(solution)/shard_map/ppermute | solution.py:883
  471.1 56.7 %collective-permute-start.33 = (bf16[128,2304]{1,0:T(8,128)(2,1)}, bf16[128,2304]{1,0:T(8,128)(2,1)}, u32[]{:S(2)}, u32[]{:S(2)}) collective-permute-start(bf16[128,2304]{1,0:T(8,128)(2,1)} %reduce-scatter.5.cloned.1.call-done), channel_id=1, source_target_pairs={{0,8},{8,0},{16,24},{24,16},{1,9},{9,1},{17,25},{25,17},{2,10},{10... | collective-permute-start | bytes 1769480 | tf_op jit(solution)/shard_map/ppermute | solution.py:883
  483.5 44.3 %collective-permute-start.35 = (bf16[128,2304]{1,0:T(8,128)(2,1)}, bf16[128,2304]{1,0:T(8,128)(2,1)}, u32[]{:S(2)}, u32[]{:S(2)}) collective-permute-start(bf16[128,2304]{1,0:T(8,128)(2,1)} %collective-permute-done.34), channel_id=1, source_target_pairs={{0,8},{8,0},{16,24},{24,16},{1,9},{9,1},{17,25},{25,17},{2,10},{10... | collective-permute-start | bytes 1769480 | tf_op jit(solution)/shard_map/ppermute | solution.py:883
  532.1 68.9 %collective-permute-start.39 = (bf16[128,2176]{1,0:T(8,128)(2,1)}, bf16[128,2176]{1,0:T(8,128)(2,1)}, u32[]{:S(2)}, u32[]{:S(2)}) collective-permute-start(bf16[128,2176]{1,0:T(8,128)(2,1)} %reduce-scatter.3.cloned.1.call-done), channel_id=1, source_target_pairs={{0,16},{8,24},{16,0},{24,8},{1,17},{9,25},{17,1},{25,9},{2,18},{10... | collective-permute-start | bytes 1671176 | tf_op jit(solution)/shard_map/ppermute | solution.py:883
  533.6 69.4 %collective-permute-start.41 = (bf16[128,2176]{1,0:T(8,128)(2,1)}, bf16[128,2176]{1,0:T(8,128)(2,1)}, u32[]{:S(2)}, u32[]{:S(2)}) collective-permute-start(bf16[128,2176]{1,0:T(8,128)(2,1)} %reduce-scatter.3.cloned.1.call-done), channel_id=1, source_target_pairs={{0,8},{8,0},{16,24},{24,16},{1,9},{9,1},{17,25},{25,17},{2,10},{10... | collective-permute-start | bytes 1671176 | tf_op jit(solution)/shard_map/ppermute | solution.py:883
  (85 other events, 924.4 us)
Sparse Core Ops, SparseCore 0:
  13.7 79.3 all-gather.2
  95.8 78.0 all-gather.4
  325.9 93.9 reduce-scatter.4
  435.8 96.2 reduce-scatter.2

commit v6 on v5

--- a/solution.py
+++ b/solution.py
@@ -832,6 +832,69 @@
     )(place, proj, proj, proj, gate, taps, coefficients, gain, *kept, grad_gated)
 
 
+def unpack_kernel(source_ref, target_ref):
+    rows = target_ref.shape[0]
+    source = source_ref[...]
+    stacked = jnp.concatenate(
+        [source[:, at : at + LANES] for at in range(0, source.shape[1], LANES)], axis=0
+    )
+    for at in range(target_ref.shape[1] // LANES):
+        target_ref[:, at * LANES : (at + 1) * LANES] = stacked[at * rows : (at + 1) * rows]
+
+
+def unpack(array, start, shards, rows, model, interpret):
+    own = array.shape[0] // shards
+    columns = array.shape[1] - start
+    return pl.pallas_call(
+        unpack_kernel,
+        grid=(shards,),
+        in_specs=[pl.BlockSpec((own, columns), lambda i: (i, start // columns))],
+        out_specs=pl.BlockSpec((rows, model), lambda i: (i, 0)),
+        out_shape=shape_of(shards * rows, model),
+        compiler_params=params(),
+        interpret=interpret,
+    )(array)
+
+
+def assemble_kernel(shards, piece, padded, *refs):
+    *pieces, gate_ref, up_ref, down_ref = refs
+    units = shards * padded
+    pieces = [item[...].astype(wide) for item in pieces]
+    for at, target_ref in enumerate((gate_ref, up_ref)):
+        target_ref[...] = jnp.concatenate(
+            [
+                item[:, at * units + block * padded : at * units + block * padded + piece]
+                for block in range(shards)
+                for item in pieces
+            ],
+            axis=1,
+        )
+    for at, item in enumerate(pieces):
+        stacked = jnp.concatenate(
+            [item[:, start : start + LANES] for start in range(2 * units, item.shape[1], LANES)],
+            axis=0,
+        )
+        for block in range(down_ref.shape[1] // LANES):
+            down_ref[
+                at * piece : (at + 1) * piece, block * LANES : (block + 1) * LANES
+            ] = stacked[block * padded : block * padded + piece]
+
+
+def assemble(pieces, shards, piece, padded, model, interpret):
+    own = pieces[0].shape[0]
+    parts = len(pieces)
+    full = (own, shards * parts * piece)
+    return row_call(
+        lambda *refs: assemble_kernel(shards, piece, padded, *refs),
+        1,
+        [fixed(item.shape) for item in pieces],
+        [fixed(full), fixed(full), fixed((parts * piece, model))],
+        [shape_of(*full, wide), shape_of(*full, wide), shape_of(parts * piece, model, wide)],
+        1024,
+        interpret,
+    )(*pieces)
+
+
 def to_lanes(array):
     groups, rows, columns = array.shape
     split = array.reshape(groups, rows, columns // LANES, LANES)
@@ -976,7 +1039,9 @@
     ffn_part = jnp.concatenate(
         [both_part, from_lanes(to_lanes(down_part[None]), own)[0]], axis=1
     )
-    ffn_part, w_all = tie((ffn_part, w_all))
+    ffn_part, w_all, token_pieces, cot_pieces = tie(
+        (ffn_part, w_all, token_pieces, gather_seq(own_cot))
+    )
     ffn_all = over_dp(ffn_part)
 
     decay_part = mine(a_log, heads, 0)
@@ -999,7 +1064,6 @@
     mixed, *kept = mixer_forward(
         heads, parts, place_row, proj, taps, coefficients, interpret
     )
-    mixed, *cot_pieces = tie((mixed, *gather_seq(own_cot)))
     out_part = jnp.swapaxes(out_part.reshape(shards, own, out_ratio, quarter), 1, 2)
     w_out_own = jnp.swapaxes(
         exchange(out_part.reshape(parts, values, quarter)), 0, 1
@@ -1012,9 +1076,13 @@
     after_mix = rows + scatter_seq(mixed_pieces)[0]
     normed_two, inverse_two = row_norm(after_mix, second_gain)
     normed_two, ffn_all = tie((lower(normed_two), ffn_all))
-    down_own = from_lanes(
-        to_lanes(ffn_all[:, 2 * ffn_own :].reshape(shards, own, -1)), padded
-    ).reshape(ffn_own, model)
+    whole_tiles = padded % (2 * HALO) == 0 and piece % HALO == 0
+    if whole_tiles:
+        down_own = unpack(ffn_all, 2 * ffn_own, shards, padded, model, interpret)
+    else:
+        down_own = from_lanes(
+            to_lanes(ffn_all[:, 2 * ffn_own :].reshape(shards, own, -1)), padded
+        ).reshape(ffn_own, model)
     across = flip(normed_two, 2)
     beside = flip(normed_two, 1)
     half = parts // 2
@@ -1118,9 +1186,25 @@
         )
         return split.reshape(own, -1).astype(wide)
 
-    grad_w_in, packed, ffn_pieces, first_pieces = tie(
-        (grad_w_in, packed, gather_seq(grad_ffn), first_pieces)
-    )
+    ffn_pieces = in_order(gather_seq(grad_ffn))
+    if whole_tiles:
+        ffn_grads = assemble(ffn_pieces, shards, piece, padded, model, interpret)
+    else:
+        ffn_grads = (
+            ffn_full([item[:, :ffn_own] for item in ffn_pieces]),
+            ffn_full([item[:, ffn_own : 2 * ffn_own] for item in ffn_pieces]),
+            jnp.concatenate(
+                [
+                    from_lanes(to_lanes(item[None, :, 2 * ffn_own :]), padded)[0][:piece]
+                    for item in ffn_pieces
+                ],
+                axis=0,
+            ).astype(wide),
+        )
+    grad_w_in, packed, first_pieces, ffn_grads = tie(
+        (grad_w_in, packed, first_pieces, ffn_grads)
+    )
+    grad_w_gate, grad_w_up, grad_w_down = ffn_grads
     in_pieces = in_order(gather_seq(grad_w_in))
     packed = sum_bits(packed, 0, bits // 2)
     back_one, unused = norm_back(
@@ -1130,16 +1214,6 @@
         sum([item.astype(wide) for item in first_pieces[1:]], first_pieces[0]),
     )
     grad_rows = lower(grad_after + back_one)[:, None, :]
-    ffn_pieces = in_order(ffn_pieces)
-    grad_w_gate = ffn_full([item[:, :ffn_own] for item in ffn_pieces])
-    grad_w_up = ffn_full([item[:, ffn_own : 2 * ffn_own] for item in ffn_pieces])
-    grad_w_down = jnp.concatenate(
-        [
-            from_lanes(to_lanes(item[None, :, 2 * ffn_own :]), padded)[0][:piece]
-            for item in ffn_pieces
-        ],
-        axis=0,
-    ).astype(wide)
     def along(weights, grads):
         return sum(
             jnp.sum(weight.astype(wide) * grad, axis=1)

time: 629 us -> 534 us (0.85)
  local copies, waits for them, and re-layouts: 104 us -> 45.3 us
  waiting for transfers between devices: 246 us -> 200 us
  Pallas kernels: 137 us -> 144 us
    all_gather x2, waiting for transfers between devices: 76.7 us -> 26.6 us  [over_dp(): return lax.all_gather(array, 'dp', axis=0, tiled=True)]
    slice x26 -> x0, local copies, waits for them, and re-layouts: 30.8 us -> none  [the longest x8 12.5 us: per_device(): item[None, :, 2 * ffn_own:]]
    unnamed x140 -> x120, local copies, waits for them, and re-layouts: 26.2 us -> 12 us
    transpose x7 -> x2, local copies, waits for them, and re-layouts: 9.54 us -> 0.04 us  [to_lanes(): return jnp.swapaxes(split, 1, 2).reshape(groups, -1, LANES)]
    another operation x8 -> x0, local copies, waits for them, and re-layouts: 8.08 us -> none  [ffn_full(): jnp.stack([item.reshape(own, shards, padded)[..., :piece] for item in pie...]
    pallas_call x0 -> x2, Pallas kernels: none -> 7.57 us  [the longest x1 4.04 us: unpack(): pl.pallas_call(unpack_kernel, grid=(shards,), in_specs=[pl.BlockSpec((own...]
  transfers between devices with their start and end apart: 47 -> 47, of which waited for: 17 -> 20; matrix products, arithmetic and copies ran while one was open for 27% -> 20% of each run, Pallas kernels for 20% -> 25%
where the time goes in v6:
time: 534 us; the launch traced here: 524 us
  waiting for transfers between devices  200 us (37%)
  Pallas kernels  144 us (27%)
  matrix products  49.3 us (9%)
  local copies, waits for them, and re-layouts  45.3 us (8%)
  other arithmetic  41 us (8%)
  starting transfers between devices  29.5 us (6%)
  between operations  15.4 us (3%)
    ppermute x39, waiting for transfers between devices, flip(): return lax.ppermute(array, 'seq', [(i, i ^ bit) for i in range(parts)])  168 us
    pallas_call x1, Pallas kernels, mixer_backward(): pl.pallas_call(lambda *refs: backward_kernel(heads, *refs), grid_spec=plt...  44.2 us
    pallas_call x2, Pallas kernels, ffn_rows(): row_call(lambda *refs: ffn_kernel(steps, *refs), steps, [fixed(item.shape...  30.9 us
    pallas_call x1, Pallas kernels, mixer_forward(): pl.pallas_call(lambda *refs: forward_kernel(heads, *refs), grid_spec=pltp...  30.7 us
    all_gather x2, waiting for transfers between devices, over_dp(): return lax.all_gather(array, 'dp', axis=0, tiled=True)  26.6 us
    dot_general x5, matrix products, over_rows(): lax.dot_general(left, right, (((0,), (0,)), ((), ())), preferred_element_...  24.7 us
    ppermute x39, starting transfers between devices, flip(): return lax.ppermute(array, 'seq', [(i, i ^ bit) for i in range(parts)])  23.6 us
    dot_general x4, matrix products, by_transpose(): lax.dot_general(left, right, (((1,), (1,)), ((), ())), preferred_element_...  18.4 us
  transfers between devices with their start and end apart: 47, of which 20 were waited for; matrix products, arithmetic and copies ran while one was open for 20% of the time, Pallas kernels for 25%

profile of v6, /device:TPU:0, one launch (start us, length us, event | category | flops | bytes accessed | tf_op | source)
XLA Modules:
  0.0 524.4 jit_solution(14858389793604830615)
XLA Ops:
  17.2 23.5 %collective-permute-done.1.refs_2_ = bf16[512,1024]{1,0:T(8,128)(2,1)} collective-permute-done((bf16[512,1024]{1,0:T(8,128)(2,1)S(1)}, bf16[512,1024]{1,0:T(8,128)(2,1)}, u32[]{:S(2)}, u32[]{:S(2)}) %collective-permute-start.1) | collective-permute-done | bytes 1048608 | tf_op jit(solution)/shard_map/ppermute | solution.py:946
  40.7 21.6 %collective-permute-done.4.refs_2_ = bf16[512,1024]{1,0:T(8,128)(2,1)} collective-permute-done((bf16[512,1024]{1,0:T(8,128)(2,1)}, bf16[512,1024]{1,0:T(8,128)(2,1)}, u32[]{:S(2)}, u32[]{:S(2)}) %collective-permute-start.4) | collective-permute-done | bytes 1048608 | tf_op jit(solution)/shard_map/ppermute | solution.py:946
  66.4 26.6 %all-gather.3.cloned.1.call-done.refs_4_.refs_5_.refs_2_ = bf16[1024,2176]{1,0:T(8,128)(2,1)} async-done(((bf16[128,2176]{1,0:T(8,128)(2,1)}), bf16[1024,2176]{1,0:T(8,128)(2,1)}) %all-gather.3.cloned.1.call-update) | async-done | bytes 4456464 | tf_op jit(solution)/shard_map/all_gather | solution.py:949
  95.2 11.1 %shard_map.262 = (bf16[2048,1024]{1,0:T(8,128)(2,1)}, bf16[2048,1152]{1,0:T(8,128)(2,1)}) custom-call(bf16[512,1024]{1,0:T(8,128)(2,1)S(1)} %bitcast.128, bf16[512,1024]{1,0:T(8,128)(2,1)} %collective-permute-done.refs_1_, bf16[512,1024]{1,0:T(8,128)(2,1)} %collective-permute-done.1.refs_2_, bf16[512,1024]{1,0:T(8,128)(2,1)} %collective-permute-done.2.refs_3_, ...), custom_call_target="tpu_custom_call" | custom-call | flops 2359296 | bytes 2304 | tf_op jit(solution)/shard_map/pallas_call | solution.py:666
  110.9 30.7 %shard_map.263 = (bf16[2048,512]{1,0:T(8,128)(2,1)}, bf16[8,2,256,256]{3,2,1,0:T(8,128)(2,1)}, bf16[8,2,256,128]{3,2,1,0:T(8,128)(2,1)S(1)}, bf16[2048,512]{1,0:...) custom-call(s32[1]{0:T(128)} %bitcast.1.refs_0_, ...), custom_call_target="tpu_custom_call" | custom-call | flops 409600000 | bytes 4194304 | tf_op jit(solution)/shard_map/pallas_call | solution.py:585
  143.8 10.7 %shard_map.264 = (bf16[2048,512]{1,0:T(8,128)(2,1)}, f32[2048,512]{1,0:T(8,128)}, bf16[512,1024]{1,0:T(8,128)(2,1)S(1)}, bf16[512,1024]{1,0:T(8,128)(2,1)}, bf16...) custom-call(bf16[2048,512]{1,0:T(8,128)(2,1)} %get-tuple-element.94.refs_0_.refs_8_, ...), custom_call_target="tpu_custom_call" | custom-call | flops 1048576 | bytes 1024 | tf_op jit(solution)/shard_map/pallas_call | solution.py:686
  160.6 24.0 %collective-permute-done.11 = bf16[512,1024]{1,0:T(8,128)(2,1)S(1)} collective-permute-done((bf16[512,1024]{1,0:T(8,128)(2,1)S(1)}, bf16[512,1024]{1,0:T(8,128)(2,1)S(1)}, u32[]{:S(2)}, u32[]{:S(2)}) %collective-permute-start.11) | collective-permute-done | bytes 1048608 | tf_op jit(solution)/shard_map/ppermute | solution.py:946
  189.3 4.0 shard_map.265.refs_5_
  195.5 15.5 %shard_map.266 = (bf16[1024,1024]{1,0:T(8,128)(2,1)}, bf16[1024,1024]{1,0:T(8,128)(2,1)}, bf16[1024,768]{1,0:T(8,128)(2,1)}, bf16[1024,1536]{1,0:T(8,128)(2,1)},...) custom-call(bf16[512,1024]{1,0:T(8,128)(2,1)} %multiply_convert_fusion.refs_0_, bf16[512,1024]{1,0:T(8,128)(2,1)} %copy-done.42, ...), custom_call_target="tpu_custom_call" | custom-call | flops 8053063680 | bytes 7864320 | tf_op jit(solution)/shard_map/pallas_call | solution.py:709
  217.3 15.5 %shard_map.267 = (bf16[1024,1024]{1,0:T(8,128)(2,1)}, bf16[1024,1024]{1,0:T(8,128)(2,1)}, bf16[1024,768]{1,0:T(8,128)(2,1)}, bf16[1024,1536]{1,0:T(8,128)(2,1)},...) custom-call(bf16[512,1024]{1,0:T(8,128)(2,1)} %copy-done.39, bf16[512,1024]{1,0:T(8,128)(2,1)} %copy-done.43, ...), custom_call_target="tpu_custom_call" | custom-call | flops 8053063680 | bytes 7864320 | tf_op jit(solution)/shard_map/pallas_call | solution.py:709
  232.9 4.0 fusion.46
  249.2 3.9 add_convert_fusion
  255.6 17.9 %collective-permute-done.17 = bf16[512,1024]{1,0:T(8,128)(2,1)} collective-permute-done((bf16[512,1024]{1,0:T(8,128)(2,1)}, bf16[512,1024]{1,0:T(8,128)(2,1)}, u32[]{:S(2)}, u32[]{:S(2)}) %collective-permute-start.17) | collective-permute-done | bytes 1048608 | tf_op jit(solution)/shard_map/ppermute | solution.py:946
  279.5 3.7 fusion.39
  290.9 17.5 %collective-permute-done.18.refs_2_ = bf16[512,1024]{1,0:T(8,128)(2,1)S(1)} collective-permute-done((bf16[512,1024]{1,0:T(8,128)(2,1)S(1)}, bf16[512,1024]{1,0:T(8,128)(2,1)S(1)}, u32[]{:S(2)}, u32[]{:S(2)}) %collective-permute-start.18) | collective-permute-done | bytes 1048608 | tf_op jit(solution)/shard_map/ppermute | solution.py:946
  312.0 9.1 %shard_map.268 = (f32[2048,512]{1,0:T(8,128)}, bf16[4,512,256]{2,1,0:T(8,128)(2,1)S(1)}) custom-call(bf16[512,1024]{1,0:T(8,128)(2,1)} %copy-done.23, bf16[512,1024]{1,0:T(8,128)(2,1)} %copy-done.41, bf16[512,1024]{1,0:T(8,128)(2,1)} %copy-done.40, bf16[512,1024]{1,0:T(8,128)(2,1)} %copy-done.44, bf16[2048,512]{1,0:T(8,128)(2,1)} %get-tuple-element.137.refs_4_, ...), custom_call_target="tpu_custom_call" | custom-call | flops 4294967296 | bytes 524288 | tf_op jit(solution)/shard_map/pallas_call | solution.py:738
  323.1 44.2 %shard_map.269 = (bf16[2048,1664]{1,0:T(8,128)(2,1)}, f32[8,1024]{1,0:T(8,128)S(1)}, f32[8,256]{1,0:T(8,128)S(1)}, f32[8,128]{1,0:T(8,128)S(1)}) custom-call(s32[1]{0:T(128)} %bitcast.1.refs_0_, bf16[2048,1152]{1,0:T(8,128)(2,1)} %get-tuple-element.93.refs_1_.refs_2_.refs_3_, bf16[2048,1152]{1,0:T(8,128)(2,1)} %get-tuple-element.93.refs_1_.refs_2_.refs_3_, ...), custom_call_target="tpu_custom_call" | custom-call | flops 409600000 | bytes 4194304 | tf_op jit(solution)/shard_map/pallas_call | solution.py:787
  367.3 11.3 %convolution_convert_fusion = bf16[1024,1664]{1,0:T(8,128)(2,1)S(1)} fusion(bf16[2048,1024]{1,0:T(8,128)(2,1)S(1)} %copy-done.12, bf16[2048,1664]{1,0:T(8,128)(2,1)} %get-tuple-element.145), kind=kOutput, calls=%fused_computation.4 | convolution fusion | flops 6981025792 | bytes 14417920 | tf_op jit(solution)/shard_map/dot_general | solution.py:32
  408.4 5.3 %fusion.14 = f32[1024,1024]{1,0:T(8,128)S(1)} fusion(f32[1024,1024]{1,0:T(8,128)S(1)} %fusion.28, bf16[1024,2176]{1,0:T(8,128)(2,1)S(1)} %bitcast.130, bf16[2048,1664]{1,0:T(8,128)(2,1)} %get-tuple-element.145), kind=kOutput, calls=%fused_computation.36 | convolution fusion | flops 3222274048 | bytes 14680064 | tf_op jit(solution)/shard_map/dot_general | solution.py:26
  421.5 7.6 %add_convert_fusion.1 = bf16[1024,1024]{1,0:T(8,128)(2,1)S(1)} fusion(f32[1024,1024]{1,0:T(8,128)} %fusion.26, bf16[1024,2176]{1,0:T(8,128)(2,1)} %all-gather.3.cloned.1.call-done.refs_4_.refs_5_.refs_2_, bf16[2048,1664]{1,0:T(8,128)(2,1)} %get-tuple-element.145), kind=kOutput, calls=%fused_computation.3 | convolution fusion | flops 3223322624 | bytes 12582912 | tf_op jit(solution)/shard_map/dot_general | solution.py:26
  429.2 8.0 %collective-permute-done.36 = bf16[128,2304]{1,0:T(8,128)(2,1)S(1)} collective-permute-done((bf16[128,2304]{1,0:T(8,128)(2,1)}, bf16[128,2304]{1,0:T(8,128)(2,1)S(1)}, u32[]{:S(2)}, u32[]{:S(2)}) %collective-permute-start.36) | collective-permute-done | bytes 589856 | tf_op jit(solution)/shard_map/ppermute | solution.py:946
  447.5 15.9 %collective-permute-done.34 = bf16[512,1024]{1,0:T(8,128)(2,1)S(1)} collective-permute-done((bf16[512,1024]{1,0:T(8,128)(2,1)S(1)}, bf16[512,1024]{1,0:T(8,128)(2,1)S(1)}, u32[]{:S(2)}, u32[]{:S(2)}) %collective-permute-start.34) | collective-permute-done | bytes 1048608 | tf_op jit(solution)/shard_map/ppermute | solution.py:946
  463.4 21.8 %collective-permute-done.35 = bf16[512,1024]{1,0:T(8,128)(2,1)} collective-permute-done((bf16[512,1024]{1,0:T(8,128)(2,1)S(1)}, bf16[512,1024]{1,0:T(8,128)(2,1)}, u32[]{:S(2)}, u32[]{:S(2)}) %collective-permute-start.35) | collective-permute-done | bytes 1048608 | tf_op jit(solution)/shard_map/ppermute | solution.py:946
  490.8 3.7 fusion.25
  (344 shorter events, 151.7 us)
Async XLA Ops:
  7.2 85.8 %all-gather.3.cloned.1.call-start = ((), (), s32[]{:S(2)}) async-start(), calls=%async_computation.2 | async-start | bytes 5013504 | tf_op jit(solution)/shard_map/all_gather | solution.py:949
  13.5 174.3 %all-gather.5.cloned.1.call-start = ((), (), s32[]{:S(2)}) async-start(), calls=%async_computation.3 | async-start | bytes 5308416 | tf_op jit(solution)/shard_map/all_gather | solution.py:949
  13.6 27.1 %collective-permute-start.1 = (bf16[512,1024]{1,0:T(8,128)(2,1)S(1)}, bf16[512,1024]{1,0:T(8,128)(2,1)}, u32[]{:S(2)}, u32[]{:S(2)}) collective-permute-start(bf16[512,1024]{1,0:T(8,128)(2,1)S(1)} %bitcast.126), channel_id=1, source_target_pairs={{0,16},{8,24},{16,0},{24,8},{1,17},{9,25},{17,1},{25,9},{2,18},{10... | collective-permute-start | bytes 3145736 | tf_op jit(solution)/shard_map/ppermute | solution.py:946
  16.6 45.7 %collective-permute-start.4 = (bf16[512,1024]{1,0:T(8,128)(2,1)}, bf16[512,1024]{1,0:T(8,128)(2,1)}, u32[]{:S(2)}, u32[]{:S(2)}) collective-permute-start(bf16[512,1024]{1,0:T(8,128)(2,1)} %bitcast.143), channel_id=1, source_target_pairs={{0,16},{8,24},{16,0},{24,8},{1,17},{9,25},{17,1},{25,9},{2,18},{10... | collective-permute-start | bytes 3145736 | tf_op jit(solution)/shard_map/ppermute | solution.py:946
  16.7 49.7 %collective-permute-start = (bf16[512,1024]{1,0:T(8,128)(2,1)S(1)}, bf16[512,1024]{1,0:T(8,128)(2,1)}, u32[]{:S(2)}, u32[]{:S(2)}) collective-permute-start(bf16[512,1024]{1,0:T(8,128)(2,1)S(1)} %bitcast.127), channel_id=1, source_target_pairs={{0,8},{8,0},{16,24},{24,16},{1,9},{9,1},{17,25},{25,17},{2,10},{10... | collective-permute-start | bytes 3145736 | tf_op jit(solution)/shard_map/ppermute | solution.py:946
  16.7 49.7 %collective-permute-start.3 = (bf16[512,1024]{1,0:T(8,128)(2,1)}, bf16[512,1024]{1,0:T(8,128)(2,1)}, u32[]{:S(2)}, u32[]{:S(2)}) collective-permute-start(bf16[512,1024]{1,0:T(8,128)(2,1)} %bitcast.144), channel_id=1, source_target_pairs={{0,8},{8,0},{16,24},{24,16},{1,9},{9,1},{17,25},{25,17},{2,10},{10... | collective-permute-start | bytes 3145736 | tf_op jit(solution)/shard_map/ppermute | solution.py:946
  40.7 25.7 %collective-permute-start.2 = (bf16[512,1024]{1,0:T(8,128)(2,1)}, bf16[512,1024]{1,0:T(8,128)(2,1)}, u32[]{:S(2)}, u32[]{:S(2)}) collective-permute-start(bf16[512,1024]{1,0:T(8,128)(2,1)} %collective-permute-done.1.refs_2_), channel_id=1, source_target_pairs={{0,8},{8,0},{16,24},{24,16},{1,9},{9,1},{17,25},{25,17},{2,10},{10... | collective-permute-start | bytes 3145736 | tf_op jit(solution)/shard_map/ppermute | solution.py:946
  93.0 327.0 %reduce-scatter.5.cloned.1.call-start = ((), (), s32[]{:S(2)}) async-start(), calls=%async_computation.5 | async-start | bytes 5308416 | tf_op jit(solution)/shard_map/reduce_scatter | solution.py:952
  108.9 32.7 %collective-permute-start.6 = (bf16[1,512,256]{2,1,0:T(8,128)(2,1)S(1)}, bf16[1,512,256]{2,1,0:T(8,128)(2,1)S(1)}, u32[]{:S(2)}, u32[]{:S(2)}) collective-permute-start(bf16[1,512,256]{2,1,0:T(8,128)(2,1)S(1)} %get-tuple-element.241), channel_id=1, source_target_pairs={{0,8},{8,0},{16,24},{24,16},{1,9},{9,1},{17,25},{25,17},{2,10},{10... | collective-permute-start | bytes 786440 | tf_op jit(solution)/shard_map/ppermute | solution.py:946
  109.0 32.6 %collective-permute-start.7 = (bf16[1,512,256]{2,1,0:T(8,128)(2,1)S(1)}, bf16[1,512,256]{2,1,0:T(8,128)(2,1)S(1)}, u32[]{:S(2)}, u32[]{:S(2)}) collective-permute-start(bf16[1,512,256]{2,1,0:T(8,128)(2,1)S(1)} %get-tuple-element.240), channel_id=1, source_target_pairs={{0,16},{8,24},{16,0},{24,8},{1,17},{9,25},{17,1},{25,9},{2,18},{10... | collective-permute-start | bytes 786440 | tf_op jit(solution)/shard_map/ppermute | solution.py:946
  110.5 31.1 %collective-permute-start.8 = (bf16[1,512,256]{2,1,0:T(8,128)(2,1)S(1)}, bf16[1,512,256]{2,1,0:T(8,128)(2,1)S(1)}, u32[]{:S(2)}, u32[]{:S(2)}) collective-permute-start(bf16[1,512,256]{2,1,0:T(8,128)(2,1)S(1)} %get-tuple-element.239), channel_id=1, source_target_pairs={{0,24},{8,16},{16,8},{24,0},{1,25},{9,17},{17,9},{25,1},{2,26},{10... | collective-permute-start | bytes 786440 | tf_op jit(solution)/shard_map/ppermute | solution.py:946
  159.1 25.6 %collective-permute-start.11 = (bf16[512,1024]{1,0:T(8,128)(2,1)S(1)}, bf16[512,1024]{1,0:T(8,128)(2,1)S(1)}, u32[]{:S(2)}, u32[]{:S(2)}) collective-permute-start(bf16[512,1024]{1,0:T(8,128)(2,1)S(1)} %add_convert_fusion.6), channel_id=1, source_target_pairs={{0,16},{8,24},{16,0},{24,8},{1,17},{9,25},{17,1},{25,9},{2,18},{10... | collective-permute-start | bytes 3145736 | tf_op jit(solution)/shard_map/ppermute | solution.py:946
  187.8 25.8 %collective-permute-start.12 = (bf16[512,1024]{1,0:T(8,128)(2,1)}, bf16[512,1024]{1,0:T(8,128)(2,1)S(1)}, u32[]{:S(2)}, u32[]{:S(2)}) collective-permute-start(bf16[512,1024]{1,0:T(8,128)(2,1)} %multiply_convert_fusion.refs_0_), channel_id=1, source_target_pairs={{0,16},{8,24},{16,0},{24,8},{1,17},{9,25},{17,1},{25,9},{2,18},{10... | collective-permute-start | bytes 3145736 | tf_op jit(solution)/shard_map/ppermute | solution.py:946
  247.8 25.8 %collective-permute-start.17 = (bf16[512,1024]{1,0:T(8,128)(2,1)}, bf16[512,1024]{1,0:T(8,128)(2,1)}, u32[]{:S(2)}, u32[]{:S(2)}) collective-permute-start(bf16[512,1024]{1,0:T(8,128)(2,1)} %add_convert_fusion.5), channel_id=1, source_target_pairs={{0,16},{8,24},{16,0},{24,8},{1,17},{9,25},{17,1},{25,9},{2,18},{10... | collective-permute-start | bytes 3145736 | tf_op jit(solution)/shard_map/ppermute | solution.py:946
  273.5 211.7 %reduce-scatter.3.cloned.1.call-start = ((), (), s32[]{:S(2)}) async-start(), calls=%async_computation.4 | async-start | bytes 5013504 | tf_op jit(solution)/shard_map/reduce_scatter | solution.py:952
  283.2 25.2 %collective-permute-start.18 = (bf16[512,1024]{1,0:T(8,128)(2,1)S(1)}, bf16[512,1024]{1,0:T(8,128)(2,1)S(1)}, u32[]{:S(2)}, u32[]{:S(2)}) collective-permute-start(bf16[512,1024]{1,0:T(8,128)(2,1)S(1)} %get-tuple-element.212.refs_0_), channel_id=1, source_target_pairs={{0,16},{8,24},{16,0},{24,8},{1,17},{9,25},{17,1},{25,9},{2,18},{10... | collective-permute-start | bytes 3145736 | tf_op jit(solution)/shard_map/ppermute | solution.py:946
  321.2 57.5 %collective-permute-start.24 = (bf16[1,512,256]{2,1,0:T(8,128)(2,1)S(1)}, bf16[1,512,256]{2,1,0:T(8,128)(2,1)S(1)}, u32[]{:S(2)}, u32[]{:S(2)}) collective-permute-start(bf16[1,512,256]{2,1,0:T(8,128)(2,1)S(1)} %get-tuple-element.233), channel_id=1, source_target_pairs={{0,8},{8,0},{16,24},{24,16},{1,9},{9,1},{17,25},{25,17},{2,10},{10... | collective-permute-start | bytes 786440 | tf_op jit(solution)/shard_map/ppermute | solution.py:946
  321.4 57.3 %collective-permute-start.25 = (bf16[1,512,256]{2,1,0:T(8,128)(2,1)S(1)}, bf16[1,512,256]{2,1,0:T(8,128)(2,1)S(1)}, u32[]{:S(2)}, u32[]{:S(2)}) collective-permute-start(bf16[1,512,256]{2,1,0:T(8,128)(2,1)S(1)} %get-tuple-element.232), channel_id=1, source_target_pairs={{0,16},{8,24},{16,0},{24,8},{1,17},{9,25},{17,1},{25,9},{2,18},{10... | collective-permute-start | bytes 786440 | tf_op jit(solution)/shard_map/ppermute | solution.py:946
  322.8 55.9 %collective-permute-start.26 = (bf16[1,512,256]{2,1,0:T(8,128)(2,1)S(1)}, bf16[1,512,256]{2,1,0:T(8,128)(2,1)S(1)}, u32[]{:S(2)}, u32[]{:S(2)}) collective-permute-start(bf16[1,512,256]{2,1,0:T(8,128)(2,1)S(1)} %get-tuple-element.231), channel_id=1, source_target_pairs={{0,24},{8,16},{16,8},{24,0},{1,25},{9,17},{17,9},{25,1},{2,26},{10... | collective-permute-start | bytes 786440 | tf_op jit(solution)/shard_map/ppermute | solution.py:946
  390.8 48.1 %collective-permute-start.19 = (bf16[512,1024]{1,0:T(8,128)(2,1)}, bf16[512,1024]{1,0:T(8,128)(2,1)}, u32[]{:S(2)}, u32[]{:S(2)}) collective-permute-start(bf16[512,1024]{1,0:T(8,128)(2,1)} %slice.150), channel_id=1, source_target_pairs={{0,8},{8,0},{16,24},{24,16},{1,9},{9,1},{17,25},{25,17},{2,10},{10... | collective-permute-start | bytes 3145736 | tf_op jit(solution)/shard_map/ppermute | solution.py:946
  399.7 39.7 %collective-permute-start.21 = (bf16[512,1024]{1,0:T(8,128)(2,1)}, bf16[512,1024]{1,0:T(8,128)(2,1)}, u32[]{:S(2)}, u32[]{:S(2)}) collective-permute-start(bf16[512,1024]{1,0:T(8,128)(2,1)} %add_convert_fusion.4), channel_id=1, source_target_pairs={{0,16},{8,24},{16,0},{24,8},{1,17},{9,25},{17,1},{25,9},{2,18},{10... | collective-permute-start | bytes 3145736 | tf_op jit(solution)/shard_map/ppermute | solution.py:946
  437.4 26.0 %collective-permute-start.34 = (bf16[512,1024]{1,0:T(8,128)(2,1)S(1)}, bf16[512,1024]{1,0:T(8,128)(2,1)S(1)}, u32[]{:S(2)}, u32[]{:S(2)}) collective-permute-start(bf16[512,1024]{1,0:T(8,128)(2,1)S(1)} %get-tuple-element.225), channel_id=1, source_target_pairs={{0,16},{8,24},{16,0},{24,8},{1,17},{9,25},{17,1},{25,9},{2,18},{10... | collective-permute-start | bytes 3145736 | tf_op jit(solution)/shard_map/ppermute | solution.py:946
  438.9 46.3 %collective-permute-start.35 = (bf16[512,1024]{1,0:T(8,128)(2,1)S(1)}, bf16[512,1024]{1,0:T(8,128)(2,1)}, u32[]{:S(2)}, u32[]{:S(2)}) collective-permute-start(bf16[512,1024]{1,0:T(8,128)(2,1)S(1)} %get-tuple-element.224), channel_id=1, source_target_pairs={{0,24},{8,16},{16,8},{24,0},{1,25},{9,17},{17,9},{25,1},{2,26},{10... | collective-permute-start | bytes 3145736 | tf_op jit(solution)/shard_map/ppermute | solution.py:946
  439.3 45.9 %collective-permute-start.33 = (bf16[512,1024]{1,0:T(8,128)(2,1)S(1)}, bf16[512,1024]{1,0:T(8,128)(2,1)}, u32[]{:S(2)}, u32[]{:S(2)}) collective-permute-start(bf16[512,1024]{1,0:T(8,128)(2,1)S(1)} %copy-done.21), channel_id=1, source_target_pairs={{0,8},{8,0},{16,24},{24,16},{1,9},{9,1},{17,25},{25,17},{2,10},{10... | collective-permute-start | bytes 3145736 | tf_op jit(solution)/shard_map/ppermute | solution.py:946
  (79 other events, 699.4 us)
Sparse Core Ops, SparseCore 0:
  13.6 79.3 all-gather.2
  95.8 78.0 all-gather.4
  273.7 93.2 reduce-scatter.4
  383.0 94.9 reduce-scatter.2

commit v7 on v6

--- a/solution.py
+++ b/solution.py
@@ -244,8 +244,9 @@
 
 
 def gate_kernel(
-    heads, mixed_ref, normed_ref, weight_ref, gain_ref, out_ref, gated_ref, gate_ref, *partials
+    heads, earlier, mixed_ref, normed_ref, weight_ref, gain_ref, out_ref, *refs
 ):
+    gated_ref, gate_ref, *partials = refs[earlier:]
     gate = by_weight(normed_ref[...], weight_ref[...])
     gate_ref[...] = gate
     gain = gain_ref[0:1]
@@ -290,22 +291,29 @@
     on_piece(normed_pieces, body)
 
 
-def branch_kernel(count, *refs):
-    gated_ref, weight_ref, grad_ref, out_ref, total = refs[count:]
-    quarter = out_ref.shape[2]
+def branch_kernel(count, earlier, *refs):
+    gated_ref, weight_ref = refs[count : count + 2]
+    grad_ref, out_ref, *scratch = refs[count + 2 + earlier :]
 
     def body(at, piece):
         branch = piece[...]
         grad_ref[...] = by_transpose(branch, weight_ref[...])
         product = over_rows(gated_ref[...], branch)
-        total[...] = product if at == 0 else total[...] + product
+        if not earlier:
+            out_ref[...] = product if at == 0 else out_ref[...] + product
+        elif at == 0:
+            scratch[0][...] = refs[count + 2][...] + product
+        else:
+            scratch[0][...] += product
 
     on_piece(refs[:count], body)
-
-    @pl.when(pl.program_id(0) == count - 1)
-    def _():
-        for at in range(out_ref.shape[0]):
-            out_ref[at] = lower(total[:, at * quarter : (at + 1) * quarter])
+    if earlier:
+        quarter = out_ref.shape[2]
+
+        @pl.when(pl.program_id(0) == count - 1)
+        def _():
+            for at in range(out_ref.shape[0]):
+                out_ref[at] = lower(scratch[0][:, at * quarter : (at + 1) * quarter])
 
 
 def backward_kernel(
@@ -679,26 +687,37 @@
     )(*pieces, weights, weights, gain)
 
 
-def gate_rows(heads, steps, mixed, normed, weights, start, gain, w_out, interpret):
+def rows_from(rows, columns, first):
+    return pl.BlockSpec((rows, columns), lambda i: (i + first, 0))
+
+
+def gate_rows(
+    heads, parts, first, steps, mixed, normed, weights, start, gain, w_out, earlier, interpret
+):
     length, values = mixed.shape
     model = normed.shape[1]
-    rows = length // steps
-    return row_call(
-        lambda *refs: gate_kernel(heads, *refs),
-        steps,
-        [
-            rows_of(rows, values),
-            rows_of(rows, model),
+    rows = length // parts
+    return pl.pallas_call(
+        lambda *refs: gate_kernel(heads, len(earlier), *refs),
+        grid=(steps,),
+        in_specs=[
+            rows_from(rows, values, first),
+            rows_from(rows, model, first),
             columns_at(model, values, start),
             fixed(gain.shape),
             fixed(w_out.shape),
-        ],
-        [rows_of(rows, values), rows_of(rows, values)] + [fixed((rows, model))] * steps,
-        [shape_of(length, values), shape_of(length, values, wide)]
+        ]
+        + [pl.BlockSpec(memory_space=pl.ANY)] * len(earlier),
+        out_specs=[rows_from(rows, values, first)] * 2 + [fixed((rows, model))] * steps,
+        out_shape=[shape_of(length, values), shape_of(length, values, wide)]
         + [shape_of(rows, model)] * steps,
-        length * values,
-        interpret,
-    )(mixed, normed, weights, gain, w_out)
+        input_output_aliases={5 + at: at for at in range(len(earlier))},
+        compiler_params=params(),
+        cost_estimate=pl.CostEstimate(
+            flops=length * values, bytes_accessed=length, transcendentals=0
+        ),
+        interpret=interpret,
+    )(mixed, normed, weights, gain, w_out, *earlier)
 
 
 def ffn_rows(normed_pieces, cot_pieces, both, down, interpret):
@@ -730,29 +749,35 @@
     )(*normed_pieces, *cot_pieces, both, down)
 
 
-def branch_rows(pieces, gated, weight, interpret):
+def branch_rows(parts, first, pieces, gated, weight, earlier, interpret):
     steps = len(pieces)
     rows, model = pieces[0].shape
     values = weight.shape[0]
-    split = (steps, values, model // steps)
+    split = (parts, values, model // parts)
+    total = shape_of(values, model, wide)
     return pl.pallas_call(
-        lambda *refs: branch_kernel(steps, *refs),
+        lambda *refs: branch_kernel(steps, len(earlier), *refs),
         grid=(steps,),
         in_specs=[fixed(item.shape) for item in pieces]
-        + [rows_of(rows, values), fixed(weight.shape)],
-        out_specs=[rows_of(rows, values), fixed(split)],
+        + [rows_from(rows, values, first), fixed(weight.shape)]
+        + ([fixed(total.shape), pl.BlockSpec(memory_space=pl.ANY)] if earlier else []),
+        out_specs=[
+            rows_from(rows, values, first),
+            fixed(split) if earlier else fixed(total.shape),
+        ],
         out_shape=[
-            shape_of(steps * rows, values, wide),
-            jax.ShapeDtypeStruct(split, narrow),
+            shape_of(parts * rows, values, wide),
+            jax.ShapeDtypeStruct(split, narrow) if earlier else total,
         ],
-        scratch_shapes=[pltpu.VMEM((values, model), wide)],
+        scratch_shapes=[pltpu.VMEM(total.shape, wide)] if earlier else [],
+        input_output_aliases={steps + 3: 0} if earlier else {},
         compiler_params=params(),
         cost_estimate=pl.CostEstimate(
             flops=4 * steps * rows * model * values, bytes_accessed=rows * model,
             transcendentals=0,
         ),
         interpret=interpret,
-    )(*pieces, gated, weight)
+    )(*pieces, gated, weight, *earlier)
 
 
 def mixer_backward(
@@ -895,6 +920,50 @@
     )(*pieces)
 
 
+def finish_kernel(heads, gain_ref, weight_refs, pieces, grad_refs):
+    qkv_ref, rates_ref, gate_ref, out_ref, norm_ref = grad_refs
+    own = qkv_ref.shape[0]
+    parts = len(pieces)
+    width, values = qkv_ref.shape[1] // parts, gate_ref.shape[1] // parts
+    split, total = width + values, width + values + LANES
+    quarter = out_ref.shape[1] // parts
+    norm = jnp.zeros((own, 1), wide)
+    rates = []
+    for at, piece in enumerate(pieces):
+        item = piece[...].astype(wide)
+        for target_ref, weight_ref, start, size in (
+            (qkv_ref, weight_refs[0], 0, width),
+            (gate_ref, weight_refs[2], width, values),
+        ):
+            span = slice(at * size, (at + 1) * size)
+            grad = item[:, start : start + size]
+            target_ref[:, span] = grad
+            norm = norm + row_sum(grad * weight_ref[:, span].astype(wide))
+        rates.append(item[:, split : split + 2 * heads])
+        for row in range(out_ref.shape[0] // own):
+            out_ref[row * own : (row + 1) * own, at * quarter : (at + 1) * quarter] = item[
+                :, total + row * quarter : total + (row + 1) * quarter
+            ]
+    rates = jnp.concatenate(rates, axis=1)
+    rates_ref[...] = rates
+    norm = norm + row_sum(rates * weight_refs[1][...].astype(wide))
+    norm_ref[...] = jnp.broadcast_to(norm / gain_ref[...], norm_ref.shape)
+
+
+def finish(heads, gain, weights, pieces, out_shape, interpret):
+    own = pieces[0].shape[0]
+    shapes = [item.shape for item in weights] + [out_shape, (own, LANES)]
+    return row_call(
+        lambda *refs: finish_kernel(heads, refs[0], refs[1:4], refs[4:-5], refs[-5:]),
+        1,
+        [fixed(item.shape) for item in (gain, *weights, *pieces)],
+        [fixed(item) for item in shapes],
+        [shape_of(*item, wide) for item in shapes],
+        1024,
+        interpret,
+    )(gain, *weights, *pieces)
+
+
 def to_lanes(array):
     groups, rows, columns = array.shape
     split = array.reshape(groups, rows, columns // LANES, LANES)
@@ -1068,9 +1137,15 @@
     w_out_own = jnp.swapaxes(
         exchange(out_part.reshape(parts, values, quarter)), 0, 1
     ).reshape(values, model)
-    gated, out_gate, *mixed_pieces = gate_rows(
-        heads, parts, mixed, normed_one, w_all, width, gain, w_out_own, interpret
-    )
+    half = parts // 2
+    gate_args = (mixed, normed_one, w_all, width, gain, w_out_own)
+    *both_halves, corner_across, corner = gate_rows(
+        heads, parts, half, half, *gate_args, (), interpret
+    )
+    gated, out_gate, *mixed_near = gate_rows(
+        heads, parts, 0, half, *gate_args, tuple(both_halves), interpret
+    )
+    mixed_pieces = [*mixed_near, corner_across, corner]
     rows = own_tokens.astype(wide)
     inverse_one = row_norm(rows, first_gain)[1]
     after_mix = rows + scatter_seq(mixed_pieces)[0]
@@ -1085,7 +1160,6 @@
         ).reshape(ffn_own, model)
     across = flip(normed_two, 2)
     beside = flip(normed_two, 1)
-    half = parts // 2
     normed_near, cot_near, hidden_near, grad_near, *back_near = ffn_rows(
         [normed_two, beside], cot_pieces[:half], ffn_all, down_own, interpret
     )
@@ -1109,8 +1183,18 @@
     down_near = lower(by_weight(hidden_near, down_own))
     down_far = lower(by_weight(hidden_far, down_own))
     across, down_near, down_far = tie((across, down_near, down_far))
+    grad_gated, out_total = branch_rows(
+        parts, 0, [grad_low, beside], gated, w_out_own, (), interpret
+    )
+    across, out_total = tie((across, out_total))
     grad_gated, grad_out = branch_rows(
-        [grad_low, beside, across, flip(across, 1)], gated, w_out_own, interpret
+        parts,
+        half,
+        [across, flip(across, 1)],
+        gated,
+        w_out_own,
+        (out_total, grad_gated),
+        interpret,
     )
     grad_out = exchange(grad_out)
     grad_out = jnp.swapaxes(grad_out.reshape(shards, out_ratio, own, quarter), 1, 2).reshape(
@@ -1176,9 +1260,6 @@
             )
             for at in range(parts)
         ]
-
-    def side_by_side(pieces):
-        return jnp.concatenate(pieces, axis=1).astype(wide)
 
     def ffn_full(pieces):
         split = jnp.stack(
@@ -1227,21 +1308,15 @@
     taps_total = lax.dynamic_slice_in_dim(
         packed[:taps_rows].reshape(CONV, -1), lax.axis_index("dp") * own_taps, own_taps, 1
     )
-    total = split + LANES
-    grad_w_qkv = side_by_side([item[:, :width] for item in in_pieces])
-    grad_w_ba = side_by_side([item[:, split : split + 2 * heads] for item in in_pieces])
-    grad_w_outgate = side_by_side([item[:, width:split] for item in in_pieces])
-    grad_w_out = side_by_side(
-        [
-            jnp.swapaxes(item[:, total:].reshape(own, out_ratio, quarter), 0, 1).reshape(
-                out_rows, quarter
-            )
-            for item in in_pieces
-        ]
-    )
-    grad_norm_attn = along(
-        (w_qkv, w_ba, w_outgate), (grad_w_qkv, grad_w_ba, grad_w_outgate)
-    ) / norm_attn.astype(wide)
+    grad_w_qkv, grad_w_ba, grad_w_outgate, grad_w_out, norm_lanes = finish(
+        heads,
+        norm_attn.astype(wide)[:, None],
+        (w_qkv, w_ba, w_outgate),
+        in_pieces,
+        (out_rows, model),
+        interpret,
+    )
+    grad_norm_attn = norm_lanes[:, 0]
     return (
         lower(result)[:, None, :],
         grad_rows,

time: 534 us -> 529 us (level)
  Pallas kernels: 144 us -> 154 us
  local copies, waits for them, and re-layouts: 45.3 us -> 37.9 us
  other arithmetic: 41 us -> 34.6 us
    pallas_call x2 -> x5, Pallas kernels: 19.8 us -> 29.4 us  [the longest x2 13 us: gate_rows(): pl.pallas_call(lambda *refs: gate_kernel(heads, len(earlier), *refs), gri...]
    unnamed x120 -> x109, local copies, waits for them, and re-layouts: 12 us -> 14.4 us
  transfers between devices with their start and end apart: 47 -> 47, of which waited for: 20 -> 21; matrix products, arithmetic and copies ran while one was open for 20% -> 19% of each run, Pallas kernels for 25% -> 26%
where the time goes in v7:
time: 529 us; the launch traced here: 520 us
  waiting for transfers between devices  201 us (38%)
  Pallas kernels  154 us (29%)
  matrix products  49.4 us (9%)
  local copies, waits for them, and re-layouts  37.9 us (7%)
  other arithmetic  34.6 us (7%)
  starting transfers between devices  28.3 us (5%)
  between operations  15 us (3%)
    ppermute x39, waiting for transfers between devices, flip(): return lax.ppermute(array, 'seq', [(i, i ^ bit) for i in range(parts)])  168 us
    pallas_call x1, Pallas kernels, mixer_backward(): pl.pallas_call(lambda *refs: backward_kernel(heads, *refs), grid_spec=plt...  44.6 us
    pallas_call x2, Pallas kernels, ffn_rows(): row_call(lambda *refs: ffn_kernel(steps, *refs), steps, [fixed(item.shape...  31.1 us
    pallas_call x1, Pallas kernels, mixer_forward(): pl.pallas_call(lambda *refs: forward_kernel(heads, *refs), grid_spec=pltp...  30.4 us
    all_gather x2, waiting for transfers between devices, over_dp(): return lax.all_gather(array, 'dp', axis=0, tiled=True)  27.7 us
    dot_general x5, matrix products, over_rows(): lax.dot_general(left, right, (((0,), (0,)), ((), ())), preferred_element_...  24.7 us
    ppermute x39, starting transfers between devices, flip(): return lax.ppermute(array, 'seq', [(i, i ^ bit) for i in range(parts)])  22.7 us
    dot_general x4, matrix products, by_transpose(): lax.dot_general(left, right, (((1,), (1,)), ((), ())), preferred_element_...  18.4 us
  transfers between devices with their start and end apart: 47, of which 21 were waited for; matrix products, arithmetic and copies ran while one was open for 19% of the time, Pallas kernels for 26%

profile of v7, /device:TPU:0, one launch (start us, length us, event | category | flops | bytes accessed | tf_op | source)
XLA Modules:
  0.0 520.3 jit_solution(3707197726646815171)
XLA Ops:
  17.2 23.5 %collective-permute-done.1.refs_2_ = bf16[512,1024]{1,0:T(8,128)(2,1)} collective-permute-done((bf16[512,1024]{1,0:T(8,128)(2,1)S(1)}, bf16[512,1024]{1,0:T(8,128)(2,1)}, u32[]{:S(2)}, u32[]{:S(2)}) %collective-permute-start.1) | collective-permute-done | bytes 1048608 | tf_op jit(solution)/shard_map/ppermute | solution.py:1015
  40.8 21.6 %collective-permute-done.4.refs_2_ = bf16[512,1024]{1,0:T(8,128)(2,1)} collective-permute-done((bf16[512,1024]{1,0:T(8,128)(2,1)}, bf16[512,1024]{1,0:T(8,128)(2,1)}, u32[]{:S(2)}, u32[]{:S(2)}) %collective-permute-start.4) | collective-permute-done | bytes 1048608 | tf_op jit(solution)/shard_map/ppermute | solution.py:1015
  65.4 27.7 %all-gather.3.cloned.1.call-done.refs_4_.refs_5_.refs_2_ = bf16[1024,2176]{1,0:T(8,128)(2,1)} async-done(((bf16[128,2176]{1,0:T(8,128)(2,1)}), bf16[1024,2176]{1,0:T(8,128)(2,1)}) %all-gather.3.cloned.1.call-update) | async-done | bytes 4456464 | tf_op jit(solution)/shard_map/all_gather | solution.py:1018
  95.2 11.1 %shard_map.262 = (bf16[2048,1024]{1,0:T(8,128)(2,1)}, bf16[2048,1152]{1,0:T(8,128)(2,1)}) custom-call(bf16[512,1024]{1,0:T(8,128)(2,1)S(1)} %bitcast.122, bf16[512,1024]{1,0:T(8,128)(2,1)} %collective-permute-done.refs_1_, bf16[512,1024]{1,0:T(8,128)(2,1)} %collective-permute-done.1.refs_2_, bf16[512,1024]{1,0:T(8,128)(2,1)} %collective-permute-done.2.refs_3_, ...), custom_call_target="tpu_custom_call" | custom-call | flops 2359296 | bytes 2304 | tf_op jit(solution)/shard_map/pallas_call | solution.py:674
  110.9 30.4 %shard_map.263 = (bf16[2048,512]{1,0:T(8,128)(2,1)}, bf16[8,2,256,256]{3,2,1,0:T(8,128)(2,1)}, bf16[8,2,256,128]{3,2,1,0:T(8,128)(2,1)S(1)}, bf16[2048,512]{1,0:...) custom-call(s32[1]{0:T(128)} %bitcast.1.refs_0_, ...), custom_call_target="tpu_custom_call" | custom-call | flops 409600000 | bytes 4194304 | tf_op jit(solution)/shard_map/pallas_call | solution.py:593
  143.5 6.5 %shard_map.264 = (bf16[2048,512]{1,0:T(8,128)(2,1)}, f32[2048,512]{1,0:T(8,128)}, bf16[512,1024]{1,0:T(8,128)(2,1)S(1)}, bf16[512,1024]{1,0:T(8,128)(2,1)}) custom-call(bf16[2048,512]{1,0:T(8,128)(2,1)} %get-tuple-element.105.refs_0_.refs_8_, bf16[2048,1024]{1,0:T(8,128)(2,1)} %get-tuple-element.106.refs_1_, ...), custom_call_target="tpu_custom_call" | custom-call | flops 1048576 | bytes 2048 | tf_op jit(solution)/shard_map/pallas_call | solution.py:700
  150.4 6.5 %shard_map.265 = (bf16[2048,512]{1,0:T(8,128)(2,1)}, f32[2048,512]{1,0:T(8,128)}, bf16[512,1024]{1,0:T(8,128)(2,1)S(1)}, bf16[512,1024]{1,0:T(8,128)(2,1)}) custom-call(bf16[2048,512]{1,0:T(8,128)(2,1)} %get-tuple-element.105.refs_0_.refs_8_, bf16[2048,1024]{1,0:T(8,128)(2,1)} %get-tuple-element.106.refs_1_, ...), custom_call_target="tpu_custom_call", output_to_operand_aliasing={{0}: (5, {}), {1}: (6, {})} | custom-call | flops 1048576 | bytes 2048 | tf_op jit(solution)/shard_map/pallas_call | solution.py:700
  159.8 23.2 %collective-permute-done.11 = bf16[512,1024]{1,0:T(8,128)(2,1)S(1)} collective-permute-done((bf16[512,1024]{1,0:T(8,128)(2,1)S(1)}, bf16[512,1024]{1,0:T(8,128)(2,1)S(1)}, u32[]{:S(2)}, u32[]{:S(2)}) %collective-permute-start.11) | collective-permute-done | bytes 1048608 | tf_op jit(solution)/shard_map/ppermute | solution.py:1015
  187.7 4.0 shard_map.266.refs_5_
  193.9 15.7 %shard_map.267 = (bf16[1024,1024]{1,0:T(8,128)(2,1)}, bf16[1024,1024]{1,0:T(8,128)(2,1)}, bf16[1024,768]{1,0:T(8,128)(2,1)}, bf16[1024,1536]{1,0:T(8,128)(2,1)},...) custom-call(bf16[512,1024]{1,0:T(8,128)(2,1)} %multiply_convert_fusion.refs_0_, bf16[512,1024]{1,0:T(8,128)(2,1)} %copy-done.36, ...), custom_call_target="tpu_custom_call" | custom-call | flops 8053063680 | bytes 7864320 | tf_op jit(solution)/shard_map/pallas_call | solution.py:728
  215.7 15.4 %shard_map.268 = (bf16[1024,1024]{1,0:T(8,128)(2,1)}, bf16[1024,1024]{1,0:T(8,128)(2,1)}, bf16[1024,768]{1,0:T(8,128)(2,1)}, bf16[1024,1536]{1,0:T(8,128)(2,1)},...) custom-call(bf16[512,1024]{1,0:T(8,128)(2,1)} %copy-done.35, bf16[512,1024]{1,0:T(8,128)(2,1)} %copy-done.38, ...), custom_call_target="tpu_custom_call" | custom-call | flops 8053063680 | bytes 7864320 | tf_op jit(solution)/shard_map/pallas_call | solution.py:728
  231.3 4.0 fusion.42
  253.9 18.0 %collective-permute-done.17 = bf16[512,1024]{1,0:T(8,128)(2,1)} collective-permute-done((bf16[512,1024]{1,0:T(8,128)(2,1)}, bf16[512,1024]{1,0:T(8,128)(2,1)}, u32[]{:S(2)}, u32[]{:S(2)}) %collective-permute-start.17) | collective-permute-done | bytes 1048608 | tf_op jit(solution)/shard_map/ppermute | solution.py:1015
  289.2 17.5 %collective-permute-done.18.refs_0_ = bf16[512,1024]{1,0:T(8,128)(2,1)S(1)} collective-permute-done((bf16[512,1024]{1,0:T(8,128)(2,1)S(1)}, bf16[512,1024]{1,0:T(8,128)(2,1)S(1)}, u32[]{:S(2)}, u32[]{:S(2)}) %collective-permute-start.18) | collective-permute-done | bytes 1048608 | tf_op jit(solution)/shard_map/ppermute | solution.py:1015
  307.6 6.0 %shard_map.269 = (f32[2048,512]{1,0:T(8,128)}, f32[512,1024]{1,0:T(8,128)}) custom-call(bf16[512,1024]{1,0:T(8,128)(2,1)S(1)} %get-tuple-element.228.refs_0_, bf16[512,1024]{1,0:T(8,128)(2,1)} %copy-done.37, bf16[2048,512]{1,0:T(8,128)(2,1)} %get-tuple-element.150.refs_2_, bf16[512,1024]{1,0:T(8,128)(2,1)} %bitcast.127), custom_call_target="tpu_custom_call" | custom-call | flops 2147483648 | bytes 524288 | tf_op jit(solution)/shard_map/pallas_call | solution.py:758
  317.4 6.5 %shard_map.270 = (f32[2048,512]{1,0:T(8,128)}, bf16[4,512,256]{2,1,0:T(8,128)(2,1)S(1)}) custom-call(bf16[512,1024]{1,0:T(8,128)(2,1)} %copy-done.26, bf16[512,1024]{1,0:T(8,128)(2,1)} %copy-done.27, bf16[2048,512]{1,0:T(8,128)(2,1)} %get-tuple-element.150.refs_2_, bf16[512,1024]{1,0:T(8,128)(2,1)} %bitcast.128, ...), custom_call_target="tpu_custom_call", output_to_operand_aliasing={{0}: (5, {})} | custom-call | flops 2147483648 | bytes 524288 | tf_op jit(solution)/shard_map/pallas_call | solution.py:758
  325.9 44.6 %shard_map.271 = (bf16[2048,1664]{1,0:T(8,128)(2,1)}, f32[8,1024]{1,0:T(8,128)S(1)}, f32[8,256]{1,0:T(8,128)S(1)}, f32[8,128]{1,0:T(8,128)S(1)}) custom-call(s32[1]{0:T(128)} %bitcast.1.refs_0_, bf16[2048,1152]{1,0:T(8,128)(2,1)} %get-tuple-element.104.refs_1_.refs_2_.refs_3_, bf16[2048,1152]{1,0:T(8,128)(2,1)} %get-tuple-element.104.refs_1_.refs_2_.refs_3_, ...), custom_call_target="tpu_custom_call" | custom-call | flops 409600000 | bytes 4194304 | tf_op jit(solution)/shard_map/pallas_call | solution.py:812
  370.5 11.3 %convolution_convert_fusion = bf16[1024,1664]{1,0:T(8,128)(2,1)S(1)} fusion(bf16[2048,1024]{1,0:T(8,128)(2,1)S(1)} %copy-done.14, bf16[2048,1664]{1,0:T(8,128)(2,1)} %get-tuple-element.162), kind=kOutput, calls=%fused_computation.4 | convolution fusion | flops 6981025792 | bytes 14417920 | tf_op jit(solution)/shard_map/dot_general | solution.py:32
  411.1 5.3 %fusion.14 = f32[1024,1024]{1,0:T(8,128)S(1)} fusion(f32[1024,1024]{1,0:T(8,128)S(1)} %fusion.28, bf16[1024,2176]{1,0:T(8,128)(2,1)S(1)} %bitcast.124, bf16[2048,1664]{1,0:T(8,128)(2,1)} %get-tuple-element.162), kind=kOutput, calls=%fused_computation.35 | convolution fusion | flops 3222274048 | bytes 14680064 | tf_op jit(solution)/shard_map/dot_general | solution.py:26
  423.7 7.6 %add_convert_fusion.1 = bf16[1024,1024]{1,0:T(8,128)(2,1)S(1)} fusion(f32[1024,1024]{1,0:T(8,128)} %fusion.26, bf16[1024,2176]{1,0:T(8,128)(2,1)} %all-gather.3.cloned.1.call-done.refs_4_.refs_5_.refs_2_, bf16[2048,1664]{1,0:T(8,128)(2,1)} %get-tuple-element.162), kind=kOutput, calls=%fused_computation.3 | convolution fusion | flops 3223322624 | bytes 12582912 | tf_op jit(solution)/shard_map/dot_general | solution.py:26
  431.4 8.8 %collective-permute-done.36 = bf16[128,2304]{1,0:T(8,128)(2,1)S(1)} collective-permute-done((bf16[128,2304]{1,0:T(8,128)(2,1)}, bf16[128,2304]{1,0:T(8,128)(2,1)S(1)}, u32[]{:S(2)}, u32[]{:S(2)}) %collective-permute-start.36) | collective-permute-done | bytes 589856 | tf_op jit(solution)/shard_map/ppermute | solution.py:1015
  450.5 15.9 %collective-permute-done.34 = bf16[512,1024]{1,0:T(8,128)(2,1)S(1)} collective-permute-done((bf16[512,1024]{1,0:T(8,128)(2,1)S(1)}, bf16[512,1024]{1,0:T(8,128)(2,1)S(1)}, u32[]{:S(2)}, u32[]{:S(2)}) %collective-permute-start.34) | collective-permute-done | bytes 1048608 | tf_op jit(solution)/shard_map/ppermute | solution.py:1015
  466.4 21.8 %collective-permute-done.35 = bf16[512,1024]{1,0:T(8,128)(2,1)} collective-permute-done((bf16[512,1024]{1,0:T(8,128)(2,1)S(1)}, bf16[512,1024]{1,0:T(8,128)(2,1)}, u32[]{:S(2)}, u32[]{:S(2)}) %collective-permute-start.35) | collective-permute-done | bytes 1048608 | tf_op jit(solution)/shard_map/ppermute | solution.py:1015
  508.3 3.9 shard_map.273
  (310 shorter events, 148.4 us)
Async XLA Ops:
  7.2 85.9 %all-gather.3.cloned.1.call-start = ((), (), s32[]{:S(2)}) async-start(), calls=%async_computation.2 | async-start | bytes 5013504 | tf_op jit(solution)/shard_map/all_gather | solution.py:1018
  13.6 172.7 %all-gather.5.cloned.1.call-start = ((), (), s32[]{:S(2)}) async-start(), calls=%async_computation.3 | async-start | bytes 5308416 | tf_op jit(solution)/shard_map/all_gather | solution.py:1018
  13.7 27.1 %collective-permute-start.1 = (bf16[512,1024]{1,0:T(8,128)(2,1)S(1)}, bf16[512,1024]{1,0:T(8,128)(2,1)}, u32[]{:S(2)}, u32[]{:S(2)}) collective-permute-start(bf16[512,1024]{1,0:T(8,128)(2,1)S(1)} %bitcast.120), channel_id=1, source_target_pairs={{0,16},{8,24},{16,0},{24,8},{1,17},{9,25},{17,1},{25,9},{2,18},{10... | collective-permute-start | bytes 3145736 | tf_op jit(solution)/shard_map/ppermute | solution.py:1015
  16.7 45.7 %collective-permute-start.4 = (bf16[512,1024]{1,0:T(8,128)(2,1)}, bf16[512,1024]{1,0:T(8,128)(2,1)}, u32[]{:S(2)}, u32[]{:S(2)}) collective-permute-start(bf16[512,1024]{1,0:T(8,128)(2,1)} %bitcast.139), channel_id=1, source_target_pairs={{0,16},{8,24},{16,0},{24,8},{1,17},{9,25},{17,1},{25,9},{2,18},{10... | collective-permute-start | bytes 3145736 | tf_op jit(solution)/shard_map/ppermute | solution.py:1015
  16.7 48.1 %collective-permute-start = (bf16[512,1024]{1,0:T(8,128)(2,1)S(1)}, bf16[512,1024]{1,0:T(8,128)(2,1)}, u32[]{:S(2)}, u32[]{:S(2)}) collective-permute-start(bf16[512,1024]{1,0:T(8,128)(2,1)S(1)} %bitcast.121), channel_id=1, source_target_pairs={{0,8},{8,0},{16,24},{24,16},{1,9},{9,1},{17,25},{25,17},{2,10},{10... | collective-permute-start | bytes 3145736 | tf_op jit(solution)/shard_map/ppermute | solution.py:1015
  16.7 48.1 %collective-permute-start.3 = (bf16[512,1024]{1,0:T(8,128)(2,1)}, bf16[512,1024]{1,0:T(8,128)(2,1)}, u32[]{:S(2)}, u32[]{:S(2)}) collective-permute-start(bf16[512,1024]{1,0:T(8,128)(2,1)} %bitcast.140), channel_id=1, source_target_pairs={{0,8},{8,0},{16,24},{24,16},{1,9},{9,1},{17,25},{25,17},{2,10},{10... | collective-permute-start | bytes 3145736 | tf_op jit(solution)/shard_map/ppermute | solution.py:1015
  40.7 24.1 %collective-permute-start.2 = (bf16[512,1024]{1,0:T(8,128)(2,1)}, bf16[512,1024]{1,0:T(8,128)(2,1)}, u32[]{:S(2)}, u32[]{:S(2)}) collective-permute-start(bf16[512,1024]{1,0:T(8,128)(2,1)} %collective-permute-done.1.refs_2_), channel_id=1, source_target_pairs={{0,8},{8,0},{16,24},{24,16},{1,9},{9,1},{17,25},{25,17},{2,10},{10... | collective-permute-start | bytes 3145736 | tf_op jit(solution)/shard_map/ppermute | solution.py:1015
  93.1 329.6 %reduce-scatter.5.cloned.1.call-start = ((), (), s32[]{:S(2)}) async-start(), calls=%async_computation.5 | async-start | bytes 5308416 | tf_op jit(solution)/shard_map/reduce_scatter | solution.py:1021
  108.9 32.4 %collective-permute-start.6 = (bf16[1,512,256]{2,1,0:T(8,128)(2,1)S(1)}, bf16[1,512,256]{2,1,0:T(8,128)(2,1)S(1)}, u32[]{:S(2)}, u32[]{:S(2)}) collective-permute-start(bf16[1,512,256]{2,1,0:T(8,128)(2,1)S(1)} %get-tuple-element.257), channel_id=1, source_target_pairs={{0,8},{8,0},{16,24},{24,16},{1,9},{9,1},{17,25},{25,17},{2,10},{10... | collective-permute-start | bytes 786440 | tf_op jit(solution)/shard_map/ppermute | solution.py:1015
  109.0 32.3 %collective-permute-start.7 = (bf16[1,512,256]{2,1,0:T(8,128)(2,1)S(1)}, bf16[1,512,256]{2,1,0:T(8,128)(2,1)S(1)}, u32[]{:S(2)}, u32[]{:S(2)}) collective-permute-start(bf16[1,512,256]{2,1,0:T(8,128)(2,1)S(1)} %get-tuple-element.256), channel_id=1, source_target_pairs={{0,16},{8,24},{16,0},{24,8},{1,17},{9,25},{17,1},{25,9},{2,18},{10... | collective-permute-start | bytes 786440 | tf_op jit(solution)/shard_map/ppermute | solution.py:1015
  110.5 30.8 %collective-permute-start.8 = (bf16[1,512,256]{2,1,0:T(8,128)(2,1)S(1)}, bf16[1,512,256]{2,1,0:T(8,128)(2,1)S(1)}, u32[]{:S(2)}, u32[]{:S(2)}) collective-permute-start(bf16[1,512,256]{2,1,0:T(8,128)(2,1)S(1)} %get-tuple-element.255), channel_id=1, source_target_pairs={{0,24},{8,16},{16,8},{24,0},{1,25},{9,17},{17,9},{25,1},{2,26},{10... | collective-permute-start | bytes 786440 | tf_op jit(solution)/shard_map/ppermute | solution.py:1015
  157.5 25.5 %collective-permute-start.11 = (bf16[512,1024]{1,0:T(8,128)(2,1)S(1)}, bf16[512,1024]{1,0:T(8,128)(2,1)S(1)}, u32[]{:S(2)}, u32[]{:S(2)}) collective-permute-start(bf16[512,1024]{1,0:T(8,128)(2,1)S(1)} %add_convert_fusion.6), channel_id=1, source_target_pairs={{0,16},{8,24},{16,0},{24,8},{1,17},{9,25},{17,1},{25,9},{2,18},{10... | collective-permute-start | bytes 3145736 | tf_op jit(solution)/shard_map/ppermute | solution.py:1015
  186.2 25.8 %collective-permute-start.12 = (bf16[512,1024]{1,0:T(8,128)(2,1)}, bf16[512,1024]{1,0:T(8,128)(2,1)S(1)}, u32[]{:S(2)}, u32[]{:S(2)}) collective-permute-start(bf16[512,1024]{1,0:T(8,128)(2,1)} %multiply_convert_fusion.refs_0_), channel_id=1, source_target_pairs={{0,16},{8,24},{16,0},{24,8},{1,17},{9,25},{17,1},{25,9},{2,18},{10... | collective-permute-start | bytes 3145736 | tf_op jit(solution)/shard_map/ppermute | solution.py:1015
  246.1 25.8 %collective-permute-start.17 = (bf16[512,1024]{1,0:T(8,128)(2,1)}, bf16[512,1024]{1,0:T(8,128)(2,1)}, u32[]{:S(2)}, u32[]{:S(2)}) collective-permute-start(bf16[512,1024]{1,0:T(8,128)(2,1)} %add_convert_fusion.5), channel_id=1, source_target_pairs={{0,16},{8,24},{16,0},{24,8},{1,17},{9,25},{17,1},{25,9},{2,18},{10... | collective-permute-start | bytes 3145736 | tf_op jit(solution)/shard_map/ppermute | solution.py:1015
  271.9 216.3 %reduce-scatter.3.cloned.1.call-start = ((), (), s32[]{:S(2)}) async-start(), calls=%async_computation.4 | async-start | bytes 5013504 | tf_op jit(solution)/shard_map/reduce_scatter | solution.py:1021
  281.4 25.2 %collective-permute-start.18 = (bf16[512,1024]{1,0:T(8,128)(2,1)S(1)}, bf16[512,1024]{1,0:T(8,128)(2,1)S(1)}, u32[]{:S(2)}, u32[]{:S(2)}) collective-permute-start(bf16[512,1024]{1,0:T(8,128)(2,1)S(1)} %get-tuple-element.228.refs_0_), channel_id=1, source_target_pairs={{0,16},{8,24},{16,0},{24,8},{1,17},{9,25},{17,1},{25,9},{2,18},{10... | collective-permute-start | bytes 3145736 | tf_op jit(solution)/shard_map/ppermute | solution.py:1015
  323.9 57.9 %collective-permute-start.24 = (bf16[1,512,256]{2,1,0:T(8,128)(2,1)S(1)}, bf16[1,512,256]{2,1,0:T(8,128)(2,1)S(1)}, u32[]{:S(2)}, u32[]{:S(2)}) collective-permute-start(bf16[1,512,256]{2,1,0:T(8,128)(2,1)S(1)} %get-tuple-element.249), channel_id=1, source_target_pairs={{0,8},{8,0},{16,24},{24,16},{1,9},{9,1},{17,25},{25,17},{2,10},{10... | collective-permute-start | bytes 786440 | tf_op jit(solution)/shard_map/ppermute | solution.py:1015
  324.0 57.8 %collective-permute-start.25 = (bf16[1,512,256]{2,1,0:T(8,128)(2,1)S(1)}, bf16[1,512,256]{2,1,0:T(8,128)(2,1)S(1)}, u32[]{:S(2)}, u32[]{:S(2)}) collective-permute-start(bf16[1,512,256]{2,1,0:T(8,128)(2,1)S(1)} %get-tuple-element.248), channel_id=1, source_target_pairs={{0,16},{8,24},{16,0},{24,8},{1,17},{9,25},{17,1},{25,9},{2,18},{10... | collective-permute-start | bytes 786440 | tf_op jit(solution)/shard_map/ppermute | solution.py:1015
  325.5 56.3 %collective-permute-start.26 = (bf16[1,512,256]{2,1,0:T(8,128)(2,1)S(1)}, bf16[1,512,256]{2,1,0:T(8,128)(2,1)S(1)}, u32[]{:S(2)}, u32[]{:S(2)}) collective-permute-start(bf16[1,512,256]{2,1,0:T(8,128)(2,1)S(1)} %get-tuple-element.247), channel_id=1, source_target_pairs={{0,24},{8,16},{16,8},{24,0},{1,25},{9,17},{17,9},{25,1},{2,26},{10... | collective-permute-start | bytes 786440 | tf_op jit(solution)/shard_map/ppermute | solution.py:1015
  394.0 47.9 %collective-permute-start.19 = (bf16[512,1024]{1,0:T(8,128)(2,1)}, bf16[512,1024]{1,0:T(8,128)(2,1)}, u32[]{:S(2)}, u32[]{:S(2)}) collective-permute-start(bf16[512,1024]{1,0:T(8,128)(2,1)} %slice.105), channel_id=1, source_target_pairs={{0,8},{8,0},{16,24},{24,16},{1,9},{9,1},{17,25},{25,17},{2,10},{10... | collective-permute-start | bytes 3145736 | tf_op jit(solution)/shard_map/ppermute | solution.py:1015
  402.8 39.5 %collective-permute-start.21 = (bf16[512,1024]{1,0:T(8,128)(2,1)}, bf16[512,1024]{1,0:T(8,128)(2,1)}, u32[]{:S(2)}, u32[]{:S(2)}) collective-permute-start(bf16[512,1024]{1,0:T(8,128)(2,1)} %add_convert_fusion.4), channel_id=1, source_target_pairs={{0,16},{8,24},{16,0},{24,8},{1,17},{9,25},{17,1},{25,9},{2,18},{10... | collective-permute-start | bytes 3145736 | tf_op jit(solution)/shard_map/ppermute | solution.py:1015
  440.4 26.0 %collective-permute-start.34 = (bf16[512,1024]{1,0:T(8,128)(2,1)S(1)}, bf16[512,1024]{1,0:T(8,128)(2,1)S(1)}, u32[]{:S(2)}, u32[]{:S(2)}) collective-permute-start(bf16[512,1024]{1,0:T(8,128)(2,1)S(1)} %get-tuple-element.241), channel_id=1, source_target_pairs={{0,16},{8,24},{16,0},{24,8},{1,17},{9,25},{17,1},{25,9},{2,18},{10... | collective-permute-start | bytes 3145736 | tf_op jit(solution)/shard_map/ppermute | solution.py:1015
  441.8 46.4 %collective-permute-start.35 = (bf16[512,1024]{1,0:T(8,128)(2,1)S(1)}, bf16[512,1024]{1,0:T(8,128)(2,1)}, u32[]{:S(2)}, u32[]{:S(2)}) collective-permute-start(bf16[512,1024]{1,0:T(8,128)(2,1)S(1)} %get-tuple-element.240), channel_id=1, source_target_pairs={{0,24},{8,16},{16,8},{24,0},{1,25},{9,17},{17,9},{25,1},{2,26},{10... | collective-permute-start | bytes 3145736 | tf_op jit(solution)/shard_map/ppermute | solution.py:1015
  442.4 45.9 %collective-permute-start.33 = (bf16[512,1024]{1,0:T(8,128)(2,1)S(1)}, bf16[512,1024]{1,0:T(8,128)(2,1)}, u32[]{:S(2)}, u32[]{:S(2)}) collective-permute-start(bf16[512,1024]{1,0:T(8,128)(2,1)S(1)} %copy-done.24), channel_id=1, source_target_pairs={{0,8},{8,0},{16,24},{24,16},{1,9},{9,1},{17,25},{25,17},{2,10},{10... | collective-permute-start | bytes 3145736 | tf_op jit(solution)/shard_map/ppermute | solution.py:1015
  (73 other events, 745.7 us)
Sparse Core Ops, SparseCore 0:
  13.7 79.3 all-gather.2
  95.8 78.0 all-gather.4
  272.0 93.3 reduce-scatter.4
  386.0 95.1 reduce-scatter.2

commit v8 on v7

--- a/solution.py
+++ b/solution.py
@@ -1201,27 +1201,33 @@
         model, -1
     )
     count = own_tokens.shape[0]
-    result = after_mix + scatter_seq(
-        [down_near[:count], down_near[count:], down_far[:count], down_far[count:]]
-    )[0]
+    down_across = down_far[:count].astype(wide) + flip(down_far[count:], 1).astype(wide)
+    down_across, grad_gated = tie((lower(down_across), grad_gated))
+    down_across = flip(down_across, 2)
+    down_beside = flip(down_near[count:], 1)
     grad_in, grad_taps, grad_gain, grad_small = mixer_backward(
         heads, parts, place_row, proj, out_gate, taps, coefficients, gain, [mixed, *kept],
         grad_gated, interpret
+    )
+    grad_taps, down_across, down_beside = tie((grad_taps, down_across, down_beside))
+    result = (
+        after_mix
+        + down_near[:count].astype(wide)
+        + down_beside.astype(wide)
+        + down_across.astype(wide)
     )
     grad_w_in = jnp.concatenate([lower(over_rows(normed_one, grad_in)), grad_out], axis=1)
     grad_in, grad_w_in = tie((grad_in, grad_w_in))
     grad_w_in = sum_dp(grad_w_in)
     split = width + values
-    one_far, one_near = (
-        by_transpose(grad_in[span, :split], w_all[:, :split])
-        + by_transpose(grad_in[span, split:], w_all[:, rates_at:])
-        for span in (slice(2 * count, None), slice(0, 2 * count))
-    )
+    w_cat = jnp.concatenate([w_all[:, :split], w_all[:, rates_at:]], axis=1)
+    one_far = lower(by_transpose(grad_in[2 * count :], w_cat))
+    one_near = lower(by_transpose(grad_in[: 2 * count], w_cat))
     first_pieces = [
         one_near[:count],
-        flip(lower(one_near[count:]), 1),
-        flip(lower(one_far[:count]), 2),
-        flip(lower(one_far[count:]), 3),
+        flip(one_near[count:], 1),
+        flip(one_far[:count], 2),
+        flip(one_far[count:], 3),
     ]
 
     taps_full = lax.dynamic_update_slice_in_dim(
@@ -1292,7 +1298,7 @@
         rows,
         inverse_one,
         first_gain,
-        sum([item.astype(wide) for item in first_pieces[1:]], first_pieces[0]),
+        sum([item.astype(wide) for item in first_pieces]),
     )
     grad_rows = lower(grad_after + back_one)[:, None, :]
     def along(weights, grads):

time: 529 us -> 534 us (level)
  waiting for transfers between devices: 201 us -> 210 us
  matrix products: 49.4 us -> 44 us
    ppermute x39, waiting for transfers between devices: 168 us -> 181 us  [flip(): return lax.ppermute(array, 'seq', [(i, i ^ bit) for i in range(parts)])]
    dot_general x4 -> x2, matrix products: 18.4 us -> 14.3 us  [by_transpose(): lax.dot_general(left, right, (((1,), (1,)), ((), ())), preferred_element_...]
    unnamed x109 -> x101, local copies, waits for them, and re-layouts: 14.4 us -> 16.1 us
  transfers between devices with their start and end apart: 47 -> 47, of which waited for: 21 -> 20; matrix products, arithmetic and copies ran while one was open for 19% -> 18% of each run, Pallas kernels for 26% -> 26%
where the time goes in v8:
time: 534 us; the launch traced here: 527 us
  waiting for transfers between devices  210 us (39%)
  Pallas kernels  154 us (29%)
  matrix products  44 us (8%)
  local copies, waits for them, and re-layouts  42.1 us (8%)
  other arithmetic  33.4 us (6%)
  starting transfers between devices  28.8 us (5%)
  between operations  15 us (3%)
    ppermute x39, waiting for transfers between devices, flip(): return lax.ppermute(array, 'seq', [(i, i ^ bit) for i in range(parts)])  181 us
    pallas_call x1, Pallas kernels, mixer_backward(): pl.pallas_call(lambda *refs: backward_kernel(heads, *refs), grid_spec=plt...  44.5 us
    pallas_call x2, Pallas kernels, ffn_rows(): row_call(lambda *refs: ffn_kernel(steps, *refs), steps, [fixed(item.shape...  31.1 us
    pallas_call x1, Pallas kernels, mixer_forward(): pl.pallas_call(lambda *refs: forward_kernel(heads, *refs), grid_spec=pltp...  30.4 us
    all_gather x2, waiting for transfers between devices, over_dp(): return lax.all_gather(array, 'dp', axis=0, tiled=True)  27.7 us
    dot_general x5, matrix products, over_rows(): lax.dot_general(left, right, (((0,), (0,)), ((), ())), preferred_element_...  24.7 us
    ppermute x39, starting transfers between devices, flip(): return lax.ppermute(array, 'seq', [(i, i ^ bit) for i in range(parts)])  23.5 us
    unnamed x101, local copies, waits for them, and re-layouts  16.1 us
  transfers between devices with their start and end apart: 47, of which 20 were waited for; matrix products, arithmetic and copies ran while one was open for 18% of the time, Pallas kernels for 26%

profile of v8, /device:TPU:0, one launch (start us, length us, event | category | flops | bytes accessed | tf_op | source)
XLA Modules:
  0.0 526.9 jit_solution(15383122822728963732)
XLA Ops:
  17.2 23.5 %collective-permute-done.1.refs_2_ = bf16[512,1024]{1,0:T(8,128)(2,1)} collective-permute-done((bf16[512,1024]{1,0:T(8,128)(2,1)S(1)}, bf16[512,1024]{1,0:T(8,128)(2,1)}, u32[]{:S(2)}, u32[]{:S(2)}) %collective-permute-start.1) | collective-permute-done | bytes 1048608 | tf_op jit(solution)/shard_map/ppermute | solution.py:1015
  40.7 21.6 %collective-permute-done.4.refs_2_ = bf16[512,1024]{1,0:T(8,128)(2,1)} collective-permute-done((bf16[512,1024]{1,0:T(8,128)(2,1)}, bf16[512,1024]{1,0:T(8,128)(2,1)}, u32[]{:S(2)}, u32[]{:S(2)}) %collective-permute-start.4) | collective-permute-done | bytes 1048608 | tf_op jit(solution)/shard_map/ppermute | solution.py:1015
  65.4 27.7 %all-gather.3.cloned.1.call-done.refs_4_.refs_5_.refs_2_ = bf16[1024,2176]{1,0:T(8,128)(2,1)} async-done(((bf16[128,2176]{1,0:T(8,128)(2,1)}), bf16[1024,2176]{1,0:T(8,128)(2,1)}) %all-gather.3.cloned.1.call-update) | async-done | bytes 4456464 | tf_op jit(solution)/shard_map/all_gather | solution.py:1018
  96.5 11.0 %shard_map.262 = (bf16[2048,1024]{1,0:T(8,128)(2,1)}, bf16[2048,1152]{1,0:T(8,128)(2,1)}) custom-call(bf16[512,1024]{1,0:T(8,128)(2,1)S(1)} %bitcast.122, bf16[512,1024]{1,0:T(8,128)(2,1)} %collective-permute-done.refs_1_, bf16[512,1024]{1,0:T(8,128)(2,1)} %collective-permute-done.1.refs_2_, bf16[512,1024]{1,0:T(8,128)(2,1)} %collective-permute-done.2.refs_3_, ...), custom_call_target="tpu_custom_call" | custom-call | flops 2359296 | bytes 2304 | tf_op jit(solution)/shard_map/pallas_call | solution.py:674
  112.1 30.4 %shard_map.263 = (bf16[2048,512]{1,0:T(8,128)(2,1)}, bf16[8,2,256,256]{3,2,1,0:T(8,128)(2,1)}, bf16[8,2,256,128]{3,2,1,0:T(8,128)(2,1)S(1)}, bf16[2048,512]{1,0:...) custom-call(s32[1]{0:T(128)} %bitcast.1.refs_0_, ...), custom_call_target="tpu_custom_call" | custom-call | flops 409600000 | bytes 4194304 | tf_op jit(solution)/shard_map/pallas_call | solution.py:593
  144.7 6.5 %shard_map.264 = (bf16[2048,512]{1,0:T(8,128)(2,1)}, f32[2048,512]{1,0:T(8,128)}, bf16[512,1024]{1,0:T(8,128)(2,1)S(1)}, bf16[512,1024]{1,0:T(8,128)(2,1)}) custom-call(bf16[2048,512]{1,0:T(8,128)(2,1)} %get-tuple-element.110.refs_0_.refs_8_, bf16[2048,1024]{1,0:T(8,128)(2,1)} %get-tuple-element.111.refs_1_, ...), custom_call_target="tpu_custom_call" | custom-call | flops 1048576 | bytes 2048 | tf_op jit(solution)/shard_map/pallas_call | solution.py:700
  151.5 6.5 %shard_map.265 = (bf16[2048,512]{1,0:T(8,128)(2,1)}, f32[2048,512]{1,0:T(8,128)}, bf16[512,1024]{1,0:T(8,128)(2,1)S(1)}, bf16[512,1024]{1,0:T(8,128)(2,1)}) custom-call(bf16[2048,512]{1,0:T(8,128)(2,1)} %get-tuple-element.110.refs_0_.refs_8_, bf16[2048,1024]{1,0:T(8,128)(2,1)} %get-tuple-element.111.refs_1_, ...), custom_call_target="tpu_custom_call", output_to_operand_aliasing={{0}: (5, {}), {1}: (6, {})} | custom-call | flops 1048576 | bytes 2048 | tf_op jit(solution)/shard_map/pallas_call | solution.py:700
  161.0 23.2 %collective-permute-done.11 = bf16[512,1024]{1,0:T(8,128)(2,1)S(1)} collective-permute-done((bf16[512,1024]{1,0:T(8,128)(2,1)S(1)}, bf16[512,1024]{1,0:T(8,128)(2,1)S(1)}, u32[]{:S(2)}, u32[]{:S(2)}) %collective-permute-start.11) | collective-permute-done | bytes 1048608 | tf_op jit(solution)/shard_map/ppermute | solution.py:1015
  194.9 15.7 %shard_map.267 = (bf16[1024,1024]{1,0:T(8,128)(2,1)}, bf16[1024,1024]{1,0:T(8,128)(2,1)}, bf16[1024,768]{1,0:T(8,128)(2,1)}, bf16[1024,1536]{1,0:T(8,128)(2,1)},...) custom-call(bf16[512,1024]{1,0:T(8,128)(2,1)} %multiply_convert_fusion.refs_0_, bf16[512,1024]{1,0:T(8,128)(2,1)} %copy-done.34, ...), custom_call_target="tpu_custom_call" | custom-call | flops 8053063680 | bytes 7864320 | tf_op jit(solution)/shard_map/pallas_call | solution.py:728
  216.8 15.4 %shard_map.268 = (bf16[1024,1024]{1,0:T(8,128)(2,1)}, bf16[1024,1024]{1,0:T(8,128)(2,1)}, bf16[1024,768]{1,0:T(8,128)(2,1)}, bf16[1024,1536]{1,0:T(8,128)(2,1)},...) custom-call(bf16[512,1024]{1,0:T(8,128)(2,1)} %copy-done.33, bf16[512,1024]{1,0:T(8,128)(2,1)} %copy-done.36, ...), custom_call_target="tpu_custom_call" | custom-call | flops 8053063680 | bytes 7864320 | tf_op jit(solution)/shard_map/pallas_call | solution.py:728
  232.5 4.0 fusion.34
  255.0 18.0 %collective-permute-done.17 = bf16[512,1024]{1,0:T(8,128)(2,1)} collective-permute-done((bf16[512,1024]{1,0:T(8,128)(2,1)}, bf16[512,1024]{1,0:T(8,128)(2,1)}, u32[]{:S(2)}, u32[]{:S(2)}) %collective-permute-start.17) | collective-permute-done | bytes 1048608 | tf_op jit(solution)/shard_map/ppermute | solution.py:1015
  288.8 18.9 %collective-permute-done.18.refs_0_ = bf16[512,1024]{1,0:T(8,128)(2,1)S(1)} collective-permute-done((bf16[512,1024]{1,0:T(8,128)(2,1)S(1)}, bf16[512,1024]{1,0:T(8,128)(2,1)S(1)}, u32[]{:S(2)}, u32[]{:S(2)}) %collective-permute-start.18) | collective-permute-done | bytes 1048608 | tf_op jit(solution)/shard_map/ppermute | solution.py:1015
  308.7 6.0 %shard_map.269 = (f32[2048,512]{1,0:T(8,128)}, f32[512,1024]{1,0:T(8,128)}) custom-call(bf16[512,1024]{1,0:T(8,128)(2,1)S(1)} %get-tuple-element.238.refs_0_, bf16[512,1024]{1,0:T(8,128)(2,1)} %copy-done.35, bf16[2048,512]{1,0:T(8,128)(2,1)} %get-tuple-element.155.refs_2_, bf16[512,1024]{1,0:T(8,128)(2,1)} %bitcast.125), custom_call_target="tpu_custom_call" | custom-call | flops 2147483648 | bytes 524288 | tf_op jit(solution)/shard_map/pallas_call | solution.py:758
  318.4 6.5 %shard_map.270 = (f32[2048,512]{1,0:T(8,128)}, bf16[4,512,256]{2,1,0:T(8,128)(2,1)S(1)}) custom-call(bf16[512,1024]{1,0:T(8,128)(2,1)} %copy-done.25, bf16[512,1024]{1,0:T(8,128)(2,1)} %copy-done.26, bf16[2048,512]{1,0:T(8,128)(2,1)} %get-tuple-element.155.refs_2_, bf16[512,1024]{1,0:T(8,128)(2,1)} %bitcast.126, ...), custom_call_target="tpu_custom_call", output_to_operand_aliasing={{0}: (5, {})} | custom-call | flops 2147483648 | bytes 524288 | tf_op jit(solution)/shard_map/pallas_call | solution.py:758
  328.3 44.5 %shard_map.271 = (bf16[2048,1664]{1,0:T(8,128)(2,1)}, f32[8,1024]{1,0:T(8,128)S(1)}, f32[8,256]{1,0:T(8,128)S(1)}, f32[8,128]{1,0:T(8,128)S(1)}) custom-call(s32[1]{0:T(128)} %bitcast.1.refs_0_, bf16[2048,1152]{1,0:T(8,128)(2,1)} %get-tuple-element.109.refs_1_.refs_2_.refs_3_, bf16[2048,1152]{1,0:T(8,128)(2,1)} %get-tuple-element.109.refs_1_.refs_2_.refs_3_, ...), custom_call_target="tpu_custom_call" | custom-call | flops 409600000 | bytes 4194304 | tf_op jit(solution)/shard_map/pallas_call | solution.py:812
  372.8 11.3 %convolution_convert_fusion = bf16[1024,1664]{1,0:T(8,128)(2,1)S(1)} fusion(bf16[2048,1024]{1,0:T(8,128)(2,1)S(1)} %copy-done.11, bf16[2048,1664]{1,0:T(8,128)(2,1)} %get-tuple-element.172), kind=kOutput, calls=%fused_computation.3 | convolution fusion | flops 6981025792 | bytes 14417920 | tf_op jit(solution)/shard_map/dot_general | solution.py:32
  397.1 6.9 %fusion.12 = bf16[1024,1024]{1,0:T(8,128)(2,1)S(1)} fusion(bf16[1024,128]{1,0:T(8,128)(2,1)S(1)} %slice.105, bf16[1024,1536]{1,0:T(8,128)(2,1)} %slice.104, bf16[2048,1664]{1,0:T(8,128)(2,1)} %get-tuple-element.172), kind=kOutput, calls=%fused_computation.32 | convolution fusion | flops 3497525248 | bytes 8912896 | tf_op jit(solution)/shard_map/dot_general | solution.py:26
  406.3 7.4 %fusion.15 = bf16[1024,1024]{1,0:T(8,128)(2,1)} fusion(bf16[1024,128]{1,0:T(8,128)(2,1)S(1)} %slice.105, bf16[1024,1536]{1,0:T(8,128)(2,1)S(1)} %copy-done.13, bf16[2048,1664]{1,0:T(8,128)(2,1)} %get-tuple-element.172), kind=kOutput, calls=%fused_computation.33 | convolution fusion | flops 3497525248 | bytes 8912896 | tf_op jit(solution)/shard_map/dot_general | solution.py:26
  413.7 7.2 %collective-permute-done.22 = bf16[512,1024]{1,0:T(8,128)(2,1)} collective-permute-done((bf16[512,1024]{1,0:T(8,128)(2,1)}, bf16[512,1024]{1,0:T(8,128)(2,1)}, u32[]{:S(2)}, u32[]{:S(2)}) %collective-permute-start.22) | collective-permute-done | bytes 1048608 | tf_op jit(solution)/shard_map/ppermute | solution.py:1015
  426.1 11.0 %collective-permute-done.29 = f32[136,128]{1,0:T(8,128)S(1)} collective-permute-done((f32[136,128]{1,0:T(8,128)S(1)}, f32[136,128]{1,0:T(8,128)S(1)}, u32[]{:S(2)}, u32[]{:S(2)}) %collective-permute-start.29) | collective-permute-done | bytes 69664 | tf_op jit(solution)/shard_map/ppermute | solution.py:1015
  453.8 20.0 %collective-permute-done.34 = bf16[512,1024]{1,0:T(8,128)(2,1)} collective-permute-done((bf16[512,1024]{1,0:T(8,128)(2,1)S(1)}, bf16[512,1024]{1,0:T(8,128)(2,1)}, u32[]{:S(2)}, u32[]{:S(2)}) %collective-permute-start.34) | collective-permute-done | bytes 1048608 | tf_op jit(solution)/shard_map/ppermute | solution.py:1015
  473.8 20.6 %collective-permute-done.35 = bf16[512,1024]{1,0:T(8,128)(2,1)} collective-permute-done((bf16[512,1024]{1,0:T(8,128)(2,1)S(1)}, bf16[512,1024]{1,0:T(8,128)(2,1)}, u32[]{:S(2)}, u32[]{:S(2)}) %collective-permute-start.35) | collective-permute-done | bytes 1048608 | tf_op jit(solution)/shard_map/ppermute | solution.py:1015
  499.8 4.1 fusion.20
  (298 shorter events, 143.9 us)
Async XLA Ops:
  7.2 85.9 %all-gather.3.cloned.1.call-start = ((), (), s32[]{:S(2)}) async-start(), calls=%async_computation.2 | async-start | bytes 5013504 | tf_op jit(solution)/shard_map/all_gather | solution.py:1018
  13.6 173.8 %all-gather.5.cloned.1.call-start = ((), (), s32[]{:S(2)}) async-start(), calls=%async_computation.3 | async-start | bytes 5308416 | tf_op jit(solution)/shard_map/all_gather | solution.py:1018
  13.6 27.1 %collective-permute-start.1 = (bf16[512,1024]{1,0:T(8,128)(2,1)S(1)}, bf16[512,1024]{1,0:T(8,128)(2,1)}, u32[]{:S(2)}, u32[]{:S(2)}) collective-permute-start(bf16[512,1024]{1,0:T(8,128)(2,1)S(1)} %bitcast.120), channel_id=1, source_target_pairs={{0,16},{8,24},{16,0},{24,8},{1,17},{9,25},{17,1},{25,9},{2,18},{10... | collective-permute-start | bytes 3145736 | tf_op jit(solution)/shard_map/ppermute | solution.py:1015
  16.6 45.7 %collective-permute-start.4 = (bf16[512,1024]{1,0:T(8,128)(2,1)}, bf16[512,1024]{1,0:T(8,128)(2,1)}, u32[]{:S(2)}, u32[]{:S(2)}) collective-permute-start(bf16[512,1024]{1,0:T(8,128)(2,1)} %bitcast.137), channel_id=1, source_target_pairs={{0,16},{8,24},{16,0},{24,8},{1,17},{9,25},{17,1},{25,9},{2,18},{10... | collective-permute-start | bytes 3145736 | tf_op jit(solution)/shard_map/ppermute | solution.py:1015
  16.7 48.1 %collective-permute-start = (bf16[512,1024]{1,0:T(8,128)(2,1)S(1)}, bf16[512,1024]{1,0:T(8,128)(2,1)}, u32[]{:S(2)}, u32[]{:S(2)}) collective-permute-start(bf16[512,1024]{1,0:T(8,128)(2,1)S(1)} %bitcast.121), channel_id=1, source_target_pairs={{0,8},{8,0},{16,24},{24,16},{1,9},{9,1},{17,25},{25,17},{2,10},{10... | collective-permute-start | bytes 3145736 | tf_op jit(solution)/shard_map/ppermute | solution.py:1015
  16.7 48.1 %collective-permute-start.3 = (bf16[512,1024]{1,0:T(8,128)(2,1)}, bf16[512,1024]{1,0:T(8,128)(2,1)}, u32[]{:S(2)}, u32[]{:S(2)}) collective-permute-start(bf16[512,1024]{1,0:T(8,128)(2,1)} %bitcast.138), channel_id=1, source_target_pairs={{0,8},{8,0},{16,24},{24,16},{1,9},{9,1},{17,25},{25,17},{2,10},{10... | collective-permute-start | bytes 3145736 | tf_op jit(solution)/shard_map/ppermute | solution.py:1015
  40.7 24.1 %collective-permute-start.2 = (bf16[512,1024]{1,0:T(8,128)(2,1)}, bf16[512,1024]{1,0:T(8,128)(2,1)}, u32[]{:S(2)}, u32[]{:S(2)}) collective-permute-start(bf16[512,1024]{1,0:T(8,128)(2,1)} %collective-permute-done.1.refs_2_), channel_id=1, source_target_pairs={{0,8},{8,0},{16,24},{24,16},{1,9},{9,1},{17,25},{25,17},{2,10},{10... | collective-permute-start | bytes 3145736 | tf_op jit(solution)/shard_map/ppermute | solution.py:1015
  93.1 327.9 %reduce-scatter.5.cloned.1.call-start = ((), (), s32[]{:S(2)}) async-start(), calls=%async_computation.5 | async-start | bytes 5308416 | tf_op jit(solution)/shard_map/reduce_scatter | solution.py:1021
  110.1 32.3 %collective-permute-start.8 = (bf16[1,512,256]{2,1,0:T(8,128)(2,1)S(1)}, bf16[1,512,256]{2,1,0:T(8,128)(2,1)S(1)}, u32[]{:S(2)}, u32[]{:S(2)}) collective-permute-start(bf16[1,512,256]{2,1,0:T(8,128)(2,1)S(1)} %get-tuple-element.267), channel_id=1, source_target_pairs={{0,24},{8,16},{16,8},{24,0},{1,25},{9,17},{17,9},{25,1},{2,26},{10... | collective-permute-start | bytes 786440 | tf_op jit(solution)/shard_map/ppermute | solution.py:1015
  110.2 32.3 %collective-permute-start.7 = (bf16[1,512,256]{2,1,0:T(8,128)(2,1)S(1)}, bf16[1,512,256]{2,1,0:T(8,128)(2,1)S(1)}, u32[]{:S(2)}, u32[]{:S(2)}) collective-permute-start(bf16[1,512,256]{2,1,0:T(8,128)(2,1)S(1)} %get-tuple-element.268), channel_id=1, source_target_pairs={{0,16},{8,24},{16,0},{24,8},{1,17},{9,25},{17,1},{25,9},{2,18},{10... | collective-permute-start | bytes 786440 | tf_op jit(solution)/shard_map/ppermute | solution.py:1015
  111.8 30.7 %collective-permute-start.6 = (bf16[1,512,256]{2,1,0:T(8,128)(2,1)S(1)}, bf16[1,512,256]{2,1,0:T(8,128)(2,1)S(1)}, u32[]{:S(2)}, u32[]{:S(2)}) collective-permute-start(bf16[1,512,256]{2,1,0:T(8,128)(2,1)S(1)} %get-tuple-element.269), channel_id=1, source_target_pairs={{0,8},{8,0},{16,24},{24,16},{1,9},{9,1},{17,25},{25,17},{2,10},{10... | collective-permute-start | bytes 786440 | tf_op jit(solution)/shard_map/ppermute | solution.py:1015
  158.8 25.4 %collective-permute-start.11 = (bf16[512,1024]{1,0:T(8,128)(2,1)S(1)}, bf16[512,1024]{1,0:T(8,128)(2,1)S(1)}, u32[]{:S(2)}, u32[]{:S(2)}) collective-permute-start(bf16[512,1024]{1,0:T(8,128)(2,1)S(1)} %add_convert_fusion.5), channel_id=1, source_target_pairs={{0,16},{8,24},{16,0},{24,8},{1,17},{9,25},{17,1},{25,9},{2,18},{10... | collective-permute-start | bytes 3145736 | tf_op jit(solution)/shard_map/ppermute | solution.py:1015
  187.4 25.8 %collective-permute-start.12 = (bf16[512,1024]{1,0:T(8,128)(2,1)}, bf16[512,1024]{1,0:T(8,128)(2,1)S(1)}, u32[]{:S(2)}, u32[]{:S(2)}) collective-permute-start(bf16[512,1024]{1,0:T(8,128)(2,1)} %multiply_convert_fusion.refs_0_), channel_id=1, source_target_pairs={{0,16},{8,24},{16,0},{24,8},{1,17},{9,25},{17,1},{25,9},{2,18},{10... | collective-permute-start | bytes 3145736 | tf_op jit(solution)/shard_map/ppermute | solution.py:1015
  247.3 25.8 %collective-permute-start.17 = (bf16[512,1024]{1,0:T(8,128)(2,1)}, bf16[512,1024]{1,0:T(8,128)(2,1)}, u32[]{:S(2)}, u32[]{:S(2)}) collective-permute-start(bf16[512,1024]{1,0:T(8,128)(2,1)} %add_convert_fusion.4), channel_id=1, source_target_pairs={{0,16},{8,24},{16,0},{24,8},{1,17},{9,25},{17,1},{25,9},{2,18},{10... | collective-permute-start | bytes 3145736 | tf_op jit(solution)/shard_map/ppermute | solution.py:1015
  273.0 221.4 %reduce-scatter.3.cloned.1.call-start = ((), (), s32[]{:S(2)}) async-start(), calls=%async_computation.4 | async-start | bytes 5013504 | tf_op jit(solution)/shard_map/reduce_scatter | solution.py:1021
  282.5 25.2 %collective-permute-start.18 = (bf16[512,1024]{1,0:T(8,128)(2,1)S(1)}, bf16[512,1024]{1,0:T(8,128)(2,1)S(1)}, u32[]{:S(2)}, u32[]{:S(2)}) collective-permute-start(bf16[512,1024]{1,0:T(8,128)(2,1)S(1)} %get-tuple-element.238.refs_0_), channel_id=1, source_target_pairs={{0,16},{8,24},{16,0},{24,8},{1,17},{9,25},{17,1},{25,9},{2,18},{10... | collective-permute-start | bytes 3145736 | tf_op jit(solution)/shard_map/ppermute | solution.py:1015
  283.8 23.9 %collective-permute-start.20 = (bf16[512,1024]{1,0:T(8,128)(2,1)S(1)}, bf16[512,1024]{1,0:T(8,128)(2,1)S(1)}, u32[]{:S(2)}, u32[]{:S(2)}) collective-permute-start(bf16[512,1024]{1,0:T(8,128)(2,1)S(1)} %get-tuple-element.238.refs_0_), channel_id=1, source_target_pairs={{0,8},{8,0},{16,24},{24,16},{1,9},{9,1},{17,25},{25,17},{2,10},{10... | collective-permute-start | bytes 3145736 | tf_op jit(solution)/shard_map/ppermute | solution.py:1015
  326.3 57.8 %collective-permute-start.26 = (bf16[1,512,256]{2,1,0:T(8,128)(2,1)S(1)}, bf16[1,512,256]{2,1,0:T(8,128)(2,1)S(1)}, u32[]{:S(2)}, u32[]{:S(2)}) collective-permute-start(bf16[1,512,256]{2,1,0:T(8,128)(2,1)S(1)} %get-tuple-element.259), channel_id=1, source_target_pairs={{0,24},{8,16},{16,8},{24,0},{1,25},{9,17},{17,9},{25,1},{2,26},{10... | collective-permute-start | bytes 786440 | tf_op jit(solution)/shard_map/ppermute | solution.py:1015
  327.4 56.7 %collective-permute-start.25 = (bf16[1,512,256]{2,1,0:T(8,128)(2,1)S(1)}, bf16[1,512,256]{2,1,0:T(8,128)(2,1)S(1)}, u32[]{:S(2)}, u32[]{:S(2)}) collective-permute-start(bf16[1,512,256]{2,1,0:T(8,128)(2,1)S(1)} %get-tuple-element.260), channel_id=1, source_target_pairs={{0,16},{8,24},{16,0},{24,8},{1,17},{9,25},{17,1},{25,9},{2,18},{10... | collective-permute-start | bytes 786440 | tf_op jit(solution)/shard_map/ppermute | solution.py:1015
  328.1 56.0 %collective-permute-start.24 = (bf16[1,512,256]{2,1,0:T(8,128)(2,1)S(1)}, bf16[1,512,256]{2,1,0:T(8,128)(2,1)S(1)}, u32[]{:S(2)}, u32[]{:S(2)}) collective-permute-start(bf16[1,512,256]{2,1,0:T(8,128)(2,1)S(1)} %get-tuple-element.261), channel_id=1, source_target_pairs={{0,8},{8,0},{16,24},{24,16},{1,9},{9,1},{17,25},{25,17},{2,10},{10... | collective-permute-start | bytes 786440 | tf_op jit(solution)/shard_map/ppermute | solution.py:1015
  395.2 25.6 %collective-permute-start.22 = (bf16[512,1024]{1,0:T(8,128)(2,1)}, bf16[512,1024]{1,0:T(8,128)(2,1)}, u32[]{:S(2)}, u32[]{:S(2)}) collective-permute-start(bf16[512,1024]{1,0:T(8,128)(2,1)} %add_convert_fusion.3), channel_id=1, source_target_pairs={{0,16},{8,24},{16,0},{24,8},{1,17},{9,25},{17,1},{25,9},{2,18},{10... | collective-permute-start | bytes 3145736 | tf_op jit(solution)/shard_map/ppermute | solution.py:1015
  421.0 22.4 %collective-permute-start.36 = (bf16[128,2304]{1,0:T(8,128)(2,1)}, bf16[128,2304]{1,0:T(8,128)(2,1)S(1)}, u32[]{:S(2)}, u32[]{:S(2)}) collective-permute-start(bf16[128,2304]{1,0:T(8,128)(2,1)} %reduce-scatter.5.cloned.1.call-done), channel_id=1, source_target_pairs={{0,16},{8,24},{16,0},{24,8},{1,17},{9,25},{17,1},{25,9},{2,18},{10... | collective-permute-start | bytes 1769480 | tf_op jit(solution)/shard_map/ppermute | solution.py:1015
  447.7 26.1 %collective-permute-start.34 = (bf16[512,1024]{1,0:T(8,128)(2,1)S(1)}, bf16[512,1024]{1,0:T(8,128)(2,1)}, u32[]{:S(2)}, u32[]{:S(2)}) collective-permute-start(bf16[512,1024]{1,0:T(8,128)(2,1)S(1)} %get-tuple-element.251), channel_id=1, source_target_pairs={{0,16},{8,24},{16,0},{24,8},{1,17},{9,25},{17,1},{25,9},{2,18},{10... | collective-permute-start | bytes 3145736 | tf_op jit(solution)/shard_map/ppermute | solution.py:1015
  449.2 45.3 %collective-permute-start.35 = (bf16[512,1024]{1,0:T(8,128)(2,1)S(1)}, bf16[512,1024]{1,0:T(8,128)(2,1)}, u32[]{:S(2)}, u32[]{:S(2)}) collective-permute-start(bf16[512,1024]{1,0:T(8,128)(2,1)S(1)} %get-tuple-element.250), channel_id=1, source_target_pairs={{0,24},{8,16},{16,8},{24,0},{1,25},{9,17},{17,9},{25,1},{2,26},{10... | collective-permute-start | bytes 3145736 | tf_op jit(solution)/shard_map/ppermute | solution.py:1015
  (67 other events, 629.7 us)
Sparse Core Ops, SparseCore 0:
  13.7 79.3 all-gather.2
  95.8 78.0 all-gather.4
  273.2 93.5 reduce-scatter.4
  388.4 89.8 reduce-scatter.2
